TPU v7x, 128 devices: a whole 4x4x4 slice. The times are simulated.
128 devices in a mesh: dp: 4 (over x), expert: 32 (over z, y, core).
Axes of the slice: x: 4, y: 4, z: 4, core: 2. Of those that a mesh axis runs over, the one named last changes fastest.
Arguments:
- latent_rows: bfloat16 [24576, 576], P(('dp', 'expert')), may hold values from -6 to 6
- new_rows: bfloat16 [4, 96, 576], P('dp'), may hold values from -6 to 6
- kv_gain: float32 [512], replicated, may hold values from 0.5 to 1.5
- lengths: int32 [384], replicated, may hold values from 32 to 96, as said below
- owners: int32 [384], replicated, may hold values from 0 to 3, as said below
- queries: bfloat16 [4, 96, 64, 576], P('dp'), may hold values from -300 to 300
- w_uv: bfloat16 [64, 512, 128], P('expert'), may hold values from -0.25 to 0.25
- w_out: bfloat16 [8192, 7168], P('expert'), may hold values from -0.0625 to 0.0625
- resid: bfloat16 [4, 96, 7168], P('dp', 'expert'), may hold values from -6 to 6
- moe_gain: float32 [7168], replicated, may hold values from 0.5 to 1.5
- route_ids: int32 [4, 96, 8], P('dp', 'expert'), may hold values from 0 to 31, all different within a row; in each aligned block of 3 rows (0 to 2, 3 to 5, ..., all dimensions but the last counted through in order) at most 2 rows name the same one
- route_weights: float32 [4, 96, 8], P('dp', 'expert'), may hold values from 0.1 to 0.6
- w_gate: bfloat16 [32, 7168, 1024], P('expert', None, 'dp'), may hold values from -0.0625 to 0.0625
- w_up: bfloat16 [32, 7168, 1024], P('expert', None, 'dp'), may hold values from -0.0625 to 0.0625
- w_down: bfloat16 [32, 1024, 7168], P('expert', 'dp'), may hold values from -0.1875 to 0.1875
Outputs:
- decode_cache: bfloat16 [4, 32, 192, 576], P('dp', 'expert')
- decoded: bfloat16 [4, 96, 7168], P('dp', 'expert')
Inputs may be any that keep to these rules, and one draw needn't show every extreme that they name: `lengths`: every length is a positive multiple of 32; together they cover the 24576 prefill rows. `owners`: each group owns exactly 96 requests, of 6144 rows together. `route_ids`: among the 3 tokens of one device, no expert is named by more than 2 tokens.
All inputs are finite; a program needn't handle non-finite values.
Results may differ from a plain program's by a relative error of at most 0.018.
Values may be sent and summed in bfloat16 or wider, within the bound.
No kernel may reach another device: no remote copies, remote signals or barrier semaphores. Data moves between devices by JAX's collectives and lax.ppermute only.
A program may use at most 128 MiB of HBM per device.

v0:
```python
import jax
import jax.numpy as jnp
from jax import lax
from jax.sharding import PartitionSpec as P

LAT = 512


eps = 1e-06
theta = 10000.0
score_scale = 192.0 ** (-0.5)


def table_lookup(table, where_at):
    entries = jnp.arange(table.shape[0], dtype=jnp.int32)
    return jnp.sum(jnp.where(where_at[:, None] == entries[None, :], table[None, :], 0), axis=1)


def unit_request(unit_ids, unit_end):
    return jnp.sum((unit_ids[:, None] >= unit_end[None, :]).astype(jnp.int32), axis=1)


def request_tables(lengths, owners, unit_size):
    unit_len = lengths // unit_size
    unit_end = jnp.cumsum(unit_len)
    unit_start = unit_end - unit_len
    request_order = jnp.arange(lengths.shape[0], dtype=jnp.int32)
    earlier = (owners[None, :] == owners[:, None]) & (
        request_order[None, :] < request_order[:, None]
    )
    group_start = jnp.sum(jnp.where(earlier, unit_len[None, :], 0), axis=1)
    return (unit_len, unit_start, unit_end, group_start)


def cache_rows(raw_rows, positions, kv_gain):
    raw_rows = raw_rows.astype(jnp.float32)
    latent = raw_rows[:, :LAT]
    rotary = raw_rows[:, LAT:]
    inverse = lax.rsqrt(jnp.mean(latent * latent, axis=1, keepdims=True) + eps)
    latent = latent * inverse * kv_gain[None, :]
    half_width = rotary.shape[1] // 2
    frequency = theta ** (-jnp.arange(half_width, dtype=jnp.float32) / half_width)
    angles = positions.astype(jnp.float32)[:, None] * frequency[None, :]
    cosine = jnp.cos(angles)
    sine_part = jnp.sin(angles)
    lower_half = rotary[:, :half_width]
    upper_half = rotary[:, half_width:]
    rotated = jnp.concatenate(
        [
            lower_half * cosine - upper_half * sine_part,
            upper_half * cosine + lower_half * sine_part,
        ],
        axis=1,
    )
    return jnp.concatenate([latent, rotated], axis=1).astype(jnp.bfloat16)


def shards(
    latent_rows,
    new_rows,
    kv_gain,
    lengths,
    owners,
    queries,
    w_uv,
    w_out,
    resid,
    moe_gain,
    route_ids,
    route_weights,
    w_gate,
    w_up,
    w_down,
):
    dp_count = lax.axis_size("dp")
    column_count = lax.axis_size("expert")
    pre_rows = latent_rows.shape[0]
    row_width = latent_rows.shape[1]
    local_units = pre_rows // column_count
    group_index = lax.axis_index("dp")
    column_index = lax.axis_index("expert")
    source = group_index * column_count + column_index
    unit_len, unit_start, unit_end, group_start = request_tables(lengths, owners, column_count)
    my_units = source * local_units + jnp.arange(local_units, dtype=jnp.int32)
    unit_requests = unit_request(my_units, unit_end)
    row_units = jnp.arange(pre_rows, dtype=jnp.int32) // column_count
    row_request = table_lookup(unit_requests, row_units)
    row_start = table_lookup(unit_start, row_request) * column_count
    positions = source * pre_rows + jnp.arange(pre_rows, dtype=jnp.int32) - row_start
    processed = cache_rows(latent_rows, positions, kv_gain)
    unit_group = table_lookup(owners, unit_requests)
    unit_order = jnp.arange(local_units, dtype=jnp.int32)
    same_before = (unit_group[None, :] == unit_group[:, None]) & (
        unit_order[None, :] < unit_order[:, None]
    )
    group_rank = jnp.sum(same_before.astype(jnp.int32), axis=1)
    group_ids = jnp.arange(dp_count, dtype=jnp.int32)
    selector = (
        (unit_group[None, None, :] == group_ids[:, None, None])
        & (group_rank[None, None, :] == unit_order[None, :, None])
    ).astype(jnp.bfloat16)
    outgoing = jnp.einsum(
        "gsu,uec->gesc",
        selector,
        processed.reshape(local_units, column_count, row_width),
        preferred_element_type=jnp.float32,
    ).astype(jnp.bfloat16)
    arrived = lax.all_to_all(
        lax.all_to_all(outgoing, "dp", split_axis=0, concat_axis=0, tiled=True),
        "expert",
        split_axis=1,
        concat_axis=1,
        tiled=True,
    )
    arrived = arrived.reshape(dp_count * column_count * local_units, row_width)
    all_units = jnp.arange(dp_count * column_count * local_units, dtype=jnp.int32)
    all_groups = table_lookup(owners, unit_request(all_units, unit_end))
    per_source = jnp.sum(
        (all_groups == group_index).astype(jnp.int32).reshape(dp_count * column_count, local_units),
        axis=1,
    )
    usable = (unit_order[None, :] < per_source[:, None]).reshape(-1)
    picked = jnp.nonzero(usable, size=pre_rows)[0].astype(jnp.int32)
    cache_local = arrived[picked]
    request_total = queries.shape[1]
    window = 2 * pre_rows // request_total - 1
    group_requests = jnp.nonzero(owners == group_index, size=request_total)[0].astype(jnp.int32)
    first_unit = table_lookup(group_start, group_requests)
    unit_count = table_lookup(unit_len, group_requests)
    padded_cache = jnp.concatenate(
        [cache_local, jnp.zeros((window, row_width), jnp.bfloat16)], axis=0
    )
    window_steps = jnp.arange(window, dtype=jnp.int32)
    windows = padded_cache[first_unit[:, None] + window_steps[None, :]]
    live_mask = (window_steps[None, :] < unit_count[:, None])[:, None, :]
    query_all = queries[0]
    scores = (
        jnp.einsum("jhc,jwc->jhw", query_all, windows, preferred_element_type=jnp.float32)
        * score_scale
    )
    highest = jnp.max(jnp.where(live_mask, scores, -jnp.inf), axis=2)
    weights = jnp.where(live_mask, jnp.exp(scores - highest[:, :, None]), 0.0)
    totals = jnp.sum(weights, axis=2)
    values = jnp.einsum(
        "jhw,jwl->jhl",
        weights,
        windows[:, :, :LAT].astype(jnp.float32),
        precision=lax.Precision.HIGHEST,
    )
    head_share = query_all.shape[1] // column_count
    head_first = column_index * head_share
    shared = lax.pmax(highest, "expert")
    factor = jnp.exp(highest - shared)
    values, totals = (
        lax.psum_scatter(
            (values * factor[:, :, None]).astype(jnp.bfloat16),
            "expert",
            scatter_dimension=1,
            tiled=True,
        ).astype(jnp.float32),
        lax.psum_scatter(
            (totals * factor).astype(jnp.bfloat16), "expert", scatter_dimension=1, tiled=True
        ).astype(jnp.float32),
    )
    highest = lax.dynamic_slice_in_dim(shared, head_first, head_share, 1)
    new_keys = cache_rows(new_rows[0], table_lookup(lengths, group_requests), kv_gain)
    query_own = lax.dynamic_slice_in_dim(query_all, head_first, head_share, 1)
    self_score = (
        jnp.einsum("jhc,jc->jh", query_own, new_keys, preferred_element_type=jnp.float32)
        * score_scale
    )
    ceiling = jnp.maximum(highest, self_score)
    old_part = jnp.exp(highest - ceiling)
    new_part = jnp.exp(self_score - ceiling)
    numerator = values * old_part[:, :, None] + new_part[:, :, None] * new_keys[
        :, None, :LAT
    ].astype(jnp.float32)
    attended = (numerator / (totals * old_part + new_part)[:, :, None]).astype(jnp.bfloat16)
    projected = jnp.einsum(
        "jhl,hlv->jhv", attended, w_uv, preferred_element_type=jnp.float32
    ).astype(jnp.bfloat16)
    flat_heads = projected.reshape(request_total, head_share * projected.shape[2])
    token_rows = resid.shape[1]
    attention_out = lax.psum_scatter(
        jnp.dot(flat_heads, w_out, preferred_element_type=jnp.float32).astype(jnp.bfloat16),
        "expert",
        scatter_dimension=0,
        tiled=True,
    ).astype(jnp.float32)
    residual = resid[0].astype(jnp.float32) + attention_out
    normed = (
        residual
        * lax.rsqrt(jnp.mean(residual * residual, axis=1, keepdims=True) + eps)
        * moe_gain[None, :]
    ).astype(jnp.bfloat16)
    model_width = normed.shape[1]
    local_experts = w_gate.shape[0]
    expert_total = local_experts * column_count
    route_count = route_ids.shape[2]
    capacity = min(token_rows, max(2, 2 * token_rows * route_count // expert_total))
    expert_ids = jnp.arange(expert_total, dtype=jnp.int32)
    matches = route_ids[0][:, :, None] == expert_ids[None, None, :]
    combine_weights = jnp.sum(jnp.where(matches, route_weights[0][:, :, None], 0.0), axis=1)
    routed = jnp.any(matches, axis=1)
    token_order = jnp.arange(token_rows, dtype=jnp.int32)
    before = token_order[None, :] < token_order[:, None]
    slot_rank = jnp.sum(
        jnp.where(before[:, :, None], routed.astype(jnp.int32)[None, :, :], 0), axis=1
    )
    slot_ids = jnp.arange(capacity, dtype=jnp.int32)
    slot_table = routed.T[:, None, :] & (slot_rank.T[:, None, :] == slot_ids[None, :, None])
    outgoing_tokens = jnp.einsum(
        "xct,td->xcd", slot_table.astype(jnp.bfloat16), normed, preferred_element_type=jnp.float32
    ).astype(jnp.bfloat16)
    outgoing_tokens = outgoing_tokens.reshape(column_count, local_experts, capacity, model_width)
    everyone = lax.all_gather(
        lax.all_to_all(outgoing_tokens, "expert", split_axis=0, concat_axis=0, tiled=True),
        "dp",
        axis=0,
        tiled=True,
    )
    gate_out = jnp.einsum("sktd,kdf->sktf", everyone, w_gate, preferred_element_type=jnp.float32)
    up_out = jnp.einsum("sktd,kdf->sktf", everyone, w_up, preferred_element_type=jnp.float32)
    hidden = (jax.nn.silu(gate_out) * up_out).astype(jnp.bfloat16)
    partial_out = jnp.einsum("sktf,kfd->sktd", hidden, w_down, preferred_element_type=jnp.float32)
    row_sums = lax.psum_scatter(
        partial_out.astype(jnp.bfloat16), "dp", scatter_dimension=0, tiled=True
    ).astype(jnp.float32)
    returned = lax.all_to_all(
        row_sums.astype(jnp.bfloat16), "expert", split_axis=0, concat_axis=0, tiled=True
    ).astype(row_sums.dtype)
    expert_out = returned.reshape(expert_total, returned.shape[2], model_width)
    slot_weights = jnp.where(slot_table, combine_weights.T[:, None, :], 0.0)
    moe_sum = jnp.einsum("xct,xcd->td", slot_weights, expert_out, precision=lax.Precision.HIGHEST)
    decoded = (residual + moe_sum).astype(jnp.bfloat16)
    return (cache_local[None, None], decoded[None])


def solution(mesh):
    return jax.shard_map(
        shards,
        mesh=mesh,
        in_specs=(
            P(("dp", "expert"), None),
            P("dp", None, None),
            P(),
            P(),
            P(),
            P("dp", None, None, None),
            P("expert", None, None),
            P("expert", None),
            P("dp", "expert", None),
            P(),
            P("dp", "expert", None),
            P("dp", "expert", None),
            P("expert", None, "dp"),
            P("expert", None, "dp"),
            P("expert", "dp", None),
        ),
        out_specs=(P("dp", "expert", None, None), P("dp", "expert", None)),
        check_vma=False,
    )
```

profile of v0, /device:TPU:1, one launch (start us, length us, event | category | flops | bytes accessed | tf_op | source)
XLA Modules:
  0.0 608.9 jit_solution(10671489765275234956)
XLA Ops:
  7.2 0.7 fusion.127
  8.0 0.3 reduce-window.41
  8.5 0.8 fusion.123
  9.4 0.9 select_reduce_fusion.8
  10.6 1.1 copy.106
  12.8 0.8 multiply_convert_fusion.1
  13.8 0.5 fusion.14
  14.3 1.3 copy.111
  15.6 4.8 all-to-all-start
  20.6 0.6 convert_reduce_fusion.3
  21.3 0.3 select_reduce_fusion
  22.7 5.8 scatter_custom_fusion
  28.6 0.3 reduce-window.56
  29.0 0.3 reduce-window.58
  29.6 3.9 scatter_custom_fusion.1
  33.9 0.7 compare_select_fusion.4
  35.4 0.7 fusion.77
  36.1 1.7 copy.112
  37.8 9.1 %all-to-all-start.1 = ((bf16[4,32,6,576]{3,0,2,1:T(4,128)(2,1)}), bf16[4,32,6,576]{3,0,2,1:T(4,128)(2,1)S(1)}, u32[]{:S(2)}, u32[]{:S(2)}) async-start(bf16[4,32,6,576]{3,0,2,1:T(4,128)(2,1)} %copy.112), calls=%async_computation.1 | async-start | bytes 1966080 | tf_op jit(solution)/shard_map/all_to_all | solution.py:108
  47.2 0.7 compare_select_fusion.3
  48.0 15.4 %all-to-all-done.1 = bf16[4,32,6,576]{3,0,2,1:T(4,128)(2,1)S(1)} async-done(((bf16[4,32,6,576]{3,0,2,1:T(4,128)(2,1)}), bf16[4,32,6,576]{3,0,2,1:T(4,128)(2,1)S(1)}, u32[]{:S(2)}, u32[]{:S(2)}) %all-to-all-start.1) | async-done | bytes 884768 | tf_op jit(solution)/shard_map/all_to_all | solution.py:108
  63.5 0.6 reshape.422
  64.2 1.0 gather_fusion
  65.3 2.1 gather_fusion.1
  67.5 5.8 select_reduce_fusion.3
  73.8 120.4 %pmax.7 = f32[96,64]{0,1:T(8,128)S(1)} all-reduce(f32[96,64]{0,1:T(8,128)S(1)} %copy.116), channel_id=1, replica_groups=mesh['dp'=4,'expert'=32] {'expert'}, use_global_device_ids=true, to_apply=%region_26.27 | all-reduce | flops 6144 | bytes 49152 | tf_op jit(solution)/shard_map/pmax | solution.py:152
  194.3 6.3 %multiply_convert_fusion = bf16[96,64,512]{2,1,0:T(8,128)(2,1)S(1)} fusion(f32[96,64]{1,0:T(8,128)S(1)} %copy.117, bf16[96,3,576]{2,1,0:T(4,128)(2,1)S(1)} %reshape.450, f32[96,3,64]{2,1,0:T(4,128)S(1)} %get-tuple-element.19, f32[96,64]{1,0:T(8,128)S(1)} %get-tuple-element.18, pred[96,3]{1,0:T(8,128)(4,1)S(1)} %iota_compare_fusion.6), kind=kOutput, calls=%fused_computation.4 | convolution fusion | flops 119574528 | bytes 6991872 | tf_op jit(solution)/shard_map/jhw,jwl->jhl/dot_general | solution.py:144
  200.6 6.3 %copy.118 = bf16[96,64,512]{2,0,1:T(8,128)(2,1)} copy(bf16[96,64,512]{2,1,0:T(8,128)(2,1)S(1)} %multiply_convert_fusion) | data formatting | bytes 12582912 | tf_op jit(solution)/shard_map/convert_element_type | solution.py:156
  207.2 0.6 copy-done.3
  208.7 1.7 multiply_reduce_fusion.1
  210.4 0.6 dynamic-slice.1
  211.8 124.4 %all-reduce.2 = bf16[96,64]{1,0:T(8,128)(2,1)S(1)} all-reduce(bf16[96,64]{1,0:T(8,128)(2,1)S(1)} %copy.122), channel_id=3, replica_groups=mesh['dp'=4,'expert'=32] {'expert'}, use_global_device_ids=true, to_apply=%region_31.32.clone | all-reduce | flops 6144 | bytes 24576
  336.4 1.2 fusion.43
  337.6 3.9 convolution_convert_fusion.1
  342.4 106.5 %all-reduce.6.cloned.1.call-done = bf16[96,7168]{1,0:T(8,128)(2,1)} async-done(((bf16[96,7168]{1,0:T(8,128)(2,1)}), bf16[96,7168]{1,0:T(8,128)(2,1)}) %all-reduce.6.cloned.1.call-update) | async-done | bytes 1376272
  449.0 1.1 multiply_reduce_fusion.3
  450.1 1.4 fusion.1
  451.5 0.9 copy.125
  452.5 21.5 %all_to_all.20 = bf16[32,1,2,7168]{3,2,1,0:T(2,128)(2,1)S(1)} all-to-all(bf16[32,1,2,7168]{3,2,1,0:T(2,128)(2,1)S(1)} %copy.125), channel_id=1, replica_groups=mesh['dp'=4,'expert'=32] {'expert'}, dimensions={0} | all-to-all | bytes 1835008 | tf_op jit(solution)/shard_map/all_to_all | solution.py:217
  474.0 1.1 copy.126
  475.1 41.3 %all-gather.2.cloned.1.call-done = bf16[128,1,2,7168]{3,0,2,1:T(8,128)(2,1)} async-done(((bf16[32,1,2,7168]{3,0,2,1:T(8,128)(2,1)}), bf16[128,1,2,7168]{3,0,2,1:T(8,128)(2,1)}) %all-gather.2.cloned.1.call-update) | async-done | bytes 3670032 | tf_op jit(solution)/shard_map/all_gather | solution.py:216
  516.4 4.3 fusion.15
  520.7 10.0 %fusion = bf16[128,1,2,7168]{3,0,2,1:T(8,128)(2,1)} fusion(bf16[1,256,7168]{2,1,0:T(8,128)(2,1)} %param.29, bf16[1,7168,256]{2,1,0:T(8,128)(2,1)} %param.28, bf16[128,1,2,7168]{3,0,2,1:T(8,128)(2,1)} %all-gather.2.cloned.1.call-done, f32[128,1,2,256]{3,0,2,1:T(8,128)S(1)} %fusion.15), kind=kOutput, calls=%fused_computation.6 | convolution fusion | flops 1881276416 | bytes 14942208 | tf_op jit(solution)/shard_map/sktf,kfd->sktd/dot_general | solution.py:225
  530.7 43.0 %reduce-scatter.6.cloned.1.call-done = bf16[32,1,2,7168]{3,0,2,1:T(8,128)(2,1)} async-done(((bf16[128,1,2,7168]{3,0,2,1:T(8,128)(2,1)}), bf16[32,1,2,7168]{3,0,2,1:T(8,128)(2,1)}) %reduce-scatter.6.cloned.1.call-update) | async-done | bytes 917520 | tf_op jit(solution)/shard_map/reduce_scatter | solution.py:226
  573.7 3.1 copy.127
  576.8 7.7 %all-to-all-start.3 = ((bf16[32,1,2,7168]{3,2,1,0:T(2,128)(2,1)}), bf16[32,1,2,7168]{3,2,1,0:T(2,128)(2,1)S(1)}, u32[]{:S(2)}, u32[]{:S(2)}) async-start(bf16[32,1,2,7168]{3,2,1,0:T(2,128)(2,1)} %copy.127), calls=%async_computation.5 | async-start | bytes 1835008 | tf_op jit(solution)/shard_map/all_to_all | solution.py:229
  584.6 15.7 %all-to-all-done.3 = bf16[32,1,2,7168]{3,2,1,0:T(2,128)(2,1)S(1)} async-done(((bf16[32,1,2,7168]{3,2,1,0:T(2,128)(2,1)}), bf16[32,1,2,7168]{3,2,1,0:T(2,128)(2,1)S(1)}, u32[]{:S(2)}, u32[]{:S(2)}) %all-to-all-start.3) | async-done | bytes 917536 | tf_op jit(solution)/shard_map/all_to_all | solution.py:229
  600.3 2.1 fusion.6
  (121 shorter events, 8.1 us)
Async XLA Ops:
  7.2 329.2 %copy-start = (bf16[2,512,128]{2,1,0:T(8,128)(2,1)S(1)}, bf16[2,512,128]{2,1,0:T(8,128)(2,1)}, u32[]{:S(2)}) copy-start(bf16[2,512,128]{2,1,0:T(8,128)(2,1)} %param.21) | copy-start | bytes 786436
  12.7 7.9 %copy-start.4 = (s32[384]{0:T(512)S(1)}, s32[384]{0:T(512)}, u32[]{:S(2)}) copy-start(s32[384]{0:T(512)} %param.19) | copy-start | bytes 4612
  12.7 8.5 %copy-start.5 = (s32[384]{0:T(512)S(1)}, s32[384]{0:T(512)}, u32[]{:S(2)}) copy-start(s32[384]{0:T(512)} %param.18) | copy-start | bytes 4612
  15.6 20.5 %all-to-all-start = ((bf16[4,32,6,576]{3,1,2,0:T(8,128)(2,1)}), bf16[4,32,6,576]{3,1,2,0:T(8,128)(2,1)S(1)}, u32[]{:S(2)}, u32[]{:S(2)}) async-start(bf16[4,32,6,576]{3,1,2,0:T(8,128)(2,1)} %copy.111), calls=%async_computation | async-start | bytes 1966080 | tf_op jit(solution)/shard_map/all_to_all | solution.py:109
  37.8 25.5 %all-to-all-start.1 = ((bf16[4,32,6,576]{3,0,2,1:T(4,128)(2,1)}), bf16[4,32,6,576]{3,0,2,1:T(4,128)(2,1)S(1)}, u32[]{:S(2)}, u32[]{:S(2)}) async-start(bf16[4,32,6,576]{3,0,2,1:T(4,128)(2,1)} %copy.112), calls=%async_computation.1 | async-start | bytes 1966080 | tf_op jit(solution)/shard_map/all_to_all | solution.py:108
  46.9 289.5 %reduce-scatter.4.cloned.1.call-start = ((), (), s32[]{:S(2)}) async-start(), calls=%async_computation.6 | async-start | bytes 6488064 | tf_op jit(solution)/shard_map/reduce_scatter | solution.py:155
  65.2 8.1 %copy-start.1 = (bf16[192,576]{1,0:T(8,128)(2,1)}, bf16[192,576]{1,0:T(8,128)(2,1)S(1)}, u32[]{:S(2)}) copy-start(bf16[192,576]{1,0:T(8,128)(2,1)S(1)} %gather_fusion) | copy-start | bytes 663556
  206.9 0.9 copy-start.3
  206.9 1.2 copy-start.7
  206.9 3.5 copy-start.10
  207.0 242.0 %all-reduce.6.cloned.1.call-start = ((), (), s32[]{:S(2)}) async-start(), calls=%async_computation.9 | async-start | bytes 2752512
  337.6 4.6 copy-start.8
  337.6 111.3 %copy-start.2 = (bf16[1,3,7168]{2,1,0:T(4,128)(2,1)S(1)}, bf16[1,3,7168]{2,1,0:T(4,128)(2,1)}, u32[]{:S(2)}) copy-start(bf16[1,3,7168]{2,1,0:T(4,128)(2,1)} %param.23) | copy-start | bytes 129028
  337.6 112.5 %copy-start.6 = (f32[7168]{0:T(1024)S(1)}, f32[7168]{0:T(1024)}, u32[]{:S(2)}) copy-start(f32[7168]{0:T(1024)} %param.24) | copy-start | bytes 86020
  341.5 174.9 %all-gather.2.cloned.1.call-start = ((), (), s32[]{:S(2)}) async-start(), calls=%async_computation.7 | async-start | bytes 4587520 | tf_op jit(solution)/shard_map/all_gather | solution.py:216
  475.1 98.7 %reduce-scatter.6.cloned.1.call-start = ((), (), s32[]{:S(2)}) async-start(), calls=%async_computation.8 | async-start | bytes 4587520 | tf_op jit(solution)/shard_map/reduce_scatter | solution.py:226
  530.7 53.8 %copy-start.9 = (f32[1,3,8]{2,0,1:T(1,128)S(1)}, f32[1,3,8]{2,0,1:T(1,128)}, u32[]{:S(2)}) copy-start(f32[1,3,8]{2,0,1:T(1,128)} %param.26) | copy-start | bytes 292
  576.8 23.4 %all-to-all-start.3 = ((bf16[32,1,2,7168]{3,2,1,0:T(2,128)(2,1)}), bf16[32,1,2,7168]{3,2,1,0:T(2,128)(2,1)S(1)}, u32[]{:S(2)}, u32[]{:S(2)}) async-start(bf16[32,1,2,7168]{3,2,1,0:T(2,128)(2,1)} %copy.127), calls=%async_computation.5 | async-start | bytes 1835008 | tf_op jit(solution)/shard_map/all_to_all | solution.py:229
Sparse Core Ops, SparseCore 0:
  207.1 86.6 reduce-scatter.3
  341.7 107.2 all-reduce.5
  475.2 41.1 all-gather.1
  530.9 42.8 reduce-scatter.5
where the time goes:
time: 610 us; the launch traced here: 609 us
  blocking collectives  266 us (44%)
  waiting for transfers between devices  222 us (36%)
  matrix products  35.5 us (6%)
  local copies, waits for them, and re-layouts  23.8 us (4%)
  other arithmetic  23.6 us (4%)
  starting transfers between devices  22.1 us (4%)
  between operations  15.6 us (3%)
    unnamed x1, blocking collectives  124 us
    pmax x1, blocking collectives, shards(): shared = lax.pmax(highest, 'expert')  120 us
    unnamed x5, waiting for transfers between devices  107 us
    reduce_scatter x1, waiting for transfers between devices, shards(): lax.psum_scatter(partial_out.astype(jnp.bfloat16), 'dp', scatter_dimensio...  43 us
    all_gather x1, waiting for transfers between devices, shards(): lax.all_gather(lax.all_to_all(outgoing_tokens, 'expert', split_axis=0, co...  41.3 us
    all_to_all x1, blocking collectives, shards(): lax.all_to_all(outgoing_tokens, 'expert', split_axis=0, concat_axis=0, ti...  21.5 us
    all_to_all x1, waiting for transfers between devices, shards(): lax.all_to_all(row_sums.astype(jnp.bfloat16), 'expert', split_axis=0, con...  15.7 us
    all_to_all x1, waiting for transfers between devices, shards(): lax.all_to_all(lax.all_to_all(outgoing, 'dp', split_axis=0, concat_axis=0...  15.4 us
  transfers between devices with their start and end apart: 7, of which 5 were waited for; matrix products, arithmetic and copies ran while one was open for 3% of the time, Pallas kernels for 0%

commit v1 on v0

v1 whole, which is shorter than its diff:
```python
import jax
import jax.numpy as jnp
from jax import lax
from jax.sharding import PartitionSpec as P

LAT = 512
UNIT = 32

eps = 1e-06
theta = 10000.0
score_scale = 192.0 ** (-0.5)
BF = jnp.bfloat16
F32 = jnp.float32


def norm_rotate(raw_rows, positions, kv_gain):
    raw_rows = raw_rows.astype(F32)
    latent = raw_rows[:, :LAT]
    rotary = raw_rows[:, LAT:]
    inverse = lax.rsqrt(jnp.mean(latent * latent, axis=1, keepdims=True) + eps)
    latent = latent * inverse * kv_gain[None, :]
    half_width = rotary.shape[1] // 2
    frequency = theta ** (-jnp.arange(half_width, dtype=F32) / half_width)
    angles = positions.astype(F32)[:, None] * frequency[None, :]
    cosine = jnp.cos(angles)
    sine_part = jnp.sin(angles)
    lower_half = rotary[:, :half_width]
    upper_half = rotary[:, half_width:]
    rotated = jnp.concatenate(
        [
            lower_half * cosine - upper_half * sine_part,
            upper_half * cosine + lower_half * sine_part,
        ],
        axis=1,
    )
    return jnp.concatenate([latent, rotated], axis=1).astype(BF)


def shift(x, step, size, axis):
    return lax.ppermute(x, axis, [((i + step) % size, i) for i in range(size)])


def shards(
    latent_rows,
    new_rows,
    kv_gain,
    lengths,
    owners,
    queries,
    w_uv,
    w_out,
    resid,
    moe_gain,
    route_ids,
    route_weights,
    w_gate,
    w_up,
    w_down,
):
    dp_count = lax.axis_size("dp")
    columns = lax.axis_size("expert")
    group = lax.axis_index("dp")
    column = lax.axis_index("expert")
    pre_rows, width = latent_rows.shape
    local_units = pre_rows // UNIT
    block_units = columns * local_units

    by_row = latent_rows.reshape(local_units, UNIT, width).transpose(1, 0, 2)
    dealt = lax.all_to_all(by_row, "expert", split_axis=0, concat_axis=0, tiled=True)
    dealt = dealt.reshape(block_units, width)
    blocks = jnp.concatenate(
        [dealt] + [shift(dealt, k, dp_count, "dp") for k in range(1, dp_count)], axis=0
    )

    requests = lengths.shape[0]
    request_total = queries.shape[1]
    unit_len = lengths // UNIT
    order = jnp.arange(requests, dtype=jnp.int32)
    before = order[None, :] < order[:, None]
    unit_start = jnp.sum(jnp.where(before, unit_len[None, :], 0), axis=1)
    own = owners == group
    own_before = before & own[None, :]
    group_start = jnp.sum(jnp.where(own_before, unit_len[None, :], 0), axis=1)
    group_rank = jnp.sum(own_before.astype(jnp.int32), axis=1)
    slots = jnp.arange(pre_rows, dtype=jnp.int32)
    offset = slots[:, None] - group_start[None, :]
    covers = own[None, :] & (offset >= 0) & (offset < unit_len[None, :])
    slot_offset = jnp.sum(jnp.where(covers, offset, 0), axis=1)
    slot_unit = jnp.sum(jnp.where(covers, offset + unit_start[None, :], 0), axis=1)
    relative = (slot_unit // block_units - group + dp_count) % dp_count
    slot_place = relative * block_units + slot_unit % block_units
    members = jnp.arange(request_total, dtype=jnp.int32)
    is_member = own[None, :] & (group_rank[None, :] == members[:, None])
    first_unit = jnp.sum(jnp.where(is_member, group_start[None, :], 0), axis=1)
    unit_count = jnp.sum(jnp.where(is_member, unit_len[None, :], 0), axis=1)

    places = jnp.arange(dp_count * block_units, dtype=jnp.int32)
    pick = (slot_place[:, None] == places[None, :]).astype(BF)
    raw_cache = jnp.dot(pick, blocks, preferred_element_type=F32)
    cache_local = norm_rotate(raw_cache, slot_offset * UNIT + column, kv_gain)

    window = 2 * pre_rows // request_total - 1
    share = request_total // columns
    steps = jnp.arange(window, dtype=jnp.int32)
    wanted = (first_unit[:, None] + steps[None, :]).reshape(-1)
    take = (wanted[:, None] == slots[None, :]).astype(BF)
    outgoing = jnp.dot(take, cache_local, preferred_element_type=F32).astype(BF)
    keys = lax.all_to_all(
        outgoing.reshape(columns, share * window, width),
        "expert",
        split_axis=0,
        concat_axis=0,
        tiled=True,
    )
    keys = keys.reshape(UNIT, share, window, width).transpose(1, 2, 0, 3)
    keys = keys.reshape(share, window * UNIT, width)
    own_first = column * share
    own_queries = lax.dynamic_slice_in_dim(queries[0], own_first, share, 0)
    own_counts = lax.dynamic_slice_in_dim(unit_count, own_first, share, 0)
    own_new = lax.dynamic_slice_in_dim(new_rows[0], own_first, share, 0)
    new_keys = norm_rotate(own_new, own_counts * UNIT, kv_gain)
    scores = (
        jnp.einsum("jhc,jkc->jhk", own_queries, keys, preferred_element_type=F32) * score_scale
    )
    live = (jnp.arange(window * UNIT, dtype=jnp.int32) // UNIT)[None, :] < own_counts[:, None]
    self_score = (
        jnp.einsum("jhc,jc->jh", own_queries, new_keys, preferred_element_type=F32) * score_scale
    )
    scores = jnp.where(live[:, None, :], scores, -jnp.inf)
    highest = jnp.maximum(jnp.max(scores, axis=2), self_score)
    weights = jnp.exp(scores - highest[:, :, None])
    self_weight = jnp.exp(self_score - highest)
    total = jnp.sum(weights, axis=2) + self_weight
    mixture = (
        jnp.einsum(
            "jhk,jkl->jhl", weights.astype(BF), keys[:, :, :LAT], preferred_element_type=F32
        )
        + self_weight[:, :, None] * new_keys[:, None, :LAT].astype(F32)
    )
    attended = (mixture / total[:, :, None]).astype(BF)

    head_share = w_uv.shape[0]
    by_head = attended.reshape(share, columns, head_share, LAT).transpose(1, 0, 2, 3)
    by_head = lax.all_to_all(by_head, "expert", split_axis=0, concat_axis=0, tiled=True)
    by_head = by_head.reshape(request_total, head_share, LAT)
    projected = jnp.einsum("jhl,hlv->jhv", by_head, w_uv, preferred_element_type=F32).astype(BF)
    partial_sums = jnp.dot(
        projected.reshape(request_total, -1), w_out, preferred_element_type=F32
    ).astype(BF)

    model_width = w_out.shape[1]
    chips = columns // 2
    core = column % 2
    by_core = partial_sums.reshape(chips, 2, share, model_width)
    mine = lax.dynamic_index_in_dim(by_core, core, 1, keepdims=False)
    other = lax.dynamic_index_in_dim(by_core, 1 - core, 1, keepdims=False)
    other = lax.ppermute(other, "expert", [(i, i ^ 1) for i in range(columns)])
    pair_sums = (mine.astype(F32) + other.astype(F32)).astype(BF)
    chip_sums = lax.all_to_all(
        pair_sums,
        "expert",
        split_axis=0,
        concat_axis=0,
        tiled=True,
        axis_index_groups=[[2 * i + c for i in range(chips)] for c in range(2)],
    )
    attention_out = jnp.sum(chip_sums.astype(F32), axis=0)
    residual = resid[0].astype(F32) + attention_out
    normed = (
        residual
        * lax.rsqrt(jnp.mean(residual * residual, axis=1, keepdims=True) + eps)
        * moe_gain[None, :]
    ).astype(BF)

    piece = model_width // dp_count
    gates, ups, downs = [], [], []
    for k in range(dp_count):
        to = (group - k + dp_count) % dp_count * piece
        parts = (
            lax.dynamic_slice_in_dim(w_gate[0], to, piece, 0),
            lax.dynamic_slice_in_dim(w_up[0], to, piece, 0),
            lax.dynamic_slice_in_dim(w_down[0], to, piece, 1),
        )
        if k:
            parts = tuple(shift(part, k, dp_count, "dp") for part in parts)
        for held, part in zip((gates, ups, downs), parts):
            held.append(part)

    tokens = resid.shape[1]
    capacity = 2
    expert_ids = jnp.arange(columns, dtype=jnp.int32)
    matches = route_ids[0][:, :, None] == expert_ids[None, None, :]
    combine_weights = jnp.sum(jnp.where(matches, route_weights[0][:, :, None], 0.0), axis=1)
    routed = jnp.any(matches, axis=1)
    token_order = jnp.arange(tokens, dtype=jnp.int32)
    earlier = token_order[None, :] < token_order[:, None]
    slot_rank = jnp.sum(
        jnp.where(earlier[:, :, None], routed.astype(jnp.int32)[None, :, :], 0), axis=1
    )
    slot_ids = jnp.arange(capacity, dtype=jnp.int32)
    slot_table = routed.T[:, None, :] & (slot_rank.T[:, None, :] == slot_ids[None, :, None])
    outgoing_tokens = jnp.einsum(
        "xct,tfd->fxcd",
        slot_table.astype(BF),
        normed.reshape(tokens, dp_count, piece),
        preferred_element_type=F32,
    ).astype(BF)
    arrived = lax.all_to_all(
        outgoing_tokens.reshape(dp_count * columns, capacity, piece),
        ("dp", "expert"),
        split_axis=0,
        concat_axis=0,
        tiled=True,
    )
    rows = arrived.reshape(dp_count * columns * capacity, piece)

    sums = None
    for k in range(dp_count):
        pair = jnp.concatenate(
            [
                jnp.dot(rows, gates[k], preferred_element_type=F32),
                jnp.dot(rows, ups[k], preferred_element_type=F32),
            ],
            axis=1,
        )
        if k:
            pair = shift(pair.astype(BF), dp_count - k, dp_count, "dp").astype(F32)
        sums = pair if sums is None else sums + pair
    half = sums.shape[1] // 2
    hidden = (jax.nn.silu(sums[:, :half]) * sums[:, half:]).astype(BF)
    out = None
    for k in range(dp_count):
        block = shift(hidden, k, dp_count, "dp") if k else hidden
        term = jnp.dot(block, downs[k], preferred_element_type=F32)
        out = term if out is None else out + term
    returned = lax.all_to_all(
        out.astype(BF).reshape(dp_count * columns, capacity, piece),
        ("dp", "expert"),
        split_axis=0,
        concat_axis=0,
        tiled=True,
    )
    slot_weights = jnp.where(slot_table, combine_weights.T[:, None, :], 0.0)
    moe_sum = jnp.einsum(
        "xct,fxcd->tfd",
        slot_weights,
        returned.reshape(dp_count, columns, capacity, piece).astype(F32),
        precision=lax.Precision.HIGHEST,
    ).reshape(tokens, model_width)
    decoded = (residual + moe_sum).astype(BF)
    return (cache_local[None, None], decoded[None])


def solution(mesh):
    return jax.shard_map(
        shards,
        mesh=mesh,
        in_specs=(
            P(("dp", "expert"), None),
            P("dp", None, None),
            P(),
            P(),
            P(),
            P("dp", None, None, None),
            P("expert", None, None),
            P("expert", None),
            P("dp", "expert", None),
            P(),
            P("dp", "expert", None),
            P("dp", "expert", None),
            P("expert", None, "dp"),
            P("expert", None, "dp"),
            P("expert", "dp", None),
        ),
        out_specs=(P("dp", "expert", None, None), P("dp", "expert", None)),
        check_vma=False,
    )
```

time: 610 us -> 288 us (0.47)
  blocking collectives: 266 us -> 0 us
  waiting for transfers between devices: 222 us -> 173 us
  starting transfers between devices: 22.1 us -> 59.3 us
  other arithmetic: 23.6 us -> 8.74 us
  between operations: 15.6 us -> 1.3 us
  matrix products: 35.5 us -> 23.2 us
    unnamed x1 -> x0, blocking collectives: 124 us -> none
    pmax x1 -> x0, blocking collectives: 120 us -> none  [shards(): shared = lax.pmax(highest, 'expert')]
    ppermute x0 -> x19, waiting for transfers between devices: none -> 115 us  [the longest x18 113 us: shift(): return lax.ppermute(x, axis, [((i + step) % size, i) for i in range(size)])]
    unnamed x5 -> x0, waiting for transfers between devices: 107 us -> none
    reduce_scatter x2 -> x0, waiting for transfers between devices: 43 us -> none  [the longest x1 43 us: shards(): lax.psum_scatter(partial_out.astype(jnp.bfloat16), 'dp', scatter_dimensio...]
    all_gather x1 -> x0, waiting for transfers between devices: 41.3 us -> none  [shards(): lax.all_gather(lax.all_to_all(outgoing_tokens, 'expert', split_axis=0, co...]
    all_to_all x3 -> x6, waiting for transfers between devices: 31 us -> 58.1 us  [the longest x1 16.7 us: shards(): lax.all_to_all(out.astype(BF).reshape(dp_count * columns, capacity, piece...]
    ppermute x0 -> x19, starting transfers between devices: none -> 24.1 us  [the longest x18 23.8 us: shift(): return lax.ppermute(x, axis, [((i + step) % size, i) for i in range(size)])]
  transfers between devices with their start and end apart: 7 -> 25, of which waited for: 5 -> 17; matrix products, arithmetic and copies ran while one was open for 3% -> 12% of each run, Pallas kernels for 0% -> 0%
where the time goes in v1:
time: 288 us; the launch traced here: 287 us
  waiting for transfers between devices  173 us (60%)
  starting transfers between devices  59.3 us (21%)
  matrix products  23.2 us (8%)
  local copies, waits for them, and re-layouts  21.4 us (7%)
  other arithmetic  8.74 us (3%)
    ppermute x18, waiting for transfers between devices, shift(): return lax.ppermute(x, axis, [((i + step) % size, i) for i in range(size)])  113 us
    ppermute x18, starting transfers between devices, shift(): return lax.ppermute(x, axis, [((i + step) % size, i) for i in range(size)])  23.8 us
    all_to_all x1, waiting for transfers between devices, shards(): lax.all_to_all(out.astype(BF).reshape(dp_count * columns, capacity, piece...  16.7 us
    all_to_all x1, waiting for transfers between devices, shards(): lax.all_to_all(outgoing.reshape(columns, share * window, width), 'expert'...  11.8 us
    all_to_all x1, waiting for transfers between devices, shards(): lax.all_to_all(pair_sums, 'expert', split_axis=0, concat_axis=0, tiled=Tr...  10.7 us
    all_to_all x1, starting transfers between devices, shards(): lax.all_to_all(by_row, 'expert', split_axis=0, concat_axis=0, tiled=True)  9.6 us
    all_to_all x1, waiting for transfers between devices, shards(): lax.all_to_all(by_head, 'expert', split_axis=0, concat_axis=0, tiled=True)  8.36 us
    all_to_all x1, starting transfers between devices, shards(): lax.all_to_all(out.astype(BF).reshape(dp_count * columns, capacity, piece...  7.67 us
  transfers between devices with their start and end apart: 25, of which 17 were waited for; matrix products, arithmetic and copies ran while one was open for 12% of the time, Pallas kernels for 0%

profile of v1, /device:TPU:1, one launch (start us, length us, event | category | flops | bytes accessed | tf_op | source)
XLA Modules:
  0.0 287.2 jit_solution(18112096904793733187)
XLA Ops:
  0.6 1.8 copy.106
  2.4 9.6 %all-to-all-start = ((bf16[32,6,576]{2,1,0:T(8,128)(2,1)}), bf16[32,6,576]{2,1,0:T(8,128)(2,1)S(1)}, u32[]{:S(2)}, u32[]{:S(2)}) async-start(bf16[32,6,576]{2,1,0:T(8,128)(2,1)} %bitcast.137), calls=%async_computation | async-start | bytes 655360 | tf_op jit(solution)/shard_map/all_to_all | solution.py:69
  16.2 5.4 %all-to-all-done = bf16[32,6,576]{2,1,0:T(8,128)(2,1)S(1)} async-done(((bf16[32,6,576]{2,1,0:T(8,128)(2,1)}), bf16[32,6,576]{2,1,0:T(8,128)(2,1)S(1)}, u32[]{:S(2)}, u32[]{:S(2)}) %all-to-all-start) | async-done | bytes 221216 | tf_op jit(solution)/shard_map/all_to_all | solution.py:69
  23.0 2.5 collective-permute-start.1
  26.7 3.6 %collective-permute-done.2 = bf16[192,576]{1,0:T(8,128)(2,1)S(1)} collective-permute-done((bf16[192,576]{1,0:T(8,128)(2,1)S(1)}, bf16[192,576]{1,0:T(8,128)(2,1)S(1)}, u32[]{:S(2)}, u32[]{:S(2)}) %collective-permute-start.2) | collective-permute-done | bytes 221216 | tf_op jit(solution)/shard_map/ppermute | solution.py:40
  30.3 6.3 %collective-permute-done.1 = bf16[192,576]{1,0:T(8,128)(2,1)S(1)} collective-permute-done((bf16[192,576]{1,0:T(8,128)(2,1)S(1)}, bf16[192,576]{1,0:T(8,128)(2,1)S(1)}, u32[]{:S(2)}, u32[]{:S(2)}) %collective-permute-start.1) | collective-permute-done | bytes 221216 | tf_op jit(solution)/shard_map/ppermute | solution.py:40
  39.8 4.7 %all-to-all-start.1 = ((bf16[32,9,576]{2,1,0:T(8,128)(2,1)}), bf16[32,9,576]{2,1,0:T(8,128)(2,1)S(1)}, u32[]{:S(2)}, u32[]{:S(2)}) async-start(bf16[32,9,576]{2,1,0:T(8,128)(2,1)} %reshape.275), calls=%async_computation.1 | async-start | bytes 1310720 | tf_op jit(solution)/shard_map/all_to_all | solution.py:108
  45.6 11.8 %all-to-all-done.1 = bf16[32,9,576]{2,1,0:T(8,128)(2,1)S(1)} async-done(((bf16[32,9,576]{2,1,0:T(8,128)(2,1)}), bf16[32,9,576]{2,1,0:T(8,128)(2,1)S(1)}, u32[]{:S(2)}, u32[]{:S(2)}) %all-to-all-start.1) | async-done | bytes 331808 | tf_op jit(solution)/shard_map/all_to_all | solution.py:108
  57.5 1.3 fusion.104
  60.2 4.1 %all-to-all-start.2 = ((bf16[32,3,2,512]{3,2,1,0:T(2,128)(2,1)}), bf16[32,3,2,512]{3,2,1,0:T(2,128)(2,1)S(1)}, u32[]{:S(2)}, u32[]{:S(2)}) async-start(bf16[32,3,2,512]{3,2,1,0:T(2,128)(2,1)} %bitcast.138), calls=%async_computation.2 | async-start | bytes 393216 | tf_op jit(solution)/shard_map/all_to_all | solution.py:144
  64.3 8.4 %all-to-all-done.2 = bf16[32,3,2,512]{3,2,1,0:T(2,128)(2,1)S(1)} async-done(((bf16[32,3,2,512]{3,2,1,0:T(2,128)(2,1)}), bf16[32,3,2,512]{3,2,1,0:T(2,128)(2,1)S(1)}, u32[]{:S(2)}, u32[]{:S(2)}) %all-to-all-start.2) | async-done | bytes 196640 | tf_op jit(solution)/shard_map/all_to_all | solution.py:144
  72.9 2.8 convolution_convert_fusion
  77.4 2.0 collective-permute-done.3
  79.4 1.7 fusion.6
  81.1 3.6 %all-to-all-start.3 = ((bf16[16,3,7168]{2,1,0:T(4,128)(2,1)}), bf16[16,3,7168]{2,1,0:T(4,128)(2,1)S(1)}, u32[]{:S(2)}, u32[]{:S(2)}) async-start(bf16[16,3,7168]{2,1,0:T(4,128)(2,1)} %fusion.6), calls=%async_computation.3 | async-start | bytes 1835008 | tf_op jit(solution)/shard_map/all_to_all | solution.py:159
  84.8 3.2 %dynamic-slice_bitcast_fusion.8 = (bf16[1792,256]{1,0:T(8,128)(2,1)}, bf16[1792,256]{1,0:T(8,128)(2,1)}, bf16[1792,256]{1,0:T(8,128)(2,1)S(1)}) fusion(bf16[1,7168,256]{2,1,0:T(8,128)(2,1)} %param.27, s32[]{:T(128)S(6)} %select_n.155, s32[]{:T(128)S(6)} %select_n.159, s32[]{:T(128)S(6)} %select_n.157), kind=kLoop, calls=%fused_computation.52 | loop fusion | bytes 5505036 | tf_op jit(solution)/shard_map/dynamic_slice | solution.py:180
  88.0 2.0 collective-permute-start.4
  90.3 10.7 %all-to-all-done.3 = bf16[16,3,7168]{2,1,0:T(4,128)(2,1)S(1)} async-done(((bf16[16,3,7168]{2,1,0:T(4,128)(2,1)}), bf16[16,3,7168]{2,1,0:T(4,128)(2,1)S(1)}, u32[]{:S(2)}, u32[]{:S(2)}) %all-to-all-start.3) | async-done | bytes 688160 | tf_op jit(solution)/shard_map/all_to_all | solution.py:159
  102.3 1.9 copy.69
  104.1 5.6 %all-to-all-start.4 = ((bf16[128,2,1792]{2,1,0:T(2,128)(2,1)}), bf16[128,2,1792]{2,1,0:T(2,128)(2,1)S(1)}, u32[]{:S(2)}, u32[]{:S(2)}) async-start(bf16[128,2,1792]{2,1,0:T(2,128)(2,1)} %copy.69), calls=%async_computation.4 | async-start | bytes 1835008 | tf_op jit(solution)/shard_map/all_to_all | solution.py:208
  109.7 3.4 %dynamic-slice_bitcast_fusion.7 = (bf16[1792,256]{1,0:T(8,128)(2,1)}, bf16[1792,256]{1,0:T(8,128)(2,1)}, bf16[1792,256]{1,0:T(8,128)(2,1)}) fusion(bf16[1,7168,256]{2,1,0:T(8,128)(2,1)} %param.28, s32[]{:T(128)S(6)} %select_n.155, s32[]{:T(128)S(6)} %select_n.159, s32[]{:T(128)S(6)} %select_n.157), kind=kLoop, calls=%fused_computation.51 | loop fusion | bytes 5505036 | tf_op jit(solution)/shard_map/dynamic_slice | solution.py:181
  113.1 2.6 collective-permute-start.5
  115.7 1.8 collective-permute-start.7
  117.5 1.5 collective-permute-start.11
  118.9 3.4 %dynamic-slice_bitcast_fusion.1 = (bf16[256,1792]{1,0:T(8,128)(2,1)}, bf16[256,1792]{1,0:T(8,128)(2,1)}, bf16[256,1792]{1,0:T(8,128)(2,1)}) fusion(bf16[1,256,7168]{2,1,0:T(8,128)(2,1)} %param.29, s32[]{:T(128)S(6)} %select_n.157, s32[]{:T(128)S(6)} %select_n.155, s32[]{:T(128)S(6)} %select_n.159), kind=kLoop, calls=%fused_computation.44 | loop fusion | bytes 5505036 | tf_op jit(solution)/shard_map/dynamic_slice | solution.py:182
  122.3 5.1 %all-to-all-done.4 = bf16[128,2,1792]{2,1,0:T(2,128)(2,1)S(1)} async-done(((bf16[128,2,1792]{2,1,0:T(2,128)(2,1)}), bf16[128,2,1792]{2,1,0:T(2,128)(2,1)S(1)}, u32[]{:S(2)}, u32[]{:S(2)}) %all-to-all-start.4) | async-done | bytes 917536 | tf_op jit(solution)/shard_map/all_to_all | solution.py:208
  127.8 1.6 collective-permute-start.8
  129.4 1.7 convolution_convert_fusion.8
  131.1 9.8 %collective-permute-done.5 = bf16[1792,256]{1,0:T(8,128)(2,1)} collective-permute-done((bf16[1792,256]{1,0:T(8,128)(2,1)}, bf16[1792,256]{1,0:T(8,128)(2,1)}, u32[]{:S(2)}, u32[]{:S(2)}) %collective-permute-start.5) | collective-permute-done | bytes 917536 | tf_op jit(solution)/shard_map/ppermute | solution.py:40
  140.8 2.4 collective-permute-start.16
  143.2 1.7 convolution_convert_fusion.7
  146.2 1.7 convolution_convert_fusion.4
  147.9 33.6 %collective-permute-done.11 = bf16[1792,256]{1,0:T(8,128)(2,1)} collective-permute-done((bf16[1792,256]{1,0:T(8,128)(2,1)}, bf16[1792,256]{1,0:T(8,128)(2,1)}, u32[]{:S(2)}, u32[]{:S(2)}) %collective-permute-start.11) | collective-permute-done | bytes 917536 | tf_op jit(solution)/shard_map/ppermute | solution.py:40
  181.5 1.7 convolution_convert_fusion.3
  183.2 2.7 collective-permute-start.12
  186.0 1.7 convolution_convert_fusion.6
  187.6 13.7 %collective-permute-done.8 = bf16[1792,256]{1,0:T(8,128)(2,1)S(1)} collective-permute-done((bf16[1792,256]{1,0:T(8,128)(2,1)}, bf16[1792,256]{1,0:T(8,128)(2,1)S(1)}, u32[]{:S(2)}, u32[]{:S(2)}) %collective-permute-start.8) | collective-permute-done | bytes 917536 | tf_op jit(solution)/shard_map/ppermute | solution.py:40
  201.9 1.7 fusion.21
  203.7 1.7 fusion.23
  205.3 21.9 %collective-permute-done.6 = bf16[256,512]{0,1:T(8,128)(2,1)S(1)} collective-permute-done((bf16[256,512]{0,1:T(8,128)(2,1)S(1)}, bf16[256,512]{0,1:T(8,128)(2,1)S(1)}, u32[]{:S(2)}, u32[]{:S(2)}) %collective-permute-start.6) | collective-permute-done | bytes 262176 | tf_op jit(solution)/shard_map/ppermute | solution.py:40
  227.3 4.9 %collective-permute-done.9 = bf16[256,512]{0,1:T(8,128)(2,1)S(1)} collective-permute-done((bf16[256,512]{0,1:T(8,128)(2,1)S(1)}, bf16[256,512]{0,1:T(8,128)(2,1)S(1)}, u32[]{:S(2)}, u32[]{:S(2)}) %collective-permute-start.9) | collective-permute-done | bytes 262176 | tf_op jit(solution)/shard_map/ppermute | solution.py:40
  232.7 2.4 collective-permute-start.13
  235.1 1.6 fusion.19
  237.6 14.7 %collective-permute-done.18 = bf16[256,1792]{1,0:T(8,128)(2,1)S(1)} collective-permute-done((bf16[256,1792]{1,0:T(8,128)(2,1)S(1)}, bf16[256,1792]{1,0:T(8,128)(2,1)S(1)}, u32[]{:S(2)}, u32[]{:S(2)}) %collective-permute-start.18) | collective-permute-done | bytes 917536 | tf_op jit(solution)/shard_map/ppermute | solution.py:40
  252.2 3.2 %collective-permute-done.17 = bf16[256,256]{0,1:T(8,128)(2,1)S(1)} collective-permute-done((bf16[256,256]{0,1:T(8,128)(2,1)S(1)}, bf16[256,256]{0,1:T(8,128)(2,1)S(1)}, u32[]{:S(2)}, u32[]{:S(2)}) %collective-permute-start.17) | collective-permute-done | bytes 131104 | tf_op jit(solution)/shard_map/ppermute | solution.py:40
  255.9 1.6 collective-permute-done.15
  259.2 7.7 %all-to-all-start.5 = ((bf16[128,2,1792]{2,1,0:T(2,128)(2,1)}), bf16[128,2,1792]{2,1,0:T(2,128)(2,1)S(1)}, u32[]{:S(2)}, u32[]{:S(2)}) async-start(bf16[128,2,1792]{2,1,0:T(2,128)(2,1)} %reshape.284), calls=%async_computation.5 | async-start | bytes 1835008 | tf_op jit(solution)/shard_map/all_to_all | solution.py:236
  267.9 16.7 %all-to-all-done.5 = bf16[128,2,1792]{2,1,0:T(2,128)(2,1)S(1)} async-done(((bf16[128,2,1792]{2,1,0:T(2,128)(2,1)}), bf16[128,2,1792]{2,1,0:T(2,128)(2,1)S(1)}, u32[]{:S(2)}, u32[]{:S(2)}) %all-to-all-start.5) | async-done | bytes 917536 | tf_op jit(solution)/shard_map/all_to_all | solution.py:236
  (116 shorter events, 25.3 us)
Async XLA Ops:
  0.6 72.1 %copy-start = (bf16[2,512,128]{2,1,0:T(8,128)(2,1)S(1)}, bf16[2,512,128]{2,1,0:T(8,128)(2,1)}, u32[]{:S(2)}) copy-start(bf16[2,512,128]{2,1,0:T(8,128)(2,1)} %param.21) | copy-start | bytes 786436
  2.4 19.1 %all-to-all-start = ((bf16[32,6,576]{2,1,0:T(8,128)(2,1)}), bf16[32,6,576]{2,1,0:T(8,128)(2,1)S(1)}, u32[]{:S(2)}, u32[]{:S(2)}) async-start(bf16[32,6,576]{2,1,0:T(8,128)(2,1)} %bitcast.137), calls=%async_computation | async-start | bytes 655360 | tf_op jit(solution)/shard_map/all_to_all | solution.py:69
  21.7 8.5 %collective-permute-start.2 = (bf16[192,576]{1,0:T(8,128)(2,1)S(1)}, bf16[192,576]{1,0:T(8,128)(2,1)S(1)}, u32[]{:S(2)}, u32[]{:S(2)}) collective-permute-start(bf16[192,576]{1,0:T(8,128)(2,1)S(1)} %reshape.274), channel_id=1, source_target_pairs={{96,0},{0,32},{32,64},{64,96},{97,1},{1,33},{33,65},{65,97},{98,2}... | collective-permute-start | bytes 663560 | tf_op jit(solution)/shard_map/ppermute | solution.py:40
  23.0 13.5 %collective-permute-start.1 = (bf16[192,576]{1,0:T(8,128)(2,1)S(1)}, bf16[192,576]{1,0:T(8,128)(2,1)S(1)}, u32[]{:S(2)}, u32[]{:S(2)}) collective-permute-start(bf16[192,576]{1,0:T(8,128)(2,1)S(1)} %reshape.274), channel_id=1, source_target_pairs={{64,0},{96,32},{0,64},{32,96},{65,1},{97,33},{1,65},{33,97},{66,2}... | collective-permute-start | bytes 663560 | tf_op jit(solution)/shard_map/ppermute | solution.py:40
  25.5 11.0 %collective-permute-start = (bf16[192,576]{1,0:T(8,128)(2,1)S(1)}, bf16[192,576]{1,0:T(8,128)(2,1)S(1)}, u32[]{:S(2)}, u32[]{:S(2)}) collective-permute-start(bf16[192,576]{1,0:T(8,128)(2,1)S(1)} %reshape.274), channel_id=1, source_target_pairs={{32,0},{64,32},{96,64},{0,96},{33,1},{65,33},{97,65},{1,97},{34,2}... | collective-permute-start | bytes 663560 | tf_op jit(solution)/shard_map/ppermute | solution.py:40
  36.5 1.3 copy-start.11
  37.0 0.8 copy-start.2
  37.8 0.6 copy-start.8
  39.8 17.7 %all-to-all-start.1 = ((bf16[32,9,576]{2,1,0:T(8,128)(2,1)}), bf16[32,9,576]{2,1,0:T(8,128)(2,1)S(1)}, u32[]{:S(2)}, u32[]{:S(2)}) async-start(bf16[32,9,576]{2,1,0:T(8,128)(2,1)} %reshape.275), calls=%async_computation.1 | async-start | bytes 1310720 | tf_op jit(solution)/shard_map/all_to_all | solution.py:108
  60.2 12.4 %all-to-all-start.2 = ((bf16[32,3,2,512]{3,2,1,0:T(2,128)(2,1)}), bf16[32,3,2,512]{3,2,1,0:T(2,128)(2,1)S(1)}, u32[]{:S(2)}, u32[]{:S(2)}) async-start(bf16[32,3,2,512]{3,2,1,0:T(2,128)(2,1)} %bitcast.138), calls=%async_computation.2 | async-start | bytes 393216 | tf_op jit(solution)/shard_map/all_to_all | solution.py:144
  77.1 2.2 collective-permute-start.3
  81.1 19.9 %all-to-all-start.3 = ((bf16[16,3,7168]{2,1,0:T(4,128)(2,1)}), bf16[16,3,7168]{2,1,0:T(4,128)(2,1)S(1)}, u32[]{:S(2)}, u32[]{:S(2)}) async-start(bf16[16,3,7168]{2,1,0:T(4,128)(2,1)} %fusion.6), calls=%async_computation.3 | async-start | bytes 1835008 | tf_op jit(solution)/shard_map/all_to_all | solution.py:159
  84.8 5.2 %copy-start.12 = (s32[1,3,8]{2,0,1:T(1,128)S(1)}, s32[1,3,8]{2,0,1:T(1,128)}, u32[]{:S(2)}) copy-start(s32[1,3,8]{2,0,1:T(1,128)} %param.25) | copy-start | bytes 292
  84.8 5.3 %copy-start.10 = (f32[7168]{0:T(1024)S(1)}, f32[7168]{0:T(1024)}, u32[]{:S(2)}) copy-start(f32[7168]{0:T(1024)} %param.24) | copy-start | bytes 86020
  84.8 5.3 %copy-start.7 = (bf16[1,3,7168]{2,1,0:T(4,128)(2,1)S(1)}, bf16[1,3,7168]{2,1,0:T(4,128)(2,1)}, u32[]{:S(2)}) copy-start(bf16[1,3,7168]{2,1,0:T(4,128)(2,1)} %param.23) | copy-start | bytes 129028
  88.0 39.8 %collective-permute-start.4 = (bf16[1792,256]{1,0:T(8,128)(2,1)}, bf16[1792,256]{1,0:T(8,128)(2,1)}, u32[]{:S(2)}, u32[]{:S(2)}) collective-permute-start(bf16[1792,256]{1,0:T(8,128)(2,1)} %get-tuple-element.18), channel_id=1, source_target_pairs={{32,0},{64,32},{96,64},{0,96},{33,1},{65,33},{97,65},{1,97},{34,2}... | collective-permute-start | bytes 2752520 | tf_op jit(solution)/shard_map/ppermute | solution.py:40
  104.1 23.3 %all-to-all-start.4 = ((bf16[128,2,1792]{2,1,0:T(2,128)(2,1)}), bf16[128,2,1792]{2,1,0:T(2,128)(2,1)S(1)}, u32[]{:S(2)}, u32[]{:S(2)}) async-start(bf16[128,2,1792]{2,1,0:T(2,128)(2,1)} %copy.69), calls=%async_computation.4 | async-start | bytes 1835008 | tf_op jit(solution)/shard_map/all_to_all | solution.py:208
  113.1 27.7 %collective-permute-start.5 = (bf16[1792,256]{1,0:T(8,128)(2,1)}, bf16[1792,256]{1,0:T(8,128)(2,1)}, u32[]{:S(2)}, u32[]{:S(2)}) collective-permute-start(bf16[1792,256]{1,0:T(8,128)(2,1)} %get-tuple-element.21), channel_id=1, source_target_pairs={{32,0},{64,32},{96,64},{0,96},{33,1},{65,33},{97,65},{1,97},{34,2}... | collective-permute-start | bytes 2752520 | tf_op jit(solution)/shard_map/ppermute | solution.py:40
  115.7 29.2 %collective-permute-start.10 = (bf16[1792,256]{1,0:T(8,128)(2,1)}, bf16[1792,256]{1,0:T(8,128)(2,1)}, u32[]{:S(2)}, u32[]{:S(2)}) collective-permute-start(bf16[1792,256]{1,0:T(8,128)(2,1)} %get-tuple-element.19), channel_id=1, source_target_pairs={{96,0},{0,32},{32,64},{64,96},{97,1},{1,33},{33,65},{65,97},{98,2}... | collective-permute-start | bytes 2752520 | tf_op jit(solution)/shard_map/ppermute | solution.py:40
  115.7 67.5 %collective-permute-start.7 = (bf16[1792,256]{1,0:T(8,128)(2,1)S(1)}, bf16[1792,256]{1,0:T(8,128)(2,1)}, u32[]{:S(2)}, u32[]{:S(2)}) collective-permute-start(bf16[1792,256]{1,0:T(8,128)(2,1)S(1)} %get-tuple-element.20), channel_id=1, source_target_pairs={{64,0},{96,32},{0,64},{32,96},{65,1},{97,33},{1,65},{33,97},{66,2}... | collective-permute-start | bytes 2752520 | tf_op jit(solution)/shard_map/ppermute | solution.py:40
  117.5 64.1 %collective-permute-start.11 = (bf16[1792,256]{1,0:T(8,128)(2,1)}, bf16[1792,256]{1,0:T(8,128)(2,1)}, u32[]{:S(2)}, u32[]{:S(2)}) collective-permute-start(bf16[1792,256]{1,0:T(8,128)(2,1)} %get-tuple-element.22), channel_id=1, source_target_pairs={{96,0},{0,32},{32,64},{64,96},{97,1},{1,33},{33,65},{65,97},{98,2}... | collective-permute-start | bytes 2752520 | tf_op jit(solution)/shard_map/ppermute | solution.py:40
  127.8 13.0 %copy-start.4 = (bf16[256,1792]{1,0:T(8,128)(2,1)S(1)}, bf16[256,1792]{1,0:T(8,128)(2,1)}, u32[]{:S(2)}) copy-start(bf16[256,1792]{1,0:T(8,128)(2,1)} %get-tuple-element.15) | copy-start | bytes 2752516
  127.8 17.1 %copy-start.6 = (bf16[256,1792]{1,0:T(8,128)(2,1)S(1)}, bf16[256,1792]{1,0:T(8,128)(2,1)}, u32[]{:S(2)}) copy-start(bf16[256,1792]{1,0:T(8,128)(2,1)} %get-tuple-element.16) | copy-start | bytes 2752516
  127.8 73.5 %collective-permute-start.8 = (bf16[1792,256]{1,0:T(8,128)(2,1)}, bf16[1792,256]{1,0:T(8,128)(2,1)S(1)}, u32[]{:S(2)}, u32[]{:S(2)}) collective-permute-start(bf16[1792,256]{1,0:T(8,128)(2,1)} %get-tuple-element.23), channel_id=1, source_target_pairs={{64,0},{96,32},{0,64},{32,96},{65,1},{97,33},{1,65},{33,97},{66,2}... | collective-permute-start | bytes 2752520 | tf_op jit(solution)/shard_map/ppermute | solution.py:40
  140.8 115.0 %collective-permute-start.16 = (bf16[256,1792]{1,0:T(8,128)(2,1)S(1)}, bf16[256,1792]{1,0:T(8,128)(2,1)S(1)}, u32[]{:S(2)}, u32[]{:S(2)}) collective-permute-start(bf16[256,1792]{1,0:T(8,128)(2,1)S(1)} %copy-done.4), channel_id=1, source_target_pairs={{64,0},{96,32},{0,64},{32,96},{65,1},{97,33},{1,65},{33,97},{66,2}... | collective-permute-start | bytes 2752520 | tf_op jit(solution)/shard_map/ppermute | solution.py:40
  144.9 91.8 %collective-permute-start.14 = (bf16[256,1792]{1,0:T(8,128)(2,1)S(1)}, bf16[256,1792]{1,0:T(8,128)(2,1)S(1)}, u32[]{:S(2)}, u32[]{:S(2)}) collective-permute-start(bf16[256,1792]{1,0:T(8,128)(2,1)S(1)} %copy-done.6), channel_id=1, source_target_pairs={{32,0},{64,32},{96,64},{0,96},{33,1},{65,33},{97,65},{1,97},{34,2}... | collective-permute-start | bytes 2752520 | tf_op jit(solution)/shard_map/ppermute | solution.py:40
  181.5 45.7 %collective-permute-start.6 = (bf16[256,512]{0,1:T(8,128)(2,1)S(1)}, bf16[256,512]{0,1:T(8,128)(2,1)S(1)}, u32[]{:S(2)}, u32[]{:S(2)}) collective-permute-start(bf16[256,512]{0,1:T(8,128)(2,1)S(1)} %pad_maximum_fusion), channel_id=1, source_target_pairs={{96,0},{0,32},{32,64},{64,96},{97,1},{1,33},{33,65},{65,97},{98,2}... | collective-permute-start | bytes 786440 | tf_op jit(solution)/shard_map/ppermute | solution.py:40
  183.2 44.0 %collective-permute-start.12 = (bf16[256,512]{0,1:T(8,128)(2,1)S(1)}, bf16[256,512]{0,1:T(8,128)(2,1)S(1)}, u32[]{:S(2)}, u32[]{:S(2)}) collective-permute-start(bf16[256,512]{0,1:T(8,128)(2,1)S(1)} %pad_maximum_fusion.2), channel_id=1, source_target_pairs={{32,0},{64,32},{96,64},{0,96},{33,1},{65,33},{97,65},{1,97},{34,2}... | collective-permute-start | bytes 786440 | tf_op jit(solution)/shard_map/ppermute | solution.py:40
  201.8 25.4 %copy-start.5 = (bf16[256,1792]{1,0:T(8,128)(2,1)S(1)}, bf16[256,1792]{1,0:T(8,128)(2,1)}, u32[]{:S(2)}) copy-start(bf16[256,1792]{1,0:T(8,128)(2,1)} %get-tuple-element.17) | copy-start | bytes 2752516
  201.8 30.4 %collective-permute-start.9 = (bf16[256,512]{0,1:T(8,128)(2,1)S(1)}, bf16[256,512]{0,1:T(8,128)(2,1)S(1)}, u32[]{:S(2)}, u32[]{:S(2)}) collective-permute-start(bf16[256,512]{0,1:T(8,128)(2,1)S(1)} %pad_maximum_fusion.1), channel_id=1, source_target_pairs={{64,0},{96,32},{0,64},{32,96},{65,1},{97,33},{1,65},{33,97},{66,2}... | collective-permute-start | bytes 786440 | tf_op jit(solution)/shard_map/ppermute | solution.py:40
  227.2 25.0 %collective-permute-start.18 = (bf16[256,1792]{1,0:T(8,128)(2,1)S(1)}, bf16[256,1792]{1,0:T(8,128)(2,1)S(1)}, u32[]{:S(2)}, u32[]{:S(2)}) collective-permute-start(bf16[256,1792]{1,0:T(8,128)(2,1)S(1)} %copy-done.5), channel_id=1, source_target_pairs={{96,0},{0,32},{32,64},{64,96},{97,1},{1,33},{33,65},{65,97},{98,2}... | collective-permute-start | bytes 2752520 | tf_op jit(solution)/shard_map/ppermute | solution.py:40
  232.4 23.0 %collective-permute-start.17 = (bf16[256,256]{0,1:T(8,128)(2,1)S(1)}, bf16[256,256]{0,1:T(8,128)(2,1)S(1)}, u32[]{:S(2)}, u32[]{:S(2)}) collective-permute-start(bf16[256,256]{0,1:T(8,128)(2,1)S(1)} %fusion.37), channel_id=1, source_target_pairs={{96,0},{0,32},{32,64},{64,96},{97,1},{1,33},{33,65},{65,97},{98,2}... | collective-permute-start | bytes 393224 | tf_op jit(solution)/shard_map/ppermute | solution.py:40
  232.7 4.4 %collective-permute-start.13 = (bf16[256,256]{0,1:T(8,128)(2,1)S(1)}, bf16[256,256]{0,1:T(8,128)(2,1)S(1)}, u32[]{:S(2)}, u32[]{:S(2)}) collective-permute-start(bf16[256,256]{0,1:T(8,128)(2,1)S(1)} %fusion.37), channel_id=1, source_target_pairs={{32,0},{64,32},{96,64},{0,96},{33,1},{65,33},{97,65},{1,97},{34,2}... | collective-permute-start | bytes 393224 | tf_op jit(solution)/shard_map/ppermute | solution.py:40
  236.8 20.7 %collective-permute-start.15 = (bf16[256,256]{0,1:T(8,128)(2,1)S(1)}, bf16[256,256]{0,1:T(8,128)(2,1)S(1)}, u32[]{:S(2)}, u32[]{:S(2)}) collective-permute-start(bf16[256,256]{0,1:T(8,128)(2,1)S(1)} %fusion.37), channel_id=1, source_target_pairs={{64,0},{96,32},{0,64},{32,96},{65,1},{97,33},{1,65},{33,97},{66,2}... | collective-permute-start | bytes 393224 | tf_op jit(solution)/shard_map/ppermute | solution.py:40
  257.9 9.0 %copy-start.13 = (f32[1,3,8]{2,0,1:T(1,128)S(1)}, f32[1,3,8]{2,0,1:T(1,128)}, u32[]{:S(2)}) copy-start(f32[1,3,8]{2,0,1:T(1,128)} %param.26) | copy-start | bytes 292
  257.9 9.1 %copy-start.3 = (f32[192,576]{1,0:T(8,128)S(1)}, f32[192,576]{1,0:T(8,128)}, u32[]{:S(2)}) copy-start(f32[192,576]{1,0:T(8,128)} %copy-done.2) | copy-start | bytes 1327108
  258.0 9.2 %copy-start.9 = (bf16[192,32]{1,0:T(8,128)(2,1)S(1)}, bf16[192,32]{1,0:T(8,128)(2,1)}, u32[]{:S(2)}) copy-start(bf16[192,32]{1,0:T(8,128)(2,1)} %copy-done.8) | copy-start | bytes 36868
  259.2 25.4 %all-to-all-start.5 = ((bf16[128,2,1792]{2,1,0:T(2,128)(2,1)}), bf16[128,2,1792]{2,1,0:T(2,128)(2,1)S(1)}, u32[]{:S(2)}, u32[]{:S(2)}) async-start(bf16[128,2,1792]{2,1,0:T(2,128)(2,1)} %reshape.284), calls=%async_computation.5 | async-start | bytes 1835008 | tf_op jit(solution)/shard_map/all_to_all | solution.py:236
  284.6 2.6 copy-start.1

commit v2 on v1

v2 whole, which is shorter than its diff:
```python
import jax
import jax.numpy as jnp
from jax import lax
from jax.experimental import pallas as pl
from jax.experimental.pallas import tpu as pltpu
from jax.sharding import PartitionSpec as P

LAT = 512
UNIT = 32
MOST = 3
SLOTS = 10

eps = 1e-06
theta = 10000.0
score_scale = 192.0 ** (-0.5)
BF = jnp.bfloat16
F32 = jnp.float32
I32 = jnp.int32


def turn(positions, half_width):
    frequency = theta ** (-jnp.arange(half_width, dtype=F32) / half_width)
    angles = positions.astype(F32)[:, None] * frequency[None, :]
    return jnp.cos(angles), jnp.sin(angles)


def norm_rotate(raw_rows, cosine, sine, kv_gain):
    raw_rows = raw_rows.astype(F32)
    latent = raw_rows[:, :LAT]
    half_width = cosine.shape[1]
    inverse = lax.rsqrt(jnp.mean(latent * latent, axis=1, keepdims=True) + eps)
    latent = latent * inverse * kv_gain
    lower = raw_rows[:, LAT : LAT + half_width]
    upper = raw_rows[:, LAT + half_width :]
    return jnp.concatenate(
        [latent, lower * cosine - upper * sine, upper * cosine + lower * sine], axis=1
    ).astype(BF)


def shift(x, step, size, axis):
    return lax.ppermute(x, axis, [((i + step) % size, i) for i in range(size)])


def attend_kernel(
    place_ref,
    count_ref,
    member_ref,
    number_ref,
    *refs,
    blocks,
    most_slots,
    sent_slots,
):
    rows_in = refs[:blocks]
    extra_in = refs[blocks : 2 * blocks]
    cos_ref, sin_ref, gain_ref, new_ref, query_ref, out_ref, keys, query, sems = refs[2 * blocks :]
    number = number_ref[0]

    def fetch(slot):
        return pltpu.make_async_copy(
            query_ref.at[member_ref[slot]], query.at[slot], sems.at[slot]
        )

    @pl.loop(0, number)
    def _(slot):
        fetch(slot).start()

    gain = gain_ref[...]
    start = 0
    for block in range(blocks):
        for ref in (rows_in[block], extra_in[block]):
            size = ref.shape[0]
            span = slice(start, start + size)
            keys[span, :] = norm_rotate(ref[...], cos_ref[span, :], sin_ref[span, :], gain)
            start += size

    @pl.loop(number, sent_slots)
    def _(slot):
        out_ref[slot] = jnp.zeros(out_ref.shape[1:], BF)

    heads = out_ref.shape[1]
    window = MOST * UNIT
    lanes = window + UNIT
    lane = lax.broadcasted_iota(I32, (heads, lanes), 1)

    @pl.loop(0, number)
    def _(slot):
        fetch(slot).wait()
        place = pl.multiple_of(place_ref[slot], UNIT)
        own = keys[pl.ds(place, window), :]
        new = jnp.broadcast_to(
            new_ref[pl.ds(member_ref[slot], 1), :].astype(BF), (UNIT, own.shape[1])
        )
        held = jnp.concatenate([own, new], axis=0)
        scores = (
            lax.dot_general(
                query[slot], held, (((1,), (1,)), ((), ())), preferred_element_type=F32
            )
            * score_scale
        )
        live = (lane < count_ref[slot] * UNIT) | (lane == window)
        scores = jnp.where(live, scores, -jnp.inf)
        weights = jnp.exp(scores - jnp.max(scores, axis=1, keepdims=True))
        total = jnp.sum(weights, axis=1, keepdims=True)
        mixture = jnp.dot(weights.astype(BF), held[:, :LAT], preferred_element_type=F32)
        out_ref[slot] = (mixture / total).astype(BF)


def attend(tables, rows, extras, cosine, sine, gain, new_keys, queries, most_slots):
    heads = queries.shape[1]
    blocks = len(rows)
    total_rows = cosine.shape[0]
    whole = pl.BlockSpec(memory_space=pltpu.VMEM)
    scalar = pl.BlockSpec(memory_space=pltpu.SMEM)

    def body(*refs):
        attend_kernel(*refs, blocks=blocks, most_slots=most_slots, sent_slots=SLOTS)

    return pl.pallas_call(
        body,
        out_shape=jax.ShapeDtypeStruct((most_slots, heads, LAT), BF),
        in_specs=[scalar] * 4
        + [whole] * (2 * blocks + 4)
        + [pl.BlockSpec(memory_space=pl.ANY)],
        out_specs=whole,
        scratch_shapes=[
            pltpu.VMEM((total_rows, queries.shape[2]), BF),
            pltpu.VMEM((most_slots,) + queries.shape[1:], BF),
            pltpu.SemaphoreType.DMA((most_slots,)),
        ],
        compiler_params=pltpu.CompilerParams(vmem_limit_bytes=32 * 1024 * 1024),
        cost_estimate=pl.CostEstimate(
            flops=10**8, bytes_accessed=4 * 10**6, transcendentals=10**5
        ),
        name="attend",
    )(*tables, *rows, *extras, cosine, sine, gain, new_keys, queries)


def shards(
    latent_rows,
    new_rows,
    kv_gain,
    lengths,
    owners,
    queries,
    w_uv,
    w_out,
    resid,
    moe_gain,
    route_ids,
    route_weights,
    w_gate,
    w_up,
    w_down,
):
    dp_count = lax.axis_size("dp")
    columns = lax.axis_size("expert")
    devices = dp_count * columns
    group = lax.axis_index("dp")
    column = lax.axis_index("expert")
    core = column % 2
    pre_rows, width = latent_rows.shape
    half_rope = (width - LAT) // 2
    local_units = pre_rows // UNIT
    block_units = columns * local_units
    gain = kv_gain[None, :]

    border = (MOST - 1) * UNIT
    next_rows = lax.ppermute(
        latent_rows[:border],
        ("dp", "expert"),
        [((i + 1) % devices, i) for i in range(devices)],
    )
    rows = [latent_rows] + [shift(latent_rows, k, dp_count, "dp") for k in range(1, dp_count)]
    extras = [next_rows] + [shift(next_rows, k, dp_count, "dp") for k in range(1, dp_count)]

    by_row = latent_rows.reshape(local_units, UNIT, width).transpose(1, 0, 2)
    dealt = lax.all_to_all(by_row, "expert", split_axis=0, concat_axis=0, tiled=True)
    dealt = dealt.reshape(block_units, width)

    requests = lengths.shape[0]
    request_total = queries.shape[1]
    unit_len = lengths // UNIT
    order = jnp.arange(requests, dtype=I32)
    before = order[None, :] < order[:, None]
    unit_start = jnp.sum(jnp.where(before, unit_len[None, :], 0), axis=1)
    home = owners * columns + unit_start // local_units % columns
    home_rank = jnp.sum((before & (home[None, :] == home[:, None])).astype(I32), axis=1)
    own = owners == group
    own_before = before & own[None, :]
    group_start = jnp.sum(jnp.where(own_before, unit_len[None, :], 0), axis=1)
    group_rank = jnp.sum(own_before.astype(I32), axis=1)

    most_slots = dp_count * local_units
    slot_order = jnp.arange(most_slots, dtype=I32)
    here = home == group * columns + column
    is_slot = here[None, :] & (home_rank[None, :] == slot_order[:, None])
    start_block = (unit_start // block_units - group + dp_count) % dp_count
    start_place = start_block * (pre_rows + border) + unit_start % local_units * UNIT
    slot_place = jnp.sum(jnp.where(is_slot, start_place[None, :], 0), axis=1)
    slot_count = jnp.sum(jnp.where(is_slot, unit_len[None, :], 0), axis=1)
    slot_member = jnp.sum(jnp.where(is_slot, group_rank[None, :], 0), axis=1)
    slot_number = jnp.sum(here.astype(I32), keepdims=True)

    near_units = local_units + MOST - 1
    near = jnp.arange(near_units * dp_count, dtype=I32)
    near_block = (group + near // near_units) % dp_count
    near_unit = near_block * block_units + column * local_units + near % near_units
    near_start = jnp.max(
        jnp.where(unit_start[None, :] <= near_unit[:, None], unit_start[None, :], 0), axis=1
    )
    near_position = ((near_unit - near_start) * UNIT)[:, None] + jnp.arange(UNIT, dtype=I32)
    cosine, sine = turn(near_position.reshape(-1), half_rope)
    members = jnp.arange(request_total, dtype=I32)
    is_member = own[None, :] & (group_rank[None, :] == members[:, None])
    member_length = jnp.sum(jnp.where(is_member, lengths[None, :], 0), axis=1)
    new_keys = norm_rotate(new_rows[0], *turn(member_length, half_rope), gain).astype(F32)

    attended = attend(
        (slot_place, slot_count, slot_member, slot_number),
        rows,
        extras,
        cosine,
        sine,
        gain,
        new_keys,
        queries[0],
        most_slots,
    )

    model_width = w_out.shape[1]
    piece = model_width // dp_count
    halves = (0, 1, 1, 0)
    quarters = (0, 2, 3, 1)

    def pair_perm(partner):
        perm = []
        for f in range(dp_count):
            for x in range(columns):
                g = (f - x % 2) % dp_count
                perm.append((f * columns + x, (partner(g) + x % 2) % dp_count * columns + x))
        return perm

    weight_perm = pair_perm(lambda g: g ^ 1)
    token_perm = pair_perm(lambda g: dp_count - 1 - g)
    place = (group - core + dp_count) % dp_count
    quarter_of = jnp.array(quarters, I32)
    my_quarter = quarter_of[place]
    their_quarter = quarter_of[place ^ 1]

    def width_half(first):
        def side(q):
            return jnp.concatenate(
                [
                    lax.dynamic_slice_in_dim(w_gate[0], q * piece, piece, 0),
                    lax.dynamic_slice_in_dim(w_up[0], q * piece, piece, 0),
                ],
                axis=1,
            )

        return jnp.stack([side(first), side(first ^ 1)])

    to_partner, attended = lax.optimization_barrier((width_half(their_quarter), attended))
    from_partner = lax.ppermute(to_partner, ("dp", "expert"), weight_perm)
    dealt, attended = lax.optimization_barrier((dealt, attended))

    blocks = jnp.concatenate(
        [dealt] + [shift(dealt, k, dp_count, "dp") for k in range(1, dp_count)], axis=0
    )
    slots = jnp.arange(pre_rows, dtype=I32)
    offset = slots[:, None] - group_start[None, :]
    covers = own[None, :] & (offset >= 0) & (offset < unit_len[None, :])
    slot_offset = jnp.sum(jnp.where(covers, offset, 0), axis=1)
    slot_unit = jnp.sum(jnp.where(covers, offset + unit_start[None, :], 0), axis=1)
    relative = (slot_unit // block_units - group + dp_count) % dp_count
    cache_place = relative * block_units + slot_unit % block_units
    places = jnp.arange(dp_count * block_units, dtype=I32)
    pick = (cache_place[:, None] == places[None, :]).astype(BF)
    raw_cache = jnp.dot(pick, blocks, preferred_element_type=F32)
    cache_local = norm_rotate(
        raw_cache, *turn(slot_offset * UNIT + column, half_rope), gain
    )

    head_share = w_uv.shape[0]
    share = request_total // columns
    chips = columns // 2

    def to_heads(part):
        count = part.shape[0]
        part = part.reshape(count, columns, head_share * LAT).transpose(1, 0, 2)
        part = lax.all_to_all(part, "expert", split_axis=0, concat_axis=0, tiled=True)
        return part.reshape(columns * count, head_share * LAT)

    member_column = group_rank // share
    member_row = (
        (member_column % 2 ^ core) * (chips * share)
        + member_column // 2 * share
        + group_rank % share
    )
    member_home = unit_start // local_units % columns
    is_row = own[None, :] & (member_row[None, :] == members[:, None])
    row_home = jnp.sum(jnp.where(is_row, member_home[None, :], 0), axis=1)
    row_slot = jnp.sum(jnp.where(is_row, home_rank[None, :], 0), axis=1)

    def in_order(part, first):
        count = part.shape[0]
        came = to_heads(part)
        cells = jnp.arange(columns * count, dtype=I32)
        wanted = row_home * count + row_slot - first
        inside = (row_slot >= first) & (row_slot < first + count)
        pick = (inside[:, None] & (wanted[:, None] == cells[None, :])).astype(BF)
        return jnp.dot(pick, came, preferred_element_type=F32)

    by_head = in_order(attended[:SLOTS], 0)
    by_head = lax.cond(
        jnp.max(home_rank) >= SLOTS,
        lambda held: held
        + in_order(
            jnp.where(
                slot_order[SLOTS:, None, None] < slot_number[0], attended[SLOTS:], jnp.zeros((), BF)
            ),
            SLOTS,
        ),
        lambda held: held,
        by_head,
    )
    by_head, cache_local = lax.optimization_barrier((by_head, cache_local))
    by_head = by_head.astype(BF).reshape(request_total, head_share, LAT)
    projected = jnp.einsum("jhl,hlv->jhv", by_head, w_uv, preferred_element_type=F32).astype(BF)
    partial_sums = jnp.dot(
        projected.reshape(request_total, -1), w_out, preferred_element_type=F32
    ).astype(BF)

    keep = chips * share
    other = lax.ppermute(partial_sums[keep:], "expert", [(i, i ^ 1) for i in range(columns)])
    pair_sums = (partial_sums[:keep].astype(F32) + other.astype(F32)).astype(BF)
    chip_sums = lax.all_to_all(
        pair_sums.reshape(chips, share, model_width),
        "expert",
        split_axis=0,
        concat_axis=0,
        tiled=True,
        axis_index_groups=[[2 * i + c for i in range(chips)] for c in range(2)],
    )
    attention_out = jnp.sum(chip_sums.astype(F32), axis=0)
    residual = resid[0].astype(F32) + attention_out
    normed = (
        residual
        * lax.rsqrt(jnp.mean(residual * residual, axis=1, keepdims=True) + eps)
        * moe_gain[None, :]
    ).astype(BF)

    downs = []
    down_held, _ = lax.optimization_barrier((w_down[0], by_head))
    for k in range(dp_count):
        to = (group - k + dp_count) % dp_count * piece
        part = lax.dynamic_slice_in_dim(down_held, to, piece, 1)
        downs.append(shift(part, k, dp_count, "dp") if k else part)

    tokens = resid.shape[1]
    capacity = 2
    expert_ids = jnp.arange(columns, dtype=I32)
    matches = route_ids[0][:, :, None] == expert_ids[None, None, :]
    combine_weights = jnp.sum(jnp.where(matches, route_weights[0][:, :, None], 0.0), axis=1)
    routed = jnp.any(matches, axis=1)
    token_order = jnp.arange(tokens, dtype=I32)
    earlier = token_order[None, :] < token_order[:, None]
    slot_rank = jnp.sum(jnp.where(earlier[:, :, None], routed.astype(I32)[None, :, :], 0), axis=1)
    slot_ids = jnp.arange(capacity, dtype=I32)
    slot_table = routed.T[:, None, :] & (slot_rank.T[:, None, :] == slot_ids[None, :, None])
    table = slot_table.reshape(columns * capacity, tokens)
    even = (jnp.arange(columns * capacity, dtype=I32) // capacity % 2 == 0)[:, None]
    table = jnp.concatenate([table & even, table & ~even], axis=1).astype(BF)
    outgoing = []
    for f in range(dp_count):
        both = jnp.concatenate(
            [
                normed[:, q * piece : (q + 1) * piece]
                for q in (quarters[f], quarters[(f - 1) % dp_count])
            ],
            axis=0,
        )
        outgoing.append(jnp.dot(table, both, preferred_element_type=F32).astype(BF))
    outgoing = jnp.stack(outgoing).reshape(devices, capacity, piece)
    outgoing, from_partner = lax.optimization_barrier((outgoing, from_partner))
    arrived = lax.all_to_all(
        outgoing, ("dp", "expert"), split_axis=0, concat_axis=0, tiled=True
    ).reshape(devices * capacity, piece)
    beside = lax.ppermute(arrived, ("dp", "expert"), token_perm)

    def gate_up(first, second):
        return jnp.dot(arrived, first, preferred_element_type=F32) + jnp.dot(
            beside, second, preferred_element_type=F32
        )

    given = gate_up(from_partner[0], from_partner[1]).astype(BF)
    given = lax.ppermute(given, ("dp", "expert"), weight_perm)
    own_half = width_half(my_quarter)
    sums = gate_up(own_half[0], own_half[1]) + given.astype(F32)
    half = sums.shape[1] // 2
    hidden = (jax.nn.silu(sums[:, :half]) * sums[:, half:]).astype(BF)
    hidden_all = jnp.concatenate(
        [hidden] + [shift(hidden, k, dp_count, "dp") for k in range(1, dp_count)], axis=1
    )
    out = jnp.dot(hidden_all, jnp.concatenate(downs, axis=0), preferred_element_type=F32)
    returned = lax.all_to_all(
        out.astype(BF).reshape(devices, capacity, piece),
        ("dp", "expert"),
        split_axis=0,
        concat_axis=0,
        tiled=True,
    )
    slot_weights = jnp.where(slot_table, combine_weights.T[:, None, :], 0.0)
    moe_sum = jnp.einsum(
        "xct,fxcd->tfd",
        slot_weights,
        returned.reshape(dp_count, columns, capacity, piece).astype(F32),
        precision=lax.Precision.HIGHEST,
    ).reshape(tokens, model_width)
    decoded = (residual + moe_sum).astype(BF)
    return (cache_local[None, None], decoded[None])


def solution(mesh):
    return jax.shard_map(
        shards,
        mesh=mesh,
        in_specs=(
            P(("dp", "expert"), None),
            P("dp", None, None),
            P(),
            P(),
            P(),
            P("dp", None, None, None),
            P("expert", None, None),
            P("expert", None),
            P("dp", "expert", None),
            P(),
            P("dp", "expert", None),
            P("dp", "expert", None),
            P("expert", None, "dp"),
            P("expert", None, "dp"),
            P("expert", "dp", None),
        ),
        out_specs=(P("dp", "expert", None, None), P("dp", "expert", None)),
        check_vma=False,
    )
```

time: 288 us -> 255 us (0.89)
  waiting for transfers between devices: 173 us -> 121 us
  blocking collectives: 0 us -> 24.2 us
  starting transfers between devices: 59.3 us -> 46.7 us
  matrix products: 23.2 us -> 13.8 us
  Pallas kernels: 0 us -> 6.08 us
  other arithmetic: 8.74 us -> 13.9 us
  between operations: 1.3 us -> 4.65 us
    ppermute x18 -> x15, waiting for transfers between devices: 113 us -> 14.8 us  [shift(): return lax.ppermute(x, axis, [((i + step) % size, i) for i in range(size)])]
    ppermute x1 -> x5, waiting for transfers between devices: 1.97 us -> 59 us  [the longest x1 32.1 us: shards(): given = lax.ppermute(given, ('dp', 'expert'), weight_perm)]
    all_to_all x0 -> x1, blocking collectives: none -> 24.2 us  [shards(): lax.all_to_all(outgoing, ('dp', 'expert'), split_axis=0, concat_axis=0, t...]
    ppermute x18 -> x15, starting transfers between devices: 23.8 us -> 12.2 us  [shift(): return lax.ppermute(x, axis, [((i + step) % size, i) for i in range(size)])]
    dot_general x17 -> x10, matrix products: 18.6 us -> 8.18 us  [the longest x2 2.9 us: gate_up(): jnp.dot(arrived, first, preferred_element_type=F32)]
    all_to_all x5 -> x3, starting transfers between devices: 25.6 us -> 19.2 us  [the longest x1 10.1 us: to_heads(): lax.all_to_all(part, 'expert', split_axis=0, concat_axis=0, tiled=True)]
    pallas_call x0 -> x1, Pallas kernels: none -> 6.08 us  [attend(): pl.pallas_call(body, out_shape=jax.ShapeDtypeStruct((most_slots, heads, L...]
    all_to_all x1, waiting for transfers between devices: 5.37 us -> 0.01 us  [shards(): lax.all_to_all(by_row, 'expert', split_axis=0, concat_axis=0, tiled=True)]
  transfers between devices with their start and end apart: 25 -> 24, of which waited for: 17 -> 13; matrix products, arithmetic and copies ran while one was open for 12% -> 15% of each run, Pallas kernels for 0% -> 0%
where the time goes in v2:
time: 255 us; the launch traced here: 254 us
  waiting for transfers between devices  121 us (47%)
  starting transfers between devices  46.7 us (18%)
  blocking collectives  24.2 us (9%)
  local copies, waits for them, and re-layouts  23.6 us (9%)
  other arithmetic  13.9 us (5%)
  matrix products  13.8 us (5%)
  Pallas kernels  6.08 us (2%)
  between operations  4.65 us (2%)
    ppermute x1, waiting for transfers between devices, shards(): given = lax.ppermute(given, ('dp', 'expert'), weight_perm)  32.1 us
    all_to_all x1, blocking collectives, shards(): lax.all_to_all(outgoing, ('dp', 'expert'), split_axis=0, concat_axis=0, t...  24.2 us
    all_to_all x1, waiting for transfers between devices, shards(): lax.all_to_all(pair_sums.reshape(chips, share, model_width), 'expert', sp...  17.7 us
    all_to_all x1, waiting for transfers between devices, shards(): lax.all_to_all(out.astype(BF).reshape(devices, capacity, piece), ('dp', '...  17.5 us
    ppermute x1, waiting for transfers between devices, shards(): from_partner = lax.ppermute(to_partner, ('dp', 'expert'), weight_perm)  15.2 us
    ppermute x15, waiting for transfers between devices, shift(): return lax.ppermute(x, axis, [((i + step) % size, i) for i in range(size)])  14.8 us
    all_to_all x1, waiting for transfers between devices, to_heads(): lax.all_to_all(part, 'expert', split_axis=0, concat_axis=0, tiled=True)  12.4 us
    ppermute x15, starting transfers between devices, shift(): return lax.ppermute(x, axis, [((i + step) % size, i) for i in range(size)])  12.2 us
  transfers between devices with their start and end apart: 24, of which 13 were waited for; matrix products, arithmetic and copies ran while one was open for 15% of the time, Pallas kernels for 0%

profile of v2, /device:TPU:1, one launch (start us, length us, event | category | flops | bytes accessed | tf_op | source)
XLA Modules:
  0.0 254.4 jit_solution(15527870210104705788)
XLA Ops:
  0.6 3.4 %collective-permute-start = (bf16[192,576]{1,0:T(8,128)(2,1)}, bf16[192,576]{1,0:T(8,128)(2,1)S(1)}, u32[]{:S(2)}, u32[]{:S(2)}) collective-permute-start(bf16[192,576]{1,0:T(8,128)(2,1)} %refs_4_.1), channel_id=1, source_target_pairs={{32,0},{64,32},{96,64},{0,96},{33,1},{65,33},{97,65},{1,97},{34,2}... | collective-permute-start | bytes 663560 | tf_op jit(solution)/shard_map/ppermute | solution.py:41
  5.2 0.9 slice.64
  6.1 1.5 collective-permute-start.3
  7.6 1.7 copy.70
  9.3 10.4 %all-to-all-start.1 = ((bf16[32,6,576]{2,1,0:T(8,128)(2,1)}), bf16[32,6,576]{2,1,0:T(8,128)(2,1)S(1)}, u32[]{:S(2)}, u32[]{:S(2)}) async-start(bf16[32,6,576]{2,1,0:T(8,128)(2,1)} %bitcast.115), calls=%async_computation.1 | async-start | bytes 655360 | tf_op jit(solution)/shard_map/all_to_all | solution.py:178
  19.8 1.3 fusion.152
  25.4 1.3 convert_reduce_fusion.3
  26.9 0.9 select_reduce_fusion.5
  27.8 0.9 bitcast_convert_fusion
  29.5 1.9 multiply_sine_fusion
  31.8 5.1 %dynamic-slice_bitcast_fusion = (bf16[1792,256]{1,0:T(8,128)(2,1)}, bf16[1792,256]{1,0:T(8,128)(2,1)S(1)}, bf16[1792,256]{1,0:T(8,128)(2,1)S(1)}, bf16[1792,256]...) fusion(bf16[1,7168,256]{2,1,0:T(8,128)(2,1)} %param.31, ...), kind=kLoop, calls=%fused_computation.68 | loop fusion | bytes 14680080 | tf_op jit(solution)/shard_map/dynamic_slice | solution.py:256
  37.2 2.1 pad_maximum_fusion
  40.9 1.2 collective-permute-start.5
  42.1 2.3 collective-permute-done.4.refs_9_
  44.8 1.0 collective-permute-done.5.refs_10_
  45.8 3.2 %collective-permute-done.6.refs_11_ = bf16[64,576]{1,0:T(8,128)(2,1)S(1)} collective-permute-done((bf16[64,576]{1,0:T(8,128)(2,1)S(1)}, bf16[64,576]{1,0:T(8,128)(2,1)S(1)}, u32[]{:S(2)}, u32[]{:S(2)}) %collective-permute-start.6) | collective-permute-done | bytes 73760 | tf_op jit(solution)/shard_map/ppermute | solution.py:41
  49.0 3.2 %copy-done.2 = bf16[1,96,64,576]{3,2,1,0:T(8,128)(2,1)S(1)} copy-done((bf16[1,96,64,576]{3,2,1,0:T(8,128)(2,1)S(1)}, bf16[1,96,64,576]{3,2,1,0:T(8,128)(2,1)}, u32[]{:S(2)}) %copy-start.2) | copy-done | bytes 7077912
  52.2 6.1 %attend.1 = bf16[24,64,512]{2,1,0:T(8,128)(2,1)S(1)} custom-call(s32[24]{0:T(128)S(1)} %get-tuple-element.48.refs_0_, s32[24]{0:T(128)S(1)} %get-tuple-element.47.refs_1_, s32[24]{0:T(128)S(1)} %get-tuple-element.46.refs_2_, s32[1]{0:T(128)} %bitcast.11.refs_3_, bf16[192,576]{1,0:T(8,128)(2,1)S(1)} %copy-done.3, ...), custom_call_target="tpu_custom_call" | custom-call | flops 100000000 | bytes 4000000 | tf_op jit(solution)/shard_map/attend/pallas_call | solution.py:119
  58.5 1.4 collective-permute-start.9
  60.1 1.4 copy.68
  61.5 10.1 %all-to-all-start.2 = ((bf16[32,10,1024]{2,1,0:T(8,128)(2,1)}), bf16[32,10,1024]{2,1,0:T(8,128)(2,1)}, u32[]{:S(2)}, u32[]{:S(2)}) async-start(bf16[32,10,1024]{2,1,0:T(8,128)(2,1)} %bitcast.113), calls=%async_computation.2 | async-start | bytes 2097152 | tf_op jit(solution)/shard_map/all_to_all | solution.py:291
  71.6 1.6 collective-permute-done.9
  73.2 1.5 fusion.49
  76.5 12.4 %all-to-all-done.2 = bf16[32,10,1024]{2,1,0:T(8,128)(2,1)} async-done(((bf16[32,10,1024]{2,1,0:T(8,128)(2,1)}), bf16[32,10,1024]{2,1,0:T(8,128)(2,1)}, u32[]{:S(2)}, u32[]{:S(2)}) %all-to-all-start.2) | async-done | bytes 655392 | tf_op jit(solution)/shard_map/all_to_all | solution.py:291
  88.8 1.4 reshape.369
  90.8 2.8 %convolution_convert_fusion = bf16[96,7168]{1,0:T(8,128)(2,1)S(1)} fusion(bf16[256,7168]{1,0:T(8,128)(2,1)} %param.25, bf16[2,12,8,128]{3,2,1,0:T(8,128)(2,1)S(1)} %fusion.48), kind=kOutput, calls=%fused_computation.10 | convolution fusion | flops 353009664 | bytes 5095424 | tf_op jit(solution)/shard_map/dot_general | solution.py:330
  94.3 2.5 collective-permute-start.11
  96.9 1.2 reshape.372
  98.1 3.6 %all-to-all-start.3 = ((bf16[16,3,7168]{2,1,0:T(4,128)(2,1)}), bf16[16,3,7168]{2,1,0:T(4,128)(2,1)S(1)}, u32[]{:S(2)}, u32[]{:S(2)}) async-start(bf16[16,3,7168]{2,1,0:T(4,128)(2,1)} %reshape.372), calls=%async_computation.3 | async-start | bytes 1835008 | tf_op jit(solution)/shard_map/all_to_all | solution.py:337
  102.4 17.7 %all-to-all-done.3 = bf16[16,3,7168]{2,1,0:T(4,128)(2,1)S(1)} async-done(((bf16[16,3,7168]{2,1,0:T(4,128)(2,1)}), bf16[16,3,7168]{2,1,0:T(4,128)(2,1)S(1)}, u32[]{:S(2)}, u32[]{:S(2)}) %all-to-all-start.3) | async-done | bytes 688160 | tf_op jit(solution)/shard_map/all_to_all | solution.py:337
  122.4 15.2 %collective-permute-done.11 = bf16[2,1792,512]{2,1,0:T(8,128)(2,1)} collective-permute-done((bf16[2,1792,512]{2,1,0:T(8,128)(2,1)}, bf16[2,1792,512]{2,1,0:T(8,128)(2,1)}, u32[]{:S(2)}, u32[]{:S(2)}) %collective-permute-start.11) | collective-permute-done | bytes 3670048 | tf_op jit(solution)/shard_map/ppermute | solution.py:264
  137.6 24.2 %all_to_all.29 = bf16[128,2,1792]{2,1,0:T(2,128)(2,1)S(1)} all-to-all(bf16[128,2,1792]{2,1,0:T(2,128)(2,1)S(1)} %reshape.373), channel_id=1, replica_groups=mesh['dp'=4,'expert'=32] {'dp','expert'}, dimensions={0} | all-to-all | bytes 1835008 | tf_op jit(solution)/shard_map/all_to_all | solution.py:386
  162.5 2.3 constant_dynamic-slice_fusion.2
  164.7 1.2 collective-permute-start.17
  166.0 1.8 collective-permute-start.18
  167.8 11.6 %collective-permute-done.12 = bf16[256,1792]{1,0:T(8,128)(2,1)S(1)} collective-permute-done((bf16[256,1792]{1,0:T(8,128)(2,1)S(1)}, bf16[256,1792]{1,0:T(8,128)(2,1)S(1)}, u32[]{:S(2)}, u32[]{:S(2)}) %collective-permute-start.12) | collective-permute-done | bytes 917536 | tf_op jit(solution)/shard_map/ppermute | solution.py:389
  179.4 2.1 fusion.30
  181.6 2.3 fusion.45
  184.6 32.1 %collective-permute-done.13 = bf16[256,512]{1,0:T(8,128)(2,1)S(1)} collective-permute-done((bf16[256,512]{1,0:T(8,128)(2,1)S(1)}, bf16[256,512]{1,0:T(8,128)(2,1)S(1)}, u32[]{:S(2)}, u32[]{:S(2)}) %collective-permute-start.13) | collective-permute-done | bytes 262176 | tf_op jit(solution)/shard_map/ppermute | solution.py:397
  217.9 1.4 collective-permute-start.16
  219.2 3.2 %collective-permute-done.14 = bf16[256,256]{1,0:T(8,128)(2,1)S(1)} collective-permute-done((bf16[256,256]{1,0:T(8,128)(2,1)S(1)}, bf16[256,256]{1,0:T(8,128)(2,1)S(1)}, u32[]{:S(2)}, u32[]{:S(2)}) %collective-permute-start.14) | collective-permute-done | bytes 131104 | tf_op jit(solution)/shard_map/ppermute | solution.py:41
  222.4 0.8 collective-permute-done.15
  223.2 2.7 %collective-permute-done.16 = bf16[256,256]{1,0:T(8,128)(2,1)S(1)} collective-permute-done((bf16[256,256]{1,0:T(8,128)(2,1)S(1)}, bf16[256,256]{1,0:T(8,128)(2,1)S(1)}, u32[]{:S(2)}, u32[]{:S(2)}) %collective-permute-start.16) | collective-permute-done | bytes 131104 | tf_op jit(solution)/shard_map/ppermute | solution.py:41
  225.9 1.1 fusion.15
  227.1 1.3 reshape.375
  228.3 5.6 %all-to-all-start.5 = ((bf16[128,2,1792]{2,1,0:T(2,128)(2,1)}), bf16[128,2,1792]{2,1,0:T(2,128)(2,1)S(1)}, u32[]{:S(2)}, u32[]{:S(2)}) async-start(bf16[128,2,1792]{2,1,0:T(2,128)(2,1)} %reshape.375), calls=%async_computation.5 | async-start | bytes 1835008 | tf_op jit(solution)/shard_map/all_to_all | solution.py:406
  234.2 17.5 %all-to-all-done.5 = bf16[128,2,1792]{2,1,0:T(2,128)(2,1)S(1)} async-done(((bf16[128,2,1792]{2,1,0:T(2,128)(2,1)}), bf16[128,2,1792]{2,1,0:T(2,128)(2,1)S(1)}, u32[]{:S(2)}, u32[]{:S(2)}) %all-to-all-start.5) | async-done | bytes 917536 | tf_op jit(solution)/shard_map/all_to_all | solution.py:406
  253.2 1.2 fusion.6
  (132 shorter events, 16.2 us)
Async XLA Ops:
  0.6 90.0 %copy-start = (bf16[2,512,128]{2,1,0:T(8,128)(2,1)S(1)}, bf16[2,512,128]{2,1,0:T(8,128)(2,1)}, u32[]{:S(2)}) copy-start(bf16[2,512,128]{2,1,0:T(8,128)(2,1)} %param.24) | copy-start | bytes 786436
  0.6 48.3 %collective-permute-start = (bf16[192,576]{1,0:T(8,128)(2,1)}, bf16[192,576]{1,0:T(8,128)(2,1)S(1)}, u32[]{:S(2)}, u32[]{:S(2)}) collective-permute-start(bf16[192,576]{1,0:T(8,128)(2,1)} %refs_4_.1), channel_id=1, source_target_pairs={{32,0},{64,32},{96,64},{0,96},{33,1},{65,33},{97,65},{1,97},{34,2}... | collective-permute-start | bytes 663560 | tf_op jit(solution)/shard_map/ppermute | solution.py:41
  4.0 44.9 %collective-permute-start.1 = (bf16[192,576]{1,0:T(8,128)(2,1)}, bf16[192,576]{1,0:T(8,128)(2,1)S(1)}, u32[]{:S(2)}, u32[]{:S(2)}) collective-permute-start(bf16[192,576]{1,0:T(8,128)(2,1)} %refs_4_.1), channel_id=1, source_target_pairs={{64,0},{96,32},{0,64},{32,96},{65,1},{97,33},{1,65},{33,97},{66,2}... | collective-permute-start | bytes 663560 | tf_op jit(solution)/shard_map/ppermute | solution.py:41
  4.5 44.4 %collective-permute-start.2 = (bf16[192,576]{1,0:T(8,128)(2,1)}, bf16[192,576]{1,0:T(8,128)(2,1)S(1)}, u32[]{:S(2)}, u32[]{:S(2)}) collective-permute-start(bf16[192,576]{1,0:T(8,128)(2,1)} %refs_4_.1), channel_id=1, source_target_pairs={{96,0},{0,32},{32,64},{64,96},{97,1},{1,33},{33,65},{65,97},{98,2}... | collective-permute-start | bytes 663560 | tf_op jit(solution)/shard_map/ppermute | solution.py:41
  6.1 34.6 %collective-permute-start.3 = (bf16[64,576]{1,0:T(8,128)(2,1)S(1)}, bf16[64,576]{1,0:T(8,128)(2,1)S(1)}, u32[]{:S(2)}, u32[]{:S(2)}) collective-permute-start(bf16[64,576]{1,0:T(8,128)(2,1)S(1)} %slice.64), channel_id=1, source_target_pairs={{1,0},{2,1},{3,2},{4,3},{5,4},{6,5},{7,6},{8,7},{9,8},{10,9},{11,1... | collective-permute-start | bytes 221192 | tf_op jit(solution)/shard_map/ppermute | solution.py:169
  9.3 35.3 %all-to-all-start.1 = ((bf16[32,6,576]{2,1,0:T(8,128)(2,1)}), bf16[32,6,576]{2,1,0:T(8,128)(2,1)S(1)}, u32[]{:S(2)}, u32[]{:S(2)}) async-start(bf16[32,6,576]{2,1,0:T(8,128)(2,1)} %bitcast.115), calls=%async_computation.1 | async-start | bytes 655360 | tf_op jit(solution)/shard_map/all_to_all | solution.py:178
  37.2 2.1 copy-start.4
  37.2 11.8 %copy-start.3 = (bf16[192,576]{1,0:T(8,128)(2,1)S(1)}, bf16[192,576]{1,0:T(8,128)(2,1)}, u32[]{:S(2)}) copy-start(bf16[192,576]{1,0:T(8,128)(2,1)} %refs_4_.1) | copy-start | bytes 663556
  40.7 3.7 %collective-permute-start.4 = (bf16[64,576]{1,0:T(8,128)(2,1)S(1)}, bf16[64,576]{1,0:T(8,128)(2,1)S(1)}, u32[]{:S(2)}, u32[]{:S(2)}) collective-permute-start(bf16[64,576]{1,0:T(8,128)(2,1)S(1)} %collective-permute-done.3.refs_8_), channel_id=1, source_target_pairs={{32,0},{64,32},{96,64},{0,96},{33,1},{65,33},{97,65},{1,97},{34,2}... | collective-permute-start | bytes 221192 | tf_op jit(solution)/shard_map/ppermute | solution.py:41
  40.9 4.8 %collective-permute-start.5 = (bf16[64,576]{1,0:T(8,128)(2,1)S(1)}, bf16[64,576]{1,0:T(8,128)(2,1)S(1)}, u32[]{:S(2)}, u32[]{:S(2)}) collective-permute-start(bf16[64,576]{1,0:T(8,128)(2,1)S(1)} %collective-permute-done.3.refs_8_), channel_id=1, source_target_pairs={{64,0},{96,32},{0,64},{32,96},{65,1},{97,33},{1,65},{33,97},{66,2}... | collective-permute-start | bytes 221192 | tf_op jit(solution)/shard_map/ppermute | solution.py:41
  44.4 4.5 %collective-permute-start.6 = (bf16[64,576]{1,0:T(8,128)(2,1)S(1)}, bf16[64,576]{1,0:T(8,128)(2,1)S(1)}, u32[]{:S(2)}, u32[]{:S(2)}) collective-permute-start(bf16[64,576]{1,0:T(8,128)(2,1)S(1)} %collective-permute-done.3.refs_8_), channel_id=1, source_target_pairs={{96,0},{0,32},{32,64},{64,96},{97,1},{1,33},{33,65},{65,97},{98,2}... | collective-permute-start | bytes 221192 | tf_op jit(solution)/shard_map/ppermute | solution.py:41
  49.0 3.2 %copy-start.2 = (bf16[1,96,64,576]{3,2,1,0:T(8,128)(2,1)S(1)}, bf16[1,96,64,576]{3,2,1,0:T(8,128)(2,1)}, u32[]{:S(2)}) copy-start(bf16[1,96,64,576]{3,2,1,0:T(8,128)(2,1)} %param.23) | copy-start | bytes 21233668
  58.3 1.6 copy-start.5
  58.3 13.3 %collective-permute-start.7 = (bf16[192,576]{1,0:T(8,128)(2,1)S(1)}, bf16[192,576]{1,0:T(8,128)(2,1)S(1)}, u32[]{:S(2)}, u32[]{:S(2)}) collective-permute-start(bf16[192,576]{1,0:T(8,128)(2,1)S(1)} %reshape.367), channel_id=1, source_target_pairs={{32,0},{64,32},{96,64},{0,96},{33,1},{65,33},{97,65},{1,97},{34,2}... | collective-permute-start | bytes 663560 | tf_op jit(solution)/shard_map/ppermute | solution.py:41
  58.4 13.2 %collective-permute-start.8 = (bf16[192,576]{1,0:T(8,128)(2,1)S(1)}, bf16[192,576]{1,0:T(8,128)(2,1)}, u32[]{:S(2)}, u32[]{:S(2)}) collective-permute-start(bf16[192,576]{1,0:T(8,128)(2,1)S(1)} %reshape.367), channel_id=1, source_target_pairs={{64,0},{96,32},{0,64},{32,96},{65,1},{97,33},{1,65},{33,97},{66,2}... | collective-permute-start | bytes 663560 | tf_op jit(solution)/shard_map/ppermute | solution.py:41
  58.5 14.7 %collective-permute-start.9 = (bf16[192,576]{1,0:T(8,128)(2,1)S(1)}, bf16[192,576]{1,0:T(8,128)(2,1)}, u32[]{:S(2)}, u32[]{:S(2)}) collective-permute-start(bf16[192,576]{1,0:T(8,128)(2,1)S(1)} %reshape.367), channel_id=1, source_target_pairs={{96,0},{0,32},{32,64},{64,96},{97,1},{1,33},{33,65},{65,97},{98,2}... | collective-permute-start | bytes 663560 | tf_op jit(solution)/shard_map/ppermute | solution.py:41
  61.5 27.3 %all-to-all-start.2 = ((bf16[32,10,1024]{2,1,0:T(8,128)(2,1)}), bf16[32,10,1024]{2,1,0:T(8,128)(2,1)}, u32[]{:S(2)}, u32[]{:S(2)}) async-start(bf16[32,10,1024]{2,1,0:T(8,128)(2,1)} %bitcast.113), calls=%async_computation.2 | async-start | bytes 2097152 | tf_op jit(solution)/shard_map/all_to_all | solution.py:291
  71.6 18.9 %copy-start.6 = (bf16[24,64,512]{2,1,0:T(8,128)(2,1)S(1)}, bf16[24,64,512]{2,1,0:T(8,128)(2,1)}, u32[]{:S(2)}) copy-start(bf16[24,64,512]{2,1,0:T(8,128)(2,1)} %copy-done.5) | copy-start | bytes 4718596
  90.5 3.6 %copy-start.13 = (s32[1,3,8]{2,0,1:T(1,128)S(1)}, s32[1,3,8]{2,0,1:T(1,128)}, u32[]{:S(2)}) copy-start(s32[1,3,8]{2,0,1:T(1,128)} %param.28) | copy-start | bytes 292
  93.6 26.8 %copy-start.11 = (bf16[1,3,7168]{2,1,0:T(4,128)(2,1)S(1)}, bf16[1,3,7168]{2,1,0:T(4,128)(2,1)}, u32[]{:S(2)}) copy-start(bf16[1,3,7168]{2,1,0:T(4,128)(2,1)} %param.26) | copy-start | bytes 129028
  93.7 27.0 %copy-start.12 = (f32[7168]{0:T(1024)S(1)}, f32[7168]{0:T(1024)}, u32[]{:S(2)}) copy-start(f32[7168]{0:T(1024)} %param.27) | copy-start | bytes 86020
  93.7 3.1 %collective-permute-start.10 = (bf16[48,7168]{1,0:T(8,128)(2,1)S(1)}, bf16[48,7168]{1,0:T(8,128)(2,1)S(1)}, u32[]{:S(2)}, u32[]{:S(2)}) collective-permute-start(bf16[48,7168]{1,0:T(8,128)(2,1)S(1)} %slice.89), channel_id=1, source_target_pairs={{0,1},{1,0},{2,3},{3,2},{4,5},{5,4},{6,7},{7,6},{8,9},{9,8},{10,11... | collective-permute-start | bytes 2064392 | tf_op jit(solution)/shard_map/ppermute | solution.py:335
  94.3 43.3 %collective-permute-start.11 = (bf16[2,1792,512]{2,1,0:T(8,128)(2,1)}, bf16[2,1792,512]{2,1,0:T(8,128)(2,1)}, u32[]{:S(2)}, u32[]{:S(2)}) collective-permute-start(bf16[2,1792,512]{2,1,0:T(8,128)(2,1)} %pad_maximum_fusion), channel_id=1, source_target_pairs={{0,32},{1,97},{2,34},{3,99},{4,36},{5,101},{6,38},{7,103},{8,40},{... | collective-permute-start | bytes 11010056 | tf_op jit(solution)/shard_map/ppermute | solution.py:264
  98.1 22.0 %all-to-all-start.3 = ((bf16[16,3,7168]{2,1,0:T(4,128)(2,1)}), bf16[16,3,7168]{2,1,0:T(4,128)(2,1)S(1)}, u32[]{:S(2)}, u32[]{:S(2)}) async-start(bf16[16,3,7168]{2,1,0:T(4,128)(2,1)} %reshape.372), calls=%async_computation.3 | async-start | bytes 1835008 | tf_op jit(solution)/shard_map/all_to_all | solution.py:337
  162.1 17.3 %collective-permute-start.12 = (bf16[256,1792]{1,0:T(8,128)(2,1)S(1)}, bf16[256,1792]{1,0:T(8,128)(2,1)S(1)}, u32[]{:S(2)}, u32[]{:S(2)}) collective-permute-start(bf16[256,1792]{1,0:T(8,128)(2,1)S(1)} %reshape.374), channel_id=1, source_target_pairs={{0,96},{1,33},{2,98},{3,35},{4,100},{5,37},{6,102},{7,39},{8,104},... | collective-permute-start | bytes 2752520 | tf_op jit(solution)/shard_map/ppermute | solution.py:389
  164.7 53.1 %collective-permute-start.17 = (bf16[256,1792]{1,0:T(8,128)(2,1)S(1)}, bf16[256,1792]{1,0:T(8,128)(2,1)S(1)}, u32[]{:S(2)}, u32[]{:S(2)}) collective-permute-start(bf16[256,1792]{1,0:T(8,128)(2,1)S(1)} %get-tuple-element.70), channel_id=1, source_target_pairs={{32,0},{64,32},{96,64},{0,96},{33,1},{65,33},{97,65},{1,97},{34,2}... | collective-permute-start | bytes 2752520 | tf_op jit(solution)/shard_map/ppermute | solution.py:41
  166.0 53.2 %collective-permute-start.18 = (bf16[256,1792]{1,0:T(8,128)(2,1)S(1)}, bf16[256,1792]{1,0:T(8,128)(2,1)S(1)}, u32[]{:S(2)}, u32[]{:S(2)}) collective-permute-start(bf16[256,1792]{1,0:T(8,128)(2,1)S(1)} %get-tuple-element.69), channel_id=1, source_target_pairs={{64,0},{96,32},{0,64},{32,96},{65,1},{97,33},{1,65},{33,97},{66,2}... | collective-permute-start | bytes 2752520 | tf_op jit(solution)/shard_map/ppermute | solution.py:41
  167.8 16.2 %copy-start.9 = (bf16[1792,256]{1,0:T(8,128)(2,1)S(1)}, bf16[1792,256]{1,0:T(8,128)(2,1)}, u32[]{:S(2)}) copy-start(bf16[1792,256]{1,0:T(8,128)(2,1)} %get-tuple-element.66) | copy-start | bytes 2752516
  167.8 16.2 %copy-start.10 = (bf16[1792,256]{1,0:T(8,128)(2,1)S(1)}, bf16[1792,256]{1,0:T(8,128)(2,1)}, u32[]{:S(2)}) copy-start(bf16[1792,256]{1,0:T(8,128)(2,1)} %get-tuple-element.89) | copy-start | bytes 2752516
  167.8 51.4 %collective-permute-start.19 = (bf16[256,1792]{1,0:T(8,128)(2,1)S(1)}, bf16[256,1792]{1,0:T(8,128)(2,1)S(1)}, u32[]{:S(2)}, u32[]{:S(2)}) collective-permute-start(bf16[256,1792]{1,0:T(8,128)(2,1)S(1)} %get-tuple-element.68), channel_id=1, source_target_pairs={{96,0},{0,32},{32,64},{64,96},{97,1},{1,33},{33,65},{65,97},{98,2}... | collective-permute-start | bytes 2752520 | tf_op jit(solution)/shard_map/ppermute | solution.py:41
  181.6 35.1 %copy-start.7 = (bf16[1792,256]{1,0:T(8,128)(2,1)S(1)}, bf16[1792,256]{1,0:T(8,128)(2,1)}, u32[]{:S(2)}) copy-start(bf16[1792,256]{1,0:T(8,128)(2,1)} %get-tuple-element.63) | copy-start | bytes 2752516
  181.6 35.1 %copy-start.8 = (bf16[1792,256]{1,0:T(8,128)(2,1)S(1)}, bf16[1792,256]{1,0:T(8,128)(2,1)}, u32[]{:S(2)}) copy-start(bf16[1792,256]{1,0:T(8,128)(2,1)} %get-tuple-element.92) | copy-start | bytes 2752516
  183.9 32.8 %collective-permute-start.13 = (bf16[256,512]{1,0:T(8,128)(2,1)S(1)}, bf16[256,512]{1,0:T(8,128)(2,1)S(1)}, u32[]{:S(2)}, u32[]{:S(2)}) collective-permute-start(bf16[256,512]{1,0:T(8,128)(2,1)S(1)} %fusion.45), channel_id=1, source_target_pairs={{0,32},{1,97},{2,34},{3,99},{4,36},{5,101},{6,38},{7,103},{8,40},{... | collective-permute-start | bytes 786440 | tf_op jit(solution)/shard_map/ppermute | solution.py:397
  217.5 5.0 %collective-permute-start.14 = (bf16[256,256]{1,0:T(8,128)(2,1)S(1)}, bf16[256,256]{1,0:T(8,128)(2,1)S(1)}, u32[]{:S(2)}, u32[]{:S(2)}) collective-permute-start(bf16[256,256]{1,0:T(8,128)(2,1)S(1)} %fusion.71), channel_id=1, source_target_pairs={{32,0},{64,32},{96,64},{0,96},{33,1},{65,33},{97,65},{1,97},{34,2}... | collective-permute-start | bytes 393224 | tf_op jit(solution)/shard_map/ppermute | solution.py:41
  217.8 5.5 %collective-permute-start.15 = (bf16[256,256]{1,0:T(8,128)(2,1)S(1)}, bf16[256,256]{1,0:T(8,128)(2,1)S(1)}, u32[]{:S(2)}, u32[]{:S(2)}) collective-permute-start(bf16[256,256]{1,0:T(8,128)(2,1)S(1)} %fusion.71), channel_id=1, source_target_pairs={{64,0},{96,32},{0,64},{32,96},{65,1},{97,33},{1,65},{33,97},{66,2}... | collective-permute-start | bytes 393224 | tf_op jit(solution)/shard_map/ppermute | solution.py:41
  217.9 8.1 %collective-permute-start.16 = (bf16[256,256]{1,0:T(8,128)(2,1)S(1)}, bf16[256,256]{1,0:T(8,128)(2,1)S(1)}, u32[]{:S(2)}, u32[]{:S(2)}) collective-permute-start(bf16[256,256]{1,0:T(8,128)(2,1)S(1)} %fusion.71), channel_id=1, source_target_pairs={{96,0},{0,32},{32,64},{64,96},{97,1},{1,33},{33,65},{65,97},{98,2}... | collective-permute-start | bytes 393224 | tf_op jit(solution)/shard_map/ppermute | solution.py:41
  227.0 6.9 %copy-start.14 = (f32[1,3,8]{2,0,1:T(1,128)S(1)}, f32[1,3,8]{2,0,1:T(1,128)}, u32[]{:S(2)}) copy-start(f32[1,3,8]{2,0,1:T(1,128)} %param.29) | copy-start | bytes 292
  227.1 27.3 %copy-start.1 = (bf16[2,512,128]{2,1,0:T(8,128)(2,1)S(1)}, bf16[2,512,128]{2,1,0:T(8,128)(2,1)}, u32[]{:S(2)}) copy-start(bf16[2,512,128]{2,1,0:T(8,128)(2,1)} %param.24) | copy-start | bytes 786436
  228.3 23.4 %all-to-all-start.5 = ((bf16[128,2,1792]{2,1,0:T(2,128)(2,1)}), bf16[128,2,1792]{2,1,0:T(2,128)(2,1)S(1)}, u32[]{:S(2)}, u32[]{:S(2)}) async-start(bf16[128,2,1792]{2,1,0:T(2,128)(2,1)} %reshape.375), calls=%async_computation.5 | async-start | bytes 1835008 | tf_op jit(solution)/shard_map/all_to_all | solution.py:406

commit v3 on v2

--- a/solution.py
+++ b/solution.py
@@ -52,8 +52,7 @@
     sent_slots,
 ):
     rows_in = refs[:blocks]
-    extra_in = refs[blocks : 2 * blocks]
-    cos_ref, sin_ref, gain_ref, new_ref, query_ref, out_ref, keys, query, sems = refs[2 * blocks :]
+    cos_ref, sin_ref, gain_ref, new_ref, query_ref, out_ref, keys, query, sems = refs[blocks:]
     number = number_ref[0]
 
     def fetch(slot):
@@ -68,11 +67,10 @@
     gain = gain_ref[...]
     start = 0
     for block in range(blocks):
-        for ref in (rows_in[block], extra_in[block]):
-            size = ref.shape[0]
-            span = slice(start, start + size)
-            keys[span, :] = norm_rotate(ref[...], cos_ref[span, :], sin_ref[span, :], gain)
-            start += size
+        ref = rows_in[block]
+        span = slice(start, start + ref.shape[0])
+        keys[span, :] = norm_rotate(ref[...], cos_ref[span, :], sin_ref[span, :], gain)
+        start += ref.shape[0]
 
     @pl.loop(number, sent_slots)
     def _(slot):
@@ -106,7 +104,7 @@
         out_ref[slot] = (mixture / total).astype(BF)
 
 
-def attend(tables, rows, extras, cosine, sine, gain, new_keys, queries, most_slots):
+def attend(tables, rows, cosine, sine, gain, new_keys, queries, most_slots):
     heads = queries.shape[1]
     blocks = len(rows)
     total_rows = cosine.shape[0]
@@ -120,7 +118,7 @@
         body,
         out_shape=jax.ShapeDtypeStruct((most_slots, heads, LAT), BF),
         in_specs=[scalar] * 4
-        + [whole] * (2 * blocks + 4)
+        + [whole] * (blocks + 4)
         + [pl.BlockSpec(memory_space=pl.ANY)],
         out_specs=whole,
         scratch_shapes=[
@@ -133,7 +131,7 @@
             flops=10**8, bytes_accessed=4 * 10**6, transcendentals=10**5
         ),
         name="attend",
-    )(*tables, *rows, *extras, cosine, sine, gain, new_keys, queries)
+    )(*tables, *rows, cosine, sine, gain, new_keys, queries)
 
 
 def shards(
@@ -171,12 +169,8 @@
         ("dp", "expert"),
         [((i + 1) % devices, i) for i in range(devices)],
     )
-    rows = [latent_rows] + [shift(latent_rows, k, dp_count, "dp") for k in range(1, dp_count)]
-    extras = [next_rows] + [shift(next_rows, k, dp_count, "dp") for k in range(1, dp_count)]
-
-    by_row = latent_rows.reshape(local_units, UNIT, width).transpose(1, 0, 2)
-    dealt = lax.all_to_all(by_row, "expert", split_axis=0, concat_axis=0, tiled=True)
-    dealt = dealt.reshape(block_units, width)
+    near_rows = jnp.concatenate([latent_rows, next_rows], axis=0)
+    rows = [near_rows] + [shift(near_rows, k, dp_count, "dp") for k in range(1, dp_count)]
 
     requests = lengths.shape[0]
     request_total = queries.shape[1]
@@ -216,18 +210,6 @@
     member_length = jnp.sum(jnp.where(is_member, lengths[None, :], 0), axis=1)
     new_keys = norm_rotate(new_rows[0], *turn(member_length, half_rope), gain).astype(F32)
 
-    attended = attend(
-        (slot_place, slot_count, slot_member, slot_number),
-        rows,
-        extras,
-        cosine,
-        sine,
-        gain,
-        new_keys,
-        queries[0],
-        most_slots,
-    )
-
     model_width = w_out.shape[1]
     piece = model_width // dp_count
     halves = (0, 1, 1, 0)
@@ -248,37 +230,31 @@
     my_quarter = quarter_of[place]
     their_quarter = quarter_of[place ^ 1]
 
-    def width_half(first):
-        def side(q):
-            return jnp.concatenate(
-                [
-                    lax.dynamic_slice_in_dim(w_gate[0], q * piece, piece, 0),
-                    lax.dynamic_slice_in_dim(w_up[0], q * piece, piece, 0),
-                ],
-                axis=1,
-            )
-
-        return jnp.stack([side(first), side(first ^ 1)])
-
-    to_partner, attended = lax.optimization_barrier((width_half(their_quarter), attended))
-    from_partner = lax.ppermute(to_partner, ("dp", "expert"), weight_perm)
-    dealt, attended = lax.optimization_barrier((dealt, attended))
-
-    blocks = jnp.concatenate(
-        [dealt] + [shift(dealt, k, dp_count, "dp") for k in range(1, dp_count)], axis=0
-    )
-    slots = jnp.arange(pre_rows, dtype=I32)
-    offset = slots[:, None] - group_start[None, :]
-    covers = own[None, :] & (offset >= 0) & (offset < unit_len[None, :])
-    slot_offset = jnp.sum(jnp.where(covers, offset, 0), axis=1)
-    slot_unit = jnp.sum(jnp.where(covers, offset + unit_start[None, :], 0), axis=1)
-    relative = (slot_unit // block_units - group + dp_count) % dp_count
-    cache_place = relative * block_units + slot_unit % block_units
-    places = jnp.arange(dp_count * block_units, dtype=I32)
-    pick = (cache_place[:, None] == places[None, :]).astype(BF)
-    raw_cache = jnp.dot(pick, blocks, preferred_element_type=F32)
-    cache_local = norm_rotate(
-        raw_cache, *turn(slot_offset * UNIT + column, half_rope), gain
+    def width_half(weight, first):
+        return jnp.stack(
+            [
+                lax.dynamic_slice_in_dim(weight[0], q * piece, piece, 0)
+                for q in (first, first ^ 1)
+            ]
+        )
+
+    def down_part(k):
+        return lax.dynamic_slice_in_dim(
+            w_down[0], (group - k + dp_count) % dp_count * piece, piece, 1
+        )
+
+    to_partner, *rows = lax.optimization_barrier((width_half(w_gate, their_quarter), *rows))
+    gate_came = lax.ppermute(to_partner, ("dp", "expert"), weight_perm)
+
+    attended = attend(
+        (slot_place, slot_count, slot_member, slot_number),
+        rows,
+        cosine,
+        sine,
+        gain,
+        new_keys,
+        queries[0],
+        most_slots,
     )
 
     head_share = w_uv.shape[0]
@@ -324,7 +300,13 @@
         lambda held: held,
         by_head,
     )
-    by_head, cache_local = lax.optimization_barrier((by_head, cache_local))
+    up_sent, down_near, down_last = width_half(w_up, their_quarter), down_part(1), down_part(3)
+    by_head, gate_came, up_sent, down_near, down_last = lax.optimization_barrier(
+        (by_head, gate_came, up_sent, down_near, down_last)
+    )
+    up_came = lax.ppermute(up_sent, ("dp", "expert"), weight_perm)
+    down_near = shift(down_near, 1, dp_count, "dp")
+    down_last = shift(down_last, 3, dp_count, "dp")
     by_head = by_head.astype(BF).reshape(request_total, head_share, LAT)
     projected = jnp.einsum("jhl,hlv->jhv", by_head, w_uv, preferred_element_type=F32).astype(BF)
     partial_sums = jnp.dot(
@@ -342,6 +324,10 @@
         tiled=True,
         axis_index_groups=[[2 * i + c for i in range(chips)] for c in range(2)],
     )
+    chip_sums, up_came, down_near, down_last, down_far = lax.optimization_barrier(
+        (chip_sums, up_came, down_near, down_last, down_part(2))
+    )
+    down_far = shift(down_far, 2, dp_count, "dp")
     attention_out = jnp.sum(chip_sums.astype(F32), axis=0)
     residual = resid[0].astype(F32) + attention_out
     normed = (
@@ -349,13 +335,6 @@
         * lax.rsqrt(jnp.mean(residual * residual, axis=1, keepdims=True) + eps)
         * moe_gain[None, :]
     ).astype(BF)
-
-    downs = []
-    down_held, _ = lax.optimization_barrier((w_down[0], by_head))
-    for k in range(dp_count):
-        to = (group - k + dp_count) % dp_count * piece
-        part = lax.dynamic_slice_in_dim(down_held, to, piece, 1)
-        downs.append(shift(part, k, dp_count, "dp") if k else part)
 
     tokens = resid.shape[1]
     capacity = 2
@@ -382,27 +361,38 @@
         )
         outgoing.append(jnp.dot(table, both, preferred_element_type=F32).astype(BF))
     outgoing = jnp.stack(outgoing).reshape(devices, capacity, piece)
-    outgoing, from_partner = lax.optimization_barrier((outgoing, from_partner))
     arrived = lax.all_to_all(
         outgoing, ("dp", "expert"), split_axis=0, concat_axis=0, tiled=True
     ).reshape(devices * capacity, piece)
+
+    local_rows = local_units * UNIT
+    to_rows = jnp.concatenate(
+        [block[:local_rows].reshape(local_units, UNIT, width) for block in rows], axis=0
+    ).transpose(1, 0, 2)
+    arrived, down_far, to_rows = lax.optimization_barrier((arrived, down_far, to_rows))
     beside = lax.ppermute(arrived, ("dp", "expert"), token_perm)
-
-    def gate_up(first, second):
-        return jnp.dot(arrived, first, preferred_element_type=F32) + jnp.dot(
-            beside, second, preferred_element_type=F32
-        )
-
-    given = gate_up(from_partner[0], from_partner[1]).astype(BF)
-    given = lax.ppermute(given, ("dp", "expert"), weight_perm)
-    own_half = width_half(my_quarter)
-    sums = gate_up(own_half[0], own_half[1]) + given.astype(F32)
-    half = sums.shape[1] // 2
-    hidden = (jax.nn.silu(sums[:, :half]) * sums[:, half:]).astype(BF)
+    dealt = lax.all_to_all(to_rows, "expert", split_axis=0, concat_axis=0, tiled=True)
+
+    gate_own, up_own = width_half(w_gate, my_quarter), width_half(w_up, my_quarter)
+    weights = (gate_came, up_came, gate_own, up_own)
+    first = [jnp.dot(arrived, weight[0], preferred_element_type=F32) for weight in weights]
+    beside, *first = lax.optimization_barrier((beside, *first))
+    gate_given, up_given, gate_sum, up_sum = (
+        part + jnp.dot(beside, weight[1], preferred_element_type=F32)
+        for part, weight in zip(first, weights)
+    )
+    given = jnp.concatenate([gate_given, up_given], axis=1).astype(BF)
+    given = lax.ppermute(given, ("dp", "expert"), weight_perm).astype(F32)
+    half = gate_sum.shape[1]
+    hidden = (
+        jax.nn.silu(gate_sum + given[:, :half]) * (up_sum + given[:, half:])
+    ).astype(BF)
     hidden_all = jnp.concatenate(
         [hidden] + [shift(hidden, k, dp_count, "dp") for k in range(1, dp_count)], axis=1
     )
-    out = jnp.dot(hidden_all, jnp.concatenate(downs, axis=0), preferred_element_type=F32)
+    hidden_all, dealt = lax.optimization_barrier((hidden_all, dealt))
+    downs = jnp.concatenate([down_part(0), down_near, down_far, down_last], axis=0)
+    out = jnp.dot(hidden_all, downs, preferred_element_type=F32)
     returned = lax.all_to_all(
         out.astype(BF).reshape(devices, capacity, piece),
         ("dp", "expert"),
@@ -410,6 +400,25 @@
         concat_axis=0,
         tiled=True,
     )
+
+    slots = jnp.arange(pre_rows, dtype=I32)
+    offset = slots[:, None] - group_start[None, :]
+    covers = own[None, :] & (offset >= 0) & (offset < unit_len[None, :])
+    slot_offset = jnp.sum(jnp.where(covers, offset, 0), axis=1)
+    slot_unit = jnp.sum(jnp.where(covers, offset + unit_start[None, :], 0), axis=1)
+    relative = (slot_unit // block_units - group + dp_count) % dp_count
+    cache_place = (
+        slot_unit % block_units // local_units * most_slots
+        + relative * local_units
+        + slot_unit % local_units
+    )
+    places = jnp.arange(columns * most_slots, dtype=I32)
+    pick = (cache_place[:, None] == places[None, :]).astype(BF)
+    raw_cache = jnp.dot(
+        pick, dealt.reshape(columns * most_slots, width), preferred_element_type=F32
+    )
+    cache_local = norm_rotate(raw_cache, *turn(slot_offset * UNIT + column, half_rope), gain)
+
     slot_weights = jnp.where(slot_table, combine_weights.T[:, None, :], 0.0)
     moe_sum = jnp.einsum(
         "xct,fxcd->tfd",

time: 255 us -> 238 us (0.933)
  blocking collectives: 24.2 us -> 0 us
  waiting for transfers between devices: 121 us -> 103 us
  matrix products: 13.8 us -> 23.7 us
  starting transfers between devices: 46.7 us -> 54.4 us
  other arithmetic: 13.9 us -> 20 us
  local copies, waits for them, and re-layouts: 23.6 us -> 26.3 us
    ppermute x2 -> x3, waiting for transfers between devices: 47.3 us -> 1.26 us  [the longest x1 1.25 us: shards(): given = lax.ppermute(given, ('dp', 'expert'), weight_perm).astype(F32)]
    ppermute x15 -> x9, waiting for transfers between devices: 14.8 us -> 51.6 us  [shift(): return lax.ppermute(x, axis, [((i + step) % size, i) for i in range(size)])]
    all_to_all x1 -> x0, blocking collectives: 24.2 us -> none  [shards(): lax.all_to_all(outgoing, ('dp', 'expert'), split_axis=0, concat_axis=0, t...]
    all_to_all x1 -> x2, waiting for transfers between devices: 0.01 us -> 23.7 us  [the longest x1 23.7 us: shards(): lax.all_to_all(outgoing, ('dp', 'expert'), split_axis=0, concat_axis=0, t...]
    all_to_all x1, waiting for transfers between devices: 17.7 us -> 0.01 us  [shards(): lax.all_to_all(pair_sums.reshape(chips, share, model_width), 'expert', sp...]
    ppermute x1, waiting for transfers between devices: 11.6 us -> 0.08 us  [shards(): beside = lax.ppermute(arrived, ('dp', 'expert'), token_perm)]
    dot_general x6 -> x10, matrix products: 8.29 us -> 16.3 us  [the longest x4 6.35 us: shards(): jnp.dot(arrived, weight[0], preferred_element_type=F32)]
    all_to_all x1, starting transfers between devices: 10.1 us -> 16.6 us  [to_heads(): lax.all_to_all(part, 'expert', split_axis=0, concat_axis=0, tiled=True)]
  transfers between devices with their start and end apart: 24 -> 20, of which waited for: 13 -> 12; matrix products, arithmetic and copies ran while one was open for 15% -> 22% of each run, Pallas kernels for 0% -> 2%
where the time goes in v3:
time: 238 us; the launch traced here: 237 us
  waiting for transfers between devices  103 us (43%)
  starting transfers between devices  54.4 us (23%)
  local copies, waits for them, and re-layouts  26.3 us (11%)
  matrix products  23.7 us (10%)
  other arithmetic  20 us (8%)
  between operations  4.67 us (2%)
  Pallas kernels  4.65 us (2%)
    ppermute x9, waiting for transfers between devices, shift(): return lax.ppermute(x, axis, [((i + step) % size, i) for i in range(size)])  51.6 us
    all_to_all x1, waiting for transfers between devices, shards(): lax.all_to_all(outgoing, ('dp', 'expert'), split_axis=0, concat_axis=0, t...  23.7 us
    all_to_all x1, starting transfers between devices, to_heads(): lax.all_to_all(part, 'expert', split_axis=0, concat_axis=0, tiled=True)  16.6 us
    all_to_all x1, waiting for transfers between devices, shards(): lax.all_to_all(out.astype(BF).reshape(devices, capacity, piece), ('dp', '...  15.8 us
    all_to_all x1, waiting for transfers between devices, to_heads(): lax.all_to_all(part, 'expert', split_axis=0, concat_axis=0, tiled=True)  11 us
    ppermute x9, starting transfers between devices, shift(): return lax.ppermute(x, axis, [((i + step) % size, i) for i in range(size)])  9.24 us
    all_to_all x1, starting transfers between devices, shards(): lax.all_to_all(out.astype(BF).reshape(devices, capacity, piece), ('dp', '...  7.85 us
    dot_general x4, matrix products, shards(): jnp.dot(arrived, weight[0], preferred_element_type=F32)  6.35 us
  transfers between devices with their start and end apart: 20, of which 12 were waited for; matrix products, arithmetic and copies ran while one was open for 22% of the time, Pallas kernels for 2%

profile of v3, /device:TPU:1, one launch (start us, length us, event | category | flops | bytes accessed | tf_op | source)
XLA Modules:
  0.0 237.2 jit_solution(9199183897558359314)
XLA Ops:
  1.6 1.4 collective-permute-start
  3.0 1.4 fusion.141
  8.8 1.3 convert_reduce_fusion.3
  13.4 3.6 %constant_dynamic-slice_fusion.1 = (bf16[1,1792,256]{2,1,0:T(8,128)(2,1)}, bf16[1,1792,256]{2,1,0:T(8,128)(2,1)}, bf16[1,1792,256]{2,1,0:T(8,128)(2,1)S(1)}, bf16[1,1792,256]{2,1,0:T(8,128)(2,1)S(1)}) fusion(bf16[1,7168,256]{2,1,0:T(8,128)(2,1)} %param.31, s32[]{:T(128)S(6)} %select_n.329, s32[]{:T(128)S(6)} %select_n.330, bf16[1,7168,256]{2,1,0:T(8,128)(2,1)} %param.30), kind=kLoop, calls=%fused_computation.200 | loop fusion | bytes 7340040 | tf_op jit(solution)/shard_map/dynamic_slice | solution.py:236
  17.2 2.6 %collective-permute-start.1 = (bf16[256,576]{1,0:T(8,128)(2,1)S(1)}, bf16[256,576]{1,0:T(8,128)(2,1)S(1)}, u32[]{:S(2)}, u32[]{:S(2)}) collective-permute-start(bf16[256,576]{1,0:T(8,128)(2,1)S(1)} %constant_dynamic-update-slice_fusion.refs_4_), channel_id=1, source_target_pairs={{32,0},{64,32},{96,64},{0,96},{33,1},{65,33},{97,65},{1,97},{34,2}... | collective-permute-start | bytes 884744 | tf_op jit(solution)/shard_map/ppermute | solution.py:41
  21.0 1.4 pad_maximum_fusion
  22.4 5.3 %collective-permute-done.1.refs_5_ = bf16[256,576]{1,0:T(8,128)(2,1)S(1)} collective-permute-done((bf16[256,576]{1,0:T(8,128)(2,1)S(1)}, bf16[256,576]{1,0:T(8,128)(2,1)S(1)}, u32[]{:S(2)}, u32[]{:S(2)}) %collective-permute-start.1) | collective-permute-done | bytes 294944 | tf_op jit(solution)/shard_map/ppermute | solution.py:41
  27.7 3.4 %collective-permute-done.3.refs_7_ = bf16[256,576]{1,0:T(8,128)(2,1)S(1)} collective-permute-done((bf16[256,576]{1,0:T(8,128)(2,1)S(1)}, bf16[256,576]{1,0:T(8,128)(2,1)S(1)}, u32[]{:S(2)}, u32[]{:S(2)}) %collective-permute-start.3) | collective-permute-done | bytes 294944 | tf_op jit(solution)/shard_map/ppermute | solution.py:41
  31.9 1.9 multiply_sine_fusion
  33.8 3.2 %copy-done.2 = bf16[1,96,64,576]{3,2,1,0:T(8,128)(2,1)S(1)} copy-done((bf16[1,96,64,576]{3,2,1,0:T(8,128)(2,1)S(1)}, bf16[1,96,64,576]{3,2,1,0:T(8,128)(2,1)}, u32[]{:S(2)}) %copy-start.2) | copy-done | bytes 7077912
  37.0 4.7 %attend.1 = bf16[24,64,512]{2,1,0:T(8,128)(2,1)S(1)} custom-call(s32[24]{0:T(128)S(1)} %get-tuple-element.80.refs_0_, s32[24]{0:T(128)S(1)} %get-tuple-element.79.refs_1_, s32[24]{0:T(128)S(1)} %get-tuple-element.78.refs_2_, s32[1]{0:T(128)} %bitcast.4.refs_3_, bf16[256,576]{1,0:T(8,128)(2,1)S(1)} %constant_dynamic-update-slice_fusion.refs_4_, ...), custom_call_target="tpu_custom_call" | custom-call | flops 100000000 | bytes 4000000 | tf_op jit(solution)/shard_map/attend/pallas_call | solution.py:117
  42.6 2.1 reshape.444
  44.6 2.5 %copy.90 = bf16[10,32,1024]{2,0,1:T(8,128)(2,1)} copy(bf16[10,32,1024]{2,1,0:T(8,128)(2,1)} %reshape.444) | data formatting | bytes 1310720 | tf_op jit(solution)/shard_map/reshape | solution.py:266
  47.1 16.6 %all-to-all-start.1 = ((bf16[32,10,1024]{2,1,0:T(8,128)(2,1)}), bf16[32,10,1024]{2,1,0:T(8,128)(2,1)}, u32[]{:S(2)}, u32[]{:S(2)}) async-start(bf16[32,10,1024]{2,1,0:T(8,128)(2,1)} %bitcast.135), calls=%async_computation.1 | async-start | bytes 2097152 | tf_op jit(solution)/shard_map/all_to_all | solution.py:267
  65.1 3.0 %pad_maximum_fusion.1 = bf16[2,1792,256]{2,1,0:T(8,128)(2,1)} fusion(bf16[1,1792,256]{2,1,0:T(8,128)(2,1)} %get-tuple-element.96, bf16[1,1792,256]{2,1,0:T(8,128)(2,1)} %get-tuple-element.95), kind=kLoop, calls=%fused_computation.33 | loop fusion | flops 917504 | bytes 3670016 | tf_op jit(solution)/shard_map/stack | solution.py:234
  68.1 1.9 dynamic-slice_bitcast_fusion
  70.0 11.0 %all-to-all-done.1 = bf16[32,10,1024]{2,1,0:T(8,128)(2,1)} async-done(((bf16[32,10,1024]{2,1,0:T(8,128)(2,1)}), bf16[32,10,1024]{2,1,0:T(8,128)(2,1)}, u32[]{:S(2)}, u32[]{:S(2)}) %all-to-all-start.1) | async-done | bytes 655392 | tf_op jit(solution)/shard_map/all_to_all | solution.py:267
  81.0 2.1 reshape.445
  83.1 2.2 fusion.62
  86.5 2.8 %convolution_convert_fusion = bf16[96,7168]{1,0:T(8,128)(2,1)S(1)} fusion(bf16[256,7168]{1,0:T(8,128)(2,1)} %param.25, bf16[2,12,8,128]{3,2,1,0:T(8,128)(2,1)S(1)} %fusion.22), kind=kOutput, calls=%fused_computation.10 | convolution fusion | flops 353009664 | bytes 5095424 | tf_op jit(solution)/shard_map/dot_general | solution.py:312
  90.3 2.7 %collective-permute-start.7 = (bf16[256,1792]{1,0:T(8,128)(2,1)}, bf16[256,1792]{1,0:T(8,128)(2,1)}, u32[]{:S(2)}, u32[]{:S(2)}) collective-permute-start(bf16[256,1792]{1,0:T(8,128)(2,1)} %get-tuple-element.56), channel_id=1, source_target_pairs={{32,0},{64,32},{96,64},{0,96},{33,1},{65,33},{97,65},{1,97},{34,2}... | collective-permute-start | bytes 2752520 | tf_op jit(solution)/shard_map/ppermute | solution.py:41
  93.1 1.2 reshape.448
  94.3 3.8 %all-to-all-start.2 = ((bf16[16,3,7168]{2,1,0:T(4,128)(2,1)}), bf16[16,3,7168]{2,1,0:T(4,128)(2,1)S(1)}, u32[]{:S(2)}, u32[]{:S(2)}) async-start(bf16[16,3,7168]{2,1,0:T(4,128)(2,1)} %reshape.448), calls=%async_computation.2 | async-start | bytes 1835008 | tf_op jit(solution)/shard_map/all_to_all | solution.py:319
  98.7 31.7 %collective-permute-done.7 = bf16[256,1792]{1,0:T(8,128)(2,1)} collective-permute-done((bf16[256,1792]{1,0:T(8,128)(2,1)}, bf16[256,1792]{1,0:T(8,128)(2,1)}, u32[]{:S(2)}, u32[]{:S(2)}) %collective-permute-start.7) | collective-permute-done | bytes 917536 | tf_op jit(solution)/shard_map/ppermute | solution.py:41
  130.4 3.1 %collective-permute-done.8 = bf16[256,1792]{1,0:T(8,128)(2,1)} collective-permute-done((bf16[256,1792]{1,0:T(8,128)(2,1)S(1)}, bf16[256,1792]{1,0:T(8,128)(2,1)}, u32[]{:S(2)}, u32[]{:S(2)}) %collective-permute-start.8) | collective-permute-done | bytes 917536 | tf_op jit(solution)/shard_map/ppermute | solution.py:41
  135.6 1.3 reshape.449
  136.8 5.9 %all-to-all-start.3 = ((bf16[128,2,1792]{2,1,0:T(2,128)(2,1)}), bf16[128,2,1792]{2,1,0:T(2,128)(2,1)S(1)}, u32[]{:S(2)}, u32[]{:S(2)}) async-start(bf16[128,2,1792]{2,1,0:T(2,128)(2,1)} %reshape.449), calls=%async_computation.3 | async-start | bytes 1835008 | tf_op jit(solution)/shard_map/all_to_all | solution.py:364
  145.2 1.5 maximum_bitcast_fusion
  146.6 23.7 %all-to-all-done.3 = bf16[128,2,1792]{2,1,0:T(2,128)(2,1)S(1)} async-done(((bf16[128,2,1792]{2,1,0:T(2,128)(2,1)}), bf16[128,2,1792]{2,1,0:T(2,128)(2,1)S(1)}, u32[]{:S(2)}, u32[]{:S(2)}) %all-to-all-start.3) | async-done | bytes 917536 | tf_op jit(solution)/shard_map/all_to_all | solution.py:364
  170.8 1.6 fusion.31
  172.4 6.0 %all-to-all-start.4 = ((bf16[32,24,576]{2,1,0:T(8,128)(2,1)}), bf16[32,24,576]{2,1,0:T(8,128)(2,1)S(1)}, u32[]{:S(2)}, u32[]{:S(2)}) async-start(bf16[32,24,576]{2,1,0:T(8,128)(2,1)} %maximum_bitcast_fusion), calls=%async_computation.4 | async-start | bytes 1966080 | tf_op jit(solution)/shard_map/all_to_all | solution.py:374
  178.5 1.6 fusion.33
  180.1 1.6 fusion.35
  181.7 1.6 fusion.37
  183.4 1.6 fusion.27
  185.0 1.6 fusion.25
  186.7 2.4 collective-permute-start.11
  189.0 1.6 fusion.23
  190.6 1.6 fusion.29
  192.2 1.3 collective-permute-done.11
  193.7 2.1 collective-permute-start.12
  196.4 3.2 %collective-permute-done.12 = bf16[256,256]{1,0:T(8,128)(2,1)S(1)} collective-permute-done((bf16[256,256]{1,0:T(8,128)(2,1)S(1)}, bf16[256,256]{1,0:T(8,128)(2,1)S(1)}, u32[]{:S(2)}, u32[]{:S(2)}) %collective-permute-start.12) | collective-permute-done | bytes 131104 | tf_op jit(solution)/shard_map/ppermute | solution.py:41
  199.6 2.1 collective-permute-done.13
  201.8 2.8 %collective-permute-done.14 = bf16[256,256]{1,0:T(8,128)(2,1)S(1)} collective-permute-done((bf16[256,256]{1,0:T(8,128)(2,1)S(1)}, bf16[256,256]{1,0:T(8,128)(2,1)S(1)}, u32[]{:S(2)}, u32[]{:S(2)}) %collective-permute-start.14) | collective-permute-done | bytes 131104 | tf_op jit(solution)/shard_map/ppermute | solution.py:41
  204.6 3.1 %fusion.15 = bf16[256,1792]{1,0:T(8,128)(2,1)S(1)} fusion(bf16[256,1024]{1,0:T(8,128)(2,1)S(1)} %pad_maximum_fusion.3, bf16[256,1792]{1,0:T(8,128)(2,1)} %collective-permute-done.8, bf16[256,1792]{1,0:T(8,128)(2,1)} %collective-permute-done.9, bf16[256,1792]{1,0:T(8,128)(2,1)} %collective-permute-done.7, bf16[256,1792]{1,0:T(8,128)(2,1)} %get-tuple-element.91), kind=kOutput, calls=%fused_computation.23 | convolution fusion | flops 954662912 | bytes 5111808 | tf_op jit(solution)/shard_map/dot_general | solution.py:395
  207.8 1.3 reshape.456
  209.1 7.9 %all-to-all-start.5 = ((bf16[128,2,1792]{2,1,0:T(2,128)(2,1)}), bf16[128,2,1792]{2,1,0:T(2,128)(2,1)S(1)}, u32[]{:S(2)}, u32[]{:S(2)}) async-start(bf16[128,2,1792]{2,1,0:T(2,128)(2,1)} %reshape.456), calls=%async_computation.5 | async-start | bytes 1835008 | tf_op jit(solution)/shard_map/all_to_all | solution.py:396
  218.9 15.8 %all-to-all-done.5 = bf16[128,2,1792]{2,1,0:T(2,128)(2,1)S(1)} async-done(((bf16[128,2,1792]{2,1,0:T(2,128)(2,1)}), bf16[128,2,1792]{2,1,0:T(2,128)(2,1)S(1)}, u32[]{:S(2)}, u32[]{:S(2)}) %all-to-all-start.5) | async-done | bytes 917536 | tf_op jit(solution)/shard_map/all_to_all | solution.py:396
  (136 shorter events, 22.8 us)
Async XLA Ops:
  0.6 85.6 %copy-start = (bf16[2,512,128]{2,1,0:T(8,128)(2,1)S(1)}, bf16[2,512,128]{2,1,0:T(8,128)(2,1)}, u32[]{:S(2)}) copy-start(bf16[2,512,128]{2,1,0:T(8,128)(2,1)} %param.24) | copy-start | bytes 786436
  1.6 15.6 %collective-permute-start = (bf16[64,576]{1,0:T(8,128)(2,1)S(1)}, bf16[64,576]{1,0:T(8,128)(2,1)S(1)}, u32[]{:S(2)}, u32[]{:S(2)}) collective-permute-start(bf16[64,576]{1,0:T(8,128)(2,1)S(1)} %slice.82), channel_id=1, source_target_pairs={{1,0},{2,1},{3,2},{4,3},{5,4},{6,5},{7,6},{8,7},{9,8},{10,9},{11,1... | collective-permute-start | bytes 221192 | tf_op jit(solution)/shard_map/ppermute | solution.py:167
  6.7 25.2 %copy-start.12 = (f32[32]{0:T(128)}, f32[32]{0:T(128)S(1)}, u32[]{:S(2)}) copy-start(f32[32]{0:T(128)S(1)} %multiply_power_fusion) | copy-start | bytes 388
  7.4 9.6 %copy-start.10 = (pred[384]{0:T(512)(128)(4,1)}, pred[384]{0:T(512)(128)(4,1)S(1)}, u32[]{:S(2)}) copy-start(pred[384]{0:T(512)(128)(4,1)S(1)} %broadcast_compare_fusion.1) | copy-start | bytes 1156
  17.2 10.5 %collective-permute-start.1 = (bf16[256,576]{1,0:T(8,128)(2,1)S(1)}, bf16[256,576]{1,0:T(8,128)(2,1)S(1)}, u32[]{:S(2)}, u32[]{:S(2)}) collective-permute-start(bf16[256,576]{1,0:T(8,128)(2,1)S(1)} %constant_dynamic-update-slice_fusion.refs_4_), channel_id=1, source_target_pairs={{32,0},{64,32},{96,64},{0,96},{33,1},{65,33},{97,65},{1,97},{34,2}... | collective-permute-start | bytes 884744 | tf_op jit(solution)/shard_map/ppermute | solution.py:41
  19.8 7.8 %collective-permute-start.2 = (bf16[256,576]{1,0:T(8,128)(2,1)S(1)}, bf16[256,576]{1,0:T(8,128)(2,1)S(1)}, u32[]{:S(2)}, u32[]{:S(2)}) collective-permute-start(bf16[256,576]{1,0:T(8,128)(2,1)S(1)} %constant_dynamic-update-slice_fusion.refs_4_), channel_id=1, source_target_pairs={{64,0},{96,32},{0,64},{32,96},{65,1},{97,33},{1,65},{33,97},{66,2}... | collective-permute-start | bytes 884744 | tf_op jit(solution)/shard_map/ppermute | solution.py:41
  20.4 10.7 %collective-permute-start.3 = (bf16[256,576]{1,0:T(8,128)(2,1)S(1)}, bf16[256,576]{1,0:T(8,128)(2,1)S(1)}, u32[]{:S(2)}, u32[]{:S(2)}) collective-permute-start(bf16[256,576]{1,0:T(8,128)(2,1)S(1)} %constant_dynamic-update-slice_fusion.refs_4_), channel_id=1, source_target_pairs={{96,0},{0,32},{32,64},{64,96},{97,1},{1,33},{33,65},{65,97},{98,2}... | collective-permute-start | bytes 884744 | tf_op jit(solution)/shard_map/ppermute | solution.py:41
  21.0 12.8 %copy-start.3 = (f32[512]{0:T(512)S(1)}, f32[512]{0:T(512)}, u32[]{:S(2)}) copy-start(f32[512]{0:T(512)} %param.20) | copy-start | bytes 6148
  31.1 54.1 %collective-permute-start.4 = (bf16[2,1792,256]{2,1,0:T(8,128)(2,1)}, bf16[2,1792,256]{2,1,0:T(8,128)(2,1)}, u32[]{:S(2)}, u32[]{:S(2)}) collective-permute-start(bf16[2,1792,256]{2,1,0:T(8,128)(2,1)} %pad_maximum_fusion), channel_id=1, source_target_pairs={{0,32},{1,97},{2,34},{3,99},{4,36},{5,101},{6,38},{7,103},{8,40},{... | collective-permute-start | bytes 5505032 | tf_op jit(solution)/shard_map/ppermute | solution.py:247
  33.8 3.2 %copy-start.2 = (bf16[1,96,64,576]{3,2,1,0:T(8,128)(2,1)S(1)}, bf16[1,96,64,576]{3,2,1,0:T(8,128)(2,1)}, u32[]{:S(2)}) copy-start(bf16[1,96,64,576]{3,2,1,0:T(8,128)(2,1)} %param.23) | copy-start | bytes 21233668
  47.1 33.9 %all-to-all-start.1 = ((bf16[32,10,1024]{2,1,0:T(8,128)(2,1)}), bf16[32,10,1024]{2,1,0:T(8,128)(2,1)}, u32[]{:S(2)}, u32[]{:S(2)}) async-start(bf16[32,10,1024]{2,1,0:T(8,128)(2,1)} %bitcast.135), calls=%async_computation.1 | async-start | bytes 2097152 | tf_op jit(solution)/shard_map/all_to_all | solution.py:267
  65.0 3.0 %copy-start.4 = (bf16[1,256,7168]{2,1,0:T(8,128)(2,1)S(1)}, bf16[1,256,7168]{2,1,0:T(8,128)(2,1)}, u32[]{:S(2)}) copy-start(bf16[1,256,7168]{2,1,0:T(8,128)(2,1)} %param.32) | copy-start | bytes 11010052
  86.5 3.6 %copy-start.14 = (s32[1,3,8]{2,0,1:T(1,128)S(1)}, s32[1,3,8]{2,0,1:T(1,128)}, u32[]{:S(2)}) copy-start(s32[1,3,8]{2,0,1:T(1,128)} %param.28) | copy-start | bytes 292
  86.5 6.4 %copy-start.5 = (bf16[256,1792]{1,0:T(8,128)(2,1)S(1)}, bf16[256,1792]{1,0:T(8,128)(2,1)}, u32[]{:S(2)}) copy-start(bf16[256,1792]{1,0:T(8,128)(2,1)} %get-tuple-element.57) | copy-start | bytes 2752516
  89.4 3.5 %collective-permute-start.5 = (bf16[48,7168]{1,0:T(8,128)(2,1)S(1)}, bf16[48,7168]{1,0:T(8,128)(2,1)S(1)}, u32[]{:S(2)}, u32[]{:S(2)}) collective-permute-start(bf16[48,7168]{1,0:T(8,128)(2,1)S(1)} %slice.111), channel_id=1, source_target_pairs={{0,1},{1,0},{2,3},{3,2},{4,5},{5,4},{6,7},{7,6},{8,9},{9,8},{10,11... | collective-permute-start | bytes 2064392 | tf_op jit(solution)/shard_map/ppermute | solution.py:317
  90.2 43.4 %collective-permute-start.6 = (bf16[2,1792,256]{2,1,0:T(8,128)(2,1)}, bf16[2,1792,256]{2,1,0:T(8,128)(2,1)}, u32[]{:S(2)}, u32[]{:S(2)}) collective-permute-start(bf16[2,1792,256]{2,1,0:T(8,128)(2,1)} %pad_maximum_fusion.1), channel_id=1, source_target_pairs={{0,32},{1,97},{2,34},{3,99},{4,36},{5,101},{6,38},{7,103},{8,40},{... | collective-permute-start | bytes 5505032 | tf_op jit(solution)/shard_map/ppermute | solution.py:307
  90.3 40.1 %collective-permute-start.7 = (bf16[256,1792]{1,0:T(8,128)(2,1)}, bf16[256,1792]{1,0:T(8,128)(2,1)}, u32[]{:S(2)}, u32[]{:S(2)}) collective-permute-start(bf16[256,1792]{1,0:T(8,128)(2,1)} %get-tuple-element.56), channel_id=1, source_target_pairs={{32,0},{64,32},{96,64},{0,96},{33,1},{65,33},{97,65},{1,97},{34,2}... | collective-permute-start | bytes 2752520 | tf_op jit(solution)/shard_map/ppermute | solution.py:41
  92.9 40.6 %collective-permute-start.8 = (bf16[256,1792]{1,0:T(8,128)(2,1)S(1)}, bf16[256,1792]{1,0:T(8,128)(2,1)}, u32[]{:S(2)}, u32[]{:S(2)}) collective-permute-start(bf16[256,1792]{1,0:T(8,128)(2,1)S(1)} %copy-done.5), channel_id=1, source_target_pairs={{96,0},{0,32},{32,64},{64,96},{97,1},{1,33},{33,65},{65,97},{98,2}... | collective-permute-start | bytes 2752520 | tf_op jit(solution)/shard_map/ppermute | solution.py:41
  93.1 40.8 %copy-start.6 = (bf16[1,3,7168]{2,1,0:T(4,128)(2,1)S(1)}, bf16[1,3,7168]{2,1,0:T(4,128)(2,1)}, u32[]{:S(2)}) copy-start(bf16[1,3,7168]{2,1,0:T(4,128)(2,1)} %param.26) | copy-start | bytes 129028
  94.3 39.8 %copy-start.8 = (f32[7168]{0:T(1024)S(1)}, f32[7168]{0:T(1024)}, u32[]{:S(2)}) copy-start(f32[7168]{0:T(1024)} %param.27) | copy-start | bytes 86020
  94.3 39.2 %all-to-all-start.2 = ((bf16[16,3,7168]{2,1,0:T(4,128)(2,1)}), bf16[16,3,7168]{2,1,0:T(4,128)(2,1)S(1)}, u32[]{:S(2)}, u32[]{:S(2)}) async-start(bf16[16,3,7168]{2,1,0:T(4,128)(2,1)} %reshape.448), calls=%async_computation.2 | async-start | bytes 1835008 | tf_op jit(solution)/shard_map/all_to_all | solution.py:319
  135.3 35.4 %collective-permute-start.9 = (bf16[256,1792]{1,0:T(8,128)(2,1)}, bf16[256,1792]{1,0:T(8,128)(2,1)}, u32[]{:S(2)}, u32[]{:S(2)}) collective-permute-start(bf16[256,1792]{1,0:T(8,128)(2,1)} %get-tuple-element.59), channel_id=1, source_target_pairs={{64,0},{96,32},{0,64},{32,96},{65,1},{97,33},{1,65},{33,97},{66,2}... | collective-permute-start | bytes 2752520 | tf_op jit(solution)/shard_map/ppermute | solution.py:41
  135.5 8.6 %copy-start.15 = (f32[1,3,8]{2,0,1:T(1,128)S(1)}, f32[1,3,8]{2,0,1:T(1,128)}, u32[]{:S(2)}) copy-start(f32[1,3,8]{2,0,1:T(1,128)} %param.29) | copy-start | bytes 292
  135.6 8.9 %copy-start.9 = (s32[384]{0:T(512)S(1)}, s32[384]{0:T(512)}, u32[]{:S(2)}) copy-start(s32[384]{0:T(512)} %get-tuple-element.81) | copy-start | bytes 4612
  135.6 8.8 %copy-start.11 = (pred[384]{0:T(512)(128)(4,1)S(1)}, pred[384]{0:T(512)(128)(4,1)}, u32[]{:S(2)}) copy-start(pred[384]{0:T(512)(128)(4,1)} %copy-done.10) | copy-start | bytes 1156
  136.8 33.5 %all-to-all-start.3 = ((bf16[128,2,1792]{2,1,0:T(2,128)(2,1)}), bf16[128,2,1792]{2,1,0:T(2,128)(2,1)S(1)}, u32[]{:S(2)}, u32[]{:S(2)}) async-start(bf16[128,2,1792]{2,1,0:T(2,128)(2,1)} %reshape.449), calls=%async_computation.3 | async-start | bytes 1835008 | tf_op jit(solution)/shard_map/all_to_all | solution.py:364
  170.8 12.6 %collective-permute-start.10 = (bf16[256,1792]{1,0:T(8,128)(2,1)S(1)}, bf16[256,1792]{1,0:T(8,128)(2,1)S(1)}, u32[]{:S(2)}, u32[]{:S(2)}) collective-permute-start(bf16[256,1792]{1,0:T(8,128)(2,1)S(1)} %reshape.450), channel_id=1, source_target_pairs={{0,96},{1,33},{2,98},{3,35},{4,100},{5,37},{6,102},{7,39},{8,104},... | collective-permute-start | bytes 2752520 | tf_op jit(solution)/shard_map/ppermute | solution.py:373
  172.4 32.2 %all-to-all-start.4 = ((bf16[32,24,576]{2,1,0:T(8,128)(2,1)}), bf16[32,24,576]{2,1,0:T(8,128)(2,1)S(1)}, u32[]{:S(2)}, u32[]{:S(2)}) async-start(bf16[32,24,576]{2,1,0:T(8,128)(2,1)} %maximum_bitcast_fusion), calls=%async_computation.4 | async-start | bytes 1966080 | tf_op jit(solution)/shard_map/all_to_all | solution.py:374
  186.7 6.8 %collective-permute-start.11 = (bf16[256,512]{1,0:T(8,128)(2,1)S(1)}, bf16[256,512]{1,0:T(8,128)(2,1)S(1)}, u32[]{:S(2)}, u32[]{:S(2)}) collective-permute-start(bf16[256,512]{1,0:T(8,128)(2,1)S(1)} %pad_maximum_fusion.4), channel_id=1, source_target_pairs={{0,32},{1,97},{2,34},{3,99},{4,36},{5,101},{6,38},{7,103},{8,40},{... | collective-permute-start | bytes 786440 | tf_op jit(solution)/shard_map/ppermute | solution.py:385
  193.7 6.0 %collective-permute-start.12 = (bf16[256,256]{1,0:T(8,128)(2,1)S(1)}, bf16[256,256]{1,0:T(8,128)(2,1)S(1)}, u32[]{:S(2)}, u32[]{:S(2)}) collective-permute-start(bf16[256,256]{1,0:T(8,128)(2,1)S(1)} %fusion.56), channel_id=1, source_target_pairs={{32,0},{64,32},{96,64},{0,96},{33,1},{65,33},{97,65},{1,97},{34,2}... | collective-permute-start | bytes 393224 | tf_op jit(solution)/shard_map/ppermute | solution.py:41
  195.7 6.0 %collective-permute-start.13 = (bf16[256,256]{1,0:T(8,128)(2,1)S(1)}, bf16[256,256]{1,0:T(8,128)(2,1)S(1)}, u32[]{:S(2)}, u32[]{:S(2)}) collective-permute-start(bf16[256,256]{1,0:T(8,128)(2,1)S(1)} %fusion.56), channel_id=1, source_target_pairs={{64,0},{96,32},{0,64},{32,96},{65,1},{97,33},{1,65},{33,97},{66,2}... | collective-permute-start | bytes 393224 | tf_op jit(solution)/shard_map/ppermute | solution.py:41
  195.7 8.9 %collective-permute-start.14 = (bf16[256,256]{1,0:T(8,128)(2,1)S(1)}, bf16[256,256]{1,0:T(8,128)(2,1)S(1)}, u32[]{:S(2)}, u32[]{:S(2)}) collective-permute-start(bf16[256,256]{1,0:T(8,128)(2,1)S(1)} %fusion.56), channel_id=1, source_target_pairs={{96,0},{0,32},{32,64},{64,96},{97,1},{1,33},{33,65},{65,97},{98,2}... | collective-permute-start | bytes 393224 | tf_op jit(solution)/shard_map/ppermute | solution.py:41
  209.1 8.4 %copy-start.13 = (f32[32]{0:T(128)S(1)}, f32[32]{0:T(128)}, u32[]{:S(2)}) copy-start(f32[32]{0:T(128)} %copy-done.12) | copy-start | bytes 388
  209.1 25.6 %all-to-all-start.5 = ((bf16[128,2,1792]{2,1,0:T(2,128)(2,1)}), bf16[128,2,1792]{2,1,0:T(2,128)(2,1)S(1)}, u32[]{:S(2)}, u32[]{:S(2)}) async-start(bf16[128,2,1792]{2,1,0:T(2,128)(2,1)} %reshape.456), calls=%async_computation.5 | async-start | bytes 1835008 | tf_op jit(solution)/shard_map/all_to_all | solution.py:396
  218.9 17.2 %copy-start.7 = (bf16[1,3,7168]{2,1,0:T(4,128)(2,1)S(1)}, bf16[1,3,7168]{2,1,0:T(4,128)(2,1)}, u32[]{:S(2)}) copy-start(bf16[1,3,7168]{2,1,0:T(4,128)(2,1)} %param.26) | copy-start | bytes 129028
  234.6 2.6 %copy-start.1 = (bf16[2,512,128]{2,1,0:T(8,128)(2,1)S(1)}, bf16[2,512,128]{2,1,0:T(8,128)(2,1)}, u32[]{:S(2)}) copy-start(bf16[2,512,128]{2,1,0:T(8,128)(2,1)} %param.24) | copy-start | bytes 786436

commit v4 on v3

v4 whole, which is shorter than its diff:
```python
import jax
import jax.numpy as jnp
import numpy as np
from jax import lax
from jax.experimental import pallas as pl
from jax.experimental.pallas import tpu as pltpu
from jax.sharding import PartitionSpec as P

LAT = 512
UNIT = 32
MOST = 3
SLOTS = 8

eps = 1e-06
theta = 10000.0
score_scale = 192.0 ** (-0.5)
BF = jnp.bfloat16
F32 = jnp.float32
I32 = jnp.int32


def turn_table(half_width):
    exponent = -np.arange(half_width, dtype=np.float32) / np.float32(half_width)
    frequency = np.power(np.float32(theta), exponent).astype(np.float32)
    count = (MOST + 1) * UNIT
    angles = np.arange(count, dtype=np.float32)[:, None] * frequency[None, :]
    return np.cos(angles).astype(np.float32), np.sin(angles).astype(np.float32)


def norm_rotate(raw_rows, cosine, sine, kv_gain):
    raw_rows = raw_rows.astype(F32)
    latent = raw_rows[:, :LAT]
    half_width = cosine.shape[1]
    inverse = lax.rsqrt(jnp.mean(latent * latent, axis=1, keepdims=True) + eps)
    latent = latent * inverse * kv_gain
    lower = raw_rows[:, LAT : LAT + half_width]
    upper = raw_rows[:, LAT + half_width :]
    return jnp.concatenate(
        [latent, lower * cosine - upper * sine, upper * cosine + lower * sine], axis=1
    ).astype(BF)


def shift(x, step, size, axis):
    return lax.ppermute(x, axis, [((i + step) % size, i) for i in range(size)])


def table_kernel(where_ref, lengths_ref, owners_ref, slots_ref, rows_ref, *, sizes):
    dp_count, columns, local_units, near_units = sizes
    group, column = where_ref[0], where_ref[1]
    group_f, column_f = group.astype(F32), column.astype(F32)
    count = lengths_ref.shape[1]
    units = lengths_ref[...].astype(F32) * (1.0 / UNIT)
    owner = owners_ref[...].astype(F32)
    square = (count, count)
    down = lax.broadcasted_iota(I32, square, 0)
    along = lax.broadcasted_iota(I32, square, 1)
    before = down < along

    def upright(row):
        return jnp.sum(jnp.where(down == along, row, 0.0), axis=1, keepdims=True)

    def whole(x, size):
        return jnp.floor((x + 0.5) * (1.0 / size))

    units_up, owner_up = upright(units), upright(owner)
    start = jnp.sum(jnp.where(before, units_up, 0.0), axis=0, keepdims=True)
    start_source = whole(start, local_units)
    start_block = whole(start_source, columns)
    start_column = start_source - start_block * columns
    home = owner * columns + start_column
    home_up = upright(home)
    rank = jnp.sum(jnp.where(before & (home_up == home), 1.0, 0.0), axis=0, keepdims=True)
    own = owner == group_f
    own_before = before & (owner_up == group_f)
    group_start = jnp.sum(jnp.where(own_before, units_up, 0.0), axis=0, keepdims=True)
    group_rank = jnp.sum(jnp.where(own_before, 1.0, 0.0), axis=0, keepdims=True)

    lines = slots_ref.shape[0]
    line = lax.broadcasted_iota(I32, (lines, count), 0).astype(F32)
    here = home == group_f * columns + column_f
    is_slot = here & (rank == line)
    block = start_block - group_f
    block = jnp.where(block < 0.0, block + dp_count, block)
    place = block * near_units + (start - start_source * local_units)

    def pick(row):
        return jnp.sum(jnp.where(is_slot, row, 0.0), axis=1, keepdims=True)

    near = lax.broadcasted_iota(I32, (lines, 1), 0).astype(F32)
    near_block = whole(near, near_units)
    near_unit = near - near_block * near_units + column_f * local_units
    near_block = near_block + group_f
    near_block = jnp.where(near_block >= dp_count, near_block - dp_count, near_block)
    near_unit = near_unit + near_block * (columns * local_units)
    near_start = jnp.max(jnp.where(start <= near_unit, start, 0.0), axis=1, keepdims=True)
    near_offset = jnp.minimum(near_unit - near_start, MOST - 1.0)
    number = jnp.sum(jnp.where(here, 1.0, 0.0), axis=1, keepdims=True)
    lane = lax.broadcasted_iota(I32, slots_ref.shape, 1)
    packed = jnp.zeros(slots_ref.shape, F32)
    for i, value in enumerate((pick(place), pick(units), pick(group_rank), near_offset, number)):
        packed = jnp.where(lane == i, value, packed)
    slots_ref[...] = packed.astype(I32)
    rows_ref[...] = jnp.concatenate(
        [start, rank, group_start, group_rank, start_column] + [start] * 3, axis=0
    ).astype(I32)


def tables(where, lengths, owners, sizes):
    lines = sizes[0] * sizes[3]
    whole = pl.BlockSpec(memory_space=pltpu.VMEM)

    def body(*refs):
        table_kernel(*refs, sizes=sizes)

    return pl.pallas_call(
        body,
        out_shape=(
            jax.ShapeDtypeStruct((lines, 128), I32),
            jax.ShapeDtypeStruct((8, lengths.shape[0]), I32),
        ),
        in_specs=[pl.BlockSpec(memory_space=pltpu.SMEM), whole, whole],
        out_specs=(whole, whole),
        compiler_params=pltpu.CompilerParams(vmem_limit_bytes=32 * 1024 * 1024),
        cost_estimate=pl.CostEstimate(flops=1000, bytes_accessed=4096, transcendentals=0),
        name="tables",
    )(where, lengths[None, :], owners[None, :])


def slice_kernel(at_ref, gate_ref, up_ref, down_ref, gate_out, up_out, *refs):
    downs, sems = refs[:-1], refs[-1]
    piece = gate_out.shape[1]
    copies = []
    for out, weight in ((gate_out, gate_ref), (up_out, up_ref)):
        for i in range(2):
            rows = pl.ds(pl.multiple_of(at_ref[i], 128), piece)
            copies.append((weight.at[0, rows, :], out.at[i]))
    for i, out in enumerate(downs):
        columns = pl.ds(pl.multiple_of(at_ref[2 + i], 128), piece)
        copies.append((down_ref.at[0, :, columns], out))
    copies = [
        pltpu.make_async_copy(source, target, sems.at[i])
        for i, (source, target) in enumerate(copies)
    ]
    for copy in copies:
        copy.start()
    for copy in copies:
        copy.wait()


def weight_slices(at, w_gate, w_up, w_down, dp_count):
    piece = w_gate.shape[1] // dp_count
    away = pl.BlockSpec(memory_space=pl.ANY)
    halves = jax.ShapeDtypeStruct((2, piece, w_gate.shape[2]), BF)
    part = jax.ShapeDtypeStruct((w_down.shape[1], piece), BF)
    return pl.pallas_call(
        slice_kernel,
        out_shape=(halves, halves) + (part,) * (dp_count - 1),
        in_specs=[pl.BlockSpec(memory_space=pltpu.SMEM)] + [away] * 3,
        out_specs=(away,) * (dp_count + 1),
        scratch_shapes=[pltpu.SemaphoreType.DMA((dp_count + 3,))],
        cost_estimate=pl.CostEstimate(flops=1000, bytes_accessed=4096, transcendentals=0),
        name="weight_slices",
    )(at, w_gate, w_up, w_down)


def attend_kernel(slots_ref, *refs, blocks):
    rows_in = refs[:blocks]
    cos_ref, sin_ref, gain_ref, new_ref, query_ref = refs[blocks : blocks + 5]
    out_ref, rest_ref, keys, query, fresh, held_out, sems = refs[blocks + 5 :]
    number = slots_ref[0, 4]

    def fetch(slot):
        return pltpu.make_async_copy(
            query_ref.at[slots_ref[slot, 2]], query.at[slot], sems.at[slot]
        )

    @pl.loop(0, number)
    def _(slot):
        fetch(slot).start()

    gain = gain_ref[...]
    unit = 0
    for ref in rows_in:
        for first in range(0, ref.shape[0], UNIT):
            span = pl.ds(pl.multiple_of(slots_ref[unit, 3] * UNIT, UNIT), UNIT)
            keys[unit * UNIT : (unit + 1) * UNIT, :] = norm_rotate(
                ref[first : first + UNIT, :], cos_ref[span, :], sin_ref[span, :], gain
            )
            unit += 1
    fresh[...] = new_ref[...].astype(F32)
    held_out[...] = jnp.zeros(held_out.shape, F32)

    heads = out_ref.shape[0]
    sent = out_ref.shape[1]
    window = MOST * UNIT
    lanes = window + UNIT
    lane = lax.broadcasted_iota(I32, (heads, lanes), 1)

    def one(slot):
        fetch(slot).wait()
        count = slots_ref[slot, 1]
        own = keys[pl.ds(pl.multiple_of(slots_ref[slot, 0] * UNIT, UNIT), window), :]
        at = pl.ds(count * UNIT, 1)
        new = norm_rotate(
            fresh[pl.ds(slots_ref[slot, 2], 1), :], cos_ref[at, :], sin_ref[at, :], gain
        )
        new = jnp.broadcast_to(new.astype(F32), (UNIT, own.shape[1])).astype(BF)
        held = jnp.concatenate([own, new], axis=0)
        scores = (
            lax.dot_general(
                query[slot], held, (((1,), (1,)), ((), ())), preferred_element_type=F32
            )
            * score_scale
        )
        live = (lane < count * UNIT) | (lane == window)
        scores = jnp.where(live, scores, -jnp.inf)
        weights = jnp.exp(scores - jnp.max(scores, axis=1, keepdims=True))
        total = jnp.sum(weights, axis=1, keepdims=True)
        mixture = jnp.dot(weights.astype(BF), held[:, :LAT], preferred_element_type=F32)
        return mixture / total

    @pl.loop(0, jnp.minimum(number, sent))
    def _(slot):
        held_out[slot] = one(slot)

    out_ref[...] = jnp.swapaxes(held_out[...], 0, 1).astype(BF)

    @pl.loop(sent, number)
    def _(slot):
        rest_ref[slot - sent] = one(slot).astype(BF)


def attend(slots, rows, cosine, sine, gain, new_rows, queries, most_slots):
    heads = queries.shape[1]
    blocks = len(rows)
    total_rows = sum(block.shape[0] for block in rows)
    whole = pl.BlockSpec(memory_space=pltpu.VMEM)

    def body(*refs):
        attend_kernel(*refs, blocks=blocks)

    return pl.pallas_call(
        body,
        out_shape=(
            jax.ShapeDtypeStruct((heads, SLOTS, LAT), BF),
            jax.ShapeDtypeStruct((most_slots - SLOTS, heads, LAT), BF),
        ),
        in_specs=[pl.BlockSpec(memory_space=pltpu.SMEM)]
        + [whole] * (blocks + 4)
        + [pl.BlockSpec(memory_space=pl.ANY)],
        out_specs=(whole, whole),
        scratch_shapes=[
            pltpu.VMEM((total_rows, queries.shape[2]), BF),
            pltpu.VMEM((most_slots,) + queries.shape[1:], BF),
            pltpu.VMEM(new_rows.shape, F32),
            pltpu.VMEM((SLOTS, heads, LAT), F32),
            pltpu.SemaphoreType.DMA((most_slots,)),
        ],
        compiler_params=pltpu.CompilerParams(vmem_limit_bytes=32 * 1024 * 1024),
        cost_estimate=pl.CostEstimate(
            flops=10**8, bytes_accessed=4 * 10**6, transcendentals=10**5
        ),
        name="attend",
    )(slots, *rows, cosine, sine, gain, new_rows, queries)


def shards(
    latent_rows,
    new_rows,
    kv_gain,
    lengths,
    owners,
    queries,
    w_uv,
    w_out,
    resid,
    moe_gain,
    route_ids,
    route_weights,
    w_gate,
    w_up,
    w_down,
):
    dp_count = lax.axis_size("dp")
    columns = lax.axis_size("expert")
    devices = dp_count * columns
    group = lax.axis_index("dp")
    column = lax.axis_index("expert")
    core = column % 2
    pre_rows, width = latent_rows.shape
    half_rope = (width - LAT) // 2
    local_units = pre_rows // UNIT
    block_units = columns * local_units
    gain = kv_gain[None, :]

    border = (MOST - 1) * UNIT
    next_rows = lax.ppermute(
        latent_rows[:border],
        ("dp", "expert"),
        [((i + 1) % devices, i) for i in range(devices)],
    )
    near_rows = jnp.concatenate([latent_rows, next_rows], axis=0)
    rows = [near_rows] + [shift(near_rows, k, dp_count, "dp") for k in range(1, dp_count)]

    request_total = queries.shape[1]
    most_slots = dp_count * local_units
    near_units = local_units + MOST - 1
    where = jnp.stack([group, column]).astype(I32)
    slot_table_rows, request_rows = tables(
        where, lengths, owners, (dp_count, columns, local_units, near_units)
    )
    cosine, sine = turn_table(half_rope)

    model_width = w_out.shape[1]
    piece = model_width // dp_count
    halves = (0, 1, 1, 0)
    quarters = (0, 2, 3, 1)

    def pair_perm(partner):
        perm = []
        for f in range(dp_count):
            for x in range(columns):
                g = (f - x % 2) % dp_count
                perm.append((f * columns + x, (partner(g) + x % 2) % dp_count * columns + x))
        return perm

    weight_perm = pair_perm(lambda g: g ^ 1)
    token_perm = pair_perm(lambda g: dp_count - 1 - g)
    place = (group - core + dp_count) % dp_count
    quarter_of = jnp.array(quarters, I32)
    my_quarter = quarter_of[place]
    their_quarter = quarter_of[place ^ 1]

    def width_half(weight, first):
        return [
            lax.dynamic_slice_in_dim(weight[0], q * piece, piece, 0) for q in (first, first ^ 1)
        ]

    at = jnp.stack(
        [their_quarter, their_quarter ^ 1]
        + [(group - k + dp_count) % dp_count for k in range(1, dp_count)]
    ).astype(I32)
    gate_sent, up_sent, down_near, down_far, down_last = weight_slices(
        at * piece, w_gate, w_up, w_down, dp_count
    )
    gate_sent, up_sent, slot_table_rows, *rows = lax.optimization_barrier(
        (gate_sent, up_sent, slot_table_rows, *rows)
    )
    gate_came = lax.ppermute(gate_sent, ("dp", "expert"), weight_perm)
    up_came = lax.ppermute(up_sent, ("dp", "expert"), weight_perm)

    attended, attended_rest = attend(
        slot_table_rows, rows, cosine, sine, gain, new_rows[0], queries[0], most_slots
    )
    unit_start, home_rank, group_start, group_rank, start_column = (
        request_rows[i] for i in range(5)
    )
    own = owners == group
    unit_len = lengths // UNIT
    members = jnp.arange(request_total, dtype=I32)

    head_share = w_uv.shape[0]
    share = request_total // columns
    chips = columns // 2

    member_column = group_rank // share
    member_row = (
        (member_column % 2 ^ core) * (chips * share)
        + member_column // 2 * share
        + group_rank % share
    )
    is_row = own[None, :] & (member_row[None, :] == members[:, None])
    row_home = jnp.sum(jnp.where(is_row, start_column[None, :], 0), axis=1)
    row_slot = jnp.sum(jnp.where(is_row, home_rank[None, :], 0), axis=1)

    def in_order(part, first):
        count = part.shape[1]
        came = lax.all_to_all(part, "expert", split_axis=0, concat_axis=0, tiled=True)
        came = came.reshape(columns, head_share, count, LAT)
        cells = jnp.arange(columns * count, dtype=I32)
        wanted = row_home * count + row_slot - first
        inside = (row_slot >= first) & (row_slot < first + count)
        pick = (inside[:, None] & (wanted[:, None] == cells[None, :])).astype(BF)
        return [
            jnp.dot(
                pick, came[:, h].reshape(columns * count, LAT), preferred_element_type=F32
            ).astype(BF)
            for h in range(head_share)
        ]

    def spill(held):
        used = jnp.arange(SLOTS, most_slots, dtype=I32) < slot_table_rows[0, 4]
        rest = jnp.where(used[:, None, None], attended_rest, jnp.zeros((), BF))
        return [x + y for x, y in zip(held, in_order(rest.transpose(1, 0, 2), SLOTS))]

    by_head = in_order(attended, 0)
    by_head = lax.cond(jnp.max(home_rank) >= SLOTS, spill, lambda held: held, by_head)
    projected = jnp.concatenate(
        [
            jnp.dot(rows_h, w_uv[h], preferred_element_type=F32).astype(BF)
            for h, rows_h in enumerate(by_head)
        ],
        axis=1,
    )
    partial_sums = jnp.dot(
        projected, w_out, preferred_element_type=F32
    ).astype(BF)
    partial_sums, gate_came, up_came, down_near, down_last = lax.optimization_barrier(
        (partial_sums, gate_came, up_came, down_near, down_last)
    )
    down_near = shift(down_near, 1, dp_count, "dp")
    down_last = shift(down_last, 3, dp_count, "dp")

    keep = chips * share
    other = lax.ppermute(partial_sums[keep:], "expert", [(i, i ^ 1) for i in range(columns)])
    pair_sums = (partial_sums[:keep].astype(F32) + other.astype(F32)).astype(BF)
    chip_sums = lax.all_to_all(
        pair_sums.reshape(chips, share, model_width),
        "expert",
        split_axis=0,
        concat_axis=0,
        tiled=True,
        axis_index_groups=[[2 * i + c for i in range(chips)] for c in range(2)],
    )
    chip_sums, down_near, down_last, down_far = lax.optimization_barrier(
        (chip_sums, down_near, down_last, down_far)
    )
    down_far = shift(down_far, 2, dp_count, "dp")
    attention_out = jnp.sum(chip_sums.astype(F32), axis=0)
    residual = resid[0].astype(F32) + attention_out
    normed = (
        residual
        * lax.rsqrt(jnp.mean(residual * residual, axis=1, keepdims=True) + eps)
        * moe_gain[None, :]
    ).astype(BF)

    tokens = resid.shape[1]
    capacity = 2
    expert_ids = jnp.arange(columns, dtype=I32)
    matches = route_ids[0][:, :, None] == expert_ids[None, None, :]
    combine_weights = jnp.sum(jnp.where(matches, route_weights[0][:, :, None], 0.0), axis=1)
    routed = jnp.any(matches, axis=1)
    token_order = jnp.arange(tokens, dtype=I32)
    earlier = token_order[None, :] < token_order[:, None]
    slot_rank = jnp.sum(jnp.where(earlier[:, :, None], routed.astype(I32)[None, :, :], 0), axis=1)
    slot_ids = jnp.arange(capacity, dtype=I32)
    slot_table = routed.T[:, None, :] & (slot_rank.T[:, None, :] == slot_ids[None, :, None])
    table = slot_table.reshape(columns * capacity, tokens)
    even = (jnp.arange(columns * capacity, dtype=I32) // capacity % 2 == 0)[:, None]
    table = jnp.concatenate([table & even, table & ~even], axis=1).astype(BF)
    outgoing = []
    for f in range(dp_count):
        both = jnp.concatenate(
            [
                normed[:, q * piece : (q + 1) * piece]
                for q in (quarters[f], quarters[(f - 1) % dp_count])
            ],
            axis=0,
        )
        outgoing.append(jnp.dot(table, both, preferred_element_type=F32).astype(BF))
    outgoing = jnp.stack(outgoing).reshape(devices, capacity, piece)
    arrived = lax.all_to_all(
        outgoing, ("dp", "expert"), split_axis=0, concat_axis=0, tiled=True
    ).reshape(devices * capacity, piece)

    local_rows = local_units * UNIT
    to_rows = jnp.concatenate(
        [block[:local_rows].reshape(local_units, UNIT, width) for block in rows], axis=0
    ).transpose(1, 0, 2)
    arrived, down_far, to_rows = lax.optimization_barrier((arrived, down_far, to_rows))
    beside = lax.ppermute(arrived, ("dp", "expert"), token_perm)
    dealt = lax.all_to_all(to_rows, "expert", split_axis=0, concat_axis=0, tiled=True)

    gate_own, up_own = width_half(w_gate, my_quarter), width_half(w_up, my_quarter)
    weights = (gate_came, up_came, gate_own, up_own)
    first = [jnp.dot(arrived, weight[0], preferred_element_type=F32) for weight in weights]
    beside, *first = lax.optimization_barrier((beside, *first))
    gate_given, up_given, gate_sum, up_sum = (
        part + jnp.dot(beside, weight[1], preferred_element_type=F32)
        for part, weight in zip(first, weights)
    )
    given = jnp.concatenate([gate_given, up_given], axis=1).astype(BF)
    given = lax.ppermute(given, ("dp", "expert"), weight_perm).astype(F32)
    half = gate_sum.shape[1]
    hidden = (
        jax.nn.silu(gate_sum + given[:, :half]) * (up_sum + given[:, half:])
    ).astype(BF)
    hidden_all = jnp.concatenate(
        [hidden] + [shift(hidden, k, dp_count, "dp") for k in range(1, dp_count)], axis=1
    )
    hidden_all, dealt = lax.optimization_barrier((hidden_all, dealt))
    downs = jnp.concatenate([lax.dynamic_slice_in_dim(w_down[0], group * piece, piece, 1), down_near, down_far, down_last], axis=0)
    out = jnp.dot(hidden_all, downs, preferred_element_type=F32)
    returned = lax.all_to_all(
        out.astype(BF).reshape(devices, capacity, piece),
        ("dp", "expert"),
        split_axis=0,
        concat_axis=0,
        tiled=True,
    )

    slots = jnp.arange(pre_rows, dtype=I32)
    offset = slots[:, None] - group_start[None, :]
    covers = own[None, :] & (offset >= 0) & (offset < unit_len[None, :])
    slot_offset = jnp.sum(jnp.where(covers, offset, 0), axis=1)
    slot_unit = jnp.sum(jnp.where(covers, offset + unit_start[None, :], 0), axis=1)
    relative = (slot_unit // block_units - group + dp_count) % dp_count
    cache_place = (
        slot_unit % block_units // local_units * most_slots
        + relative * local_units
        + slot_unit % local_units
    )
    places = jnp.arange(columns * most_slots, dtype=I32)
    pick = (cache_place[:, None] == places[None, :]).astype(BF)
    raw_cache = jnp.dot(
        pick, dealt.reshape(columns * most_slots, width), preferred_element_type=F32
    )
    turned = []
    for table_rows in (cosine, sine):
        mine = jnp.asarray(table_rows).reshape(MOST + 1, UNIT, half_rope)
        mine = lax.dynamic_index_in_dim(mine, column, 1, keepdims=False)
        picked = mine[:1]
        for o in range(1, MOST):
            picked = jnp.where(slot_offset[:, None] == o, mine[o : o + 1], picked)
        turned.append(picked)
    cache_local = norm_rotate(raw_cache, *turned, gain)

    slot_weights = jnp.where(slot_table, combine_weights.T[:, None, :], 0.0)
    moe_sum = jnp.einsum(
        "xct,fxcd->tfd",
        slot_weights,
        returned.reshape(dp_count, columns, capacity, piece).astype(F32),
        precision=lax.Precision.HIGHEST,
    ).reshape(tokens, model_width)
    decoded = (residual + moe_sum).astype(BF)
    return (cache_local[None, None], decoded[None])


def solution(mesh):
    return jax.shard_map(
        shards,
        mesh=mesh,
        in_specs=(
            P(("dp", "expert"), None),
            P("dp", None, None),
            P(),
            P(),
            P(),
            P("dp", None, None, None),
            P("expert", None, None),
            P("expert", None),
            P("dp", "expert", None),
            P(),
            P("dp", "expert", None),
            P("dp", "expert", None),
            P("expert", None, "dp"),
            P("expert", None, "dp"),
            P("expert", "dp", None),
        ),
        out_specs=(P("dp", "expert", None, None), P("dp", "expert", None)),
        check_vma=False,
    )
```

time: 238 us -> 430 us (1.81)
  Pallas kernels: 4.65 us -> 203 us
  other arithmetic: 20 us -> 7.13 us
  starting transfers between devices: 54.4 us -> 65.6 us
  local copies, waits for them, and re-layouts: 26.3 us -> 17.2 us
    pallas_call x1 -> x3, Pallas kernels: 4.65 us -> 203 us  [the longest x1 197 us: weight_slices(): pl.pallas_call(slice_kernel, out_shape=(halves, halves) + (part,) * (dp_c...]
    ppermute x1, waiting for transfers between devices: 0.01 us -> 19.7 us  [shards(): up_came = lax.ppermute(up_sent, ('dp', 'expert'), weight_perm)]
    all_to_all x1, waiting for transfers between devices: 23.7 us -> 10.3 us  [shards(): lax.all_to_all(outgoing, ('dp', 'expert'), split_axis=0, concat_axis=0, t...]
    ppermute x9, waiting for transfers between devices: 51.6 us -> 44.5 us  [shift(): return lax.ppermute(x, axis, [((i + step) % size, i) for i in range(size)])]
    reshape x3 -> x0, local copies, waits for them, and re-layouts: 6.63 us -> none  [the longest x2 4.55 us: to_heads(): part = part.reshape(count, columns, head_share * LAT).transpose(1, 0, 2)]
    ppermute x1, waiting for transfers between devices: 0.01 us -> 6.02 us  [shards(): gate_came = lax.ppermute(gate_sent, ('dp', 'expert'), weight_perm)]
    another operation x6 -> x3, other arithmetic: 5.51 us -> 0.16 us  [the longest x2 4.42 us: width_half(): jnp.stack([lax.dynamic_slice_in_dim(weight[0], q * piece, piece, 0) for q...]
  transfers between devices with their start and end apart: 20 -> 20, of which waited for: 12 -> 15; matrix products, arithmetic and copies ran while one was open for 22% -> 8% of each run, Pallas kernels for 2% -> 46%
where the time goes in v4:
time: 430 us; the launch traced here: 429 us
  Pallas kernels  203 us (47%)
  waiting for transfers between devices  107 us (25%)
  starting transfers between devices  65.6 us (15%)
  matrix products  24.6 us (6%)
  local copies, waits for them, and re-layouts  17.2 us (4%)
  other arithmetic  7.13 us (2%)
    pallas_call x1, Pallas kernels, weight_slices(): pl.pallas_call(slice_kernel, out_shape=(halves, halves) + (part,) * (dp_c...  197 us
    ppermute x9, waiting for transfers between devices, shift(): return lax.ppermute(x, axis, [((i + step) % size, i) for i in range(size)])  44.5 us
    ppermute x1, waiting for transfers between devices, shards(): up_came = lax.ppermute(up_sent, ('dp', 'expert'), weight_perm)  19.7 us
    all_to_all x1, starting transfers between devices, in_order(): lax.all_to_all(part, 'expert', split_axis=0, concat_axis=0, tiled=True)  17.9 us
    all_to_all x1, waiting for transfers between devices, shards(): lax.all_to_all(out.astype(BF).reshape(devices, capacity, piece), ('dp', '...  16.1 us
    ppermute x9, starting transfers between devices, shift(): return lax.ppermute(x, axis, [((i + step) % size, i) for i in range(size)])  10.8 us
    all_to_all x1, waiting for transfers between devices, shards(): lax.all_to_all(outgoing, ('dp', 'expert'), split_axis=0, concat_axis=0, t...  10.3 us
    all_to_all x1, starting transfers between devices, shards(): lax.all_to_all(to_rows, 'expert', split_axis=0, concat_axis=0, tiled=True)  9.11 us
  transfers between devices with their start and end apart: 20, of which 15 were waited for; matrix products, arithmetic and copies ran while one was open for 8% of the time, Pallas kernels for 46%

profile of v4, /device:TPU:1, one launch (start us, length us, event | category | flops | bytes accessed | tf_op | source)
XLA Modules:
  0.0 428.6 jit_solution(479968988559550881)
XLA Ops:
  1.5 1.4 collective-permute-start
  4.3 1.3 fusion.125
  8.7 196.5 %weight_slices.1 = (bf16[2,1792,256]{2,1,0:T(8,128)(2,1)}, bf16[2,1792,256]{2,1,0:T(8,128)(2,1)}, bf16[256,1792]{1,0:T(8,128)(2,1)}, bf16[256,1792]{1,0:T(8,128)(2,1)}, bf16[256,1792]{1,0:T(8,128)(2,1)}) custom-call(s32[5]{0:T(128)} %broadcast_multiply_fusion.at_ref, bf16[1,7168,256]{2,1,0:T(8,128)(2,1)} %gate_ref.1, bf16[1,7168,256]{2,1,0:T(8,128)(2,1)} %up_ref.1, ...), custom_call_target="tpu_custom_call" | custom-call | flops 1000 | bytes 4096 | tf_op jit(solution)/shard_map/weight_slices/pallas_call | solution.py:155
  205.3 2.6 collective-permute-start.1
  209.7 6.0 %collective-permute-done.1.refs_2_ = bf16[256,576]{1,0:T(8,128)(2,1)S(1)} collective-permute-done((bf16[256,576]{1,0:T(8,128)(2,1)S(1)}, bf16[256,576]{1,0:T(8,128)(2,1)S(1)}, u32[]{:S(2)}, u32[]{:S(2)}) %collective-permute-start.1) | collective-permute-done | bytes 294944 | tf_op jit(solution)/shard_map/ppermute | solution.py:44
  215.8 3.4 collective-permute-done.3.refs_4_
  219.2 3.2 copy-done
  222.4 5.4 %attend.1 = (bf16[64,8,512]{2,1,0:T(8,128)(2,1)}, bf16[16,64,512]{2,1,0:T(8,128)(2,1)S(1)}) custom-call(s32[32,128]{1,0:T(8,128)S(1)} %get-tuple-element.65.refs_0_, bf16[256,576]{1,0:T(8,128)(2,1)S(1)} %constant_dynamic-update-slice_fusion.refs_1_, bf16[256,576]{1,0:T(8,128)(2,1)S(1)} %collective-permute-done.1.refs_2_, ...), custom_call_target="tpu_custom_call" | custom-call | flops 100000000 | bytes 4000000 | tf_op jit(solution)/shard_map/attend/pallas_call | solution.py:242
  227.9 17.9 %all-to-all-start.1 = ((bf16[64,8,512]{2,1,0:T(8,128)(2,1)}), bf16[64,8,512]{2,1,0:T(8,128)(2,1)S(1)}, u32[]{:S(2)}, u32[]{:S(2)}) async-start(bf16[64,8,512]{2,1,0:T(8,128)(2,1)} %get-tuple-element.70), calls=%async_computation.1 | async-start | bytes 1048576 | tf_op jit(solution)/shard_map/all_to_all | solution.py:378
  245.8 1.2 collective-permute-start.4
  247.0 1.5 collective-permute-start.5
  249.4 8.0 %all-to-all-done.1 = bf16[64,8,512]{2,1,0:T(8,128)(2,1)S(1)} async-done(((bf16[64,8,512]{2,1,0:T(8,128)(2,1)}), bf16[64,8,512]{2,1,0:T(8,128)(2,1)S(1)}, u32[]{:S(2)}, u32[]{:S(2)}) %all-to-all-start.1) | async-done | bytes 524320 | tf_op jit(solution)/shard_map/all_to_all | solution.py:378
  260.7 2.8 convolution_convert_fusion.2
  263.5 6.0 %collective-permute-done.4 = bf16[2,1792,256]{2,1,0:T(8,128)(2,1)} collective-permute-done((bf16[2,1792,256]{2,1,0:T(8,128)(2,1)}, bf16[2,1792,256]{2,1,0:T(8,128)(2,1)}, u32[]{:S(2)}, u32[]{:S(2)}) %collective-permute-start.4) | collective-permute-done | bytes 1835040 | tf_op jit(solution)/shard_map/ppermute | solution.py:349
  269.5 19.7 %collective-permute-done.5 = bf16[2,1792,256]{2,1,0:T(8,128)(2,1)} collective-permute-done((bf16[2,1792,256]{2,1,0:T(8,128)(2,1)}, bf16[2,1792,256]{2,1,0:T(8,128)(2,1)}, u32[]{:S(2)}, u32[]{:S(2)}) %collective-permute-start.5) | collective-permute-done | bytes 1835040 | tf_op jit(solution)/shard_map/ppermute | solution.py:350
  291.5 1.2 collective-permute-start.7
  293.1 1.3 add_convert_fusion
  294.3 1.2 reshape.266
  295.5 6.8 %all-to-all-start.2 = ((bf16[16,3,7168]{2,1,0:T(4,128)(2,1)}), bf16[16,3,7168]{2,1,0:T(4,128)(2,1)S(1)}, u32[]{:S(2)}, u32[]{:S(2)}) async-start(bf16[16,3,7168]{2,1,0:T(4,128)(2,1)} %reshape.266), calls=%async_computation.2 | async-start | bytes 1835008 | tf_op jit(solution)/shard_map/all_to_all | solution.py:417
  302.7 10.9 %collective-permute-done.7 = bf16[256,1792]{1,0:T(8,128)(2,1)} collective-permute-done((bf16[256,1792]{1,0:T(8,128)(2,1)}, bf16[256,1792]{1,0:T(8,128)(2,1)}, u32[]{:S(2)}, u32[]{:S(2)}) %collective-permute-start.7) | collective-permute-done | bytes 917536 | tf_op jit(solution)/shard_map/ppermute | solution.py:44
  313.5 2.0 collective-permute-done.8
  315.5 1.3 all-to-all-done.2
  318.8 1.3 reshape.267
  320.0 6.8 %all-to-all-start.3 = ((bf16[128,2,1792]{2,1,0:T(2,128)(2,1)}), bf16[128,2,1792]{2,1,0:T(2,128)(2,1)S(1)}, u32[]{:S(2)}, u32[]{:S(2)}) async-start(bf16[128,2,1792]{2,1,0:T(2,128)(2,1)} %reshape.267), calls=%async_computation.3 | async-start | bytes 1835008 | tf_op jit(solution)/shard_map/all_to_all | solution.py:462
  326.8 3.0 collective-permute-start.9
  330.0 2.2 dynamic-slice_bitcast_fusion
  332.7 1.5 maximum_bitcast_fusion
  334.2 10.3 %all-to-all-done.3 = bf16[128,2,1792]{2,1,0:T(2,128)(2,1)S(1)} async-done(((bf16[128,2,1792]{2,1,0:T(2,128)(2,1)}), bf16[128,2,1792]{2,1,0:T(2,128)(2,1)S(1)}, u32[]{:S(2)}, u32[]{:S(2)}) %all-to-all-start.3) | async-done | bytes 917536 | tf_op jit(solution)/shard_map/all_to_all | solution.py:462
  344.9 14.5 %collective-permute-done.9 = bf16[256,1792]{1,0:T(8,128)(2,1)} collective-permute-done((bf16[256,1792]{1,0:T(8,128)(2,1)}, bf16[256,1792]{1,0:T(8,128)(2,1)}, u32[]{:S(2)}, u32[]{:S(2)}) %collective-permute-start.9) | collective-permute-done | bytes 917536 | tf_op jit(solution)/shard_map/ppermute | solution.py:44
  359.7 1.6 fusion.36
  361.3 9.1 %all-to-all-start.4 = ((bf16[32,24,576]{2,1,0:T(8,128)(2,1)}), bf16[32,24,576]{2,1,0:T(8,128)(2,1)S(1)}, u32[]{:S(2)}, u32[]{:S(2)}) async-start(bf16[32,24,576]{2,1,0:T(8,128)(2,1)} %maximum_bitcast_fusion), calls=%async_computation.4 | async-start | bytes 1966080 | tf_op jit(solution)/shard_map/all_to_all | solution.py:472
  370.4 1.6 fusion.38
  372.0 1.6 fusion.40
  373.6 1.6 fusion.42
  375.2 1.6 fusion.32
  376.8 1.6 fusion.30
  378.5 1.9 collective-permute-start.11
  380.4 1.6 fusion.28
  382.0 1.6 fusion.34
  383.6 1.4 collective-permute-done.11
  385.2 1.9 collective-permute-start.12
  388.7 1.6 collective-permute-done.12
  390.2 3.0 collective-permute-done.13
  393.3 3.0 collective-permute-done.14
  396.3 3.1 fusion.21
  399.5 1.3 reshape.276
  400.8 7.6 %all-to-all-start.5 = ((bf16[128,2,1792]{2,1,0:T(2,128)(2,1)}), bf16[128,2,1792]{2,1,0:T(2,128)(2,1)S(1)}, u32[]{:S(2)}, u32[]{:S(2)}) async-start(bf16[128,2,1792]{2,1,0:T(2,128)(2,1)} %reshape.276), calls=%async_computation.5 | async-start | bytes 1835008 | tf_op jit(solution)/shard_map/all_to_all | solution.py:494
  410.0 16.1 %all-to-all-done.5 = bf16[128,2,1792]{2,1,0:T(2,128)(2,1)S(1)} async-done(((bf16[128,2,1792]{2,1,0:T(2,128)(2,1)}), bf16[128,2,1792]{2,1,0:T(2,128)(2,1)S(1)}, u32[]{:S(2)}, u32[]{:S(2)}) %all-to-all-start.5) | async-done | bytes 917536 | tf_op jit(solution)/shard_map/all_to_all | solution.py:494
  (112 shorter events, 20.7 us)
Async XLA Ops:
  1.5 203.7 %collective-permute-start = (bf16[64,576]{1,0:T(8,128)(2,1)S(1)}, bf16[64,576]{1,0:T(8,128)(2,1)S(1)}, u32[]{:S(2)}, u32[]{:S(2)}) collective-permute-start(bf16[64,576]{1,0:T(8,128)(2,1)S(1)} %slice.129), channel_id=1, source_target_pairs={{1,0},{2,1},{3,2},{4,3},{5,4},{6,5},{7,6},{8,7},{9,8},{10,9},{11,1... | collective-permute-start | bytes 221192 | tf_op jit(solution)/shard_map/ppermute | solution.py:297
  8.6 196.6 %copy-start.6 = (bf16[192,576]{1,0:T(8,128)(2,1)S(1)}, bf16[192,576]{1,0:T(8,128)(2,1)}, u32[]{:S(2)}) copy-start(bf16[192,576]{1,0:T(8,128)(2,1)} %param.20) | copy-start | bytes 663556
  8.6 201.1 %copy-start.8 = (s32[384]{0:T(512)S(1)}, s32[384]{0:T(512)}, u32[]{:S(2)}) copy-start(s32[384]{0:T(512)} %param.24) | copy-start | bytes 4612
  8.6 210.5 %copy-start.1 = (bf16[1,96,576]{2,1,0:T(8,128)(2,1)S(1)}, bf16[1,96,576]{2,1,0:T(8,128)(2,1)}, u32[]{:S(2)}) copy-start(bf16[1,96,576]{2,1,0:T(8,128)(2,1)} %param.21) | copy-start | bytes 331780
  8.6 210.5 %copy-start.2 = (f32[128,32]{1,0:T(8,128)S(1)}, f32[128,32]{1,0:T(8,128)}, u32[]{:S(2)}) copy-start(f32[128,32]{1,0:T(8,128)} %constant.222.clone.refs_5_) | copy-start | bytes 49156
  8.7 210.5 %copy-start.3 = (f32[128,32]{1,0:T(8,128)S(1)}, f32[128,32]{1,0:T(8,128)}, u32[]{:S(2)}) copy-start(f32[128,32]{1,0:T(8,128)} %constant.223.clone.refs_6_) | copy-start | bytes 49156
  8.7 210.5 %copy-start.4 = (f32[512]{0:T(512)S(1)}, f32[512]{0:T(512)}, u32[]{:S(2)}) copy-start(f32[512]{0:T(512)} %param.22) | copy-start | bytes 6148
  205.3 10.5 %collective-permute-start.1 = (bf16[256,576]{1,0:T(8,128)(2,1)S(1)}, bf16[256,576]{1,0:T(8,128)(2,1)S(1)}, u32[]{:S(2)}, u32[]{:S(2)}) collective-permute-start(bf16[256,576]{1,0:T(8,128)(2,1)S(1)} %constant_dynamic-update-slice_fusion.refs_1_), channel_id=1, source_target_pairs={{32,0},{64,32},{96,64},{0,96},{33,1},{65,33},{97,65},{1,97},{34,2}... | collective-permute-start | bytes 884744 | tf_op jit(solution)/shard_map/ppermute | solution.py:44
  207.9 7.8 %collective-permute-start.2 = (bf16[256,576]{1,0:T(8,128)(2,1)S(1)}, bf16[256,576]{1,0:T(8,128)(2,1)S(1)}, u32[]{:S(2)}, u32[]{:S(2)}) collective-permute-start(bf16[256,576]{1,0:T(8,128)(2,1)S(1)} %constant_dynamic-update-slice_fusion.refs_1_), channel_id=1, source_target_pairs={{64,0},{96,32},{0,64},{32,96},{65,1},{97,33},{1,65},{33,97},{66,2}... | collective-permute-start | bytes 884744 | tf_op jit(solution)/shard_map/ppermute | solution.py:44
  208.4 10.7 %collective-permute-start.3 = (bf16[256,576]{1,0:T(8,128)(2,1)S(1)}, bf16[256,576]{1,0:T(8,128)(2,1)S(1)}, u32[]{:S(2)}, u32[]{:S(2)}) collective-permute-start(bf16[256,576]{1,0:T(8,128)(2,1)S(1)} %constant_dynamic-update-slice_fusion.refs_1_), channel_id=1, source_target_pairs={{96,0},{0,32},{32,64},{64,96},{97,1},{1,33},{33,65},{65,97},{98,2}... | collective-permute-start | bytes 884744 | tf_op jit(solution)/shard_map/ppermute | solution.py:44
  219.2 3.2 copy-start
  227.9 29.5 %all-to-all-start.1 = ((bf16[64,8,512]{2,1,0:T(8,128)(2,1)}), bf16[64,8,512]{2,1,0:T(8,128)(2,1)S(1)}, u32[]{:S(2)}, u32[]{:S(2)}) async-start(bf16[64,8,512]{2,1,0:T(8,128)(2,1)} %get-tuple-element.70), calls=%async_computation.1 | async-start | bytes 1048576 | tf_op jit(solution)/shard_map/all_to_all | solution.py:378
  245.8 23.7 %collective-permute-start.4 = (bf16[2,1792,256]{2,1,0:T(8,128)(2,1)}, bf16[2,1792,256]{2,1,0:T(8,128)(2,1)}, u32[]{:S(2)}, u32[]{:S(2)}) collective-permute-start(bf16[2,1792,256]{2,1,0:T(8,128)(2,1)} %get-tuple-element.74), channel_id=1, source_target_pairs={{0,32},{1,97},{2,34},{3,99},{4,36},{5,101},{6,38},{7,103},{8,40},{... | collective-permute-start | bytes 5505032 | tf_op jit(solution)/shard_map/ppermute | solution.py:349
  247.0 42.1 %collective-permute-start.5 = (bf16[2,1792,256]{2,1,0:T(8,128)(2,1)}, bf16[2,1792,256]{2,1,0:T(8,128)(2,1)}, u32[]{:S(2)}, u32[]{:S(2)}) collective-permute-start(bf16[2,1792,256]{2,1,0:T(8,128)(2,1)} %get-tuple-element.75), channel_id=1, source_target_pairs={{0,32},{1,97},{2,34},{3,99},{4,36},{5,101},{6,38},{7,103},{8,40},{... | collective-permute-start | bytes 5505032 | tf_op jit(solution)/shard_map/ppermute | solution.py:350
  258.4 32.3 %copy-start.10 = (s32[1,3,8]{2,0,1:T(1,128)S(1)}, s32[1,3,8]{2,0,1:T(1,128)}, u32[]{:S(2)}) copy-start(s32[1,3,8]{2,0,1:T(1,128)} %param.30) | copy-start | bytes 292
  258.4 33.0 %copy-start.11 = (f32[1,3,8]{2,0,1:T(1,128)S(1)}, f32[1,3,8]{2,0,1:T(1,128)}, u32[]{:S(2)}) copy-start(f32[1,3,8]{2,0,1:T(1,128)} %param.31) | copy-start | bytes 292
  258.4 33.1 %copy-start.9 = (s32[384]{0:T(512)S(1)}, s32[384]{0:T(512)}, u32[]{:S(2)}) copy-start(s32[384]{0:T(512)} %param.23) | copy-start | bytes 4612
  289.2 28.0 %copy-start.5 = (bf16[1,3,7168]{2,1,0:T(4,128)(2,1)S(1)}, bf16[1,3,7168]{2,1,0:T(4,128)(2,1)}, u32[]{:S(2)}) copy-start(bf16[1,3,7168]{2,1,0:T(4,128)(2,1)} %param.28) | copy-start | bytes 129028
  289.2 28.2 %copy-start.7 = (f32[7168]{0:T(1024)S(1)}, f32[7168]{0:T(1024)}, u32[]{:S(2)}) copy-start(f32[7168]{0:T(1024)} %param.29) | copy-start | bytes 86020
  289.2 3.8 collective-permute-start.6
  291.5 22.0 %collective-permute-start.7 = (bf16[256,1792]{1,0:T(8,128)(2,1)}, bf16[256,1792]{1,0:T(8,128)(2,1)}, u32[]{:S(2)}, u32[]{:S(2)}) collective-permute-start(bf16[256,1792]{1,0:T(8,128)(2,1)} %get-tuple-element.79), channel_id=1, source_target_pairs={{32,0},{64,32},{96,64},{0,96},{33,1},{65,33},{97,65},{1,97},{34,2}... | collective-permute-start | bytes 2752520 | tf_op jit(solution)/shard_map/ppermute | solution.py:44
  292.7 22.8 %collective-permute-start.8 = (bf16[256,1792]{1,0:T(8,128)(2,1)}, bf16[256,1792]{1,0:T(8,128)(2,1)}, u32[]{:S(2)}, u32[]{:S(2)}) collective-permute-start(bf16[256,1792]{1,0:T(8,128)(2,1)} %get-tuple-element.80), channel_id=1, source_target_pairs={{96,0},{0,32},{32,64},{64,96},{97,1},{1,33},{33,65},{65,97},{98,2}... | collective-permute-start | bytes 2752520 | tf_op jit(solution)/shard_map/ppermute | solution.py:44
  295.5 21.3 %all-to-all-start.2 = ((bf16[16,3,7168]{2,1,0:T(4,128)(2,1)}), bf16[16,3,7168]{2,1,0:T(4,128)(2,1)S(1)}, u32[]{:S(2)}, u32[]{:S(2)}) async-start(bf16[16,3,7168]{2,1,0:T(4,128)(2,1)} %reshape.266), calls=%async_computation.2 | async-start | bytes 1835008 | tf_op jit(solution)/shard_map/all_to_all | solution.py:417
  320.0 24.5 %all-to-all-start.3 = ((bf16[128,2,1792]{2,1,0:T(2,128)(2,1)}), bf16[128,2,1792]{2,1,0:T(2,128)(2,1)S(1)}, u32[]{:S(2)}, u32[]{:S(2)}) async-start(bf16[128,2,1792]{2,1,0:T(2,128)(2,1)} %reshape.267), calls=%async_computation.3 | async-start | bytes 1835008 | tf_op jit(solution)/shard_map/all_to_all | solution.py:462
  326.8 32.6 %collective-permute-start.9 = (bf16[256,1792]{1,0:T(8,128)(2,1)}, bf16[256,1792]{1,0:T(8,128)(2,1)}, u32[]{:S(2)}, u32[]{:S(2)}) collective-permute-start(bf16[256,1792]{1,0:T(8,128)(2,1)} %get-tuple-element.83), channel_id=1, source_target_pairs={{64,0},{96,32},{0,64},{32,96},{65,1},{97,33},{1,65},{33,97},{66,2}... | collective-permute-start | bytes 2752520 | tf_op jit(solution)/shard_map/ppermute | solution.py:44
  359.4 15.8 %collective-permute-start.10 = (bf16[256,1792]{1,0:T(8,128)(2,1)S(1)}, bf16[256,1792]{1,0:T(8,128)(2,1)S(1)}, u32[]{:S(2)}, u32[]{:S(2)}) collective-permute-start(bf16[256,1792]{1,0:T(8,128)(2,1)S(1)} %reshape.268), channel_id=1, source_target_pairs={{0,96},{1,33},{2,98},{3,35},{4,100},{5,37},{6,102},{7,39},{8,104},... | collective-permute-start | bytes 2752520 | tf_op jit(solution)/shard_map/ppermute | solution.py:471
  361.3 35.0 %all-to-all-start.4 = ((bf16[32,24,576]{2,1,0:T(8,128)(2,1)}), bf16[32,24,576]{2,1,0:T(8,128)(2,1)S(1)}, u32[]{:S(2)}, u32[]{:S(2)}) async-start(bf16[32,24,576]{2,1,0:T(8,128)(2,1)} %maximum_bitcast_fusion), calls=%async_computation.4 | async-start | bytes 1966080 | tf_op jit(solution)/shard_map/all_to_all | solution.py:472
  378.5 6.5 %collective-permute-start.11 = (bf16[256,512]{1,0:T(8,128)(2,1)S(1)}, bf16[256,512]{1,0:T(8,128)(2,1)S(1)}, u32[]{:S(2)}, u32[]{:S(2)}) collective-permute-start(bf16[256,512]{1,0:T(8,128)(2,1)S(1)} %pad_maximum_fusion.2), channel_id=1, source_target_pairs={{0,32},{1,97},{2,34},{3,99},{4,36},{5,101},{6,38},{7,103},{8,40},{... | collective-permute-start | bytes 786440 | tf_op jit(solution)/shard_map/ppermute | solution.py:483
  385.2 5.0 %collective-permute-start.12 = (bf16[256,256]{1,0:T(8,128)(2,1)S(1)}, bf16[256,256]{1,0:T(8,128)(2,1)S(1)}, u32[]{:S(2)}, u32[]{:S(2)}) collective-permute-start(bf16[256,256]{1,0:T(8,128)(2,1)S(1)} %fusion.59), channel_id=1, source_target_pairs={{32,0},{64,32},{96,64},{0,96},{33,1},{65,33},{97,65},{1,97},{34,2}... | collective-permute-start | bytes 393224 | tf_op jit(solution)/shard_map/ppermute | solution.py:44
  387.1 6.2 %collective-permute-start.13 = (bf16[256,256]{1,0:T(8,128)(2,1)S(1)}, bf16[256,256]{1,0:T(8,128)(2,1)S(1)}, u32[]{:S(2)}, u32[]{:S(2)}) collective-permute-start(bf16[256,256]{1,0:T(8,128)(2,1)S(1)} %fusion.59), channel_id=1, source_target_pairs={{64,0},{96,32},{0,64},{32,96},{65,1},{97,33},{1,65},{33,97},{66,2}... | collective-permute-start | bytes 393224 | tf_op jit(solution)/shard_map/ppermute | solution.py:44
  387.1 9.2 %collective-permute-start.14 = (bf16[256,256]{1,0:T(8,128)(2,1)S(1)}, bf16[256,256]{1,0:T(8,128)(2,1)S(1)}, u32[]{:S(2)}, u32[]{:S(2)}) collective-permute-start(bf16[256,256]{1,0:T(8,128)(2,1)S(1)} %fusion.59), channel_id=1, source_target_pairs={{96,0},{0,32},{32,64},{64,96},{97,1},{1,33},{33,65},{65,97},{98,2}... | collective-permute-start | bytes 393224 | tf_op jit(solution)/shard_map/ppermute | solution.py:44
  400.8 25.3 %all-to-all-start.5 = ((bf16[128,2,1792]{2,1,0:T(2,128)(2,1)}), bf16[128,2,1792]{2,1,0:T(2,128)(2,1)S(1)}, u32[]{:S(2)}, u32[]{:S(2)}) async-start(bf16[128,2,1792]{2,1,0:T(2,128)(2,1)} %reshape.276), calls=%async_computation.5 | async-start | bytes 1835008 | tf_op jit(solution)/shard_map/all_to_all | solution.py:494

commit v5 on v4

--- a/solution.py
+++ b/solution.py
@@ -126,16 +126,15 @@
     )(where, lengths[None, :], owners[None, :])
 
 
-def slice_kernel(at_ref, gate_ref, up_ref, down_ref, gate_out, up_out, *refs):
+def slice_kernel(at_ref, gate_ref, up_ref, down_ref, half_out, *refs):
     downs, sems = refs[:-1], refs[-1]
-    piece = gate_out.shape[1]
+    piece = half_out.shape[1]
     copies = []
-    for out, weight in ((gate_out, gate_ref), (up_out, up_ref)):
-        for i in range(2):
-            rows = pl.ds(pl.multiple_of(at_ref[i], 128), piece)
-            copies.append((weight.at[0, rows, :], out.at[i]))
+    for i, weight in enumerate((gate_ref, gate_ref, up_ref, up_ref)):
+        rows = pl.ds(pl.multiple_of(at_ref[i % 2] * piece, 128), piece)
+        copies.append((weight.at[0, rows, :], half_out.at[i]))
     for i, out in enumerate(downs):
-        columns = pl.ds(pl.multiple_of(at_ref[2 + i], 128), piece)
+        columns = pl.ds(pl.multiple_of(at_ref[2 + i] * piece, 128), piece)
         copies.append((down_ref.at[0, :, columns], out))
     copies = [
         pltpu.make_async_copy(source, target, sems.at[i])
@@ -149,15 +148,17 @@
 
 def weight_slices(at, w_gate, w_up, w_down, dp_count):
     piece = w_gate.shape[1] // dp_count
-    away = pl.BlockSpec(memory_space=pl.ANY)
-    halves = jax.ShapeDtypeStruct((2, piece, w_gate.shape[2]), BF)
+    away = pl.BlockSpec(memory_space=pltpu.HBM)
+    whole = pl.BlockSpec(memory_space=pltpu.VMEM)
+    halves = jax.ShapeDtypeStruct((4, piece, w_gate.shape[2]), BF)
     part = jax.ShapeDtypeStruct((w_down.shape[1], piece), BF)
     return pl.pallas_call(
         slice_kernel,
-        out_shape=(halves, halves) + (part,) * (dp_count - 1),
+        out_shape=(halves,) + (part,) * (dp_count - 1),
         in_specs=[pl.BlockSpec(memory_space=pltpu.SMEM)] + [away] * 3,
-        out_specs=(away,) * (dp_count + 1),
+        out_specs=(whole,) * dp_count,
         scratch_shapes=[pltpu.SemaphoreType.DMA((dp_count + 3,))],
+        compiler_params=pltpu.CompilerParams(vmem_limit_bytes=32 * 1024 * 1024),
         cost_estimate=pl.CostEstimate(flops=1000, bytes_accessed=4096, transcendentals=0),
         name="weight_slices",
     )(at, w_gate, w_up, w_down)
@@ -247,7 +248,7 @@
         ),
         in_specs=[pl.BlockSpec(memory_space=pltpu.SMEM)]
         + [whole] * (blocks + 4)
-        + [pl.BlockSpec(memory_space=pl.ANY)],
+        + [pl.BlockSpec(memory_space=pltpu.HBM)],
         out_specs=(whole, whole),
         scratch_shapes=[
             pltpu.VMEM((total_rows, queries.shape[2]), BF),
@@ -300,6 +301,7 @@
         [((i + 1) % devices, i) for i in range(devices)],
     )
     near_rows = jnp.concatenate([latent_rows, next_rows], axis=0)
+    near_rows, late_group = lax.optimization_barrier((near_rows, group))
     rows = [near_rows] + [shift(near_rows, k, dp_count, "dp") for k in range(1, dp_count)]
 
     request_total = queries.shape[1]
@@ -327,9 +329,12 @@
     weight_perm = pair_perm(lambda g: g ^ 1)
     token_perm = pair_perm(lambda g: dp_count - 1 - g)
     place = (group - core + dp_count) % dp_count
-    quarter_of = jnp.array(quarters, I32)
-    my_quarter = quarter_of[place]
-    their_quarter = quarter_of[place ^ 1]
+
+    def quarter_of(g):
+        return jnp.where(g == 0, 0, jnp.where(g == 1, 2, jnp.where(g == 2, 3, 1)))
+
+    my_quarter = quarter_of(place)
+    their_quarter = quarter_of(place ^ 1)
 
     def width_half(weight, first):
         return [
@@ -338,16 +343,13 @@
 
     at = jnp.stack(
         [their_quarter, their_quarter ^ 1]
-        + [(group - k + dp_count) % dp_count for k in range(1, dp_count)]
+        + [(late_group - k + dp_count) % dp_count for k in range(1, dp_count)]
     ).astype(I32)
-    gate_sent, up_sent, down_near, down_far, down_last = weight_slices(
-        at * piece, w_gate, w_up, w_down, dp_count
-    )
-    gate_sent, up_sent, slot_table_rows, *rows = lax.optimization_barrier(
-        (gate_sent, up_sent, slot_table_rows, *rows)
-    )
-    gate_came = lax.ppermute(gate_sent, ("dp", "expert"), weight_perm)
-    up_came = lax.ppermute(up_sent, ("dp", "expert"), weight_perm)
+    half_sent, down_near, down_far, down_last = weight_slices(at, w_gate, w_up, w_down, dp_count)
+    half_sent, slot_table_rows, *rows = lax.optimization_barrier(
+        (half_sent, slot_table_rows, *rows)
+    )
+    half_came = lax.ppermute(half_sent, ("dp", "expert"), weight_perm)
 
     attended, attended_rest = attend(
         slot_table_rows, rows, cosine, sine, gain, new_rows[0], queries[0], most_slots
@@ -405,8 +407,8 @@
     partial_sums = jnp.dot(
         projected, w_out, preferred_element_type=F32
     ).astype(BF)
-    partial_sums, gate_came, up_came, down_near, down_last = lax.optimization_barrier(
-        (partial_sums, gate_came, up_came, down_near, down_last)
+    partial_sums, down_near, down_last = lax.optimization_barrier(
+        (partial_sums, down_near, down_last)
     )
     down_near = shift(down_near, 1, dp_count, "dp")
     down_last = shift(down_last, 3, dp_count, "dp")
@@ -422,9 +424,7 @@
         tiled=True,
         axis_index_groups=[[2 * i + c for i in range(chips)] for c in range(2)],
     )
-    chip_sums, down_near, down_last, down_far = lax.optimization_barrier(
-        (chip_sums, down_near, down_last, down_far)
-    )
+    chip_sums, half_came, down_far = lax.optimization_barrier((chip_sums, half_came, down_far))
     down_far = shift(down_far, 2, dp_count, "dp")
     attention_out = jnp.sum(chip_sums.astype(F32), axis=0)
     residual = resid[0].astype(F32) + attention_out
@@ -467,12 +467,14 @@
     to_rows = jnp.concatenate(
         [block[:local_rows].reshape(local_units, UNIT, width) for block in rows], axis=0
     ).transpose(1, 0, 2)
-    arrived, down_far, to_rows = lax.optimization_barrier((arrived, down_far, to_rows))
+    arrived, down_near, down_last, to_rows = lax.optimization_barrier(
+        (arrived, down_near, down_last, to_rows)
+    )
     beside = lax.ppermute(arrived, ("dp", "expert"), token_perm)
     dealt = lax.all_to_all(to_rows, "expert", split_axis=0, concat_axis=0, tiled=True)
 
     gate_own, up_own = width_half(w_gate, my_quarter), width_half(w_up, my_quarter)
-    weights = (gate_came, up_came, gate_own, up_own)
+    weights = (half_came[:2], half_came[2:], gate_own, up_own)
     first = [jnp.dot(arrived, weight[0], preferred_element_type=F32) for weight in weights]
     beside, *first = lax.optimization_barrier((beside, *first))
     gate_given, up_given, gate_sum, up_sum = (

time: 430 us -> 220 us (0.51)
  Pallas kernels: 203 us -> 11.2 us
  waiting for transfers between devices: 107 us -> 68.3 us
  local copies, waits for them, and re-layouts: 17.2 us -> 25 us
  starting transfers between devices: 65.6 us -> 72.3 us
  other arithmetic: 7.13 us -> 12.4 us
    pallas_call x1, Pallas kernels: 197 us -> 1.73 us  [weight_slices(): pl.pallas_call(slice_kernel, out_shape=(halves,) + (part,) * (dp_count -...]
    ppermute x9, waiting for transfers between devices: 44.5 us -> 9.32 us  [shift(): return lax.ppermute(x, axis, [((i + step) % size, i) for i in range(size)])]
    ppermute x2 -> x1, waiting for transfers between devices: 25.7 us -> 3.84 us  [shards(): half_came = lax.ppermute(half_sent, ('dp', 'expert'), weight_perm)]
    all_to_all x1, waiting for transfers between devices: 1.29 us -> 10.7 us  [shards(): lax.all_to_all(pair_sums.reshape(chips, share, model_width), 'expert', sp...]
    ppermute x9, starting transfers between devices: 10.8 us -> 19.2 us  [shift(): return lax.ppermute(x, axis, [((i + step) % size, i) for i in range(size)])]
    ppermute x1, waiting for transfers between devices: 0.01 us -> 8.27 us  [shards(): beside = lax.ppermute(arrived, ('dp', 'expert'), token_perm)]
    all_to_all x1, starting transfers between devices: 6.76 us -> 11.7 us  [shards(): lax.all_to_all(outgoing, ('dp', 'expert'), split_axis=0, concat_axis=0, t...]
  transfers between devices with their start and end apart: 20 -> 19, of which waited for: 15 -> 13; matrix products, arithmetic and copies ran while one was open for 8% -> 22% of each run, Pallas kernels for 46% -> 1%
where the time goes in v5:
time: 220 us; the launch traced here: 218 us
  starting transfers between devices  72.3 us (33%)
  waiting for transfers between devices  68.3 us (31%)
  matrix products  27.1 us (12%)
  local copies, waits for them, and re-layouts  25 us (11%)
  other arithmetic  12.4 us (6%)
  Pallas kernels  11.2 us (5%)
    ppermute x9, starting transfers between devices, shift(): return lax.ppermute(x, axis, [((i + step) % size, i) for i in range(size)])  19.2 us
    all_to_all x1, waiting for transfers between devices, shards(): lax.all_to_all(out.astype(BF).reshape(devices, capacity, piece), ('dp', '...  16.1 us
    all_to_all x1, starting transfers between devices, in_order(): lax.all_to_all(part, 'expert', split_axis=0, concat_axis=0, tiled=True)  13.7 us
    all_to_all x1, starting transfers between devices, shards(): lax.all_to_all(outgoing, ('dp', 'expert'), split_axis=0, concat_axis=0, t...  11.7 us
    all_to_all x1, waiting for transfers between devices, shards(): lax.all_to_all(pair_sums.reshape(chips, share, model_width), 'expert', sp...  10.7 us
    all_to_all x1, waiting for transfers between devices, shards(): lax.all_to_all(outgoing, ('dp', 'expert'), split_axis=0, concat_axis=0, t...  10.1 us
    ppermute x9, waiting for transfers between devices, shift(): return lax.ppermute(x, axis, [((i + step) % size, i) for i in range(size)])  9.32 us
    all_to_all x1, starting transfers between devices, shards(): lax.all_to_all(out.astype(BF).reshape(devices, capacity, piece), ('dp', '...  9.23 us
  transfers between devices with their start and end apart: 19, of which 13 were waited for; matrix products, arithmetic and copies ran while one was open for 22% of the time, Pallas kernels for 1%

profile of v5, /device:TPU:1, one launch (start us, length us, event | category | flops | bytes accessed | tf_op | source)
XLA Modules:
  0.0 218.1 jit_solution(3698565469022459094)
XLA Ops:
  1.5 1.4 collective-permute-start
  7.3 2.5 %collective-permute-start.1 = (bf16[256,576]{1,0:T(8,128)(2,1)S(1)}, bf16[256,576]{1,0:T(8,128)(2,1)S(1)}, u32[]{:S(2)}, u32[]{:S(2)}) collective-permute-start(bf16[256,576]{1,0:T(8,128)(2,1)S(1)} %pad_maximum_fusion.2.refs_1_), channel_id=1, source_target_pairs={{32,0},{64,32},{96,64},{0,96},{33,1},{65,33},{97,65},{1,97},{34,2}... | collective-permute-start | bytes 884744 | tf_op jit(solution)/shard_map/ppermute | solution.py:44
  12.5 2.0 copy-done
  14.5 2.0 copy-done.1
  16.6 2.0 copy-done.3
  18.6 1.7 weight_slices.1
  20.4 4.4 %collective-permute-done.3.refs_4_ = bf16[256,576]{1,0:T(8,128)(2,1)S(1)} collective-permute-done((bf16[256,576]{1,0:T(8,128)(2,1)S(1)}, bf16[256,576]{1,0:T(8,128)(2,1)S(1)}, u32[]{:S(2)}, u32[]{:S(2)}) %collective-permute-start.3) | collective-permute-done | bytes 294944 | tf_op jit(solution)/shard_map/ppermute | solution.py:44
  24.9 8.5 %attend.1 = (bf16[64,8,512]{2,1,0:T(8,128)(2,1)}, bf16[16,64,512]{2,1,0:T(8,128)(2,1)}) custom-call(s32[32,128]{1,0:T(8,128)S(1)} %get-tuple-element.64.refs_0_, bf16[256,576]{1,0:T(8,128)(2,1)S(1)} %pad_maximum_fusion.2.refs_1_, bf16[256,576]{1,0:T(8,128)(2,1)S(1)} %collective-permute-done.1.refs_2_, bf16[256,576]{1,0:T(8,128)(2,1)S(1)} %collective-permute-done.2.refs_3_, ...), custom_call_target="tpu_custom_call" | custom-call | flops 100000000 | bytes 4000000 | tf_op jit(solution)/shard_map/attend/pallas_call | solution.py:243
  33.4 13.7 %all-to-all-start.1 = ((bf16[64,8,512]{2,1,0:T(8,128)(2,1)}), bf16[64,8,512]{2,1,0:T(8,128)(2,1)}, u32[]{:S(2)}, u32[]{:S(2)}) async-start(bf16[64,8,512]{2,1,0:T(8,128)(2,1)} %get-tuple-element.69), calls=%async_computation.1 | async-start | bytes 1048576 | tf_op jit(solution)/shard_map/all_to_all | solution.py:380
  47.8 4.0 %collective-permute-start.5 = (bf16[4,1792,256]{2,1,0:T(8,128)(2,1)}, bf16[4,1792,256]{2,1,0:T(8,128)(2,1)}, u32[]{:S(2)}, u32[]{:S(2)}) collective-permute-start(bf16[4,1792,256]{2,1,0:T(8,128)(2,1)} %copy-done.8), channel_id=1, source_target_pairs={{0,32},{1,97},{2,34},{3,99},{4,36},{5,101},{6,38},{7,103},{8,40},{... | collective-permute-start | bytes 11010056 | tf_op jit(solution)/shard_map/ppermute | solution.py:352
  51.8 6.8 %all-to-all-done.1 = bf16[64,8,512]{2,1,0:T(8,128)(2,1)} async-done(((bf16[64,8,512]{2,1,0:T(8,128)(2,1)}), bf16[64,8,512]{2,1,0:T(8,128)(2,1)}, u32[]{:S(2)}, u32[]{:S(2)}) %all-to-all-start.1) | async-done | bytes 524320 | tf_op jit(solution)/shard_map/all_to_all | solution.py:380
  59.8 1.2 convolution_convert_fusion.8
  63.2 2.8 %convolution_convert_fusion.2 = bf16[96,7168]{1,0:T(8,128)(2,1)S(1)} fusion(bf16[256,7168]{1,0:T(8,128)(2,1)} %param.26, bf16[96,128]{1,0:T(8,128)(2,1)S(1)} %convolution_convert_fusion.9, bf16[96,128]{1,0:T(8,128)(2,1)S(1)} %convolution_convert_fusion.10), kind=kOutput, calls=%fused_computation.15 | convolution fusion | flops 353107968 | bytes 5095424 | tf_op jit(solution)/shard_map/dot_general | solution.py:407
  69.3 1.3 collective-permute-done.4
  70.6 2.3 %add_convert_fusion = bf16[48,7168]{1,0:T(8,128)(2,1)} fusion(bf16[48,7168]{1,0:T(8,128)(2,1)} %collective-permute-done.4, bf16[96,7168]{1,0:T(8,128)(2,1)} %copy-done.10), kind=kLoop, calls=%fused_computation.38 | loop fusion | flops 1376256 | bytes 2064384 | tf_op jit(solution)/shard_map/convert_element_type | solution.py:418
  72.9 2.2 reshape.257
  75.1 4.3 %all-to-all-start.2 = ((bf16[16,3,7168]{2,1,0:T(4,128)(2,1)}), bf16[16,3,7168]{2,1,0:T(4,128)(2,1)}, u32[]{:S(2)}, u32[]{:S(2)}) async-start(bf16[16,3,7168]{2,1,0:T(4,128)(2,1)} %reshape.257), calls=%async_computation.2 | async-start | bytes 1835008 | tf_op jit(solution)/shard_map/all_to_all | solution.py:419
  79.7 4.0 %collective-permute-start.6 = (bf16[256,1792]{1,0:T(8,128)(2,1)}, bf16[256,1792]{1,0:T(8,128)(2,1)}, u32[]{:S(2)}, u32[]{:S(2)}) collective-permute-start(bf16[256,1792]{1,0:T(8,128)(2,1)} %copy-done.9), channel_id=1, source_target_pairs={{32,0},{64,32},{96,64},{0,96},{33,1},{65,33},{97,65},{1,97},{34,2}... | collective-permute-start | bytes 2752520 | tf_op jit(solution)/shard_map/ppermute | solution.py:44
  84.0 10.7 %all-to-all-done.2 = bf16[16,3,7168]{2,1,0:T(4,128)(2,1)} async-done(((bf16[16,3,7168]{2,1,0:T(4,128)(2,1)}), bf16[16,3,7168]{2,1,0:T(4,128)(2,1)}, u32[]{:S(2)}, u32[]{:S(2)}) %all-to-all-start.2) | async-done | bytes 688160 | tf_op jit(solution)/shard_map/all_to_all | solution.py:419
  94.7 3.8 %collective-permute-done.5 = bf16[4,1792,256]{2,1,0:T(8,128)(2,1)} collective-permute-done((bf16[4,1792,256]{2,1,0:T(8,128)(2,1)}, bf16[4,1792,256]{2,1,0:T(8,128)(2,1)}, u32[]{:S(2)}, u32[]{:S(2)}) %collective-permute-start.5) | collective-permute-done | bytes 3670048 | tf_op jit(solution)/shard_map/ppermute | solution.py:352
  98.5 1.6 convert_reduce_fusion
  102.6 3.1 %reshape.258 = bf16[128,2,1792]{2,1,0:T(2,128)(2,1)} reshape(bf16[4,64,1792]{2,1,0:T(8,128)(2,1)} %pad_maximum_fusion) | data formatting | bytes 1835008 | tf_op jit(solution)/shard_map/reshape | solution.py:461
  105.7 11.7 %all-to-all-start.3 = ((bf16[128,2,1792]{2,1,0:T(2,128)(2,1)}), bf16[128,2,1792]{2,1,0:T(2,128)(2,1)}, u32[]{:S(2)}, u32[]{:S(2)}) async-start(bf16[128,2,1792]{2,1,0:T(2,128)(2,1)} %reshape.258), calls=%async_computation.3 | async-start | bytes 1835008 | tf_op jit(solution)/shard_map/all_to_all | solution.py:462
  117.6 2.2 %dynamic-slice_bitcast_fusion = bf16[256,1792]{1,0:T(8,128)(2,1)} fusion(bf16[1,256,7168]{2,1,0:T(8,128)(2,1)} %down_ref.1, s32[]{:T(128)S(6)} %select_n.236), kind=kLoop, calls=%fused_computation.62 | loop fusion | bytes 1835012 | tf_op jit(solution)/shard_map/dynamic_slice | solution.py:494
  120.3 1.5 maximum_bitcast_fusion
  121.8 2.9 %collective-permute-start.13 = (bf16[256,1792]{1,0:T(8,128)(2,1)S(1)}, bf16[256,1792]{1,0:T(8,128)(2,1)}, u32[]{:S(2)}, u32[]{:S(2)}) collective-permute-start(bf16[256,1792]{1,0:T(8,128)(2,1)S(1)} %get-tuple-element.92), channel_id=1, source_target_pairs={{64,0},{96,32},{0,64},{32,96},{65,1},{97,33},{1,65},{33,97},{66,2}... | collective-permute-start | bytes 2752520 | tf_op jit(solution)/shard_map/ppermute | solution.py:44
  124.7 10.1 %all-to-all-done.3 = bf16[128,2,1792]{2,1,0:T(2,128)(2,1)} async-done(((bf16[128,2,1792]{2,1,0:T(2,128)(2,1)}), bf16[128,2,1792]{2,1,0:T(2,128)(2,1)}, u32[]{:S(2)}, u32[]{:S(2)}) %all-to-all-start.3) | async-done | bytes 917536 | tf_op jit(solution)/shard_map/all_to_all | solution.py:462
  134.8 2.5 %reshape.259 = bf16[256,1792]{1,0:T(8,128)(2,1)S(1)} reshape(bf16[128,2,1792]{2,1,0:T(2,128)(2,1)} %all-to-all-done.3) | data formatting | bytes 1835008 | tf_op jit(solution)/shard_map/reshape | solution.py:464
  137.7 1.6 fusion.36
  139.2 6.0 %all-to-all-start.4 = ((bf16[32,24,576]{2,1,0:T(8,128)(2,1)}), bf16[32,24,576]{2,1,0:T(8,128)(2,1)S(1)}, u32[]{:S(2)}, u32[]{:S(2)}) async-start(bf16[32,24,576]{2,1,0:T(8,128)(2,1)} %maximum_bitcast_fusion), calls=%async_computation.4 | async-start | bytes 1966080 | tf_op jit(solution)/shard_map/all_to_all | solution.py:474
  145.3 1.6 fusion.38
  146.9 1.6 fusion.40
  148.5 1.6 fusion.42
  150.1 8.3 %collective-permute-done.8 = bf16[256,1792]{1,0:T(8,128)(2,1)} collective-permute-done((bf16[256,1792]{1,0:T(8,128)(2,1)S(1)}, bf16[256,1792]{1,0:T(8,128)(2,1)}, u32[]{:S(2)}, u32[]{:S(2)}) %collective-permute-start.8) | collective-permute-done | bytes 917536 | tf_op jit(solution)/shard_map/ppermute | solution.py:473
  158.4 1.9 fusion.32
  160.2 1.9 fusion.30
  162.2 1.9 collective-permute-start.9
  164.1 1.9 fusion.28
  166.0 1.9 fusion.34
  168.9 1.9 collective-permute-start.10
  170.8 6.5 %collective-permute-start.11 = (bf16[256,256]{1,0:T(8,128)(2,1)S(1)}, bf16[256,256]{1,0:T(8,128)(2,1)S(1)}, u32[]{:S(2)}, u32[]{:S(2)}) collective-permute-start(bf16[256,256]{1,0:T(8,128)(2,1)S(1)} %fusion.59), channel_id=1, source_target_pairs={{64,0},{96,32},{0,64},{32,96},{65,1},{97,33},{1,65},{33,97},{66,2}... | collective-permute-start | bytes 393224 | tf_op jit(solution)/shard_map/ppermute | solution.py:44
  178.3 1.4 collective-permute-done.11
  179.7 3.4 %collective-permute-done.12 = bf16[256,256]{1,0:T(8,128)(2,1)S(1)} collective-permute-done((bf16[256,256]{1,0:T(8,128)(2,1)S(1)}, bf16[256,256]{1,0:T(8,128)(2,1)S(1)}, u32[]{:S(2)}, u32[]{:S(2)}) %collective-permute-start.12) | collective-permute-done | bytes 131104 | tf_op jit(solution)/shard_map/ppermute | solution.py:44
  183.9 3.3 %fusion.21 = bf16[256,1792]{1,0:T(8,128)(2,1)S(1)} fusion(bf16[256,1024]{1,0:T(8,128)(2,1)} %pad_maximum_fusion.1, bf16[256,1792]{1,0:T(8,128)(2,1)} %collective-permute-done.7, bf16[256,1792]{1,0:T(8,128)(2,1)} %collective-permute-done.13, bf16[256,1792]{1,0:T(8,128)(2,1)} %collective-permute-done.6, bf16[256,1792]{1,0:T(8,128)(2,1)} %dynamic-slice_bitcast_fusion), kind=kOutput, calls=%fused_computation.28 | convolution fusion | flops 954662912 | bytes 5111808 | tf_op jit(solution)/shard_map/dot_general | solution.py:495
  187.2 1.3 reshape.267
  188.5 9.2 %all-to-all-start.5 = ((bf16[128,2,1792]{2,1,0:T(2,128)(2,1)}), bf16[128,2,1792]{2,1,0:T(2,128)(2,1)S(1)}, u32[]{:S(2)}, u32[]{:S(2)}) async-start(bf16[128,2,1792]{2,1,0:T(2,128)(2,1)} %reshape.267), calls=%async_computation.5 | async-start | bytes 1835008 | tf_op jit(solution)/shard_map/all_to_all | solution.py:496
  199.4 16.1 %all-to-all-done.5 = bf16[128,2,1792]{2,1,0:T(2,128)(2,1)S(1)} async-done(((bf16[128,2,1792]{2,1,0:T(2,128)(2,1)}), bf16[128,2,1792]{2,1,0:T(2,128)(2,1)S(1)}, u32[]{:S(2)}, u32[]{:S(2)}) %all-to-all-start.5) | async-done | bytes 917536 | tf_op jit(solution)/shard_map/all_to_all | solution.py:496
  216.9 1.2 fusion.12
  (115 shorter events, 24.6 us)
Async XLA Ops:
  1.5 4.8 %collective-permute-start = (bf16[64,576]{1,0:T(8,128)(2,1)S(1)}, bf16[64,576]{1,0:T(8,128)(2,1)S(1)}, u32[]{:S(2)}, u32[]{:S(2)}) collective-permute-start(bf16[64,576]{1,0:T(8,128)(2,1)S(1)} %slice.135), channel_id=1, source_target_pairs={{1,0},{2,1},{3,2},{4,3},{5,4},{6,5},{7,6},{8,7},{9,8},{10,9},{11,1... | collective-permute-start | bytes 221192 | tf_op jit(solution)/shard_map/ppermute | solution.py:298
  7.3 13.1 %collective-permute-start.1 = (bf16[256,576]{1,0:T(8,128)(2,1)S(1)}, bf16[256,576]{1,0:T(8,128)(2,1)S(1)}, u32[]{:S(2)}, u32[]{:S(2)}) collective-permute-start(bf16[256,576]{1,0:T(8,128)(2,1)S(1)} %pad_maximum_fusion.2.refs_1_), channel_id=1, source_target_pairs={{32,0},{64,32},{96,64},{0,96},{33,1},{65,33},{97,65},{1,97},{34,2}... | collective-permute-start | bytes 884744 | tf_op jit(solution)/shard_map/ppermute | solution.py:44
  9.9 10.5 %collective-permute-start.2 = (bf16[256,576]{1,0:T(8,128)(2,1)S(1)}, bf16[256,576]{1,0:T(8,128)(2,1)S(1)}, u32[]{:S(2)}, u32[]{:S(2)}) collective-permute-start(bf16[256,576]{1,0:T(8,128)(2,1)S(1)} %pad_maximum_fusion.2.refs_1_), channel_id=1, source_target_pairs={{64,0},{96,32},{0,64},{32,96},{65,1},{97,33},{1,65},{33,97},{66,2}... | collective-permute-start | bytes 884744 | tf_op jit(solution)/shard_map/ppermute | solution.py:44
  10.4 14.4 %collective-permute-start.3 = (bf16[256,576]{1,0:T(8,128)(2,1)S(1)}, bf16[256,576]{1,0:T(8,128)(2,1)S(1)}, u32[]{:S(2)}, u32[]{:S(2)}) collective-permute-start(bf16[256,576]{1,0:T(8,128)(2,1)S(1)} %pad_maximum_fusion.2.refs_1_), channel_id=1, source_target_pairs={{96,0},{0,32},{32,64},{64,96},{97,1},{1,33},{33,65},{65,97},{98,2}... | collective-permute-start | bytes 884744 | tf_op jit(solution)/shard_map/ppermute | solution.py:44
  12.5 2.0 copy-start
  14.5 2.0 copy-start.1
  16.6 2.0 copy-start.3
  18.6 6.2 %copy-start.2 = (bf16[1,96,64,576]{3,2,1,0:T(8,128)(2,1)S(1)}, bf16[1,96,64,576]{3,2,1,0:T(8,128)(2,1)}, u32[]{:S(2)}) copy-start(bf16[1,96,64,576]{3,2,1,0:T(8,128)(2,1)} %param.24) | copy-start | bytes 21233668
  18.6 6.2 %copy-start.4 = (bf16[1,96,576]{2,1,0:T(8,128)(2,1)S(1)}, bf16[1,96,576]{2,1,0:T(8,128)(2,1)}, u32[]{:S(2)}) copy-start(bf16[1,96,576]{2,1,0:T(8,128)(2,1)} %param.20) | copy-start | bytes 331780
  18.6 6.2 %copy-start.5 = (f32[128,32]{1,0:T(8,128)S(1)}, f32[128,32]{1,0:T(8,128)}, u32[]{:S(2)}) copy-start(f32[128,32]{1,0:T(8,128)} %constant.212.clone.refs_5_) | copy-start | bytes 49156
  18.6 6.2 %copy-start.6 = (f32[128,32]{1,0:T(8,128)S(1)}, f32[128,32]{1,0:T(8,128)}, u32[]{:S(2)}) copy-start(f32[128,32]{1,0:T(8,128)} %constant.213.clone.refs_6_) | copy-start | bytes 49156
  18.6 6.2 %copy-start.7 = (f32[512]{0:T(512)S(1)}, f32[512]{0:T(512)}, u32[]{:S(2)}) copy-start(f32[512]{0:T(512)} %param.21) | copy-start | bytes 6148
  20.4 13.0 %copy-start.8 = (bf16[4,1792,256]{2,1,0:T(8,128)(2,1)}, bf16[4,1792,256]{2,1,0:T(8,128)(2,1)S(1)}, u32[]{:S(2)}) copy-start(bf16[4,1792,256]{2,1,0:T(8,128)(2,1)S(1)} %get-tuple-element.76) | copy-start | bytes 11010052
  20.4 13.0 %copy-start.9 = (bf16[256,1792]{1,0:T(8,128)(2,1)}, bf16[256,1792]{1,0:T(8,128)(2,1)S(1)}, u32[]{:S(2)}) copy-start(bf16[256,1792]{1,0:T(8,128)(2,1)S(1)} %get-tuple-element.79) | copy-start | bytes 2752516
  33.4 25.3 %all-to-all-start.1 = ((bf16[64,8,512]{2,1,0:T(8,128)(2,1)}), bf16[64,8,512]{2,1,0:T(8,128)(2,1)}, u32[]{:S(2)}, u32[]{:S(2)}) async-start(bf16[64,8,512]{2,1,0:T(8,128)(2,1)} %get-tuple-element.69), calls=%async_computation.1 | async-start | bytes 1048576 | tf_op jit(solution)/shard_map/all_to_all | solution.py:380
  47.8 50.7 %collective-permute-start.5 = (bf16[4,1792,256]{2,1,0:T(8,128)(2,1)}, bf16[4,1792,256]{2,1,0:T(8,128)(2,1)}, u32[]{:S(2)}, u32[]{:S(2)}) collective-permute-start(bf16[4,1792,256]{2,1,0:T(8,128)(2,1)} %copy-done.8), channel_id=1, source_target_pairs={{0,32},{1,97},{2,34},{3,99},{4,36},{5,101},{6,38},{7,103},{8,40},{... | collective-permute-start | bytes 11010056 | tf_op jit(solution)/shard_map/ppermute | solution.py:352
  61.0 7.5 %copy-start.14 = (s32[1,3,8]{2,0,1:T(1,128)S(1)}, s32[1,3,8]{2,0,1:T(1,128)}, u32[]{:S(2)}) copy-start(s32[1,3,8]{2,0,1:T(1,128)} %param.29) | copy-start | bytes 292
  61.0 8.2 %copy-start.15 = (f32[1,3,8]{2,0,1:T(1,128)S(1)}, f32[1,3,8]{2,0,1:T(1,128)}, u32[]{:S(2)}) copy-start(f32[1,3,8]{2,0,1:T(1,128)} %param.30) | copy-start | bytes 292
  61.0 8.2 %copy-start.13 = (s32[384]{0:T(512)S(1)}, s32[384]{0:T(512)}, u32[]{:S(2)}) copy-start(s32[384]{0:T(512)} %param.22) | copy-start | bytes 4612
  66.0 1.2 copy-start.10
  68.0 32.0 %copy-start.11 = (bf16[1,3,7168]{2,1,0:T(4,128)(2,1)S(1)}, bf16[1,3,7168]{2,1,0:T(4,128)(2,1)}, u32[]{:S(2)}) copy-start(bf16[1,3,7168]{2,1,0:T(4,128)(2,1)} %param.27) | copy-start | bytes 129028
  68.0 32.2 %copy-start.12 = (f32[7168]{0:T(1024)S(1)}, f32[7168]{0:T(1024)}, u32[]{:S(2)}) copy-start(f32[7168]{0:T(1024)} %param.28) | copy-start | bytes 86020
  68.0 2.6 %collective-permute-start.4 = (bf16[48,7168]{1,0:T(8,128)(2,1)}, bf16[48,7168]{1,0:T(8,128)(2,1)}, u32[]{:S(2)}, u32[]{:S(2)}) collective-permute-start(bf16[48,7168]{1,0:T(8,128)(2,1)} %slice.141), channel_id=1, source_target_pairs={{0,1},{1,0},{2,3},{3,2},{4,5},{5,4},{6,7},{7,6},{8,9},{9,8},{10,11... | collective-permute-start | bytes 2064392 | tf_op jit(solution)/shard_map/ppermute | solution.py:417
  75.1 19.6 %all-to-all-start.2 = ((bf16[16,3,7168]{2,1,0:T(4,128)(2,1)}), bf16[16,3,7168]{2,1,0:T(4,128)(2,1)}, u32[]{:S(2)}, u32[]{:S(2)}) async-start(bf16[16,3,7168]{2,1,0:T(4,128)(2,1)} %reshape.257), calls=%async_computation.2 | async-start | bytes 1835008 | tf_op jit(solution)/shard_map/all_to_all | solution.py:419
  79.7 57.5 %collective-permute-start.6 = (bf16[256,1792]{1,0:T(8,128)(2,1)}, bf16[256,1792]{1,0:T(8,128)(2,1)}, u32[]{:S(2)}, u32[]{:S(2)}) collective-permute-start(bf16[256,1792]{1,0:T(8,128)(2,1)} %copy-done.9), channel_id=1, source_target_pairs={{32,0},{64,32},{96,64},{0,96},{33,1},{65,33},{97,65},{1,97},{34,2}... | collective-permute-start | bytes 2752520 | tf_op jit(solution)/shard_map/ppermute | solution.py:44
  83.7 53.5 %collective-permute-start.7 = (bf16[256,1792]{1,0:T(8,128)(2,1)S(1)}, bf16[256,1792]{1,0:T(8,128)(2,1)}, u32[]{:S(2)}, u32[]{:S(2)}) collective-permute-start(bf16[256,1792]{1,0:T(8,128)(2,1)S(1)} %get-tuple-element.80), channel_id=1, source_target_pairs={{96,0},{0,32},{32,64},{64,96},{97,1},{1,33},{33,65},{65,97},{98,2}... | collective-permute-start | bytes 2752520 | tf_op jit(solution)/shard_map/ppermute | solution.py:44
  105.7 29.1 %all-to-all-start.3 = ((bf16[128,2,1792]{2,1,0:T(2,128)(2,1)}), bf16[128,2,1792]{2,1,0:T(2,128)(2,1)}, u32[]{:S(2)}, u32[]{:S(2)}) async-start(bf16[128,2,1792]{2,1,0:T(2,128)(2,1)} %reshape.258), calls=%async_computation.3 | async-start | bytes 1835008 | tf_op jit(solution)/shard_map/all_to_all | solution.py:462
  121.8 62.1 %collective-permute-start.13 = (bf16[256,1792]{1,0:T(8,128)(2,1)S(1)}, bf16[256,1792]{1,0:T(8,128)(2,1)}, u32[]{:S(2)}, u32[]{:S(2)}) collective-permute-start(bf16[256,1792]{1,0:T(8,128)(2,1)S(1)} %get-tuple-element.92), channel_id=1, source_target_pairs={{64,0},{96,32},{0,64},{32,96},{65,1},{97,33},{1,65},{33,97},{66,2}... | collective-permute-start | bytes 2752520 | tf_op jit(solution)/shard_map/ppermute | solution.py:44
  137.3 21.1 %collective-permute-start.8 = (bf16[256,1792]{1,0:T(8,128)(2,1)S(1)}, bf16[256,1792]{1,0:T(8,128)(2,1)}, u32[]{:S(2)}, u32[]{:S(2)}) collective-permute-start(bf16[256,1792]{1,0:T(8,128)(2,1)S(1)} %reshape.259), channel_id=1, source_target_pairs={{0,96},{1,33},{2,98},{3,35},{4,100},{5,37},{6,102},{7,39},{8,104},... | collective-permute-start | bytes 2752520 | tf_op jit(solution)/shard_map/ppermute | solution.py:473
  139.2 44.7 %all-to-all-start.4 = ((bf16[32,24,576]{2,1,0:T(8,128)(2,1)}), bf16[32,24,576]{2,1,0:T(8,128)(2,1)S(1)}, u32[]{:S(2)}, u32[]{:S(2)}) async-start(bf16[32,24,576]{2,1,0:T(8,128)(2,1)} %maximum_bitcast_fusion), calls=%async_computation.4 | async-start | bytes 1966080 | tf_op jit(solution)/shard_map/all_to_all | solution.py:474
  162.2 6.5 %collective-permute-start.9 = (bf16[256,512]{1,0:T(8,128)(2,1)S(1)}, bf16[256,512]{1,0:T(8,128)(2,1)S(1)}, u32[]{:S(2)}, u32[]{:S(2)}) collective-permute-start(bf16[256,512]{1,0:T(8,128)(2,1)S(1)} %pad_maximum_fusion.3), channel_id=1, source_target_pairs={{0,32},{1,97},{2,34},{3,99},{4,36},{5,101},{6,38},{7,103},{8,40},{... | collective-permute-start | bytes 786440 | tf_op jit(solution)/shard_map/ppermute | solution.py:485
  168.9 9.3 %collective-permute-start.10 = (bf16[256,256]{1,0:T(8,128)(2,1)S(1)}, bf16[256,256]{1,0:T(8,128)(2,1)S(1)}, u32[]{:S(2)}, u32[]{:S(2)}) collective-permute-start(bf16[256,256]{1,0:T(8,128)(2,1)S(1)} %fusion.59), channel_id=1, source_target_pairs={{32,0},{64,32},{96,64},{0,96},{33,1},{65,33},{97,65},{1,97},{34,2}... | collective-permute-start | bytes 393224 | tf_op jit(solution)/shard_map/ppermute | solution.py:44
  170.8 8.9 %collective-permute-start.11 = (bf16[256,256]{1,0:T(8,128)(2,1)S(1)}, bf16[256,256]{1,0:T(8,128)(2,1)S(1)}, u32[]{:S(2)}, u32[]{:S(2)}) collective-permute-start(bf16[256,256]{1,0:T(8,128)(2,1)S(1)} %fusion.59), channel_id=1, source_target_pairs={{64,0},{96,32},{0,64},{32,96},{65,1},{97,33},{1,65},{33,97},{66,2}... | collective-permute-start | bytes 393224 | tf_op jit(solution)/shard_map/ppermute | solution.py:44
  177.3 5.8 %collective-permute-start.12 = (bf16[256,256]{1,0:T(8,128)(2,1)S(1)}, bf16[256,256]{1,0:T(8,128)(2,1)S(1)}, u32[]{:S(2)}, u32[]{:S(2)}) collective-permute-start(bf16[256,256]{1,0:T(8,128)(2,1)S(1)} %fusion.59), channel_id=1, source_target_pairs={{96,0},{0,32},{32,64},{64,96},{97,1},{1,33},{33,65},{65,97},{98,2}... | collective-permute-start | bytes 393224 | tf_op jit(solution)/shard_map/ppermute | solution.py:44
  188.5 26.9 %all-to-all-start.5 = ((bf16[128,2,1792]{2,1,0:T(2,128)(2,1)}), bf16[128,2,1792]{2,1,0:T(2,128)(2,1)S(1)}, u32[]{:S(2)}, u32[]{:S(2)}) async-start(bf16[128,2,1792]{2,1,0:T(2,128)(2,1)} %reshape.267), calls=%async_computation.5 | async-start | bytes 1835008 | tf_op jit(solution)/shard_map/all_to_all | solution.py:496

commit v6 on v4

--- a/solution.py
+++ b/solution.py
@@ -44,8 +44,8 @@
     return lax.ppermute(x, axis, [((i + step) % size, i) for i in range(size)])
 
 
-def table_kernel(where_ref, lengths_ref, owners_ref, slots_ref, rows_ref, *, sizes):
-    dp_count, columns, local_units, near_units = sizes
+def table_kernel(where_ref, lengths_ref, owners_ref, slots_ref, rows_ref, cells_ref, *, sizes):
+    dp_count, columns, local_units, near_units, share = sizes
     group, column = where_ref[0], where_ref[1]
     group_f, column_f = group.astype(F32), column.astype(F32)
     count = lengths_ref.shape[1]
@@ -104,6 +104,18 @@
         [start, rank, group_start, group_rank, start_column] + [start] * 3, axis=0
     ).astype(I32)
 
+    member_column = whole(group_rank, share)
+    member_chip = whole(member_column, 2)
+    other_core = jnp.abs(member_column - 2.0 * member_chip - (column % 2).astype(F32))
+    row = (other_core * (columns // 2) + member_chip) * share + (
+        group_rank - member_column * share
+    )
+    lines = cells_ref.shape[0]
+    line = lax.broadcasted_iota(I32, (lines, count), 0).astype(F32)
+    cell = jnp.where(rank < SLOTS, start_column * SLOTS + rank, -1.0)
+    found = jnp.sum(jnp.where(own & (row == line), cell, 0.0), axis=1, keepdims=True)
+    cells_ref[...] = jnp.broadcast_to(found, cells_ref.shape).astype(I32)
+
 
 def tables(where, lengths, owners, sizes):
     lines = sizes[0] * sizes[3]
@@ -117,9 +129,10 @@
         out_shape=(
             jax.ShapeDtypeStruct((lines, 128), I32),
             jax.ShapeDtypeStruct((8, lengths.shape[0]), I32),
+            jax.ShapeDtypeStruct((sizes[1] * sizes[4], 128), I32),
         ),
         in_specs=[pl.BlockSpec(memory_space=pltpu.SMEM), whole, whole],
-        out_specs=(whole, whole),
+        out_specs=(whole, whole, whole),
         compiler_params=pltpu.CompilerParams(vmem_limit_bytes=32 * 1024 * 1024),
         cost_estimate=pl.CostEstimate(flops=1000, bytes_accessed=4096, transcendentals=0),
         name="tables",
@@ -130,12 +143,12 @@
     downs, sems = refs[:-1], refs[-1]
     piece = gate_out.shape[1]
     copies = []
-    for out, weight in ((gate_out, gate_ref), (up_out, up_ref)):
+    for weight, out in ((gate_ref, gate_out), (up_ref, up_out)):
         for i in range(2):
-            rows = pl.ds(pl.multiple_of(at_ref[i], 128), piece)
+            rows = pl.ds(pl.multiple_of(at_ref[i] * piece, 128), piece)
             copies.append((weight.at[0, rows, :], out.at[i]))
     for i, out in enumerate(downs):
-        columns = pl.ds(pl.multiple_of(at_ref[2 + i], 128), piece)
+        columns = pl.ds(pl.multiple_of(at_ref[2 + i] * piece, 128), piece)
         copies.append((down_ref.at[0, :, columns], out))
     copies = [
         pltpu.make_async_copy(source, target, sems.at[i])
@@ -149,15 +162,17 @@
 
 def weight_slices(at, w_gate, w_up, w_down, dp_count):
     piece = w_gate.shape[1] // dp_count
-    away = pl.BlockSpec(memory_space=pl.ANY)
+    away = pl.BlockSpec(memory_space=pltpu.HBM)
+    whole = pl.BlockSpec(memory_space=pltpu.VMEM)
     halves = jax.ShapeDtypeStruct((2, piece, w_gate.shape[2]), BF)
     part = jax.ShapeDtypeStruct((w_down.shape[1], piece), BF)
     return pl.pallas_call(
         slice_kernel,
         out_shape=(halves, halves) + (part,) * (dp_count - 1),
         in_specs=[pl.BlockSpec(memory_space=pltpu.SMEM)] + [away] * 3,
-        out_specs=(away,) * (dp_count + 1),
+        out_specs=(whole,) * (dp_count + 1),
         scratch_shapes=[pltpu.SemaphoreType.DMA((dp_count + 3,))],
+        compiler_params=pltpu.CompilerParams(vmem_limit_bytes=32 * 1024 * 1024),
         cost_estimate=pl.CostEstimate(flops=1000, bytes_accessed=4096, transcendentals=0),
         name="weight_slices",
     )(at, w_gate, w_up, w_down)
@@ -188,7 +203,6 @@
             )
             unit += 1
     fresh[...] = new_ref[...].astype(F32)
-    held_out[...] = jnp.zeros(held_out.shape, F32)
 
     heads = out_ref.shape[0]
     sent = out_ref.shape[1]
@@ -197,7 +211,6 @@
     lane = lax.broadcasted_iota(I32, (heads, lanes), 1)
 
     def one(slot):
-        fetch(slot).wait()
         count = slots_ref[slot, 1]
         own = keys[pl.ds(pl.multiple_of(slots_ref[slot, 0] * UNIT, UNIT), window), :]
         at = pl.ds(count * UNIT, 1)
@@ -219,9 +232,12 @@
         mixture = jnp.dot(weights.astype(BF), held[:, :LAT], preferred_element_type=F32)
         return mixture / total
 
-    @pl.loop(0, jnp.minimum(number, sent))
+    @pl.loop(0, number)
     def _(slot):
-        held_out[slot] = one(slot)
+        fetch(slot).wait()
+
+    for slot in range(sent):
+        held_out[slot] = jnp.where(slot < number, one(slot), 0.0)
 
     out_ref[...] = jnp.swapaxes(held_out[...], 0, 1).astype(BF)
 
@@ -247,7 +263,7 @@
         ),
         in_specs=[pl.BlockSpec(memory_space=pltpu.SMEM)]
         + [whole] * (blocks + 4)
-        + [pl.BlockSpec(memory_space=pl.ANY)],
+        + [pl.BlockSpec(memory_space=pltpu.HBM)],
         out_specs=(whole, whole),
         scratch_shapes=[
             pltpu.VMEM((total_rows, queries.shape[2]), BF),
@@ -262,6 +278,70 @@
         ),
         name="attend",
     )(slots, *rows, cosine, sine, gain, new_rows, queries)
+
+
+def project_kernel(cells_ref, came_ref, more_ref, uv_ref, weight_ref, mine_ref, other_ref):
+    requests = cells_ref.shape[0]
+    sources, heads, slots, _ = came_ref.shape
+    cells = sources * slots
+    pick = cells_ref[:, :1] == lax.broadcasted_iota(I32, (requests, cells), 1)
+    pick = jnp.where(pick, 1.0, 0.0).astype(BF)
+    projected = []
+    for h in range(heads):
+        came = came_ref[:, h].astype(F32).reshape(cells, LAT).astype(BF)
+        rows = jnp.dot(pick, came, preferred_element_type=F32) + more_ref[h].astype(F32)
+        projected.append(
+            jnp.dot(rows.astype(BF), uv_ref[h], preferred_element_type=F32).astype(BF)
+        )
+    projected = jnp.concatenate(projected, axis=1)
+    keep = mine_ref.shape[0]
+    step = weight_ref.shape[1] // 4
+    for first in range(0, weight_ref.shape[1], step):
+        span = slice(first, first + step)
+        sums = jnp.dot(projected, weight_ref[:, span], preferred_element_type=F32).astype(BF)
+        mine_ref[:, span] = sums[:keep]
+        other_ref[:, span] = sums[keep:]
+
+
+def project(cells, came, more, w_uv, w_out):
+    whole = pl.BlockSpec(memory_space=pltpu.VMEM)
+    half = jax.ShapeDtypeStruct((cells.shape[0] // 2, w_out.shape[1]), BF)
+    return pl.pallas_call(
+        project_kernel,
+        out_shape=(half, half),
+        in_specs=[whole] * 5,
+        out_specs=(whole, whole),
+        compiler_params=pltpu.CompilerParams(vmem_limit_bytes=32 * 1024 * 1024),
+        cost_estimate=pl.CostEstimate(
+            flops=4 * 10**8, bytes_accessed=6 * 10**6, transcendentals=0
+        ),
+        name="project",
+    )(cells, came, more, w_uv, w_out)
+
+
+def pair_kernel(mine_ref, other_ref, out_ref):
+    chips, share, width = out_ref.shape
+    step = width // 4
+    for first in range(0, width, step):
+        span = slice(first, first + step)
+        sums = mine_ref[:, span].astype(F32) + other_ref[:, span].astype(F32)
+        for chip in range(chips):
+            out_ref[chip, :, span] = sums[chip * share : (chip + 1) * share].astype(BF)
+
+
+def pair_sum(mine, other, chips):
+    whole = pl.BlockSpec(memory_space=pltpu.VMEM)
+    return pl.pallas_call(
+        pair_kernel,
+        out_shape=jax.ShapeDtypeStruct((chips, mine.shape[0] // chips, mine.shape[1]), BF),
+        in_specs=[whole] * 2,
+        out_specs=whole,
+        compiler_params=pltpu.CompilerParams(vmem_limit_bytes=32 * 1024 * 1024),
+        cost_estimate=pl.CostEstimate(
+            flops=4 * 10**5, bytes_accessed=2 * 10**6, transcendentals=0
+        ),
+        name="pair_sum",
+    )(mine, other)
 
 
 def shards(
@@ -300,14 +380,16 @@
         [((i + 1) % devices, i) for i in range(devices)],
     )
     near_rows = jnp.concatenate([latent_rows, next_rows], axis=0)
+    near_rows, late_group = lax.optimization_barrier((near_rows, group))
     rows = [near_rows] + [shift(near_rows, k, dp_count, "dp") for k in range(1, dp_count)]
 
     request_total = queries.shape[1]
     most_slots = dp_count * local_units
     near_units = local_units + MOST - 1
     where = jnp.stack([group, column]).astype(I32)
-    slot_table_rows, request_rows = tables(
-        where, lengths, owners, (dp_count, columns, local_units, near_units)
+    share = request_total // columns
+    slot_table_rows, request_rows, cells = tables(
+        where, lengths, owners, (dp_count, columns, local_units, near_units, share)
     )
     cosine, sine = turn_table(half_rope)
 
@@ -327,9 +409,12 @@
     weight_perm = pair_perm(lambda g: g ^ 1)
     token_perm = pair_perm(lambda g: dp_count - 1 - g)
     place = (group - core + dp_count) % dp_count
-    quarter_of = jnp.array(quarters, I32)
-    my_quarter = quarter_of[place]
-    their_quarter = quarter_of[place ^ 1]
+
+    def quarter_of(g):
+        return jnp.where(g == 0, 0, jnp.where(g == 1, 2, jnp.where(g == 2, 3, 1)))
+
+    my_quarter = quarter_of(place)
+    their_quarter = quarter_of(place ^ 1)
 
     def width_half(weight, first):
         return [
@@ -338,10 +423,10 @@
 
     at = jnp.stack(
         [their_quarter, their_quarter ^ 1]
-        + [(group - k + dp_count) % dp_count for k in range(1, dp_count)]
+        + [(late_group - k + dp_count) % dp_count for k in range(1, dp_count)]
     ).astype(I32)
     gate_sent, up_sent, down_near, down_far, down_last = weight_slices(
-        at * piece, w_gate, w_up, w_down, dp_count
+        at, w_gate, w_up, w_down, dp_count
     )
     gate_sent, up_sent, slot_table_rows, *rows = lax.optimization_barrier(
         (gate_sent, up_sent, slot_table_rows, *rows)
@@ -360,72 +445,61 @@
     members = jnp.arange(request_total, dtype=I32)
 
     head_share = w_uv.shape[0]
-    share = request_total // columns
     chips = columns // 2
 
-    member_column = group_rank // share
-    member_row = (
-        (member_column % 2 ^ core) * (chips * share)
-        + member_column // 2 * share
-        + group_rank % share
-    )
-    is_row = own[None, :] & (member_row[None, :] == members[:, None])
-    row_home = jnp.sum(jnp.where(is_row, start_column[None, :], 0), axis=1)
-    row_slot = jnp.sum(jnp.where(is_row, home_rank[None, :], 0), axis=1)
-
-    def in_order(part, first):
-        count = part.shape[1]
+    def to_heads(part):
         came = lax.all_to_all(part, "expert", split_axis=0, concat_axis=0, tiled=True)
-        came = came.reshape(columns, head_share, count, LAT)
-        cells = jnp.arange(columns * count, dtype=I32)
-        wanted = row_home * count + row_slot - first
-        inside = (row_slot >= first) & (row_slot < first + count)
-        pick = (inside[:, None] & (wanted[:, None] == cells[None, :])).astype(BF)
-        return [
-            jnp.dot(
-                pick, came[:, h].reshape(columns * count, LAT), preferred_element_type=F32
-            ).astype(BF)
-            for h in range(head_share)
-        ]
-
-    def spill(held):
+        return came.reshape(columns, head_share, part.shape[1], LAT)
+
+    def spill():
         used = jnp.arange(SLOTS, most_slots, dtype=I32) < slot_table_rows[0, 4]
         rest = jnp.where(used[:, None, None], attended_rest, jnp.zeros((), BF))
-        return [x + y for x, y in zip(held, in_order(rest.transpose(1, 0, 2), SLOTS))]
-
-    by_head = in_order(attended, 0)
-    by_head = lax.cond(jnp.max(home_rank) >= SLOTS, spill, lambda held: held, by_head)
-    projected = jnp.concatenate(
-        [
-            jnp.dot(rows_h, w_uv[h], preferred_element_type=F32).astype(BF)
-            for h, rows_h in enumerate(by_head)
-        ],
-        axis=1,
-    )
-    partial_sums = jnp.dot(
-        projected, w_out, preferred_element_type=F32
-    ).astype(BF)
-    partial_sums, gate_came, up_came, down_near, down_last = lax.optimization_barrier(
-        (partial_sums, gate_came, up_came, down_near, down_last)
+        came = to_heads(rest.transpose(1, 0, 2))
+        count = came.shape[2]
+        member_column = group_rank // share
+        member_row = (
+            (member_column % 2 ^ core) * (chips * share)
+            + member_column // 2 * share
+            + group_rank % share
+        )
+        member_cell = jnp.where(home_rank >= SLOTS, start_column * count + home_rank - SLOTS, -1)
+        is_row = own[None, :] & (member_row[None, :] == members[:, None])
+        cell = jnp.sum(jnp.where(is_row, member_cell[None, :], 0), axis=1)
+        pick = (cell[:, None] == jnp.arange(columns * count, dtype=I32)[None, :]).astype(BF)
+        return jnp.stack(
+            [
+                jnp.dot(
+                    pick, came[:, h].reshape(columns * count, LAT), preferred_element_type=F32
+                ).astype(BF)
+                for h in range(head_share)
+            ]
+        )
+
+    more = lax.cond(
+        jnp.max(home_rank) >= SLOTS,
+        spill,
+        lambda: jnp.zeros((head_share, request_total, LAT), BF),
+    )
+    by_head = to_heads(attended)
+    by_head, gate_came = lax.optimization_barrier((by_head, gate_came))
+    mine, other = project(cells, by_head, more, w_uv, w_out)
+    mine, other, up_came, down_near, down_far, down_last = lax.optimization_barrier(
+        (mine, other, up_came, down_near, down_far, down_last)
     )
     down_near = shift(down_near, 1, dp_count, "dp")
+    down_far = shift(down_far, 2, dp_count, "dp")
     down_last = shift(down_last, 3, dp_count, "dp")
 
-    keep = chips * share
-    other = lax.ppermute(partial_sums[keep:], "expert", [(i, i ^ 1) for i in range(columns)])
-    pair_sums = (partial_sums[:keep].astype(F32) + other.astype(F32)).astype(BF)
+    other = lax.ppermute(other, "expert", [(i, i ^ 1) for i in range(columns)])
+    pair_sums = pair_sum(mine, other, chips)
     chip_sums = lax.all_to_all(
-        pair_sums.reshape(chips, share, model_width),
+        pair_sums,
         "expert",
         split_axis=0,
         concat_axis=0,
         tiled=True,
         axis_index_groups=[[2 * i + c for i in range(chips)] for c in range(2)],
     )
-    chip_sums, down_near, down_last, down_far = lax.optimization_barrier(
-        (chip_sums, down_near, down_last, down_far)
-    )
-    down_far = shift(down_far, 2, dp_count, "dp")
     attention_out = jnp.sum(chip_sums.astype(F32), axis=0)
     residual = resid[0].astype(F32) + attention_out
     normed = (
@@ -467,7 +541,9 @@
     to_rows = jnp.concatenate(
         [block[:local_rows].reshape(local_units, UNIT, width) for block in rows], axis=0
     ).transpose(1, 0, 2)
-    arrived, down_far, to_rows = lax.optimization_barrier((arrived, down_far, to_rows))
+    arrived, down_near, down_far, down_last, to_rows = lax.optimization_barrier(
+        (arrived, down_near, down_far, down_last, to_rows)
+    )
     beside = lax.ppermute(arrived, ("dp", "expert"), token_perm)
     dealt = lax.all_to_all(to_rows, "expert", split_axis=0, concat_axis=0, tiled=True)
 

time: 430 us -> 218 us (0.51)
  Pallas kernels: 203 us -> 14.7 us
  waiting for transfers between devices: 107 us -> 72.7 us
  blocking collectives: 0 us -> 28.7 us
  starting transfers between devices: 65.6 us -> 47.5 us
  local copies, waits for them, and re-layouts: 17.2 us -> 26.1 us
  matrix products: 24.6 us -> 18.4 us
    pallas_call x1, Pallas kernels: 197 us -> 3.59 us  [weight_slices(): pl.pallas_call(slice_kernel, out_shape=(halves, halves) + (part,) * (dp_c...]
    ppermute x9, waiting for transfers between devices: 44.5 us -> 5.61 us  [shift(): return lax.ppermute(x, axis, [((i + step) % size, i) for i in range(size)])]
    all_to_all x0 -> x1, blocking collectives: none -> 28.7 us  [to_heads(): lax.all_to_all(part, 'expert', split_axis=0, concat_axis=0, tiled=True)]
    all_to_all x1, waiting for transfers between devices: 10.3 us -> 31.7 us  [shards(): lax.all_to_all(outgoing, ('dp', 'expert'), split_axis=0, concat_axis=0, t...]
    ppermute x1, waiting for transfers between devices: 19.7 us -> 0.01 us  [shards(): up_came = lax.ppermute(up_sent, ('dp', 'expert'), weight_perm)]
    all_to_all x2 -> x1, starting transfers between devices: 24.7 us -> 10.8 us  [shards(): lax.all_to_all(pair_sums, 'expert', split_axis=0, concat_axis=0, tiled=Tr...]
    unnamed x27 -> x46, local copies, waits for them, and re-layouts: 3.32 us -> 14.3 us
    dot_general x5 -> x0, matrix products: 6.08 us -> none  [the longest x1 2.77 us: shards(): jnp.dot(projected, w_out, preferred_element_type=F32).astype(BF)]
  transfers between devices with their start and end apart: 20 -> 19, of which waited for: 15 -> 9; matrix products, arithmetic and copies ran while one was open for 8% -> 13% of each run, Pallas kernels for 46% -> 6%
where the time goes in v6:
time: 218 us; the launch traced here: 217 us
  waiting for transfers between devices  72.7 us (33%)
  starting transfers between devices  47.5 us (22%)
  blocking collectives  28.7 us (13%)
  local copies, waits for them, and re-layouts  26.1 us (12%)
  matrix products  18.4 us (8%)
  Pallas kernels  14.7 us (7%)
  other arithmetic  6.93 us (3%)
    all_to_all x1, waiting for transfers between devices, shards(): lax.all_to_all(outgoing, ('dp', 'expert'), split_axis=0, concat_axis=0, t...  31.7 us
    all_to_all x1, blocking collectives, to_heads(): lax.all_to_all(part, 'expert', split_axis=0, concat_axis=0, tiled=True)  28.7 us
    all_to_all x1, waiting for transfers between devices, shards(): lax.all_to_all(out.astype(BF).reshape(devices, capacity, piece), ('dp', '...  16.1 us
    unnamed x46, local copies, waits for them, and re-layouts  14.3 us
    all_to_all x1, waiting for transfers between devices, shards(): lax.all_to_all(pair_sums, 'expert', split_axis=0, concat_axis=0, tiled=Tr...  12 us
    all_to_all x1, starting transfers between devices, shards(): lax.all_to_all(pair_sums, 'expert', split_axis=0, concat_axis=0, tiled=Tr...  10.8 us
    all_to_all x1, starting transfers between devices, shards(): lax.all_to_all(out.astype(BF).reshape(devices, capacity, piece), ('dp', '...  9.66 us
    ppermute x9, starting transfers between devices, shift(): return lax.ppermute(x, axis, [((i + step) % size, i) for i in range(size)])  7.96 us
  transfers between devices with their start and end apart: 19, of which 9 were waited for; matrix products, arithmetic and copies ran while one was open for 13% of the time, Pallas kernels for 6%

profile of v6, /device:TPU:1, one launch (start us, length us, event | category | flops | bytes accessed | tf_op | source)
XLA Modules:
  0.0 216.8 jit_solution(8962757683168762570)
XLA Ops:
  1.5 1.4 collective-permute-start
  2.9 3.4 %collective-permute-done = bf16[64,576]{1,0:T(8,128)(2,1)S(1)} collective-permute-done((bf16[64,576]{1,0:T(8,128)(2,1)S(1)}, bf16[64,576]{1,0:T(8,128)(2,1)S(1)}, u32[]{:S(2)}, u32[]{:S(2)}) %collective-permute-start) | collective-permute-done | bytes 73760 | tf_op jit(solution)/shard_map/ppermute | solution.py:377
  6.3 1.0 pad_maximum_fusion.3.refs_1_
  7.3 2.5 %collective-permute-start.1 = (bf16[256,576]{1,0:T(8,128)(2,1)S(1)}, bf16[256,576]{1,0:T(8,128)(2,1)S(1)}, u32[]{:S(2)}, u32[]{:S(2)}) collective-permute-start(bf16[256,576]{1,0:T(8,128)(2,1)S(1)} %pad_maximum_fusion.3.refs_1_), channel_id=1, source_target_pairs={{32,0},{64,32},{96,64},{0,96},{33,1},{65,33},{97,65},{1,97},{34,2}... | collective-permute-start | bytes 884744 | tf_op jit(solution)/shard_map/ppermute | solution.py:44
  12.4 1.0 tables.1
  13.6 2.0 copy-done
  15.6 2.0 copy-done.1
  17.6 2.0 copy-done.3
  19.7 3.6 %weight_slices.1 = (bf16[2,1792,256]{2,1,0:T(8,128)(2,1)}, bf16[2,1792,256]{2,1,0:T(8,128)(2,1)}, bf16[256,1792]{1,0:T(8,128)(2,1)S(1)}, bf16[256,1792]{1,0:T(8,128)(2,1)S(1)}, bf16[256,1792]{1,0:T(8,128)(2,1)S(1)}) custom-call(s32[5]{0:T(128)S(1)} %stack.59.at_ref, bf16[1,7168,256]{2,1,0:T(8,128)(2,1)S(1)} %copy-done.1, bf16[1,7168,256]{2,1,0:T(8,128)(2,1)S(1)} %copy-done, ...), custom_call_target="tpu_custom_call" | custom-call | flops 1000 | bytes 4096 | tf_op jit(solution)/shard_map/weight_slices/pallas_call | solution.py:169
  23.3 0.9 copy-done.10
  24.2 1.0 copy-done.11
  25.2 0.9 copy-done.12
  26.1 2.1 collective-permute-start.4
  30.2 3.2 %copy-done.2 = bf16[1,96,64,576]{3,2,1,0:T(8,128)(2,1)S(1)} copy-done((bf16[1,96,64,576]{3,2,1,0:T(8,128)(2,1)S(1)}, bf16[1,96,64,576]{3,2,1,0:T(8,128)(2,1)}, u32[]{:S(2)}) %copy-start.2) | copy-done | bytes 7077912
  33.4 7.6 %attend.1 = (bf16[64,8,512]{2,1,0:T(8,128)(2,1)S(1)}, bf16[16,64,512]{2,1,0:T(8,128)(2,1)S(1)}) custom-call(s32[32,128]{1,0:T(8,128)S(1)} %get-tuple-element.80.refs_0_, bf16[256,576]{1,0:T(8,128)(2,1)S(1)} %pad_maximum_fusion.3.refs_1_, bf16[256,576]{1,0:T(8,128)(2,1)S(1)} %collective-permute-done.1.refs_2_, ...), custom_call_target="tpu_custom_call" | custom-call | flops 100000000 | bytes 4000000 | tf_op jit(solution)/shard_map/attend/pallas_call | solution.py:258
  41.1 28.7 %all_to_all.29 = bf16[64,8,512]{2,1,0:T(8,128)(2,1)S(1)} all-to-all(bf16[64,8,512]{2,1,0:T(8,128)(2,1)S(1)} %get-tuple-element.85), channel_id=1, replica_groups=mesh['dp'=4,'expert'=32] {'expert'}, dimensions={0} | all-to-all | bytes 1048576 | tf_op jit(solution)/shard_map/all_to_all | solution.py:451
  69.8 2.0 copy-done.4
  71.8 1.2 project.1
  73.1 2.8 %collective-permute-start.6 = (bf16[48,7168]{1,0:T(8,128)(2,1)S(1)}, bf16[48,7168]{1,0:T(8,128)(2,1)S(1)}, u32[]{:S(2)}, u32[]{:S(2)}) collective-permute-start(bf16[48,7168]{1,0:T(8,128)(2,1)S(1)} %get-tuple-element.96), channel_id=1, source_target_pairs={{0,1},{1,0},{2,3},{3,2},{4,5},{5,4},{6,7},{7,6},{8,9},{9,8},{10,11... | collective-permute-start | bytes 2064392 | tf_op jit(solution)/shard_map/ppermute | solution.py:493
  77.7 1.4 pair_sum.1
  79.1 10.8 %all-to-all-start.2 = ((bf16[16,3,7168]{2,1,0:T(4,128)(2,1)}), bf16[16,3,7168]{2,1,0:T(4,128)(2,1)S(1)}, u32[]{:S(2)}, u32[]{:S(2)}) async-start(bf16[16,3,7168]{2,1,0:T(4,128)(2,1)} %pair_sum.1), calls=%async_computation.2 | async-start | bytes 1835008 | tf_op jit(solution)/shard_map/all_to_all | solution.py:495
  90.2 2.1 collective-permute-start.7
  93.0 12.0 %all-to-all-done.2 = bf16[16,3,7168]{2,1,0:T(4,128)(2,1)S(1)} async-done(((bf16[16,3,7168]{2,1,0:T(4,128)(2,1)}), bf16[16,3,7168]{2,1,0:T(4,128)(2,1)S(1)}, u32[]{:S(2)}, u32[]{:S(2)}) %all-to-all-start.2) | async-done | bytes 688160 | tf_op jit(solution)/shard_map/all_to_all | solution.py:495
  106.9 1.3 reshape.262
  108.2 6.1 %all-to-all-start.3 = ((bf16[128,2,1792]{2,1,0:T(2,128)(2,1)}), bf16[128,2,1792]{2,1,0:T(2,128)(2,1)S(1)}, u32[]{:S(2)}, u32[]{:S(2)}) async-start(bf16[128,2,1792]{2,1,0:T(2,128)(2,1)} %reshape.262), calls=%async_computation.3 | async-start | bytes 1835008 | tf_op jit(solution)/shard_map/all_to_all | solution.py:536
  114.5 2.2 dynamic-slice_bitcast_fusion
  117.2 1.5 maximum_bitcast_fusion
  118.7 31.7 %all-to-all-done.3 = bf16[128,2,1792]{2,1,0:T(2,128)(2,1)S(1)} async-done(((bf16[128,2,1792]{2,1,0:T(2,128)(2,1)}), bf16[128,2,1792]{2,1,0:T(2,128)(2,1)S(1)}, u32[]{:S(2)}, u32[]{:S(2)}) %all-to-all-start.3) | async-done | bytes 917536 | tf_op jit(solution)/shard_map/all_to_all | solution.py:536
  150.9 1.6 fusion.39
  152.5 4.7 %all-to-all-start.4 = ((bf16[32,24,576]{2,1,0:T(8,128)(2,1)}), bf16[32,24,576]{2,1,0:T(8,128)(2,1)S(1)}, u32[]{:S(2)}, u32[]{:S(2)}) async-start(bf16[32,24,576]{2,1,0:T(8,128)(2,1)} %maximum_bitcast_fusion), calls=%async_computation.4 | async-start | bytes 1966080 | tf_op jit(solution)/shard_map/all_to_all | solution.py:548
  157.2 1.6 fusion.41
  158.8 1.6 fusion.43
  160.4 1.6 fusion.45
  162.0 1.4 collective-permute-done.10
  163.4 1.6 fusion.35
  165.0 1.6 fusion.33
  166.7 1.1 collective-permute-start.11
  167.9 1.6 fusion.31
  169.5 1.6 fusion.37
  171.1 2.5 %collective-permute-done.11 = bf16[256,512]{1,0:T(8,128)(2,1)S(1)} collective-permute-done((bf16[256,512]{1,0:T(8,128)(2,1)S(1)}, bf16[256,512]{1,0:T(8,128)(2,1)S(1)}, u32[]{:S(2)}, u32[]{:S(2)}) %collective-permute-start.11) | collective-permute-done | bytes 262176 | tf_op jit(solution)/shard_map/ppermute | solution.py:559
  176.1 1.5 collective-permute-done.12
  177.6 2.4 %collective-permute-done.13 = bf16[256,256]{1,0:T(8,128)(2,1)S(1)} collective-permute-done((bf16[256,256]{1,0:T(8,128)(2,1)S(1)}, bf16[256,256]{1,0:T(8,128)(2,1)S(1)}, u32[]{:S(2)}, u32[]{:S(2)}) %collective-permute-start.13) | collective-permute-done | bytes 131104 | tf_op jit(solution)/shard_map/ppermute | solution.py:44
  180.0 1.8 collective-permute-done.14
  182.6 3.0 %fusion.24 = bf16[256,1792]{1,0:T(8,128)(2,1)S(1)} fusion(bf16[256,1024]{1,0:T(8,128)(2,1)} %pad_maximum_fusion.2, bf16[256,1792]{1,0:T(8,128)(2,1)} %collective-permute-done.9, bf16[256,1792]{1,0:T(8,128)(2,1)} %collective-permute-done.8, bf16[256,1792]{1,0:T(8,128)(2,1)} %collective-permute-done.7, bf16[256,1792]{1,0:T(8,128)(2,1)S(1)} %copy-done.13), kind=kOutput, calls=%fused_computation.44 | convolution fusion | flops 954662912 | bytes 5111808 | tf_op jit(solution)/shard_map/dot_general | solution.py:569
  185.6 1.3 reshape.271
  186.9 9.7 %all-to-all-start.5 = ((bf16[128,2,1792]{2,1,0:T(2,128)(2,1)}), bf16[128,2,1792]{2,1,0:T(2,128)(2,1)S(1)}, u32[]{:S(2)}, u32[]{:S(2)}) async-start(bf16[128,2,1792]{2,1,0:T(2,128)(2,1)} %reshape.271), calls=%async_computation.5 | async-start | bytes 1835008 | tf_op jit(solution)/shard_map/all_to_all | solution.py:570
  198.2 16.1 %all-to-all-done.5 = bf16[128,2,1792]{2,1,0:T(2,128)(2,1)S(1)} async-done(((bf16[128,2,1792]{2,1,0:T(2,128)(2,1)}), bf16[128,2,1792]{2,1,0:T(2,128)(2,1)S(1)}, u32[]{:S(2)}, u32[]{:S(2)}) %all-to-all-start.5) | async-done | bytes 917536 | tf_op jit(solution)/shard_map/all_to_all | solution.py:570
  215.7 1.2 fusion.15
  (121 shorter events, 17.2 us)
Async XLA Ops:
  1.5 4.8 %collective-permute-start = (bf16[64,576]{1,0:T(8,128)(2,1)S(1)}, bf16[64,576]{1,0:T(8,128)(2,1)S(1)}, u32[]{:S(2)}, u32[]{:S(2)}) collective-permute-start(bf16[64,576]{1,0:T(8,128)(2,1)S(1)} %slice.110), channel_id=1, source_target_pairs={{1,0},{2,1},{3,2},{4,3},{5,4},{6,5},{7,6},{8,7},{9,8},{10,9},{11,1... | collective-permute-start | bytes 221192 | tf_op jit(solution)/shard_map/ppermute | solution.py:377
  7.3 18.8 %collective-permute-start.1 = (bf16[256,576]{1,0:T(8,128)(2,1)S(1)}, bf16[256,576]{1,0:T(8,128)(2,1)S(1)}, u32[]{:S(2)}, u32[]{:S(2)}) collective-permute-start(bf16[256,576]{1,0:T(8,128)(2,1)S(1)} %pad_maximum_fusion.3.refs_1_), channel_id=1, source_target_pairs={{32,0},{64,32},{96,64},{0,96},{33,1},{65,33},{97,65},{1,97},{34,2}... | collective-permute-start | bytes 884744 | tf_op jit(solution)/shard_map/ppermute | solution.py:44
  9.9 16.3 %collective-permute-start.2 = (bf16[256,576]{1,0:T(8,128)(2,1)S(1)}, bf16[256,576]{1,0:T(8,128)(2,1)S(1)}, u32[]{:S(2)}, u32[]{:S(2)}) collective-permute-start(bf16[256,576]{1,0:T(8,128)(2,1)S(1)} %pad_maximum_fusion.3.refs_1_), channel_id=1, source_target_pairs={{64,0},{96,32},{0,64},{32,96},{65,1},{97,33},{1,65},{33,97},{66,2}... | collective-permute-start | bytes 884744 | tf_op jit(solution)/shard_map/ppermute | solution.py:44
  10.4 15.8 %collective-permute-start.3 = (bf16[256,576]{1,0:T(8,128)(2,1)S(1)}, bf16[256,576]{1,0:T(8,128)(2,1)S(1)}, u32[]{:S(2)}, u32[]{:S(2)}) collective-permute-start(bf16[256,576]{1,0:T(8,128)(2,1)S(1)} %pad_maximum_fusion.3.refs_1_), channel_id=1, source_target_pairs={{96,0},{0,32},{32,64},{64,96},{97,1},{1,33},{33,65},{65,97},{98,2}... | collective-permute-start | bytes 884744 | tf_op jit(solution)/shard_map/ppermute | solution.py:44
  13.6 2.0 copy-start
  15.6 2.0 copy-start.1
  17.6 2.0 copy-start.3
  19.7 10.4 %copy-start.16 = (s32[384]{0:T(512)S(1)}, s32[384]{0:T(512)}, u32[]{:S(2)}) copy-start(s32[384]{0:T(512)} %param.23) | copy-start | bytes 4612
  19.7 10.5 %copy-start.6 = (bf16[1,96,576]{2,1,0:T(8,128)(2,1)S(1)}, bf16[1,96,576]{2,1,0:T(8,128)(2,1)}, u32[]{:S(2)}) copy-start(bf16[1,96,576]{2,1,0:T(8,128)(2,1)} %param.20) | copy-start | bytes 331780
  19.7 10.5 %copy-start.7 = (f32[128,32]{1,0:T(8,128)S(1)}, f32[128,32]{1,0:T(8,128)}, u32[]{:S(2)}) copy-start(f32[128,32]{1,0:T(8,128)} %constant.223.clone.refs_5_) | copy-start | bytes 49156
  19.7 10.5 %copy-start.8 = (f32[128,32]{1,0:T(8,128)S(1)}, f32[128,32]{1,0:T(8,128)}, u32[]{:S(2)}) copy-start(f32[128,32]{1,0:T(8,128)} %constant.224.clone.refs_6_) | copy-start | bytes 49156
  19.7 10.5 %copy-start.9 = (f32[512]{0:T(512)S(1)}, f32[512]{0:T(512)}, u32[]{:S(2)}) copy-start(f32[512]{0:T(512)} %param.21) | copy-start | bytes 6148
  23.3 0.9 copy-start.10
  24.2 1.0 copy-start.11
  25.2 0.9 copy-start.12
  26.1 43.6 %collective-permute-start.4 = (bf16[2,1792,256]{2,1,0:T(8,128)(2,1)}, bf16[2,1792,256]{2,1,0:T(8,128)(2,1)}, u32[]{:S(2)}, u32[]{:S(2)}) collective-permute-start(bf16[2,1792,256]{2,1,0:T(8,128)(2,1)} %get-tuple-element.86), channel_id=1, source_target_pairs={{0,32},{1,97},{2,34},{3,99},{4,36},{5,101},{6,38},{7,103},{8,40},{... | collective-permute-start | bytes 5505032 | tf_op jit(solution)/shard_map/ppermute | solution.py:434
  28.3 44.8 %collective-permute-start.5 = (bf16[2,1792,256]{2,1,0:T(8,128)(2,1)}, bf16[2,1792,256]{2,1,0:T(8,128)(2,1)}, u32[]{:S(2)}, u32[]{:S(2)}) collective-permute-start(bf16[2,1792,256]{2,1,0:T(8,128)(2,1)} %get-tuple-element.91), channel_id=1, source_target_pairs={{0,32},{1,97},{2,34},{3,99},{4,36},{5,101},{6,38},{7,103},{8,40},{... | collective-permute-start | bytes 5505032 | tf_op jit(solution)/shard_map/ppermute | solution.py:435
  30.2 3.2 %copy-start.2 = (bf16[1,96,64,576]{3,2,1,0:T(8,128)(2,1)S(1)}, bf16[1,96,64,576]{3,2,1,0:T(8,128)(2,1)}, u32[]{:S(2)}) copy-start(bf16[1,96,64,576]{3,2,1,0:T(8,128)(2,1)} %param.24) | copy-start | bytes 21233668
  41.0 28.8 %copy-start.5 = (bf16[2,512,128]{2,1,0:T(8,128)(2,1)S(1)}, bf16[2,512,128]{2,1,0:T(8,128)(2,1)}, u32[]{:S(2)}) copy-start(bf16[2,512,128]{2,1,0:T(8,128)(2,1)} %uv_ref.1) | copy-start | bytes 786436
  41.0 34.8 %copy-start.20 = (s32[1,3,8]{2,0,1:T(1,128)S(1)}, s32[1,3,8]{2,0,1:T(1,128)}, u32[]{:S(2)}) copy-start(s32[1,3,8]{2,0,1:T(1,128)} %param.29) | copy-start | bytes 292
  41.1 36.6 %copy-start.21 = (f32[1,3,8]{2,0,1:T(1,128)S(1)}, f32[1,3,8]{2,0,1:T(1,128)}, u32[]{:S(2)}) copy-start(f32[1,3,8]{2,0,1:T(1,128)} %param.30) | copy-start | bytes 292
  41.1 36.6 %copy-start.17 = (s32[384]{0:T(512)S(1)}, s32[384]{0:T(512)}, u32[]{:S(2)}) copy-start(s32[384]{0:T(512)} %param.22) | copy-start | bytes 4612
  69.8 2.0 copy-start.4
  73.0 32.3 %copy-start.14 = (bf16[1,3,7168]{2,1,0:T(4,128)(2,1)S(1)}, bf16[1,3,7168]{2,1,0:T(4,128)(2,1)}, u32[]{:S(2)}) copy-start(bf16[1,3,7168]{2,1,0:T(4,128)(2,1)} %param.27) | copy-start | bytes 129028
  73.0 32.5 %copy-start.15 = (f32[7168]{0:T(1024)S(1)}, f32[7168]{0:T(1024)}, u32[]{:S(2)}) copy-start(f32[7168]{0:T(1024)} %param.28) | copy-start | bytes 86020
  73.1 4.6 %collective-permute-start.6 = (bf16[48,7168]{1,0:T(8,128)(2,1)S(1)}, bf16[48,7168]{1,0:T(8,128)(2,1)S(1)}, u32[]{:S(2)}, u32[]{:S(2)}) collective-permute-start(bf16[48,7168]{1,0:T(8,128)(2,1)S(1)} %get-tuple-element.96), channel_id=1, source_target_pairs={{0,1},{1,0},{2,3},{3,2},{4,5},{5,4},{6,7},{7,6},{8,9},{9,8},{10,11... | collective-permute-start | bytes 2064392 | tf_op jit(solution)/shard_map/ppermute | solution.py:493
  77.7 12.5 %copy-start.18 = (pred[64,3]{0,1:T(4,128)(4,1)S(1)}, pred[64,3]{0,1:T(4,128)(4,1)}, u32[]{:S(2)}) copy-start(pred[64,3]{0,1:T(4,128)(4,1)} %and.182) | copy-start | bytes 580
  77.7 12.5 %copy-start.19 = (s32[64]{0:T(128)S(1)}, s32[64]{0:T(128)}, u32[]{:S(2)}) copy-start(s32[64]{0:T(128)} %eq.160) | copy-start | bytes 772
  79.1 25.9 %all-to-all-start.2 = ((bf16[16,3,7168]{2,1,0:T(4,128)(2,1)}), bf16[16,3,7168]{2,1,0:T(4,128)(2,1)S(1)}, u32[]{:S(2)}, u32[]{:S(2)}) async-start(bf16[16,3,7168]{2,1,0:T(4,128)(2,1)} %pair_sum.1), calls=%async_computation.2 | async-start | bytes 1835008 | tf_op jit(solution)/shard_map/all_to_all | solution.py:495
  90.2 60.5 %collective-permute-start.7 = (bf16[256,1792]{1,0:T(8,128)(2,1)}, bf16[256,1792]{1,0:T(8,128)(2,1)}, u32[]{:S(2)}, u32[]{:S(2)}) collective-permute-start(bf16[256,1792]{1,0:T(8,128)(2,1)} %copy-done.12), channel_id=1, source_target_pairs={{32,0},{64,32},{96,64},{0,96},{33,1},{65,33},{97,65},{1,97},{34,2}... | collective-permute-start | bytes 2752520 | tf_op jit(solution)/shard_map/ppermute | solution.py:44
  92.3 58.5 %collective-permute-start.8 = (bf16[256,1792]{1,0:T(8,128)(2,1)}, bf16[256,1792]{1,0:T(8,128)(2,1)}, u32[]{:S(2)}, u32[]{:S(2)}) collective-permute-start(bf16[256,1792]{1,0:T(8,128)(2,1)} %copy-done.11), channel_id=1, source_target_pairs={{64,0},{96,32},{0,64},{32,96},{65,1},{97,33},{1,65},{33,97},{66,2}... | collective-permute-start | bytes 2752520 | tf_op jit(solution)/shard_map/ppermute | solution.py:44
  92.9 57.9 %collective-permute-start.9 = (bf16[256,1792]{1,0:T(8,128)(2,1)}, bf16[256,1792]{1,0:T(8,128)(2,1)}, u32[]{:S(2)}, u32[]{:S(2)}) collective-permute-start(bf16[256,1792]{1,0:T(8,128)(2,1)} %copy-done.10), channel_id=1, source_target_pairs={{96,0},{0,32},{32,64},{64,96},{97,1},{1,33},{33,65},{65,97},{98,2}... | collective-permute-start | bytes 2752520 | tf_op jit(solution)/shard_map/ppermute | solution.py:44
  108.2 42.2 %all-to-all-start.3 = ((bf16[128,2,1792]{2,1,0:T(2,128)(2,1)}), bf16[128,2,1792]{2,1,0:T(2,128)(2,1)S(1)}, u32[]{:S(2)}, u32[]{:S(2)}) async-start(bf16[128,2,1792]{2,1,0:T(2,128)(2,1)} %reshape.262), calls=%async_computation.3 | async-start | bytes 1835008 | tf_op jit(solution)/shard_map/all_to_all | solution.py:536
  150.8 12.6 %collective-permute-start.10 = (bf16[256,1792]{1,0:T(8,128)(2,1)S(1)}, bf16[256,1792]{1,0:T(8,128)(2,1)S(1)}, u32[]{:S(2)}, u32[]{:S(2)}) collective-permute-start(bf16[256,1792]{1,0:T(8,128)(2,1)S(1)} %reshape.263), channel_id=1, source_target_pairs={{0,96},{1,33},{2,98},{3,35},{4,100},{5,37},{6,102},{7,39},{8,104},... | collective-permute-start | bytes 2752520 | tf_op jit(solution)/shard_map/ppermute | solution.py:547
  152.5 30.1 %all-to-all-start.4 = ((bf16[32,24,576]{2,1,0:T(8,128)(2,1)}), bf16[32,24,576]{2,1,0:T(8,128)(2,1)S(1)}, u32[]{:S(2)}, u32[]{:S(2)}) async-start(bf16[32,24,576]{2,1,0:T(8,128)(2,1)} %maximum_bitcast_fusion), calls=%async_computation.4 | async-start | bytes 1966080 | tf_op jit(solution)/shard_map/all_to_all | solution.py:548
  166.7 15.9 %copy-start.13 = (bf16[256,1792]{1,0:T(8,128)(2,1)S(1)}, bf16[256,1792]{1,0:T(8,128)(2,1)}, u32[]{:S(2)}) copy-start(bf16[256,1792]{1,0:T(8,128)(2,1)} %dynamic-slice_bitcast_fusion) | copy-start | bytes 2752516
  166.7 6.8 %collective-permute-start.11 = (bf16[256,512]{1,0:T(8,128)(2,1)S(1)}, bf16[256,512]{1,0:T(8,128)(2,1)S(1)}, u32[]{:S(2)}, u32[]{:S(2)}) collective-permute-start(bf16[256,512]{1,0:T(8,128)(2,1)S(1)} %pad_maximum_fusion.4), channel_id=1, source_target_pairs={{0,32},{1,97},{2,34},{3,99},{4,36},{5,101},{6,38},{7,103},{8,40},{... | collective-permute-start | bytes 786440 | tf_op jit(solution)/shard_map/ppermute | solution.py:559
  173.7 3.9 %collective-permute-start.12 = (bf16[256,256]{1,0:T(8,128)(2,1)S(1)}, bf16[256,256]{1,0:T(8,128)(2,1)S(1)}, u32[]{:S(2)}, u32[]{:S(2)}) collective-permute-start(bf16[256,256]{1,0:T(8,128)(2,1)S(1)} %fusion.62), channel_id=1, source_target_pairs={{32,0},{64,32},{96,64},{0,96},{33,1},{65,33},{97,65},{1,97},{34,2}... | collective-permute-start | bytes 393224 | tf_op jit(solution)/shard_map/ppermute | solution.py:44
  174.6 5.4 %collective-permute-start.13 = (bf16[256,256]{1,0:T(8,128)(2,1)S(1)}, bf16[256,256]{1,0:T(8,128)(2,1)S(1)}, u32[]{:S(2)}, u32[]{:S(2)}) collective-permute-start(bf16[256,256]{1,0:T(8,128)(2,1)S(1)} %fusion.62), channel_id=1, source_target_pairs={{64,0},{96,32},{0,64},{32,96},{65,1},{97,33},{1,65},{33,97},{66,2}... | collective-permute-start | bytes 393224 | tf_op jit(solution)/shard_map/ppermute | solution.py:44
  174.6 7.2 %collective-permute-start.14 = (bf16[256,256]{1,0:T(8,128)(2,1)S(1)}, bf16[256,256]{1,0:T(8,128)(2,1)S(1)}, u32[]{:S(2)}, u32[]{:S(2)}) collective-permute-start(bf16[256,256]{1,0:T(8,128)(2,1)S(1)} %fusion.62), channel_id=1, source_target_pairs={{96,0},{0,32},{32,64},{64,96},{97,1},{1,33},{33,65},{65,97},{98,2}... | collective-permute-start | bytes 393224 | tf_op jit(solution)/shard_map/ppermute | solution.py:44
  186.9 27.4 %all-to-all-start.5 = ((bf16[128,2,1792]{2,1,0:T(2,128)(2,1)}), bf16[128,2,1792]{2,1,0:T(2,128)(2,1)S(1)}, u32[]{:S(2)}, u32[]{:S(2)}) async-start(bf16[128,2,1792]{2,1,0:T(2,128)(2,1)} %reshape.271), calls=%async_computation.5 | async-start | bytes 1835008 | tf_op jit(solution)/shard_map/all_to_all | solution.py:570

commit v7 on v6

--- a/solution.py
+++ b/solution.py
@@ -10,6 +10,7 @@
 UNIT = 32
 MOST = 3
 SLOTS = 8
+VMEM = 58 * 1024 * 1024
 
 eps = 1e-06
 theta = 10000.0
@@ -97,7 +98,9 @@
     number = jnp.sum(jnp.where(here, 1.0, 0.0), axis=1, keepdims=True)
     lane = lax.broadcasted_iota(I32, slots_ref.shape, 1)
     packed = jnp.zeros(slots_ref.shape, F32)
-    for i, value in enumerate((pick(place), pick(units), pick(group_rank), near_offset, number)):
+    wraps = jnp.where(jnp.full((1, 1), column, I32) == columns - 1, 1.0, 0.0)
+    values = (pick(place), pick(units), pick(group_rank), near_offset, number, wraps)
+    for i, value in enumerate(values):
         packed = jnp.where(lane == i, value, packed)
     slots_ref[...] = packed.astype(I32)
     rows_ref[...] = jnp.concatenate(
@@ -172,7 +175,7 @@
         in_specs=[pl.BlockSpec(memory_space=pltpu.SMEM)] + [away] * 3,
         out_specs=(whole,) * (dp_count + 1),
         scratch_shapes=[pltpu.SemaphoreType.DMA((dp_count + 3,))],
-        compiler_params=pltpu.CompilerParams(vmem_limit_bytes=32 * 1024 * 1024),
+        compiler_params=pltpu.CompilerParams(vmem_limit_bytes=VMEM),
         cost_estimate=pl.CostEstimate(flops=1000, bytes_accessed=4096, transcendentals=0),
         name="weight_slices",
     )(at, w_gate, w_up, w_down)
@@ -194,14 +197,18 @@
         fetch(slot).start()
 
     gain = gain_ref[...]
-    unit = 0
-    for ref in rows_in:
+    local_rows = rows_in[0].shape[0] - (MOST - 1) * UNIT
+    near_units = rows_in[0].shape[0] // UNIT
+    for block, ref in enumerate(rows_in):
+        before = near_units * ((block + blocks - 1) % blocks - block)
         for first in range(0, ref.shape[0], UNIT):
+            unit = block * near_units + first // UNIT
+            if first >= local_rows:
+                unit = unit + slots_ref[0, 5] * before
             span = pl.ds(pl.multiple_of(slots_ref[unit, 3] * UNIT, UNIT), UNIT)
-            keys[unit * UNIT : (unit + 1) * UNIT, :] = norm_rotate(
+            keys[pl.ds(pl.multiple_of(unit * UNIT, UNIT), UNIT), :] = norm_rotate(
                 ref[first : first + UNIT, :], cos_ref[span, :], sin_ref[span, :], gain
             )
-            unit += 1
     fresh[...] = new_ref[...].astype(F32)
 
     heads = out_ref.shape[0]
@@ -272,7 +279,7 @@
             pltpu.VMEM((SLOTS, heads, LAT), F32),
             pltpu.SemaphoreType.DMA((most_slots,)),
         ],
-        compiler_params=pltpu.CompilerParams(vmem_limit_bytes=32 * 1024 * 1024),
+        compiler_params=pltpu.CompilerParams(vmem_limit_bytes=VMEM),
         cost_estimate=pl.CostEstimate(
             flops=10**8, bytes_accessed=4 * 10**6, transcendentals=10**5
         ),
@@ -280,7 +287,17 @@
     )(slots, *rows, cosine, sine, gain, new_rows, queries)
 
 
-def project_kernel(cells_ref, came_ref, more_ref, uv_ref, weight_ref, mine_ref, other_ref):
+def project_kernel(
+    cells_ref, came_ref, more_ref, uv_ref, weight_ref, mine_ref, other_ref, weight, sems
+):
+    step = weight.shape[1] // 4
+    spans = [slice(i * step, (i + 1) * step) for i in range(4)]
+    copies = [
+        pltpu.make_async_copy(weight_ref.at[:, span], weight.at[:, span], sems.at[i])
+        for i, span in enumerate(spans)
+    ]
+    for copy in copies:
+        copy.start()
     requests = cells_ref.shape[0]
     sources, heads, slots, _ = came_ref.shape
     cells = sources * slots
@@ -295,10 +312,9 @@
         )
     projected = jnp.concatenate(projected, axis=1)
     keep = mine_ref.shape[0]
-    step = weight_ref.shape[1] // 4
-    for first in range(0, weight_ref.shape[1], step):
-        span = slice(first, first + step)
-        sums = jnp.dot(projected, weight_ref[:, span], preferred_element_type=F32).astype(BF)
+    for span, copy in zip(spans, copies):
+        copy.wait()
+        sums = jnp.dot(projected, weight[:, span], preferred_element_type=F32).astype(BF)
         mine_ref[:, span] = sums[:keep]
         other_ref[:, span] = sums[keep:]
 
@@ -309,8 +325,9 @@
     return pl.pallas_call(
         project_kernel,
         out_shape=(half, half),
-        in_specs=[whole] * 5,
+        in_specs=[whole] * 4 + [pl.BlockSpec(memory_space=pltpu.HBM)],
         out_specs=(whole, whole),
+        scratch_shapes=[pltpu.VMEM(w_out.shape, BF), pltpu.SemaphoreType.DMA((4,))],
         compiler_params=pltpu.CompilerParams(vmem_limit_bytes=32 * 1024 * 1024),
         cost_estimate=pl.CostEstimate(
             flops=4 * 10**8, bytes_accessed=6 * 10**6, transcendentals=0
@@ -375,9 +392,7 @@
 
     border = (MOST - 1) * UNIT
     next_rows = lax.ppermute(
-        latent_rows[:border],
-        ("dp", "expert"),
-        [((i + 1) % devices, i) for i in range(devices)],
+        latent_rows[:border], "expert", [((i + 1) % columns, i) for i in range(columns)]
     )
     near_rows = jnp.concatenate([latent_rows, next_rows], axis=0)
     near_rows, late_group = lax.optimization_barrier((near_rows, group))
@@ -483,11 +498,10 @@
     by_head = to_heads(attended)
     by_head, gate_came = lax.optimization_barrier((by_head, gate_came))
     mine, other = project(cells, by_head, more, w_uv, w_out)
-    mine, other, up_came, down_near, down_far, down_last = lax.optimization_barrier(
-        (mine, other, up_came, down_near, down_far, down_last)
+    mine, other, down_near, down_last = lax.optimization_barrier(
+        (mine, other, down_near, down_last)
     )
     down_near = shift(down_near, 1, dp_count, "dp")
-    down_far = shift(down_far, 2, dp_count, "dp")
     down_last = shift(down_last, 3, dp_count, "dp")
 
     other = lax.ppermute(other, "expert", [(i, i ^ 1) for i in range(columns)])
@@ -500,6 +514,8 @@
         tiled=True,
         axis_index_groups=[[2 * i + c for i in range(chips)] for c in range(2)],
     )
+    chip_sums, up_came, down_far = lax.optimization_barrier((chip_sums, up_came, down_far))
+    down_far = shift(down_far, 2, dp_count, "dp")
     attention_out = jnp.sum(chip_sums.astype(F32), axis=0)
     residual = resid[0].astype(F32) + attention_out
     normed = (

time: 218 us -> 197 us (0.904)
  blocking collectives: 28.7 us -> 0 us
  local copies, waits for them, and re-layouts: 26.1 us -> 13.3 us
  waiting for transfers between devices: 72.7 us -> 81.4 us
  starting transfers between devices: 47.5 us -> 55.1 us
  Pallas kernels: 14.7 us -> 19.3 us
    all_to_all x1 -> x0, blocking collectives: 28.7 us -> none  [to_heads(): lax.all_to_all(part, 'expert', split_axis=0, concat_axis=0, tiled=True)]
    ppermute x9, waiting for transfers between devices: 5.61 us -> 27.4 us  [shift(): return lax.ppermute(x, axis, [((i + step) % size, i) for i in range(size)])]
    all_to_all x1, waiting for transfers between devices: 31.7 us -> 10.4 us  [shards(): lax.all_to_all(outgoing, ('dp', 'expert'), split_axis=0, concat_axis=0, t...]
    unnamed x46 -> x30, local copies, waits for them, and re-layouts: 14.3 us -> 2.11 us
    all_to_all x0 -> x1, starting transfers between devices: none -> 10.4 us  [to_heads(): lax.all_to_all(part, 'expert', split_axis=0, concat_axis=0, tiled=True)]
    all_to_all x0 -> x1, waiting for transfers between devices: none -> 9.15 us  [to_heads(): lax.all_to_all(part, 'expert', split_axis=0, concat_axis=0, tiled=True)]
    all_to_all x1, starting transfers between devices: 10.8 us -> 3.63 us  [shards(): lax.all_to_all(pair_sums, 'expert', split_axis=0, concat_axis=0, tiled=Tr...]
    all_to_all x1, starting transfers between devices: 4.74 us -> 9.11 us  [shards(): lax.all_to_all(to_rows, 'expert', split_axis=0, concat_axis=0, tiled=True)]
  transfers between devices with their start and end apart: 19 -> 20, of which waited for: 9 -> 12; matrix products, arithmetic and copies ran while one was open for 13% -> 14% of each run, Pallas kernels for 6% -> 10%
where the time goes in v7:
time: 197 us; the launch traced here: 196 us
  waiting for transfers between devices  81.4 us (41%)
  starting transfers between devices  55.1 us (28%)
  Pallas kernels  19.3 us (10%)
  matrix products  18.5 us (9%)
  local copies, waits for them, and re-layouts  13.3 us (7%)
  other arithmetic  6.2 us (3%)
  between operations  2.02 us (1%)
    ppermute x9, waiting for transfers between devices, shift(): return lax.ppermute(x, axis, [((i + step) % size, i) for i in range(size)])  27.4 us
    all_to_all x1, waiting for transfers between devices, shards(): lax.all_to_all(out.astype(BF).reshape(devices, capacity, piece), ('dp', '...  16.1 us
    all_to_all x1, waiting for transfers between devices, shards(): lax.all_to_all(pair_sums, 'expert', split_axis=0, concat_axis=0, tiled=Tr...  12.5 us
    ppermute x9, starting transfers between devices, shift(): return lax.ppermute(x, axis, [((i + step) % size, i) for i in range(size)])  11.6 us
    all_to_all x1, waiting for transfers between devices, shards(): lax.all_to_all(outgoing, ('dp', 'expert'), split_axis=0, concat_axis=0, t...  10.4 us
    all_to_all x1, starting transfers between devices, to_heads(): lax.all_to_all(part, 'expert', split_axis=0, concat_axis=0, tiled=True)  10.4 us
    all_to_all x1, waiting for transfers between devices, to_heads(): lax.all_to_all(part, 'expert', split_axis=0, concat_axis=0, tiled=True)  9.15 us
    all_to_all x1, starting transfers between devices, shards(): lax.all_to_all(to_rows, 'expert', split_axis=0, concat_axis=0, tiled=True)  9.11 us
  transfers between devices with their start and end apart: 20, of which 12 were waited for; matrix products, arithmetic and copies ran while one was open for 14% of the time, Pallas kernels for 10%

profile of v7, /device:TPU:1, one launch (start us, length us, event | category | flops | bytes accessed | tf_op | source)
XLA Modules:
  0.0 195.9 jit_solution(21741472217802990)
XLA Ops:
  0.6 0.9 slice.110
  1.5 1.4 collective-permute-start
  2.9 3.4 %collective-permute-done = bf16[64,576]{1,0:T(8,128)(2,1)S(1)} collective-permute-done((bf16[64,576]{1,0:T(8,128)(2,1)S(1)}, bf16[64,576]{1,0:T(8,128)(2,1)S(1)}, u32[]{:S(2)}, u32[]{:S(2)}) %collective-permute-start) | collective-permute-done | bytes 73760 | tf_op jit(solution)/shard_map/ppermute | solution.py:394
  6.3 1.0 pad_maximum_fusion.3.refs_1_
  7.3 2.5 %collective-permute-start.1 = (bf16[256,576]{1,0:T(8,128)(2,1)S(1)}, bf16[256,576]{1,0:T(8,128)(2,1)S(1)}, u32[]{:S(2)}, u32[]{:S(2)}) collective-permute-start(bf16[256,576]{1,0:T(8,128)(2,1)S(1)} %pad_maximum_fusion.3.refs_1_), channel_id=1, source_target_pairs={{32,0},{64,32},{96,64},{0,96},{33,1},{65,33},{97,65},{1,97},{34,2}... | collective-permute-start | bytes 884744 | tf_op jit(solution)/shard_map/ppermute | solution.py:45
  12.4 1.0 tables.1
  14.2 6.3 %weight_slices.1 = (bf16[2,1792,256]{2,1,0:T(8,128)(2,1)}, bf16[2,1792,256]{2,1,0:T(8,128)(2,1)}, bf16[256,1792]{1,0:T(8,128)(2,1)}, bf16[256,1792]{1,0:T(8,128)(2,1)}, bf16[256,1792]{1,0:T(8,128)(2,1)}) custom-call(s32[5]{0:T(128)} %stack.59.at_ref, bf16[1,7168,256]{2,1,0:T(8,128)(2,1)} %gate_ref.1, bf16[1,7168,256]{2,1,0:T(8,128)(2,1)} %up_ref.1, ...), custom_call_target="tpu_custom_call" | custom-call | flops 1000 | bytes 4096 | tf_op jit(solution)/shard_map/weight_slices/pallas_call | solution.py:172
  20.6 5.3 %collective-permute-done.3.refs_4_ = bf16[256,576]{1,0:T(8,128)(2,1)S(1)} collective-permute-done((bf16[256,576]{1,0:T(8,128)(2,1)S(1)}, bf16[256,576]{1,0:T(8,128)(2,1)S(1)}, u32[]{:S(2)}, u32[]{:S(2)}) %collective-permute-start.3) | collective-permute-done | bytes 294944 | tf_op jit(solution)/shard_map/ppermute | solution.py:45
  27.2 8.5 %attend.1 = (bf16[64,8,512]{2,1,0:T(8,128)(2,1)}, bf16[16,64,512]{2,1,0:T(8,128)(2,1)S(1)}) custom-call(s32[32,128]{1,0:T(8,128)S(1)} %get-tuple-element.81.refs_0_, bf16[256,576]{1,0:T(8,128)(2,1)} %copy-done.2, bf16[256,576]{1,0:T(8,128)(2,1)} %copy-done.4, bf16[256,576]{1,0:T(8,128)(2,1)} %copy-done.5, bf16[256,576]{1,0:T(8,128)(2,1)} %copy-done.6, ...), custom_call_target="tpu_custom_call" | custom-call | flops 100000000 | bytes 4000000 | tf_op jit(solution)/shard_map/attend/pallas_call | solution.py:265
  35.9 10.4 %all-to-all-start.1 = ((bf16[64,8,512]{2,1,0:T(8,128)(2,1)}), bf16[64,8,512]{2,1,0:T(8,128)(2,1)S(1)}, u32[]{:S(2)}, u32[]{:S(2)}) async-start(bf16[64,8,512]{2,1,0:T(8,128)(2,1)} %get-tuple-element.86), calls=%async_computation.1 | async-start | bytes 1048576 | tf_op jit(solution)/shard_map/all_to_all | solution.py:466
  46.3 2.4 %collective-permute-start.6 = (bf16[2,1792,256]{2,1,0:T(8,128)(2,1)}, bf16[2,1792,256]{2,1,0:T(8,128)(2,1)}, u32[]{:S(2)}, u32[]{:S(2)}) collective-permute-start(bf16[2,1792,256]{2,1,0:T(8,128)(2,1)} %get-tuple-element.96), channel_id=1, source_target_pairs={{0,32},{1,97},{2,34},{3,99},{4,36},{5,101},{6,38},{7,103},{8,40},{... | collective-permute-start | bytes 5505032 | tf_op jit(solution)/shard_map/ppermute | solution.py:450
  48.7 9.1 %all-to-all-done.1 = bf16[64,8,512]{2,1,0:T(8,128)(2,1)S(1)} async-done(((bf16[64,8,512]{2,1,0:T(8,128)(2,1)}), bf16[64,8,512]{2,1,0:T(8,128)(2,1)S(1)}, u32[]{:S(2)}, u32[]{:S(2)}) %all-to-all-start.1) | async-done | bytes 524320 | tf_op jit(solution)/shard_map/all_to_all | solution.py:466
  57.8 2.0 %copy-done = bf16[256,7168]{1,0:T(8,128)(2,1)S(1)} copy-done((bf16[256,7168]{1,0:T(8,128)(2,1)S(1)}, bf16[256,7168]{1,0:T(8,128)(2,1)}, u32[]{:S(2)}) %copy-start) | copy-done | bytes 3670040
  59.9 2.1 %project.1 = (bf16[48,7168]{1,0:T(8,128)(2,1)S(1)}, bf16[48,7168]{1,0:T(8,128)(2,1)S(1)}) custom-call(s32[96,128]{1,0:T(8,128)S(1)} %get-tuple-element.75.cells_ref, bf16[32,2,8,512]{3,2,1,0:T(8,128)(2,1)S(1)} %bitcast.132, bf16[2,96,512]{2,1,0:T(8,128)(2,1)S(1)} %get-tuple-element.162.more_ref, bf16[2,512,128]{2,1,0:T(8,128)(2,1)S(1)} %copy-done.1, ...), custom_call_target="tpu_custom_call" | custom-call | flops 400000000 | bytes 6000000 | tf_op jit(solution)/shard_map/project/pallas_call | solution.py:325
  63.3 1.0 collective-permute-done.5.other_ref
  64.3 1.4 pair_sum.1
  65.6 3.6 %all-to-all-start.2 = ((bf16[16,3,7168]{2,1,0:T(4,128)(2,1)}), bf16[16,3,7168]{2,1,0:T(4,128)(2,1)S(1)}, u32[]{:S(2)}, u32[]{:S(2)}) async-start(bf16[16,3,7168]{2,1,0:T(4,128)(2,1)} %pair_sum.1), calls=%async_computation.2 | async-start | bytes 1835008 | tf_op jit(solution)/shard_map/all_to_all | solution.py:509
  69.6 2.4 %collective-permute-start.7 = (bf16[256,1792]{1,0:T(8,128)(2,1)}, bf16[256,1792]{1,0:T(8,128)(2,1)}, u32[]{:S(2)}, u32[]{:S(2)}) collective-permute-start(bf16[256,1792]{1,0:T(8,128)(2,1)} %get-tuple-element.99), channel_id=1, source_target_pairs={{32,0},{64,32},{96,64},{0,96},{33,1},{65,33},{97,65},{1,97},{34,2}... | collective-permute-start | bytes 2752520 | tf_op jit(solution)/shard_map/ppermute | solution.py:45
  72.0 12.5 %all-to-all-done.2 = bf16[16,3,7168]{2,1,0:T(4,128)(2,1)S(1)} async-done(((bf16[16,3,7168]{2,1,0:T(4,128)(2,1)}), bf16[16,3,7168]{2,1,0:T(4,128)(2,1)S(1)}, u32[]{:S(2)}, u32[]{:S(2)}) %all-to-all-start.2) | async-done | bytes 688160 | tf_op jit(solution)/shard_map/all_to_all | solution.py:509
  86.4 1.3 reshape.262
  87.7 6.3 %all-to-all-start.3 = ((bf16[128,2,1792]{2,1,0:T(2,128)(2,1)}), bf16[128,2,1792]{2,1,0:T(2,128)(2,1)S(1)}, u32[]{:S(2)}, u32[]{:S(2)}) async-start(bf16[128,2,1792]{2,1,0:T(2,128)(2,1)} %reshape.262), calls=%async_computation.3 | async-start | bytes 1835008 | tf_op jit(solution)/shard_map/all_to_all | solution.py:552
  94.1 3.0 %collective-permute-start.8 = (bf16[256,1792]{1,0:T(8,128)(2,1)}, bf16[256,1792]{1,0:T(8,128)(2,1)}, u32[]{:S(2)}, u32[]{:S(2)}) collective-permute-start(bf16[256,1792]{1,0:T(8,128)(2,1)} %get-tuple-element.100), channel_id=1, source_target_pairs={{64,0},{96,32},{0,64},{32,96},{65,1},{97,33},{1,65},{33,97},{66,2}... | collective-permute-start | bytes 2752520 | tf_op jit(solution)/shard_map/ppermute | solution.py:45
  97.3 2.2 %dynamic-slice_bitcast_fusion = bf16[256,1792]{1,0:T(8,128)(2,1)} fusion(bf16[1,256,7168]{2,1,0:T(8,128)(2,1)} %down_ref.1, s32[]{:T(128)S(6)} %select_n.230), kind=kLoop, calls=%fused_computation.73 | loop fusion | bytes 1835012 | tf_op jit(solution)/shard_map/dynamic_slice | solution.py:584
  99.8 1.5 maximum_bitcast_fusion
  101.4 10.4 %all-to-all-done.3 = bf16[128,2,1792]{2,1,0:T(2,128)(2,1)S(1)} async-done(((bf16[128,2,1792]{2,1,0:T(2,128)(2,1)}), bf16[128,2,1792]{2,1,0:T(2,128)(2,1)S(1)}, u32[]{:S(2)}, u32[]{:S(2)}) %all-to-all-start.3) | async-done | bytes 917536 | tf_op jit(solution)/shard_map/all_to_all | solution.py:552
  112.1 14.5 %collective-permute-done.8 = bf16[256,1792]{1,0:T(8,128)(2,1)} collective-permute-done((bf16[256,1792]{1,0:T(8,128)(2,1)}, bf16[256,1792]{1,0:T(8,128)(2,1)}, u32[]{:S(2)}, u32[]{:S(2)}) %collective-permute-start.8) | collective-permute-done | bytes 917536 | tf_op jit(solution)/shard_map/ppermute | solution.py:45
  126.9 1.6 fusion.39
  128.5 9.1 %all-to-all-start.4 = ((bf16[32,24,576]{2,1,0:T(8,128)(2,1)}), bf16[32,24,576]{2,1,0:T(8,128)(2,1)S(1)}, u32[]{:S(2)}, u32[]{:S(2)}) async-start(bf16[32,24,576]{2,1,0:T(8,128)(2,1)} %maximum_bitcast_fusion), calls=%async_computation.4 | async-start | bytes 1966080 | tf_op jit(solution)/shard_map/all_to_all | solution.py:564
  137.6 1.6 fusion.41
  139.2 1.6 fusion.43
  140.8 1.6 fusion.45
  142.4 1.6 fusion.35
  144.0 1.6 fusion.33
  145.7 1.9 collective-permute-start.11
  147.6 1.6 fusion.31
  149.2 1.6 fusion.37
  150.8 1.4 collective-permute-done.11
  152.4 1.9 collective-permute-start.12
  155.1 0.8 fusion.93
  155.9 1.6 collective-permute-done.12
  157.4 3.0 %collective-permute-done.13 = bf16[256,256]{1,0:T(8,128)(2,1)S(1)} collective-permute-done((bf16[256,256]{1,0:T(8,128)(2,1)S(1)}, bf16[256,256]{1,0:T(8,128)(2,1)S(1)}, u32[]{:S(2)}, u32[]{:S(2)}) %collective-permute-start.13) | collective-permute-done | bytes 131104 | tf_op jit(solution)/shard_map/ppermute | solution.py:45
  160.5 3.0 %collective-permute-done.14 = bf16[256,256]{1,0:T(8,128)(2,1)S(1)} collective-permute-done((bf16[256,256]{1,0:T(8,128)(2,1)S(1)}, bf16[256,256]{1,0:T(8,128)(2,1)S(1)}, u32[]{:S(2)}, u32[]{:S(2)}) %collective-permute-start.14) | collective-permute-done | bytes 131104 | tf_op jit(solution)/shard_map/ppermute | solution.py:45
  163.6 3.1 %fusion.24 = bf16[256,1792]{1,0:T(8,128)(2,1)S(1)} fusion(bf16[256,1024]{1,0:T(8,128)(2,1)S(1)} %pad_maximum_fusion.2, bf16[256,1792]{1,0:T(8,128)(2,1)} %collective-permute-done.9, bf16[256,1792]{1,0:T(8,128)(2,1)} %collective-permute-done.8, bf16[256,1792]{1,0:T(8,128)(2,1)} %collective-permute-done.7, bf16[256,1792]{1,0:T(8,128)(2,1)} %dynamic-slice_bitcast_fusion), kind=kOutput, calls=%fused_computation.44 | convolution fusion | flops 954662912 | bytes 5111808 | tf_op jit(solution)/shard_map/dot_general | solution.py:585
  166.7 1.3 reshape.271
  168.0 7.6 %all-to-all-start.5 = ((bf16[128,2,1792]{2,1,0:T(2,128)(2,1)}), bf16[128,2,1792]{2,1,0:T(2,128)(2,1)S(1)}, u32[]{:S(2)}, u32[]{:S(2)}) async-start(bf16[128,2,1792]{2,1,0:T(2,128)(2,1)} %reshape.271), calls=%async_computation.5 | async-start | bytes 1835008 | tf_op jit(solution)/shard_map/all_to_all | solution.py:586
  176.4 0.8 pad_maximum_fusion.5
  177.2 16.1 %all-to-all-done.5 = bf16[128,2,1792]{2,1,0:T(2,128)(2,1)S(1)} async-done(((bf16[128,2,1792]{2,1,0:T(2,128)(2,1)}), bf16[128,2,1792]{2,1,0:T(2,128)(2,1)S(1)}, u32[]{:S(2)}, u32[]{:S(2)}) %all-to-all-start.5) | async-done | bytes 917536 | tf_op jit(solution)/shard_map/all_to_all | solution.py:586
  194.7 1.2 fusion.15
  (109 shorter events, 12.0 us)
Async XLA Ops:
  1.5 4.8 %collective-permute-start = (bf16[64,576]{1,0:T(8,128)(2,1)S(1)}, bf16[64,576]{1,0:T(8,128)(2,1)S(1)}, u32[]{:S(2)}, u32[]{:S(2)}) collective-permute-start(bf16[64,576]{1,0:T(8,128)(2,1)S(1)} %slice.110), channel_id=1, source_target_pairs={{1,0},{2,1},{3,2},{4,3},{5,4},{6,5},{7,6},{8,7},{9,8},{10,9},{11,1... | collective-permute-start | bytes 221192 | tf_op jit(solution)/shard_map/ppermute | solution.py:394
  7.3 13.2 %copy-start.2 = (bf16[256,576]{1,0:T(8,128)(2,1)}, bf16[256,576]{1,0:T(8,128)(2,1)S(1)}, u32[]{:S(2)}) copy-start(bf16[256,576]{1,0:T(8,128)(2,1)S(1)} %pad_maximum_fusion.3.refs_1_) | copy-start | bytes 884740
  7.3 13.2 %collective-permute-start.1 = (bf16[256,576]{1,0:T(8,128)(2,1)S(1)}, bf16[256,576]{1,0:T(8,128)(2,1)S(1)}, u32[]{:S(2)}, u32[]{:S(2)}) collective-permute-start(bf16[256,576]{1,0:T(8,128)(2,1)S(1)} %pad_maximum_fusion.3.refs_1_), channel_id=1, source_target_pairs={{32,0},{64,32},{96,64},{0,96},{33,1},{65,33},{97,65},{1,97},{34,2}... | collective-permute-start | bytes 884744 | tf_op jit(solution)/shard_map/ppermute | solution.py:45
  9.9 10.7 %collective-permute-start.2 = (bf16[256,576]{1,0:T(8,128)(2,1)S(1)}, bf16[256,576]{1,0:T(8,128)(2,1)S(1)}, u32[]{:S(2)}, u32[]{:S(2)}) collective-permute-start(bf16[256,576]{1,0:T(8,128)(2,1)S(1)} %pad_maximum_fusion.3.refs_1_), channel_id=1, source_target_pairs={{64,0},{96,32},{0,64},{32,96},{65,1},{97,33},{1,65},{33,97},{66,2}... | collective-permute-start | bytes 884744 | tf_op jit(solution)/shard_map/ppermute | solution.py:45
  10.4 15.5 %collective-permute-start.3 = (bf16[256,576]{1,0:T(8,128)(2,1)S(1)}, bf16[256,576]{1,0:T(8,128)(2,1)S(1)}, u32[]{:S(2)}, u32[]{:S(2)}) collective-permute-start(bf16[256,576]{1,0:T(8,128)(2,1)S(1)} %pad_maximum_fusion.3.refs_1_), channel_id=1, source_target_pairs={{96,0},{0,32},{32,64},{64,96},{97,1},{1,33},{33,65},{65,97},{98,2}... | collective-permute-start | bytes 884744 | tf_op jit(solution)/shard_map/ppermute | solution.py:45
  14.2 13.0 %copy-start.10 = (s32[384]{0:T(512)S(1)}, s32[384]{0:T(512)}, u32[]{:S(2)}) copy-start(s32[384]{0:T(512)} %param.23) | copy-start | bytes 4612
  20.5 6.7 %copy-start.4 = (bf16[256,576]{1,0:T(8,128)(2,1)}, bf16[256,576]{1,0:T(8,128)(2,1)S(1)}, u32[]{:S(2)}) copy-start(bf16[256,576]{1,0:T(8,128)(2,1)S(1)} %collective-permute-done.1.refs_2_) | copy-start | bytes 884740
  20.6 6.7 %copy-start.5 = (bf16[256,576]{1,0:T(8,128)(2,1)}, bf16[256,576]{1,0:T(8,128)(2,1)S(1)}, u32[]{:S(2)}) copy-start(bf16[256,576]{1,0:T(8,128)(2,1)S(1)} %collective-permute-done.2.refs_3_) | copy-start | bytes 884740
  25.9 1.4 copy-start.6
  25.9 32.0 %collective-permute-start.4 = (bf16[2,1792,256]{2,1,0:T(8,128)(2,1)}, bf16[2,1792,256]{2,1,0:T(8,128)(2,1)}, u32[]{:S(2)}, u32[]{:S(2)}) collective-permute-start(bf16[2,1792,256]{2,1,0:T(8,128)(2,1)} %get-tuple-element.87), channel_id=1, source_target_pairs={{0,32},{1,97},{2,34},{3,99},{4,36},{5,101},{6,38},{7,103},{8,40},{... | collective-permute-start | bytes 5505032 | tf_op jit(solution)/shard_map/ppermute | solution.py:449
  35.8 22.0 %copy-start.1 = (bf16[2,512,128]{2,1,0:T(8,128)(2,1)S(1)}, bf16[2,512,128]{2,1,0:T(8,128)(2,1)}, u32[]{:S(2)}) copy-start(bf16[2,512,128]{2,1,0:T(8,128)(2,1)} %uv_ref.1) | copy-start | bytes 786436
  35.9 26.6 %copy-start.12 = (s32[1,3,8]{2,0,1:T(1,128)S(1)}, s32[1,3,8]{2,0,1:T(1,128)}, u32[]{:S(2)}) copy-start(s32[1,3,8]{2,0,1:T(1,128)} %param.29) | copy-start | bytes 292
  35.9 27.3 %copy-start.13 = (f32[1,3,8]{2,0,1:T(1,128)S(1)}, f32[1,3,8]{2,0,1:T(1,128)}, u32[]{:S(2)}) copy-start(f32[1,3,8]{2,0,1:T(1,128)} %param.30) | copy-start | bytes 292
  35.9 27.3 %copy-start.11 = (s32[384]{0:T(512)S(1)}, s32[384]{0:T(512)}, u32[]{:S(2)}) copy-start(s32[384]{0:T(512)} %param.22) | copy-start | bytes 4612
  35.9 21.9 %all-to-all-start.1 = ((bf16[64,8,512]{2,1,0:T(8,128)(2,1)}), bf16[64,8,512]{2,1,0:T(8,128)(2,1)S(1)}, u32[]{:S(2)}, u32[]{:S(2)}) async-start(bf16[64,8,512]{2,1,0:T(8,128)(2,1)} %get-tuple-element.86), calls=%async_computation.1 | async-start | bytes 1048576 | tf_op jit(solution)/shard_map/all_to_all | solution.py:466
  46.3 25.7 %collective-permute-start.6 = (bf16[2,1792,256]{2,1,0:T(8,128)(2,1)}, bf16[2,1792,256]{2,1,0:T(8,128)(2,1)}, u32[]{:S(2)}, u32[]{:S(2)}) collective-permute-start(bf16[2,1792,256]{2,1,0:T(8,128)(2,1)} %get-tuple-element.96), channel_id=1, source_target_pairs={{0,32},{1,97},{2,34},{3,99},{4,36},{5,101},{6,38},{7,103},{8,40},{... | collective-permute-start | bytes 5505032 | tf_op jit(solution)/shard_map/ppermute | solution.py:450
  57.8 2.0 %copy-start = (bf16[256,7168]{1,0:T(8,128)(2,1)S(1)}, bf16[256,7168]{1,0:T(8,128)(2,1)}, u32[]{:S(2)}) copy-start(bf16[256,7168]{1,0:T(8,128)(2,1)} %weight_ref.1) | copy-start | bytes 11010052
  61.9 22.9 %copy-start.7 = (bf16[1,3,7168]{2,1,0:T(4,128)(2,1)S(1)}, bf16[1,3,7168]{2,1,0:T(4,128)(2,1)}, u32[]{:S(2)}) copy-start(bf16[1,3,7168]{2,1,0:T(4,128)(2,1)} %param.27) | copy-start | bytes 129028
  61.9 23.1 %copy-start.8 = (f32[7168]{0:T(1024)S(1)}, f32[7168]{0:T(1024)}, u32[]{:S(2)}) copy-start(f32[7168]{0:T(1024)} %param.28) | copy-start | bytes 86020
  62.0 2.3 %collective-permute-start.5 = (bf16[48,7168]{1,0:T(8,128)(2,1)S(1)}, bf16[48,7168]{1,0:T(8,128)(2,1)S(1)}, u32[]{:S(2)}, u32[]{:S(2)}) collective-permute-start(bf16[48,7168]{1,0:T(8,128)(2,1)S(1)} %get-tuple-element.95), channel_id=1, source_target_pairs={{0,1},{1,0},{2,3},{3,2},{4,5},{5,4},{6,7},{7,6},{8,9},{9,8},{10,11... | collective-permute-start | bytes 2064392 | tf_op jit(solution)/shard_map/ppermute | solution.py:507
  65.6 18.8 %all-to-all-start.2 = ((bf16[16,3,7168]{2,1,0:T(4,128)(2,1)}), bf16[16,3,7168]{2,1,0:T(4,128)(2,1)S(1)}, u32[]{:S(2)}, u32[]{:S(2)}) async-start(bf16[16,3,7168]{2,1,0:T(4,128)(2,1)} %pair_sum.1), calls=%async_computation.2 | async-start | bytes 1835008 | tf_op jit(solution)/shard_map/all_to_all | solution.py:509
  69.6 42.5 %collective-permute-start.7 = (bf16[256,1792]{1,0:T(8,128)(2,1)}, bf16[256,1792]{1,0:T(8,128)(2,1)}, u32[]{:S(2)}, u32[]{:S(2)}) collective-permute-start(bf16[256,1792]{1,0:T(8,128)(2,1)} %get-tuple-element.99), channel_id=1, source_target_pairs={{32,0},{64,32},{96,64},{0,96},{33,1},{65,33},{97,65},{1,97},{34,2}... | collective-permute-start | bytes 2752520 | tf_op jit(solution)/shard_map/ppermute | solution.py:45
  72.0 40.2 %collective-permute-start.9 = (bf16[256,1792]{1,0:T(8,128)(2,1)}, bf16[256,1792]{1,0:T(8,128)(2,1)}, u32[]{:S(2)}, u32[]{:S(2)}) collective-permute-start(bf16[256,1792]{1,0:T(8,128)(2,1)} %get-tuple-element.101), channel_id=1, source_target_pairs={{96,0},{0,32},{32,64},{64,96},{97,1},{1,33},{33,65},{65,97},{98,2}... | collective-permute-start | bytes 2752520 | tf_op jit(solution)/shard_map/ppermute | solution.py:45
  86.3 13.1 %copy-start.3 = (bf16[256,576]{1,0:T(8,128)(2,1)S(1)}, bf16[256,576]{1,0:T(8,128)(2,1)}, u32[]{:S(2)}) copy-start(bf16[256,576]{1,0:T(8,128)(2,1)} %copy-done.2) | copy-start | bytes 884740
  86.4 13.1 %slice-start = ((bf16[256,576]{1,0:T(8,128)(2,1)}), bf16[192,576]{1,0:T(8,128)(2,1)S(1)}, s32[]{:S(2)}) async-start(bf16[256,576]{1,0:T(8,128)(2,1)} %copy-done.4), calls=%async_computation.6 | async-start | bytes 491520 | tf_op jit(solution)/shard_map/slice | solution.py:558
  87.7 11.9 %slice-start.1 = ((bf16[256,576]{1,0:T(8,128)(2,1)}), bf16[192,576]{1,0:T(8,128)(2,1)S(1)}, s32[]{:S(2)}) async-start(bf16[256,576]{1,0:T(8,128)(2,1)} %copy-done.5), calls=%async_computation.7 | async-start | bytes 491520 | tf_op jit(solution)/shard_map/slice | solution.py:558
  87.7 12.0 %slice-start.2 = ((bf16[256,576]{1,0:T(8,128)(2,1)}), bf16[192,576]{1,0:T(8,128)(2,1)S(1)}, s32[]{:S(2)}) async-start(bf16[256,576]{1,0:T(8,128)(2,1)} %copy-done.6), calls=%async_computation.8 | async-start | bytes 491520 | tf_op jit(solution)/shard_map/slice | solution.py:558
  87.7 24.1 %all-to-all-start.3 = ((bf16[128,2,1792]{2,1,0:T(2,128)(2,1)}), bf16[128,2,1792]{2,1,0:T(2,128)(2,1)S(1)}, u32[]{:S(2)}, u32[]{:S(2)}) async-start(bf16[128,2,1792]{2,1,0:T(2,128)(2,1)} %reshape.262), calls=%async_computation.3 | async-start | bytes 1835008 | tf_op jit(solution)/shard_map/all_to_all | solution.py:552
  94.1 32.6 %collective-permute-start.8 = (bf16[256,1792]{1,0:T(8,128)(2,1)}, bf16[256,1792]{1,0:T(8,128)(2,1)}, u32[]{:S(2)}, u32[]{:S(2)}) collective-permute-start(bf16[256,1792]{1,0:T(8,128)(2,1)} %get-tuple-element.100), channel_id=1, source_target_pairs={{64,0},{96,32},{0,64},{32,96},{65,1},{97,33},{1,65},{33,97},{66,2}... | collective-permute-start | bytes 2752520 | tf_op jit(solution)/shard_map/ppermute | solution.py:45
  126.7 15.8 %collective-permute-start.10 = (bf16[256,1792]{1,0:T(8,128)(2,1)S(1)}, bf16[256,1792]{1,0:T(8,128)(2,1)S(1)}, u32[]{:S(2)}, u32[]{:S(2)}) collective-permute-start(bf16[256,1792]{1,0:T(8,128)(2,1)S(1)} %reshape.263), channel_id=1, source_target_pairs={{0,96},{1,33},{2,98},{3,35},{4,100},{5,37},{6,102},{7,39},{8,104},... | collective-permute-start | bytes 2752520 | tf_op jit(solution)/shard_map/ppermute | solution.py:563
  128.5 35.0 %all-to-all-start.4 = ((bf16[32,24,576]{2,1,0:T(8,128)(2,1)}), bf16[32,24,576]{2,1,0:T(8,128)(2,1)S(1)}, u32[]{:S(2)}, u32[]{:S(2)}) async-start(bf16[32,24,576]{2,1,0:T(8,128)(2,1)} %maximum_bitcast_fusion), calls=%async_computation.4 | async-start | bytes 1966080 | tf_op jit(solution)/shard_map/all_to_all | solution.py:564
  145.7 6.5 %collective-permute-start.11 = (bf16[256,512]{1,0:T(8,128)(2,1)S(1)}, bf16[256,512]{1,0:T(8,128)(2,1)S(1)}, u32[]{:S(2)}, u32[]{:S(2)}) collective-permute-start(bf16[256,512]{1,0:T(8,128)(2,1)S(1)} %pad_maximum_fusion.4), channel_id=1, source_target_pairs={{0,32},{1,97},{2,34},{3,99},{4,36},{5,101},{6,38},{7,103},{8,40},{... | collective-permute-start | bytes 786440 | tf_op jit(solution)/shard_map/ppermute | solution.py:575
  152.4 5.0 %collective-permute-start.12 = (bf16[256,256]{1,0:T(8,128)(2,1)S(1)}, bf16[256,256]{1,0:T(8,128)(2,1)S(1)}, u32[]{:S(2)}, u32[]{:S(2)}) collective-permute-start(bf16[256,256]{1,0:T(8,128)(2,1)S(1)} %fusion.62), channel_id=1, source_target_pairs={{32,0},{64,32},{96,64},{0,96},{33,1},{65,33},{97,65},{1,97},{34,2}... | collective-permute-start | bytes 393224 | tf_op jit(solution)/shard_map/ppermute | solution.py:45
  154.3 6.2 %collective-permute-start.13 = (bf16[256,256]{1,0:T(8,128)(2,1)S(1)}, bf16[256,256]{1,0:T(8,128)(2,1)S(1)}, u32[]{:S(2)}, u32[]{:S(2)}) collective-permute-start(bf16[256,256]{1,0:T(8,128)(2,1)S(1)} %fusion.62), channel_id=1, source_target_pairs={{64,0},{96,32},{0,64},{32,96},{65,1},{97,33},{1,65},{33,97},{66,2}... | collective-permute-start | bytes 393224 | tf_op jit(solution)/shard_map/ppermute | solution.py:45
  154.3 9.2 %collective-permute-start.14 = (bf16[256,256]{1,0:T(8,128)(2,1)S(1)}, bf16[256,256]{1,0:T(8,128)(2,1)S(1)}, u32[]{:S(2)}, u32[]{:S(2)}) collective-permute-start(bf16[256,256]{1,0:T(8,128)(2,1)S(1)} %fusion.62), channel_id=1, source_target_pairs={{96,0},{0,32},{32,64},{64,96},{97,1},{1,33},{33,65},{65,97},{98,2}... | collective-permute-start | bytes 393224 | tf_op jit(solution)/shard_map/ppermute | solution.py:45
  166.7 9.6 %copy-start.9 = (f32[512]{0:T(512)S(1)}, f32[512]{0:T(512)}, u32[]{:S(2)}) copy-start(f32[512]{0:T(512)} %param.21) | copy-start | bytes 6148
  168.0 25.3 %all-to-all-start.5 = ((bf16[128,2,1792]{2,1,0:T(2,128)(2,1)}), bf16[128,2,1792]{2,1,0:T(2,128)(2,1)S(1)}, u32[]{:S(2)}, u32[]{:S(2)}) async-start(bf16[128,2,1792]{2,1,0:T(2,128)(2,1)} %reshape.271), calls=%async_computation.5 | async-start | bytes 1835008 | tf_op jit(solution)/shard_map/all_to_all | solution.py:586

commit v8 on v7

--- a/solution.py
+++ b/solution.py
@@ -184,7 +184,7 @@
 def attend_kernel(slots_ref, *refs, blocks):
     rows_in = refs[:blocks]
     cos_ref, sin_ref, gain_ref, new_ref, query_ref = refs[blocks : blocks + 5]
-    out_ref, rest_ref, keys, query, fresh, held_out, sems = refs[blocks + 5 :]
+    out_ref, rest_ref, keys, query, fresh, held_out, spare, sems, spare_sem = refs[blocks + 5 :]
     number = slots_ref[0, 4]
 
     def fetch(slot):
@@ -250,7 +250,10 @@
 
     @pl.loop(sent, number)
     def _(slot):
-        rest_ref[slot - sent] = one(slot).astype(BF)
+        spare[...] = one(slot).astype(BF)
+        copy = pltpu.make_async_copy(spare, rest_ref.at[slot - sent], spare_sem)
+        copy.start()
+        copy.wait()
 
 
 def attend(slots, rows, cosine, sine, gain, new_rows, queries, most_slots):
@@ -271,13 +274,15 @@
         in_specs=[pl.BlockSpec(memory_space=pltpu.SMEM)]
         + [whole] * (blocks + 4)
         + [pl.BlockSpec(memory_space=pltpu.HBM)],
-        out_specs=(whole, whole),
+        out_specs=(whole, pl.BlockSpec(memory_space=pltpu.HBM)),
         scratch_shapes=[
             pltpu.VMEM((total_rows, queries.shape[2]), BF),
             pltpu.VMEM((most_slots,) + queries.shape[1:], BF),
             pltpu.VMEM(new_rows.shape, F32),
             pltpu.VMEM((SLOTS, heads, LAT), F32),
+            pltpu.VMEM((heads, LAT), BF),
             pltpu.SemaphoreType.DMA((most_slots,)),
+            pltpu.SemaphoreType.DMA,
         ],
         compiler_params=pltpu.CompilerParams(vmem_limit_bytes=VMEM),
         cost_estimate=pl.CostEstimate(
@@ -328,7 +333,7 @@
         in_specs=[whole] * 4 + [pl.BlockSpec(memory_space=pltpu.HBM)],
         out_specs=(whole, whole),
         scratch_shapes=[pltpu.VMEM(w_out.shape, BF), pltpu.SemaphoreType.DMA((4,))],
-        compiler_params=pltpu.CompilerParams(vmem_limit_bytes=32 * 1024 * 1024),
+        compiler_params=pltpu.CompilerParams(vmem_limit_bytes=VMEM),
         cost_estimate=pl.CostEstimate(
             flops=4 * 10**8, bytes_accessed=6 * 10**6, transcendentals=0
         ),
@@ -498,10 +503,11 @@
     by_head = to_heads(attended)
     by_head, gate_came = lax.optimization_barrier((by_head, gate_came))
     mine, other = project(cells, by_head, more, w_uv, w_out)
-    mine, other, down_near, down_last = lax.optimization_barrier(
-        (mine, other, down_near, down_last)
+    mine, other, down_near, down_far, down_last = lax.optimization_barrier(
+        (mine, other, down_near, down_far, down_last)
     )
     down_near = shift(down_near, 1, dp_count, "dp")
+    down_far = shift(down_far, 2, dp_count, "dp")
     down_last = shift(down_last, 3, dp_count, "dp")
 
     other = lax.ppermute(other, "expert", [(i, i ^ 1) for i in range(columns)])
@@ -514,8 +520,7 @@
         tiled=True,
         axis_index_groups=[[2 * i + c for i in range(chips)] for c in range(2)],
     )
-    chip_sums, up_came, down_far = lax.optimization_barrier((chip_sums, up_came, down_far))
-    down_far = shift(down_far, 2, dp_count, "dp")
+    chip_sums, up_came = lax.optimization_barrier((chip_sums, up_came))
     attention_out = jnp.sum(chip_sums.astype(F32), axis=0)
     residual = resid[0].astype(F32) + attention_out
     normed = (
@@ -577,12 +582,18 @@
     hidden = (
         jax.nn.silu(gate_sum + given[:, :half]) * (up_sum + given[:, half:])
     ).astype(BF)
-    hidden_all = jnp.concatenate(
-        [hidden] + [shift(hidden, k, dp_count, "dp") for k in range(1, dp_count)], axis=1
-    )
-    hidden_all, dealt = lax.optimization_barrier((hidden_all, dealt))
-    downs = jnp.concatenate([lax.dynamic_slice_in_dim(w_down[0], group * piece, piece, 1), down_near, down_far, down_last], axis=0)
-    out = jnp.dot(hidden_all, downs, preferred_element_type=F32)
+    blocks = [hidden] + [shift(hidden, k, dp_count, "dp") for k in (1, 3, 2)]
+    downs = [
+        lax.dynamic_slice_in_dim(w_down[0], group * piece, piece, 1),
+        down_near,
+        down_last,
+        down_far,
+    ]
+    out = jnp.dot(blocks[0], downs[0], preferred_element_type=F32)
+    for block, down in zip(blocks[1:3], downs[1:3]):
+        out = out + jnp.dot(block, down, preferred_element_type=F32)
+    out, last_block, dealt = lax.optimization_barrier((out, blocks[3], dealt))
+    out = out + jnp.dot(last_block, downs[3], preferred_element_type=F32)
     returned = lax.all_to_all(
         out.astype(BF).reshape(devices, capacity, piece),
         ("dp", "expert"),

time: 197 us -> 203 us (1.030)
  starting transfers between devices: 55.1 us -> 50.9 us
  matrix products: 18.5 us -> 21.7 us
  Pallas kernels: 19.3 us -> 22.2 us
  waiting for transfers between devices: 81.4 us -> 83.9 us
    all_to_all x1, waiting for transfers between devices: 10.4 us -> 33.6 us  [shards(): lax.all_to_all(outgoing, ('dp', 'expert'), split_axis=0, concat_axis=0, t...]
    ppermute x9, waiting for transfers between devices: 27.4 us -> 6.15 us  [shift(): return lax.ppermute(x, axis, [((i + step) % size, i) for i in range(size)])]
    all_to_all x1, starting transfers between devices: 9.11 us -> 4.74 us  [shards(): lax.all_to_all(to_rows, 'expert', split_axis=0, concat_axis=0, tiled=True)]
    dot_general x1 -> x4, matrix products: 3.12 us -> 6.34 us  [the longest x2 3.17 us: shards(): out = out + jnp.dot(block, down, preferred_element_type=F32)]
    all_to_all x1, starting transfers between devices: 7.59 us -> 10.7 us  [shards(): lax.all_to_all(out.astype(BF).reshape(devices, capacity, piece), ('dp', '...]
    pallas_call x1, Pallas kernels: 2.06 us -> 5.03 us  [project(): pl.pallas_call(project_kernel, out_shape=(half, half), in_specs=[whole] *...]
    ppermute x9, starting transfers between devices: 11.6 us -> 9.37 us  [shift(): return lax.ppermute(x, axis, [((i + step) % size, i) for i in range(size)])]
    dynamic_slice x1 -> x0, local copies, waits for them, and re-layouts: 2.17 us -> none  [shards(): lax.dynamic_slice_in_dim(w_down[0], group * piece, piece, 1)]
  transfers between devices with their start and end apart: 20 -> 20, of which waited for: 12 -> 12; matrix products, arithmetic and copies ran while one was open for 14% -> 15% of each run, Pallas kernels for 10% -> 11%
where the time goes in v8:
time: 203 us; the launch traced here: 202 us
  waiting for transfers between devices  83.9 us (41%)
  starting transfers between devices  50.9 us (25%)
  Pallas kernels  22.2 us (11%)
  matrix products  21.7 us (11%)
  local copies, waits for them, and re-layouts  14 us (7%)
  other arithmetic  7.25 us (4%)
    all_to_all x1, waiting for transfers between devices, shards(): lax.all_to_all(outgoing, ('dp', 'expert'), split_axis=0, concat_axis=0, t...  33.6 us
    all_to_all x1, waiting for transfers between devices, shards(): lax.all_to_all(out.astype(BF).reshape(devices, capacity, piece), ('dp', '...  16.1 us
    all_to_all x1, waiting for transfers between devices, shards(): lax.all_to_all(pair_sums, 'expert', split_axis=0, concat_axis=0, tiled=Tr...  10.7 us
    all_to_all x1, starting transfers between devices, shards(): lax.all_to_all(out.astype(BF).reshape(devices, capacity, piece), ('dp', '...  10.7 us
    all_to_all x1, starting transfers between devices, to_heads(): lax.all_to_all(part, 'expert', split_axis=0, concat_axis=0, tiled=True)  10.3 us
    ppermute x9, starting transfers between devices, shift(): return lax.ppermute(x, axis, [((i + step) % size, i) for i in range(size)])  9.37 us
    all_to_all x1, waiting for transfers between devices, to_heads(): lax.all_to_all(part, 'expert', split_axis=0, concat_axis=0, tiled=True)  9.05 us
    pallas_call x1, Pallas kernels, attend(): pl.pallas_call(body, out_shape=(jax.ShapeDtypeStruct((heads, SLOTS, LAT),...  8.49 us
  transfers between devices with their start and end apart: 20, of which 12 were waited for; matrix products, arithmetic and copies ran while one was open for 15% of the time, Pallas kernels for 11%

profile of v8, /device:TPU:1, one launch (start us, length us, event | category | flops | bytes accessed | tf_op | source)
XLA Modules:
  0.0 201.8 jit_solution(1643560734841077018)
XLA Ops:
  0.6 0.9 slice.110
  1.5 1.4 collective-permute-start
  2.9 3.4 %collective-permute-done = bf16[64,576]{1,0:T(8,128)(2,1)S(1)} collective-permute-done((bf16[64,576]{1,0:T(8,128)(2,1)S(1)}, bf16[64,576]{1,0:T(8,128)(2,1)S(1)}, u32[]{:S(2)}, u32[]{:S(2)}) %collective-permute-start) | collective-permute-done | bytes 73760 | tf_op jit(solution)/shard_map/ppermute | solution.py:399
  6.3 1.0 pad_maximum_fusion.2.refs_1_
  7.3 2.5 %collective-permute-start.1 = (bf16[256,576]{1,0:T(8,128)(2,1)S(1)}, bf16[256,576]{1,0:T(8,128)(2,1)S(1)}, u32[]{:S(2)}, u32[]{:S(2)}) collective-permute-start(bf16[256,576]{1,0:T(8,128)(2,1)S(1)} %pad_maximum_fusion.2.refs_1_), channel_id=1, source_target_pairs={{32,0},{64,32},{96,64},{0,96},{33,1},{65,33},{97,65},{1,97},{34,2}... | collective-permute-start | bytes 884744 | tf_op jit(solution)/shard_map/ppermute | solution.py:45
  12.4 1.0 tables.1
  14.6 6.4 %weight_slices.1 = (bf16[2,1792,256]{2,1,0:T(8,128)(2,1)}, bf16[2,1792,256]{2,1,0:T(8,128)(2,1)}, bf16[256,1792]{1,0:T(8,128)(2,1)}, bf16[256,1792]{1,0:T(8,128)(2,1)}, bf16[256,1792]{1,0:T(8,128)(2,1)}) custom-call(s32[5]{0:T(128)} %stack.59.at_ref, bf16[1,7168,256]{2,1,0:T(8,128)(2,1)} %gate_ref.1, bf16[1,7168,256]{2,1,0:T(8,128)(2,1)} %up_ref.1, ...), custom_call_target="tpu_custom_call" | custom-call | flops 1000 | bytes 4096 | tf_op jit(solution)/shard_map/weight_slices/pallas_call | solution.py:172
  21.1 4.8 %collective-permute-done.3.refs_4_ = bf16[256,576]{1,0:T(8,128)(2,1)S(1)} collective-permute-done((bf16[256,576]{1,0:T(8,128)(2,1)S(1)}, bf16[256,576]{1,0:T(8,128)(2,1)S(1)}, u32[]{:S(2)}, u32[]{:S(2)}) %collective-permute-start.3) | collective-permute-done | bytes 294944 | tf_op jit(solution)/shard_map/ppermute | solution.py:45
  27.1 8.5 %attend.1 = (bf16[64,8,512]{2,1,0:T(8,128)(2,1)}, bf16[16,64,512]{2,1,0:T(8,128)(2,1)S(1)}) custom-call(s32[32,128]{1,0:T(8,128)S(1)} %get-tuple-element.82.refs_0_, bf16[256,576]{1,0:T(8,128)(2,1)} %copy-done.2, bf16[256,576]{1,0:T(8,128)(2,1)} %copy-done.5, bf16[256,576]{1,0:T(8,128)(2,1)} %copy-done.6, bf16[256,576]{1,0:T(8,128)(2,1)} %copy-done.7, ...), custom_call_target="tpu_custom_call" | custom-call | flops 100000000 | bytes 4000000 | tf_op jit(solution)/shard_map/attend/pallas_call | solution.py:268
  35.7 10.3 %all-to-all-start.1 = ((bf16[64,8,512]{2,1,0:T(8,128)(2,1)}), bf16[64,8,512]{2,1,0:T(8,128)(2,1)S(1)}, u32[]{:S(2)}, u32[]{:S(2)}) async-start(bf16[64,8,512]{2,1,0:T(8,128)(2,1)} %get-tuple-element.87), calls=%async_computation.1 | async-start | bytes 1048576 | tf_op jit(solution)/shard_map/all_to_all | solution.py:471
  45.9 2.5 %collective-permute-start.6 = (bf16[2,1792,256]{2,1,0:T(8,128)(2,1)}, bf16[2,1792,256]{2,1,0:T(8,128)(2,1)}, u32[]{:S(2)}, u32[]{:S(2)}) collective-permute-start(bf16[2,1792,256]{2,1,0:T(8,128)(2,1)} %get-tuple-element.98), channel_id=1, source_target_pairs={{0,32},{1,97},{2,34},{3,99},{4,36},{5,101},{6,38},{7,103},{8,40},{... | collective-permute-start | bytes 5505032 | tf_op jit(solution)/shard_map/ppermute | solution.py:455
  48.5 9.0 %all-to-all-done.1 = bf16[64,8,512]{2,1,0:T(8,128)(2,1)S(1)} async-done(((bf16[64,8,512]{2,1,0:T(8,128)(2,1)}), bf16[64,8,512]{2,1,0:T(8,128)(2,1)S(1)}, u32[]{:S(2)}, u32[]{:S(2)}) %all-to-all-start.1) | async-done | bytes 524320 | tf_op jit(solution)/shard_map/all_to_all | solution.py:471
  57.5 0.8 copy-done.4
  58.3 5.0 %project.1 = (bf16[48,7168]{1,0:T(8,128)(2,1)}, bf16[48,7168]{1,0:T(8,128)(2,1)}) custom-call(s32[96,128]{1,0:T(8,128)} %copy-done.1, bf16[32,2,8,512]{3,2,1,0:T(8,128)(2,1)} %bitcast.144, bf16[2,96,512]{2,1,0:T(8,128)(2,1)S(1)} %get-tuple-element.164.more_ref, bf16[2,512,128]{2,1,0:T(8,128)(2,1)} %uv_ref.1, bf16[256,7168]{1,0:T(8,128)(2,1)} %weight_ref.1), custom_call_target="tpu_custom_call" | custom-call | flops 400000000 | bytes 6000000 | tf_op jit(solution)/shard_map/project/pallas_call | solution.py:330
  64.9 1.0 collective-permute-done.5.other_ref
  65.9 1.1 copy-done
  67.0 1.4 pair_sum.1
  68.3 3.8 %all-to-all-start.2 = ((bf16[16,3,7168]{2,1,0:T(4,128)(2,1)}), bf16[16,3,7168]{2,1,0:T(4,128)(2,1)S(1)}, u32[]{:S(2)}, u32[]{:S(2)}) async-start(bf16[16,3,7168]{2,1,0:T(4,128)(2,1)} %pair_sum.1), calls=%async_computation.2 | async-start | bytes 1835008 | tf_op jit(solution)/shard_map/all_to_all | solution.py:515
  72.1 0.8 fusion.86
  72.9 2.5 %collective-permute-start.7 = (bf16[256,1792]{1,0:T(8,128)(2,1)}, bf16[256,1792]{1,0:T(8,128)(2,1)}, u32[]{:S(2)}, u32[]{:S(2)}) collective-permute-start(bf16[256,1792]{1,0:T(8,128)(2,1)} %get-tuple-element.100), channel_id=1, source_target_pairs={{32,0},{64,32},{96,64},{0,96},{33,1},{65,33},{97,65},{1,97},{34,2}... | collective-permute-start | bytes 2752520 | tf_op jit(solution)/shard_map/ppermute | solution.py:45
  75.4 1.1 collective-permute-start.8
  76.5 10.7 %all-to-all-done.2 = bf16[16,3,7168]{2,1,0:T(4,128)(2,1)S(1)} async-done(((bf16[16,3,7168]{2,1,0:T(4,128)(2,1)}), bf16[16,3,7168]{2,1,0:T(4,128)(2,1)S(1)}, u32[]{:S(2)}, u32[]{:S(2)}) %all-to-all-start.2) | async-done | bytes 688160 | tf_op jit(solution)/shard_map/all_to_all | solution.py:515
  89.3 1.3 reshape.262
  90.5 6.4 %all-to-all-start.3 = ((bf16[128,2,1792]{2,1,0:T(2,128)(2,1)}), bf16[128,2,1792]{2,1,0:T(2,128)(2,1)S(1)}, u32[]{:S(2)}, u32[]{:S(2)}) async-start(bf16[128,2,1792]{2,1,0:T(2,128)(2,1)} %reshape.262), calls=%async_computation.3 | async-start | bytes 1835008 | tf_op jit(solution)/shard_map/all_to_all | solution.py:557
  98.4 1.5 maximum_bitcast_fusion
  99.9 33.6 %all-to-all-done.3 = bf16[128,2,1792]{2,1,0:T(2,128)(2,1)S(1)} async-done(((bf16[128,2,1792]{2,1,0:T(2,128)(2,1)}), bf16[128,2,1792]{2,1,0:T(2,128)(2,1)S(1)}, u32[]{:S(2)}, u32[]{:S(2)}) %all-to-all-start.3) | async-done | bytes 917536 | tf_op jit(solution)/shard_map/all_to_all | solution.py:557
  134.0 1.6 fusion.30
  135.6 4.7 %all-to-all-start.4 = ((bf16[32,24,576]{2,1,0:T(8,128)(2,1)}), bf16[32,24,576]{2,1,0:T(8,128)(2,1)S(1)}, u32[]{:S(2)}, u32[]{:S(2)}) async-start(bf16[32,24,576]{2,1,0:T(8,128)(2,1)} %maximum_bitcast_fusion), calls=%async_computation.4 | async-start | bytes 1966080 | tf_op jit(solution)/shard_map/all_to_all | solution.py:569
  140.3 1.6 fusion.32
  141.9 1.6 fusion.34
  143.5 1.6 fusion.36
  145.1 1.4 collective-permute-done.10
  146.5 1.6 fusion.26
  148.1 1.6 fusion.24
  149.8 1.1 collective-permute-start.11
  150.9 1.6 fusion.22
  152.5 1.6 fusion.28
  154.1 2.5 %collective-permute-done.11 = bf16[256,512]{1,0:T(8,128)(2,1)S(1)} collective-permute-done((bf16[256,512]{1,0:T(8,128)(2,1)S(1)}, bf16[256,512]{1,0:T(8,128)(2,1)S(1)}, u32[]{:S(2)}, u32[]{:S(2)}) %collective-permute-start.11) | collective-permute-done | bytes 262176 | tf_op jit(solution)/shard_map/ppermute | solution.py:580
  156.8 0.8 collective-permute-start.12
  158.9 1.6 fusion.20
  160.7 1.6 convolution_add_fusion.1
  163.0 1.6 convolution_add_fusion
  165.0 1.6 fusion.99
  166.6 1.1 add_convert_fusion
  167.8 3.1 %reshape.271 = bf16[128,2,1792]{2,1,0:T(2,128)(2,1)} reshape(bf16[256,1792]{1,0:T(8,128)(2,1)} %add_convert_fusion) | data formatting | bytes 1835008 | tf_op jit(solution)/shard_map/reshape | solution.py:598
  170.8 10.7 %all-to-all-start.5 = ((bf16[128,2,1792]{2,1,0:T(2,128)(2,1)}), bf16[128,2,1792]{2,1,0:T(2,128)(2,1)S(1)}, u32[]{:S(2)}, u32[]{:S(2)}) async-start(bf16[128,2,1792]{2,1,0:T(2,128)(2,1)} %reshape.271), calls=%async_computation.5 | async-start | bytes 1835008 | tf_op jit(solution)/shard_map/all_to_all | solution.py:597
  183.2 16.1 %all-to-all-done.5 = bf16[128,2,1792]{2,1,0:T(2,128)(2,1)S(1)} async-done(((bf16[128,2,1792]{2,1,0:T(2,128)(2,1)}), bf16[128,2,1792]{2,1,0:T(2,128)(2,1)S(1)}, u32[]{:S(2)}, u32[]{:S(2)}) %all-to-all-start.5) | async-done | bytes 917536 | tf_op jit(solution)/shard_map/all_to_all | solution.py:597
  200.7 1.2 fusion.15
  (113 shorter events, 15.6 us)
Async XLA Ops:
  1.5 4.8 %collective-permute-start = (bf16[64,576]{1,0:T(8,128)(2,1)S(1)}, bf16[64,576]{1,0:T(8,128)(2,1)S(1)}, u32[]{:S(2)}, u32[]{:S(2)}) collective-permute-start(bf16[64,576]{1,0:T(8,128)(2,1)S(1)} %slice.110), channel_id=1, source_target_pairs={{1,0},{2,1},{3,2},{4,3},{5,4},{6,5},{7,6},{8,7},{9,8},{10,9},{11,1... | collective-permute-start | bytes 221192 | tf_op jit(solution)/shard_map/ppermute | solution.py:399
  7.3 13.7 %copy-start.2 = (bf16[256,576]{1,0:T(8,128)(2,1)}, bf16[256,576]{1,0:T(8,128)(2,1)S(1)}, u32[]{:S(2)}) copy-start(bf16[256,576]{1,0:T(8,128)(2,1)S(1)} %pad_maximum_fusion.2.refs_1_) | copy-start | bytes 884740
  7.3 13.7 %collective-permute-start.1 = (bf16[256,576]{1,0:T(8,128)(2,1)S(1)}, bf16[256,576]{1,0:T(8,128)(2,1)S(1)}, u32[]{:S(2)}, u32[]{:S(2)}) collective-permute-start(bf16[256,576]{1,0:T(8,128)(2,1)S(1)} %pad_maximum_fusion.2.refs_1_), channel_id=1, source_target_pairs={{32,0},{64,32},{96,64},{0,96},{33,1},{65,33},{97,65},{1,97},{34,2}... | collective-permute-start | bytes 884744 | tf_op jit(solution)/shard_map/ppermute | solution.py:45
  9.9 11.2 %collective-permute-start.2 = (bf16[256,576]{1,0:T(8,128)(2,1)S(1)}, bf16[256,576]{1,0:T(8,128)(2,1)S(1)}, u32[]{:S(2)}, u32[]{:S(2)}) collective-permute-start(bf16[256,576]{1,0:T(8,128)(2,1)S(1)} %pad_maximum_fusion.2.refs_1_), channel_id=1, source_target_pairs={{64,0},{96,32},{0,64},{32,96},{65,1},{97,33},{1,65},{33,97},{66,2}... | collective-permute-start | bytes 884744 | tf_op jit(solution)/shard_map/ppermute | solution.py:45
  10.4 15.5 %collective-permute-start.3 = (bf16[256,576]{1,0:T(8,128)(2,1)S(1)}, bf16[256,576]{1,0:T(8,128)(2,1)S(1)}, u32[]{:S(2)}, u32[]{:S(2)}) collective-permute-start(bf16[256,576]{1,0:T(8,128)(2,1)S(1)} %pad_maximum_fusion.2.refs_1_), channel_id=1, source_target_pairs={{96,0},{0,32},{32,64},{64,96},{97,1},{1,33},{33,65},{65,97},{98,2}... | collective-permute-start | bytes 884744 | tf_op jit(solution)/shard_map/ppermute | solution.py:45
  13.4 0.6 copy-start.1
  14.6 12.4 %copy-start.11 = (s32[384]{0:T(512)S(1)}, s32[384]{0:T(512)}, u32[]{:S(2)}) copy-start(s32[384]{0:T(512)} %param.23) | copy-start | bytes 4612
  21.1 6.0 %copy-start.5 = (bf16[256,576]{1,0:T(8,128)(2,1)}, bf16[256,576]{1,0:T(8,128)(2,1)S(1)}, u32[]{:S(2)}) copy-start(bf16[256,576]{1,0:T(8,128)(2,1)S(1)} %collective-permute-done.1.refs_2_) | copy-start | bytes 884740
  21.1 6.0 %copy-start.6 = (bf16[256,576]{1,0:T(8,128)(2,1)}, bf16[256,576]{1,0:T(8,128)(2,1)S(1)}, u32[]{:S(2)}) copy-start(bf16[256,576]{1,0:T(8,128)(2,1)S(1)} %collective-permute-done.2.refs_3_) | copy-start | bytes 884740
  25.9 1.3 copy-start.7
  25.9 31.6 %collective-permute-start.4 = (bf16[2,1792,256]{2,1,0:T(8,128)(2,1)}, bf16[2,1792,256]{2,1,0:T(8,128)(2,1)}, u32[]{:S(2)}, u32[]{:S(2)}) collective-permute-start(bf16[2,1792,256]{2,1,0:T(8,128)(2,1)} %get-tuple-element.88), channel_id=1, source_target_pairs={{0,32},{1,97},{2,34},{3,99},{4,36},{5,101},{6,38},{7,103},{8,40},{... | collective-permute-start | bytes 5505032 | tf_op jit(solution)/shard_map/ppermute | solution.py:454
  35.7 21.8 %all-to-all-start.1 = ((bf16[64,8,512]{2,1,0:T(8,128)(2,1)}), bf16[64,8,512]{2,1,0:T(8,128)(2,1)S(1)}, u32[]{:S(2)}, u32[]{:S(2)}) async-start(bf16[64,8,512]{2,1,0:T(8,128)(2,1)} %get-tuple-element.87), calls=%async_computation.1 | async-start | bytes 1048576 | tf_op jit(solution)/shard_map/all_to_all | solution.py:471
  45.9 30.6 %collective-permute-start.6 = (bf16[2,1792,256]{2,1,0:T(8,128)(2,1)}, bf16[2,1792,256]{2,1,0:T(8,128)(2,1)}, u32[]{:S(2)}, u32[]{:S(2)}) collective-permute-start(bf16[2,1792,256]{2,1,0:T(8,128)(2,1)} %get-tuple-element.98), channel_id=1, source_target_pairs={{0,32},{1,97},{2,34},{3,99},{4,36},{5,101},{6,38},{7,103},{8,40},{... | collective-permute-start | bytes 5505032 | tf_op jit(solution)/shard_map/ppermute | solution.py:455
  57.5 0.8 copy-start.4
  58.3 5.6 %copy-start.13 = (s32[1,3,8]{2,0,1:T(1,128)S(1)}, s32[1,3,8]{2,0,1:T(1,128)}, u32[]{:S(2)}) copy-start(s32[1,3,8]{2,0,1:T(1,128)} %param.29) | copy-start | bytes 292
  58.3 6.3 %copy-start.14 = (f32[1,3,8]{2,0,1:T(1,128)S(1)}, f32[1,3,8]{2,0,1:T(1,128)}, u32[]{:S(2)}) copy-start(f32[1,3,8]{2,0,1:T(1,128)} %param.30) | copy-start | bytes 292
  63.4 2.5 %collective-permute-start.5 = (bf16[48,7168]{1,0:T(8,128)(2,1)}, bf16[48,7168]{1,0:T(8,128)(2,1)S(1)}, u32[]{:S(2)}, u32[]{:S(2)}) collective-permute-start(bf16[48,7168]{1,0:T(8,128)(2,1)} %get-tuple-element.97), channel_id=1, source_target_pairs={{0,1},{1,0},{2,3},{3,2},{4,5},{5,4},{6,7},{7,6},{8,9},{9,8},{10,11... | collective-permute-start | bytes 2064392 | tf_op jit(solution)/shard_map/ppermute | solution.py:513
  65.9 1.1 copy-start
  68.3 19.3 %copy-start.8 = (bf16[1,3,7168]{2,1,0:T(4,128)(2,1)S(1)}, bf16[1,3,7168]{2,1,0:T(4,128)(2,1)}, u32[]{:S(2)}) copy-start(bf16[1,3,7168]{2,1,0:T(4,128)(2,1)} %param.27) | copy-start | bytes 129028
  68.3 19.5 %copy-start.9 = (f32[7168]{0:T(1024)S(1)}, f32[7168]{0:T(1024)}, u32[]{:S(2)}) copy-start(f32[7168]{0:T(1024)} %param.28) | copy-start | bytes 86020
  68.3 19.0 %all-to-all-start.2 = ((bf16[16,3,7168]{2,1,0:T(4,128)(2,1)}), bf16[16,3,7168]{2,1,0:T(4,128)(2,1)S(1)}, u32[]{:S(2)}, u32[]{:S(2)}) async-start(bf16[16,3,7168]{2,1,0:T(4,128)(2,1)} %pair_sum.1), calls=%async_computation.2 | async-start | bytes 1835008 | tf_op jit(solution)/shard_map/all_to_all | solution.py:515
  72.9 60.9 %collective-permute-start.7 = (bf16[256,1792]{1,0:T(8,128)(2,1)}, bf16[256,1792]{1,0:T(8,128)(2,1)}, u32[]{:S(2)}, u32[]{:S(2)}) collective-permute-start(bf16[256,1792]{1,0:T(8,128)(2,1)} %get-tuple-element.100), channel_id=1, source_target_pairs={{32,0},{64,32},{96,64},{0,96},{33,1},{65,33},{97,65},{1,97},{34,2}... | collective-permute-start | bytes 2752520 | tf_op jit(solution)/shard_map/ppermute | solution.py:45
  75.4 58.4 %collective-permute-start.8 = (bf16[256,1792]{1,0:T(8,128)(2,1)}, bf16[256,1792]{1,0:T(8,128)(2,1)}, u32[]{:S(2)}, u32[]{:S(2)}) collective-permute-start(bf16[256,1792]{1,0:T(8,128)(2,1)} %get-tuple-element.101), channel_id=1, source_target_pairs={{64,0},{96,32},{0,64},{32,96},{65,1},{97,33},{1,65},{33,97},{66,2}... | collective-permute-start | bytes 2752520 | tf_op jit(solution)/shard_map/ppermute | solution.py:45
  76.5 57.3 %collective-permute-start.9 = (bf16[256,1792]{1,0:T(8,128)(2,1)}, bf16[256,1792]{1,0:T(8,128)(2,1)}, u32[]{:S(2)}, u32[]{:S(2)}) collective-permute-start(bf16[256,1792]{1,0:T(8,128)(2,1)} %get-tuple-element.102), channel_id=1, source_target_pairs={{96,0},{0,32},{32,64},{64,96},{97,1},{1,33},{33,65},{65,97},{98,2}... | collective-permute-start | bytes 2752520 | tf_op jit(solution)/shard_map/ppermute | solution.py:45
  89.2 7.7 %copy-start.12 = (s32[384]{0:T(512)S(1)}, s32[384]{0:T(512)}, u32[]{:S(2)}) copy-start(s32[384]{0:T(512)} %param.22) | copy-start | bytes 4612
  89.2 8.1 %copy-start.3 = (bf16[256,576]{1,0:T(8,128)(2,1)S(1)}, bf16[256,576]{1,0:T(8,128)(2,1)}, u32[]{:S(2)}) copy-start(bf16[256,576]{1,0:T(8,128)(2,1)} %copy-done.2) | copy-start | bytes 884740
  90.5 6.9 %slice-start = ((bf16[256,576]{1,0:T(8,128)(2,1)}), bf16[192,576]{1,0:T(8,128)(2,1)S(1)}, s32[]{:S(2)}) async-start(bf16[256,576]{1,0:T(8,128)(2,1)} %copy-done.5), calls=%async_computation.6 | async-start | bytes 491520 | tf_op jit(solution)/shard_map/slice | solution.py:563
  90.5 43.0 %all-to-all-start.3 = ((bf16[128,2,1792]{2,1,0:T(2,128)(2,1)}), bf16[128,2,1792]{2,1,0:T(2,128)(2,1)S(1)}, u32[]{:S(2)}, u32[]{:S(2)}) async-start(bf16[128,2,1792]{2,1,0:T(2,128)(2,1)} %reshape.262), calls=%async_computation.3 | async-start | bytes 1835008 | tf_op jit(solution)/shard_map/all_to_all | solution.py:557
  97.0 0.9 slice-start.1
  97.3 1.0 slice-start.2
  133.9 12.6 %collective-permute-start.10 = (bf16[256,1792]{1,0:T(8,128)(2,1)S(1)}, bf16[256,1792]{1,0:T(8,128)(2,1)S(1)}, u32[]{:S(2)}, u32[]{:S(2)}) collective-permute-start(bf16[256,1792]{1,0:T(8,128)(2,1)S(1)} %reshape.263), channel_id=1, source_target_pairs={{0,96},{1,33},{2,98},{3,35},{4,100},{5,37},{6,102},{7,39},{8,104},... | collective-permute-start | bytes 2752520 | tf_op jit(solution)/shard_map/ppermute | solution.py:568
  135.6 29.1 %all-to-all-start.4 = ((bf16[32,24,576]{2,1,0:T(8,128)(2,1)}), bf16[32,24,576]{2,1,0:T(8,128)(2,1)S(1)}, u32[]{:S(2)}, u32[]{:S(2)}) async-start(bf16[32,24,576]{2,1,0:T(8,128)(2,1)} %maximum_bitcast_fusion), calls=%async_computation.4 | async-start | bytes 1966080 | tf_op jit(solution)/shard_map/all_to_all | solution.py:569
  149.8 6.8 %collective-permute-start.11 = (bf16[256,512]{1,0:T(8,128)(2,1)S(1)}, bf16[256,512]{1,0:T(8,128)(2,1)S(1)}, u32[]{:S(2)}, u32[]{:S(2)}) collective-permute-start(bf16[256,512]{1,0:T(8,128)(2,1)S(1)} %pad_maximum_fusion.3), channel_id=1, source_target_pairs={{0,32},{1,97},{2,34},{3,99},{4,36},{5,101},{6,38},{7,103},{8,40},{... | collective-permute-start | bytes 786440 | tf_op jit(solution)/shard_map/ppermute | solution.py:580
  156.8 3.9 %collective-permute-start.12 = (bf16[256,256]{1,0:T(8,128)(2,1)S(1)}, bf16[256,256]{1,0:T(8,128)(2,1)S(1)}, u32[]{:S(2)}, u32[]{:S(2)}) collective-permute-start(bf16[256,256]{1,0:T(8,128)(2,1)S(1)} %fusion.54), channel_id=1, source_target_pairs={{32,0},{64,32},{96,64},{0,96},{33,1},{65,33},{97,65},{1,97},{34,2}... | collective-permute-start | bytes 393224 | tf_op jit(solution)/shard_map/ppermute | solution.py:45
  157.6 5.4 %collective-permute-start.13 = (bf16[256,256]{1,0:T(8,128)(2,1)S(1)}, bf16[256,256]{1,0:T(8,128)(2,1)S(1)}, u32[]{:S(2)}, u32[]{:S(2)}) collective-permute-start(bf16[256,256]{1,0:T(8,128)(2,1)S(1)} %fusion.54), channel_id=1, source_target_pairs={{96,0},{0,32},{32,64},{64,96},{97,1},{1,33},{33,65},{65,97},{98,2}... | collective-permute-start | bytes 393224 | tf_op jit(solution)/shard_map/ppermute | solution.py:45
  158.3 6.7 %collective-permute-start.14 = (bf16[256,256]{1,0:T(8,128)(2,1)S(1)}, bf16[256,256]{1,0:T(8,128)(2,1)S(1)}, u32[]{:S(2)}, u32[]{:S(2)}) collective-permute-start(bf16[256,256]{1,0:T(8,128)(2,1)S(1)} %fusion.54), channel_id=1, source_target_pairs={{64,0},{96,32},{0,64},{32,96},{65,1},{97,33},{1,65},{33,97},{66,2}... | collective-permute-start | bytes 393224 | tf_op jit(solution)/shard_map/ppermute | solution.py:45
  170.8 11.4 %copy-start.10 = (f32[512]{0:T(512)S(1)}, f32[512]{0:T(512)}, u32[]{:S(2)}) copy-start(f32[512]{0:T(512)} %param.21) | copy-start | bytes 6148
  170.8 28.4 %all-to-all-start.5 = ((bf16[128,2,1792]{2,1,0:T(2,128)(2,1)}), bf16[128,2,1792]{2,1,0:T(2,128)(2,1)S(1)}, u32[]{:S(2)}, u32[]{:S(2)}) async-start(bf16[128,2,1792]{2,1,0:T(2,128)(2,1)} %reshape.271), calls=%async_computation.5 | async-start | bytes 1835008 | tf_op jit(solution)/shard_map/all_to_all | solution.py:597

commit v9 on v7

--- a/solution.py
+++ b/solution.py
@@ -184,7 +184,7 @@
 def attend_kernel(slots_ref, *refs, blocks):
     rows_in = refs[:blocks]
     cos_ref, sin_ref, gain_ref, new_ref, query_ref = refs[blocks : blocks + 5]
-    out_ref, rest_ref, keys, query, fresh, held_out, sems = refs[blocks + 5 :]
+    out_ref, rest_ref, keys, query, fresh, held_out, spare, sems, spare_sem = refs[blocks + 5 :]
     number = slots_ref[0, 4]
 
     def fetch(slot):
@@ -250,7 +250,10 @@
 
     @pl.loop(sent, number)
     def _(slot):
-        rest_ref[slot - sent] = one(slot).astype(BF)
+        spare[...] = one(slot).astype(BF)
+        copy = pltpu.make_async_copy(spare, rest_ref.at[slot - sent], spare_sem)
+        copy.start()
+        copy.wait()
 
 
 def attend(slots, rows, cosine, sine, gain, new_rows, queries, most_slots):
@@ -271,13 +274,15 @@
         in_specs=[pl.BlockSpec(memory_space=pltpu.SMEM)]
         + [whole] * (blocks + 4)
         + [pl.BlockSpec(memory_space=pltpu.HBM)],
-        out_specs=(whole, whole),
+        out_specs=(whole, pl.BlockSpec(memory_space=pltpu.HBM)),
         scratch_shapes=[
             pltpu.VMEM((total_rows, queries.shape[2]), BF),
             pltpu.VMEM((most_slots,) + queries.shape[1:], BF),
             pltpu.VMEM(new_rows.shape, F32),
             pltpu.VMEM((SLOTS, heads, LAT), F32),
+            pltpu.VMEM((heads, LAT), BF),
             pltpu.SemaphoreType.DMA((most_slots,)),
+            pltpu.SemaphoreType.DMA,
         ],
         compiler_params=pltpu.CompilerParams(vmem_limit_bytes=VMEM),
         cost_estimate=pl.CostEstimate(
@@ -287,17 +292,7 @@
     )(slots, *rows, cosine, sine, gain, new_rows, queries)
 
 
-def project_kernel(
-    cells_ref, came_ref, more_ref, uv_ref, weight_ref, mine_ref, other_ref, weight, sems
-):
-    step = weight.shape[1] // 4
-    spans = [slice(i * step, (i + 1) * step) for i in range(4)]
-    copies = [
-        pltpu.make_async_copy(weight_ref.at[:, span], weight.at[:, span], sems.at[i])
-        for i, span in enumerate(spans)
-    ]
-    for copy in copies:
-        copy.start()
+def project_kernel(cells_ref, came_ref, more_ref, uv_ref, weight_ref, mine_ref, other_ref):
     requests = cells_ref.shape[0]
     sources, heads, slots, _ = came_ref.shape
     cells = sources * slots
@@ -312,9 +307,10 @@
         )
     projected = jnp.concatenate(projected, axis=1)
     keep = mine_ref.shape[0]
-    for span, copy in zip(spans, copies):
-        copy.wait()
-        sums = jnp.dot(projected, weight[:, span], preferred_element_type=F32).astype(BF)
+    step = weight_ref.shape[1] // 4
+    for first in range(0, weight_ref.shape[1], step):
+        span = slice(first, first + step)
+        sums = jnp.dot(projected, weight_ref[:, span], preferred_element_type=F32).astype(BF)
         mine_ref[:, span] = sums[:keep]
         other_ref[:, span] = sums[keep:]
 
@@ -325,9 +321,8 @@
     return pl.pallas_call(
         project_kernel,
         out_shape=(half, half),
-        in_specs=[whole] * 4 + [pl.BlockSpec(memory_space=pltpu.HBM)],
+        in_specs=[whole] * 5,
         out_specs=(whole, whole),
-        scratch_shapes=[pltpu.VMEM(w_out.shape, BF), pltpu.SemaphoreType.DMA((4,))],
         compiler_params=pltpu.CompilerParams(vmem_limit_bytes=32 * 1024 * 1024),
         cost_estimate=pl.CostEstimate(
             flops=4 * 10**8, bytes_accessed=6 * 10**6, transcendentals=0
@@ -359,6 +354,37 @@
         ),
         name="pair_sum",
     )(mine, other)
+
+
+def gate_up_kernel(rows_ref, gate_ref, up_ref, *refs):
+    base_ref, out_ref = refs if len(refs) == 2 else (None, refs[0])
+    half = gate_ref.shape[2]
+    for i, weight_ref in enumerate((gate_ref, up_ref)):
+        span = slice(i * half, (i + 1) * half)
+        sums = jnp.dot(rows_ref[...], weight_ref[0], preferred_element_type=F32)
+        if base_ref is not None:
+            sums = sums + base_ref[:, span]
+        out_ref[:, span] = sums.astype(out_ref.dtype)
+
+
+def gate_up(rows, gate, up, quarter, base=None):
+    half = gate.shape[2]
+    shape = (rows.shape[0], 2 * half)
+    whole = pl.BlockSpec(shape, lambda i: (0, 0))
+    weight = pl.BlockSpec((1,) + gate.shape[1:], lambda i: (quarter, 0, 0))
+    return pl.pallas_call(
+        gate_up_kernel,
+        grid=(1,),
+        out_shape=jax.ShapeDtypeStruct(shape, F32 if base is None else BF),
+        in_specs=[pl.BlockSpec(rows.shape, lambda i: (0, 0)), weight, weight]
+        + ([] if base is None else [whole]),
+        out_specs=whole,
+        compiler_params=pltpu.CompilerParams(vmem_limit_bytes=32 * 1024 * 1024),
+        cost_estimate=pl.CostEstimate(
+            flops=5 * 10**8, bytes_accessed=4 * 10**6, transcendentals=0
+        ),
+        name="gate_up",
+    )(rows, gate, up, *(() if base is None else (base,)))
 
 
 def shards(
@@ -514,8 +540,7 @@
         tiled=True,
         axis_index_groups=[[2 * i + c for i in range(chips)] for c in range(2)],
     )
-    chip_sums, up_came, down_far = lax.optimization_barrier((chip_sums, up_came, down_far))
-    down_far = shift(down_far, 2, dp_count, "dp")
+    chip_sums, up_came = lax.optimization_barrier((chip_sums, up_came))
     attention_out = jnp.sum(chip_sums.astype(F32), axis=0)
     residual = resid[0].astype(F32) + attention_out
     normed = (
@@ -557,22 +582,24 @@
     to_rows = jnp.concatenate(
         [block[:local_rows].reshape(local_units, UNIT, width) for block in rows], axis=0
     ).transpose(1, 0, 2)
-    arrived, down_near, down_far, down_last, to_rows = lax.optimization_barrier(
-        (arrived, down_near, down_far, down_last, to_rows)
+    arrived, down_near, down_last, to_rows = lax.optimization_barrier(
+        (arrived, down_near, down_last, to_rows)
     )
     beside = lax.ppermute(arrived, ("dp", "expert"), token_perm)
     dealt = lax.all_to_all(to_rows, "expert", split_axis=0, concat_axis=0, tiled=True)
 
     gate_own, up_own = width_half(w_gate, my_quarter), width_half(w_up, my_quarter)
-    weights = (gate_came, up_came, gate_own, up_own)
-    first = [jnp.dot(arrived, weight[0], preferred_element_type=F32) for weight in weights]
-    beside, *first = lax.optimization_barrier((beside, *first))
-    gate_given, up_given, gate_sum, up_sum = (
+    own_halves = (gate_own, up_own)
+    first = [jnp.dot(arrived, weight[0], preferred_element_type=F32) for weight in own_halves]
+    given = gate_up(arrived, gate_came, up_came, 0)
+    beside, given, down_far, *first = lax.optimization_barrier((beside, given, down_far, *first))
+    given = gate_up(beside, gate_came, up_came, 1, given)
+    given = lax.ppermute(given, ("dp", "expert"), weight_perm).astype(F32)
+    down_far = shift(down_far, 2, dp_count, "dp")
+    gate_sum, up_sum = (
         part + jnp.dot(beside, weight[1], preferred_element_type=F32)
-        for part, weight in zip(first, weights)
-    )
-    given = jnp.concatenate([gate_given, up_given], axis=1).astype(BF)
-    given = lax.ppermute(given, ("dp", "expert"), weight_perm).astype(F32)
+        for part, weight in zip(first, own_halves)
+    )
     half = gate_sum.shape[1]
     hidden = (
         jax.nn.silu(gate_sum + given[:, :half]) * (up_sum + given[:, half:])

time: 197 us -> 196 us (level)
  matrix products: 18.5 us -> 9.8 us
  waiting for transfers between devices: 81.4 us -> 88.1 us
  starting transfers between devices: 55.1 us -> 49.9 us
  local copies, waits for them, and re-layouts: 13.3 us -> 16.5 us
  Pallas kernels: 19.3 us -> 22.1 us
    all_to_all x1, waiting for transfers between devices: 10.4 us -> 15.3 us  [shards(): lax.all_to_all(outgoing, ('dp', 'expert'), split_axis=0, concat_axis=0, t...]
    dot_general x4 -> x2, matrix products: 6.35 us -> 2 us  [shards(): jnp.dot(beside, weight[1], preferred_element_type=F32)]
    dot_general x4 -> x2, matrix products: 6.34 us -> 2.01 us  [shards(): jnp.dot(arrived, weight[0], preferred_element_type=F32)]
    pallas_call x0 -> x2, Pallas kernels: none -> 3.78 us  [gate_up(): pl.pallas_call(gate_up_kernel, grid=(1,), out_shape=jax.ShapeDtypeStruct(...]
    all_to_all x1, starting transfers between devices: 9.11 us -> 5.57 us  [shards(): lax.all_to_all(to_rows, 'expert', split_axis=0, concat_axis=0, tiled=True)]
    unnamed x30 -> x36, local copies, waits for them, and re-layouts: 2.11 us -> 5.33 us
  transfers between devices with their start and end apart: 20 -> 20, of which waited for: 12 -> 10; matrix products, arithmetic and copies ran while one was open for 14% -> 9% of each run, Pallas kernels for 10% -> 11%
where the time goes in v9:
time: 196 us; the launch traced here: 195 us
  waiting for transfers between devices  88.1 us (45%)
  starting transfers between devices  49.9 us (25%)
  Pallas kernels  22.1 us (11%)
  local copies, waits for them, and re-layouts  16.5 us (8%)
  matrix products  9.8 us (5%)
  other arithmetic  6.14 us (3%)
  between operations  2.08 us (1%)
    ppermute x9, waiting for transfers between devices, shift(): return lax.ppermute(x, axis, [((i + step) % size, i) for i in range(size)])  27.6 us
    all_to_all x1, waiting for transfers between devices, shards(): lax.all_to_all(out.astype(BF).reshape(devices, capacity, piece), ('dp', '...  16.5 us
    all_to_all x1, waiting for transfers between devices, shards(): lax.all_to_all(outgoing, ('dp', 'expert'), split_axis=0, concat_axis=0, t...  15.3 us
    all_to_all x1, waiting for transfers between devices, shards(): lax.all_to_all(pair_sums, 'expert', split_axis=0, concat_axis=0, tiled=Tr...  12.1 us
    all_to_all x1, starting transfers between devices, to_heads(): lax.all_to_all(part, 'expert', split_axis=0, concat_axis=0, tiled=True)  10.4 us
    ppermute x9, starting transfers between devices, shift(): return lax.ppermute(x, axis, [((i + step) % size, i) for i in range(size)])  9.95 us
    all_to_all x1, waiting for transfers between devices, to_heads(): lax.all_to_all(part, 'expert', split_axis=0, concat_axis=0, tiled=True)  9.07 us
    pallas_call x1, Pallas kernels, attend(): pl.pallas_call(body, out_shape=(jax.ShapeDtypeStruct((heads, SLOTS, LAT),...  8.51 us
  transfers between devices with their start and end apart: 20, of which 10 were waited for; matrix products, arithmetic and copies ran while one was open for 9% of the time, Pallas kernels for 11%

profile of v9, /device:TPU:1, one launch (start us, length us, event | category | flops | bytes accessed | tf_op | source)
XLA Modules:
  0.0 194.7 jit_solution(10619630649132631131)
XLA Ops:
  0.6 0.9 slice.98
  1.5 1.4 collective-permute-start
  2.9 3.4 %collective-permute-done = bf16[64,576]{1,0:T(8,128)(2,1)S(1)} collective-permute-done((bf16[64,576]{1,0:T(8,128)(2,1)S(1)}, bf16[64,576]{1,0:T(8,128)(2,1)S(1)}, u32[]{:S(2)}, u32[]{:S(2)}) %collective-permute-start) | collective-permute-done | bytes 73760 | tf_op jit(solution)/shard_map/ppermute | solution.py:420
  6.3 1.0 pad_maximum_fusion.3.refs_1_
  7.3 2.5 %collective-permute-start.1 = (bf16[256,576]{1,0:T(8,128)(2,1)S(1)}, bf16[256,576]{1,0:T(8,128)(2,1)S(1)}, u32[]{:S(2)}, u32[]{:S(2)}) collective-permute-start(bf16[256,576]{1,0:T(8,128)(2,1)S(1)} %pad_maximum_fusion.3.refs_1_), channel_id=1, source_target_pairs={{32,0},{64,32},{96,64},{0,96},{33,1},{65,33},{97,65},{1,97},{34,2}... | collective-permute-start | bytes 884744 | tf_op jit(solution)/shard_map/ppermute | solution.py:45
  11.0 0.7 broadcast_in_dim.190.refs_1_
  11.8 0.7 broadcast_in_dim.191.refs_2_
  12.4 1.0 tables.1
  14.2 6.3 %weight_slices.1 = (bf16[2,1792,256]{2,1,0:T(8,128)(2,1)}, bf16[2,1792,256]{2,1,0:T(8,128)(2,1)}, bf16[256,1792]{1,0:T(8,128)(2,1)}, bf16[256,1792]{1,0:T(8,128)(2,1)}, bf16[256,1792]{1,0:T(8,128)(2,1)}) custom-call(s32[5]{0:T(128)} %stack.59.at_ref, bf16[1,7168,256]{2,1,0:T(8,128)(2,1)} %gate_ref.1, bf16[1,7168,256]{2,1,0:T(8,128)(2,1)} %up_ref.1, ...), custom_call_target="tpu_custom_call" | custom-call | flops 1000 | bytes 4096 | tf_op jit(solution)/shard_map/weight_slices/pallas_call | solution.py:172
  20.6 5.3 %collective-permute-done.3.refs_4_ = bf16[256,576]{1,0:T(8,128)(2,1)S(1)} collective-permute-done((bf16[256,576]{1,0:T(8,128)(2,1)S(1)}, bf16[256,576]{1,0:T(8,128)(2,1)S(1)}, u32[]{:S(2)}, u32[]{:S(2)}) %collective-permute-start.3) | collective-permute-done | bytes 294944 | tf_op jit(solution)/shard_map/ppermute | solution.py:45
  25.9 0.7 copy-done.9
  26.6 0.7 slice_reduce_fusion.1
  28.0 8.5 %attend.1 = (bf16[64,8,512]{2,1,0:T(8,128)(2,1)}, bf16[16,64,512]{2,1,0:T(8,128)(2,1)S(1)}) custom-call(s32[32,128]{1,0:T(8,128)S(1)} %get-tuple-element.79.refs_0_, bf16[256,576]{1,0:T(8,128)(2,1)} %copy-done.5, bf16[256,576]{1,0:T(8,128)(2,1)} %copy-done.7, bf16[256,576]{1,0:T(8,128)(2,1)} %copy-done.8, bf16[256,576]{1,0:T(8,128)(2,1)} %copy-done.9, ...), custom_call_target="tpu_custom_call" | custom-call | flops 100000000 | bytes 4000000 | tf_op jit(solution)/shard_map/attend/pallas_call | solution.py:268
  36.6 10.4 %all-to-all-start.1 = ((bf16[64,8,512]{2,1,0:T(8,128)(2,1)}), bf16[64,8,512]{2,1,0:T(8,128)(2,1)S(1)}, u32[]{:S(2)}, u32[]{:S(2)}) async-start(bf16[64,8,512]{2,1,0:T(8,128)(2,1)} %get-tuple-element.84), calls=%async_computation.1 | async-start | bytes 1048576 | tf_op jit(solution)/shard_map/all_to_all | solution.py:492
  47.1 2.5 %collective-permute-start.6 = (bf16[2,1792,256]{2,1,0:T(8,128)(2,1)}, bf16[2,1792,256]{2,1,0:T(8,128)(2,1)}, u32[]{:S(2)}, u32[]{:S(2)}) collective-permute-start(bf16[2,1792,256]{2,1,0:T(8,128)(2,1)} %get-tuple-element.94), channel_id=1, source_target_pairs={{0,32},{1,97},{2,34},{3,99},{4,36},{5,101},{6,38},{7,103},{8,40},{... | collective-permute-start | bytes 5505032 | tf_op jit(solution)/shard_map/ppermute | solution.py:476
  49.6 9.1 %all-to-all-done.1 = bf16[64,8,512]{2,1,0:T(8,128)(2,1)S(1)} async-done(((bf16[64,8,512]{2,1,0:T(8,128)(2,1)}), bf16[64,8,512]{2,1,0:T(8,128)(2,1)S(1)}, u32[]{:S(2)}, u32[]{:S(2)}) %all-to-all-start.1) | async-done | bytes 524320 | tf_op jit(solution)/shard_map/all_to_all | solution.py:492
  58.6 2.7 %copy-done.2 = bf16[256,7168]{1,0:T(8,128)(2,1)S(1)} copy-done((bf16[256,7168]{1,0:T(8,128)(2,1)S(1)}, bf16[256,7168]{1,0:T(8,128)(2,1)}, u32[]{:S(2)}) %copy-start.2) | copy-done | bytes 3670040
  61.3 1.2 project.1
  63.2 1.7 collective-permute-done.5.other_ref
  64.8 1.4 pair_sum.1
  66.2 3.6 %all-to-all-start.2 = ((bf16[16,3,7168]{2,1,0:T(4,128)(2,1)}), bf16[16,3,7168]{2,1,0:T(4,128)(2,1)S(1)}, u32[]{:S(2)}, u32[]{:S(2)}) async-start(bf16[16,3,7168]{2,1,0:T(4,128)(2,1)} %pair_sum.1), calls=%async_computation.2 | async-start | bytes 1835008 | tf_op jit(solution)/shard_map/all_to_all | solution.py:535
  70.5 2.5 %collective-permute-start.7 = (bf16[256,1792]{1,0:T(8,128)(2,1)}, bf16[256,1792]{1,0:T(8,128)(2,1)}, u32[]{:S(2)}, u32[]{:S(2)}) collective-permute-start(bf16[256,1792]{1,0:T(8,128)(2,1)} %get-tuple-element.96), channel_id=1, source_target_pairs={{32,0},{64,32},{96,64},{0,96},{33,1},{65,33},{97,65},{1,97},{34,2}... | collective-permute-start | bytes 2752520 | tf_op jit(solution)/shard_map/ppermute | solution.py:45
  73.0 12.1 %all-to-all-done.2 = bf16[16,3,7168]{2,1,0:T(4,128)(2,1)S(1)} async-done(((bf16[16,3,7168]{2,1,0:T(4,128)(2,1)}), bf16[16,3,7168]{2,1,0:T(4,128)(2,1)S(1)}, u32[]{:S(2)}, u32[]{:S(2)}) %all-to-all-start.2) | async-done | bytes 688160 | tf_op jit(solution)/shard_map/all_to_all | solution.py:535
  87.1 1.3 reshape.262
  88.3 6.4 %all-to-all-start.3 = ((bf16[128,2,1792]{2,1,0:T(2,128)(2,1)}), bf16[128,2,1792]{2,1,0:T(2,128)(2,1)S(1)}, u32[]{:S(2)}, u32[]{:S(2)}) async-start(bf16[128,2,1792]{2,1,0:T(2,128)(2,1)} %reshape.262), calls=%async_computation.3 | async-start | bytes 1835008 | tf_op jit(solution)/shard_map/all_to_all | solution.py:577
  95.7 1.5 maximum_bitcast_fusion
  97.2 15.3 %all-to-all-done.3 = bf16[128,2,1792]{2,1,0:T(2,128)(2,1)S(1)} async-done(((bf16[128,2,1792]{2,1,0:T(2,128)(2,1)}), bf16[128,2,1792]{2,1,0:T(2,128)(2,1)S(1)}, u32[]{:S(2)}, u32[]{:S(2)}) %all-to-all-start.3) | async-done | bytes 917536 | tf_op jit(solution)/shard_map/all_to_all | solution.py:577
  113.2 2.2 %dynamic-slice_bitcast_fusion = bf16[256,1792]{1,0:T(8,128)(2,1)} fusion(bf16[1,256,7168]{2,1,0:T(8,128)(2,1)} %down_ref.1, s32[]{:T(128)S(6)} %select_n.230), kind=kLoop, calls=%fused_computation.65 | loop fusion | bytes 1835012 | tf_op jit(solution)/shard_map/dynamic_slice | solution.py:611
  115.4 5.6 %all-to-all-start.4 = ((bf16[32,24,576]{2,1,0:T(8,128)(2,1)}), bf16[32,24,576]{2,1,0:T(8,128)(2,1)S(1)}, u32[]{:S(2)}, u32[]{:S(2)}) async-start(bf16[32,24,576]{2,1,0:T(8,128)(2,1)} %maximum_bitcast_fusion), calls=%async_computation.4 | async-start | bytes 1966080 | tf_op jit(solution)/shard_map/all_to_all | solution.py:589
  121.0 1.5 copy-done.1
  122.5 2.0 %gate_up.2.refs_0_ = f32[256,512]{1,0:T(8,128)S(1)} custom-call(bf16[256,1792]{1,0:T(8,128)(2,1)S(1)} %reshape.263.rows_ref, bf16[2,1792,256]{2,1,0:T(8,128)(2,1)S(1)} %copy-done.1, bf16[2,1792,256]{2,1,0:T(8,128)(2,1)} %collective-permute-done.6.up_ref), custom_call_target="tpu_custom_call" | custom-call | flops 500000000 | bytes 4000000 | tf_op jit(solution)/shard_map/gate_up/pallas_call | solution.py:375
  125.2 1.6 fusion.37
  126.8 1.8 gate_up.3
  128.7 1.9 collective-permute-start.10
  131.1 1.6 fusion.33
  132.7 2.6 %collective-permute-done.10 = bf16[256,512]{1,0:T(8,128)(2,1)S(1)} collective-permute-done((bf16[256,512]{1,0:T(8,128)(2,1)S(1)}, bf16[256,512]{1,0:T(8,128)(2,1)S(1)}, u32[]{:S(2)}, u32[]{:S(2)}) %collective-permute-start.10) | collective-permute-done | bytes 262176 | tf_op jit(solution)/shard_map/ppermute | solution.py:597
  135.4 3.0 %collective-permute-start.11 = (bf16[256,256]{1,0:T(8,128)(2,1)S(1)}, bf16[256,256]{1,0:T(8,128)(2,1)S(1)}, u32[]{:S(2)}, u32[]{:S(2)}) collective-permute-start(bf16[256,256]{1,0:T(8,128)(2,1)S(1)} %fusion.50), channel_id=1, source_target_pairs={{32,0},{64,32},{96,64},{0,96},{33,1},{65,33},{97,65},{1,97},{34,2}... | collective-permute-start | bytes 393224 | tf_op jit(solution)/shard_map/ppermute | solution.py:45
  139.2 0.8 fusion.81
  140.0 19.1 %collective-permute-done.11 = bf16[256,256]{1,0:T(8,128)(2,1)S(1)} collective-permute-done((bf16[256,256]{1,0:T(8,128)(2,1)S(1)}, bf16[256,256]{1,0:T(8,128)(2,1)S(1)}, u32[]{:S(2)}, u32[]{:S(2)}) %collective-permute-start.11) | collective-permute-done | bytes 131104 | tf_op jit(solution)/shard_map/ppermute | solution.py:45
  159.1 3.1 %collective-permute-done.13 = bf16[256,256]{1,0:T(8,128)(2,1)S(1)} collective-permute-done((bf16[256,256]{1,0:T(8,128)(2,1)S(1)}, bf16[256,256]{1,0:T(8,128)(2,1)S(1)}, u32[]{:S(2)}, u32[]{:S(2)}) %collective-permute-start.13) | collective-permute-done | bytes 131104 | tf_op jit(solution)/shard_map/ppermute | solution.py:45
  162.8 3.1 %fusion.24 = bf16[256,1792]{1,0:T(8,128)(2,1)S(1)} fusion(bf16[256,1024]{1,0:T(8,128)(2,1)S(1)} %pad_maximum_fusion.2, bf16[256,1792]{1,0:T(8,128)(2,1)} %collective-permute-done.8, bf16[256,1792]{1,0:T(8,128)(2,1)} %collective-permute-done.14, bf16[256,1792]{1,0:T(8,128)(2,1)} %collective-permute-done.7, bf16[256,1792]{1,0:T(8,128)(2,1)} %dynamic-slice_bitcast_fusion), kind=kOutput, calls=%fused_computation.44 | convolution fusion | flops 954662912 | bytes 5111808 | tf_op jit(solution)/shard_map/dot_general | solution.py:612
  165.9 1.3 reshape.271
  167.2 7.2 %all-to-all-start.5 = ((bf16[128,2,1792]{2,1,0:T(2,128)(2,1)}), bf16[128,2,1792]{2,1,0:T(2,128)(2,1)S(1)}, u32[]{:S(2)}, u32[]{:S(2)}) async-start(bf16[128,2,1792]{2,1,0:T(2,128)(2,1)} %reshape.271), calls=%async_computation.5 | async-start | bytes 1835008 | tf_op jit(solution)/shard_map/all_to_all | solution.py:613
  174.8 0.8 pad_maximum_fusion.4
  175.6 16.5 %all-to-all-done.5 = bf16[128,2,1792]{2,1,0:T(2,128)(2,1)S(1)} async-done(((bf16[128,2,1792]{2,1,0:T(2,128)(2,1)}), bf16[128,2,1792]{2,1,0:T(2,128)(2,1)S(1)}, u32[]{:S(2)}, u32[]{:S(2)}) %all-to-all-start.5) | async-done | bytes 917536 | tf_op jit(solution)/shard_map/all_to_all | solution.py:613
  192.1 0.7 copy.58
  192.9 0.7 dot_general.54
  193.6 1.2 fusion.15
  (110 shorter events, 9.8 us)
Async XLA Ops:
  1.5 4.8 %collective-permute-start = (bf16[64,576]{1,0:T(8,128)(2,1)S(1)}, bf16[64,576]{1,0:T(8,128)(2,1)S(1)}, u32[]{:S(2)}, u32[]{:S(2)}) collective-permute-start(bf16[64,576]{1,0:T(8,128)(2,1)S(1)} %slice.98), channel_id=1, source_target_pairs={{1,0},{2,1},{3,2},{4,3},{5,4},{6,5},{7,6},{8,7},{9,8},{10,9},{11,1... | collective-permute-start | bytes 221192 | tf_op jit(solution)/shard_map/ppermute | solution.py:420
  7.3 13.2 %copy-start.5 = (bf16[256,576]{1,0:T(8,128)(2,1)}, bf16[256,576]{1,0:T(8,128)(2,1)S(1)}, u32[]{:S(2)}) copy-start(bf16[256,576]{1,0:T(8,128)(2,1)S(1)} %pad_maximum_fusion.3.refs_1_) | copy-start | bytes 884740
  7.3 13.2 %collective-permute-start.1 = (bf16[256,576]{1,0:T(8,128)(2,1)S(1)}, bf16[256,576]{1,0:T(8,128)(2,1)S(1)}, u32[]{:S(2)}, u32[]{:S(2)}) collective-permute-start(bf16[256,576]{1,0:T(8,128)(2,1)S(1)} %pad_maximum_fusion.3.refs_1_), channel_id=1, source_target_pairs={{32,0},{64,32},{96,64},{0,96},{33,1},{65,33},{97,65},{1,97},{34,2}... | collective-permute-start | bytes 884744 | tf_op jit(solution)/shard_map/ppermute | solution.py:45
  9.9 10.7 %collective-permute-start.2 = (bf16[256,576]{1,0:T(8,128)(2,1)S(1)}, bf16[256,576]{1,0:T(8,128)(2,1)S(1)}, u32[]{:S(2)}, u32[]{:S(2)}) collective-permute-start(bf16[256,576]{1,0:T(8,128)(2,1)S(1)} %pad_maximum_fusion.3.refs_1_), channel_id=1, source_target_pairs={{64,0},{96,32},{0,64},{32,96},{65,1},{97,33},{1,65},{33,97},{66,2}... | collective-permute-start | bytes 884744 | tf_op jit(solution)/shard_map/ppermute | solution.py:45
  10.4 15.5 %collective-permute-start.3 = (bf16[256,576]{1,0:T(8,128)(2,1)S(1)}, bf16[256,576]{1,0:T(8,128)(2,1)S(1)}, u32[]{:S(2)}, u32[]{:S(2)}) collective-permute-start(bf16[256,576]{1,0:T(8,128)(2,1)S(1)} %pad_maximum_fusion.3.refs_1_), channel_id=1, source_target_pairs={{96,0},{0,32},{32,64},{64,96},{97,1},{1,33},{33,65},{65,97},{98,2}... | collective-permute-start | bytes 884744 | tf_op jit(solution)/shard_map/ppermute | solution.py:45
  14.2 13.8 %copy-start.13 = (s32[384]{0:T(512)S(1)}, s32[384]{0:T(512)}, u32[]{:S(2)}) copy-start(s32[384]{0:T(512)} %param.23) | copy-start | bytes 4612
  20.5 5.3 %copy-start.7 = (bf16[256,576]{1,0:T(8,128)(2,1)}, bf16[256,576]{1,0:T(8,128)(2,1)S(1)}, u32[]{:S(2)}) copy-start(bf16[256,576]{1,0:T(8,128)(2,1)S(1)} %collective-permute-done.1.refs_2_) | copy-start | bytes 884740
  20.5 5.3 %copy-start.8 = (bf16[256,576]{1,0:T(8,128)(2,1)}, bf16[256,576]{1,0:T(8,128)(2,1)S(1)}, u32[]{:S(2)}) copy-start(bf16[256,576]{1,0:T(8,128)(2,1)S(1)} %collective-permute-done.2.refs_3_) | copy-start | bytes 884740
  25.9 0.7 copy-start.9
  26.6 32.0 %collective-permute-start.4 = (bf16[2,1792,256]{2,1,0:T(8,128)(2,1)}, bf16[2,1792,256]{2,1,0:T(8,128)(2,1)S(1)}, u32[]{:S(2)}, u32[]{:S(2)}) collective-permute-start(bf16[2,1792,256]{2,1,0:T(8,128)(2,1)} %get-tuple-element.85), channel_id=1, source_target_pairs={{0,32},{1,97},{2,34},{3,99},{4,36},{5,101},{6,38},{7,103},{8,40},{... | collective-permute-start | bytes 5505032 | tf_op jit(solution)/shard_map/ppermute | solution.py:475
  36.6 22.1 %copy-start.3 = (bf16[2,512,128]{2,1,0:T(8,128)(2,1)S(1)}, bf16[2,512,128]{2,1,0:T(8,128)(2,1)}, u32[]{:S(2)}) copy-start(bf16[2,512,128]{2,1,0:T(8,128)(2,1)} %uv_ref.1) | copy-start | bytes 786436
  36.6 26.5 %copy-start.15 = (s32[1,3,8]{2,0,1:T(1,128)S(1)}, s32[1,3,8]{2,0,1:T(1,128)}, u32[]{:S(2)}) copy-start(s32[1,3,8]{2,0,1:T(1,128)} %param.29) | copy-start | bytes 292
  36.6 22.0 %all-to-all-start.1 = ((bf16[64,8,512]{2,1,0:T(8,128)(2,1)}), bf16[64,8,512]{2,1,0:T(8,128)(2,1)S(1)}, u32[]{:S(2)}, u32[]{:S(2)}) async-start(bf16[64,8,512]{2,1,0:T(8,128)(2,1)} %get-tuple-element.84), calls=%async_computation.1 | async-start | bytes 1048576 | tf_op jit(solution)/shard_map/all_to_all | solution.py:492
  47.1 25.9 %collective-permute-start.6 = (bf16[2,1792,256]{2,1,0:T(8,128)(2,1)}, bf16[2,1792,256]{2,1,0:T(8,128)(2,1)}, u32[]{:S(2)}, u32[]{:S(2)}) collective-permute-start(bf16[2,1792,256]{2,1,0:T(8,128)(2,1)} %get-tuple-element.94), channel_id=1, source_target_pairs={{0,32},{1,97},{2,34},{3,99},{4,36},{5,101},{6,38},{7,103},{8,40},{... | collective-permute-start | bytes 5505032 | tf_op jit(solution)/shard_map/ppermute | solution.py:476
  58.6 7.6 %copy-start = (bf16[2,1792,256]{2,1,0:T(8,128)(2,1)}, bf16[2,1792,256]{2,1,0:T(8,128)(2,1)S(1)}, u32[]{:S(2)}) copy-start(bf16[2,1792,256]{2,1,0:T(8,128)(2,1)S(1)} %collective-permute-done.4.gate_ref) | copy-start | bytes 5505028
  58.6 2.7 %copy-start.2 = (bf16[256,7168]{1,0:T(8,128)(2,1)S(1)}, bf16[256,7168]{1,0:T(8,128)(2,1)}, u32[]{:S(2)}) copy-start(bf16[256,7168]{1,0:T(8,128)(2,1)} %weight_ref.1) | copy-start | bytes 11010052
  62.5 22.9 %copy-start.10 = (bf16[1,3,7168]{2,1,0:T(4,128)(2,1)S(1)}, bf16[1,3,7168]{2,1,0:T(4,128)(2,1)}, u32[]{:S(2)}) copy-start(bf16[1,3,7168]{2,1,0:T(4,128)(2,1)} %param.27) | copy-start | bytes 129028
  62.5 23.1 %copy-start.11 = (f32[7168]{0:T(1024)S(1)}, f32[7168]{0:T(1024)}, u32[]{:S(2)}) copy-start(f32[7168]{0:T(1024)} %param.28) | copy-start | bytes 86020
  62.6 2.3 %collective-permute-start.5 = (bf16[48,7168]{1,0:T(8,128)(2,1)S(1)}, bf16[48,7168]{1,0:T(8,128)(2,1)S(1)}, u32[]{:S(2)}, u32[]{:S(2)}) collective-permute-start(bf16[48,7168]{1,0:T(8,128)(2,1)S(1)} %get-tuple-element.93), channel_id=1, source_target_pairs={{0,1},{1,0},{2,3},{3,2},{4,5},{5,4},{6,7},{7,6},{8,9},{9,8},{10,11... | collective-permute-start | bytes 2064392 | tf_op jit(solution)/shard_map/ppermute | solution.py:533
  66.2 18.8 %all-to-all-start.2 = ((bf16[16,3,7168]{2,1,0:T(4,128)(2,1)}), bf16[16,3,7168]{2,1,0:T(4,128)(2,1)S(1)}, u32[]{:S(2)}, u32[]{:S(2)}) async-start(bf16[16,3,7168]{2,1,0:T(4,128)(2,1)} %pair_sum.1), calls=%async_computation.2 | async-start | bytes 1835008 | tf_op jit(solution)/shard_map/all_to_all | solution.py:535
  70.5 42.3 %collective-permute-start.7 = (bf16[256,1792]{1,0:T(8,128)(2,1)}, bf16[256,1792]{1,0:T(8,128)(2,1)}, u32[]{:S(2)}, u32[]{:S(2)}) collective-permute-start(bf16[256,1792]{1,0:T(8,128)(2,1)} %get-tuple-element.96), channel_id=1, source_target_pairs={{32,0},{64,32},{96,64},{0,96},{33,1},{65,33},{97,65},{1,97},{34,2}... | collective-permute-start | bytes 2752520 | tf_op jit(solution)/shard_map/ppermute | solution.py:45
  73.0 39.8 %collective-permute-start.8 = (bf16[256,1792]{1,0:T(8,128)(2,1)}, bf16[256,1792]{1,0:T(8,128)(2,1)}, u32[]{:S(2)}, u32[]{:S(2)}) collective-permute-start(bf16[256,1792]{1,0:T(8,128)(2,1)} %get-tuple-element.97), channel_id=1, source_target_pairs={{96,0},{0,32},{32,64},{64,96},{97,1},{1,33},{33,65},{65,97},{98,2}... | collective-permute-start | bytes 2752520 | tf_op jit(solution)/shard_map/ppermute | solution.py:45
  85.4 9.3 %copy-start.16 = (f32[1,3,8]{2,0,1:T(1,128)S(1)}, f32[1,3,8]{2,0,1:T(1,128)}, u32[]{:S(2)}) copy-start(f32[1,3,8]{2,0,1:T(1,128)} %param.30) | copy-start | bytes 292
  85.4 9.4 %copy-start.14 = (s32[384]{0:T(512)S(1)}, s32[384]{0:T(512)}, u32[]{:S(2)}) copy-start(s32[384]{0:T(512)} %param.22) | copy-start | bytes 4612
  85.5 9.8 %copy-start.6 = (bf16[256,576]{1,0:T(8,128)(2,1)S(1)}, bf16[256,576]{1,0:T(8,128)(2,1)}, u32[]{:S(2)}) copy-start(bf16[256,576]{1,0:T(8,128)(2,1)} %copy-done.5) | copy-start | bytes 884740
  86.9 8.5 %slice-start = ((bf16[256,576]{1,0:T(8,128)(2,1)}), bf16[192,576]{1,0:T(8,128)(2,1)S(1)}, s32[]{:S(2)}) async-start(bf16[256,576]{1,0:T(8,128)(2,1)} %copy-done.7), calls=%async_computation.6 | async-start | bytes 491520 | tf_op jit(solution)/shard_map/slice | solution.py:583
  87.0 8.4 %slice-start.1 = ((bf16[256,576]{1,0:T(8,128)(2,1)}), bf16[192,576]{1,0:T(8,128)(2,1)S(1)}, s32[]{:S(2)}) async-start(bf16[256,576]{1,0:T(8,128)(2,1)} %copy-done.8), calls=%async_computation.7 | async-start | bytes 491520 | tf_op jit(solution)/shard_map/slice | solution.py:583
  87.0 8.5 %slice-start.2 = ((bf16[256,576]{1,0:T(8,128)(2,1)}), bf16[192,576]{1,0:T(8,128)(2,1)S(1)}, s32[]{:S(2)}) async-start(bf16[256,576]{1,0:T(8,128)(2,1)} %copy-done.9), calls=%async_computation.8 | async-start | bytes 491520 | tf_op jit(solution)/shard_map/slice | solution.py:583
  88.3 24.1 %all-to-all-start.3 = ((bf16[128,2,1792]{2,1,0:T(2,128)(2,1)}), bf16[128,2,1792]{2,1,0:T(2,128)(2,1)S(1)}, u32[]{:S(2)}, u32[]{:S(2)}) async-start(bf16[128,2,1792]{2,1,0:T(2,128)(2,1)} %reshape.262), calls=%async_computation.3 | async-start | bytes 1835008 | tf_op jit(solution)/shard_map/all_to_all | solution.py:577
  112.8 14.0 %collective-permute-start.9 = (bf16[256,1792]{1,0:T(8,128)(2,1)S(1)}, bf16[256,1792]{1,0:T(8,128)(2,1)S(1)}, u32[]{:S(2)}, u32[]{:S(2)}) collective-permute-start(bf16[256,1792]{1,0:T(8,128)(2,1)S(1)} %reshape.263.rows_ref), channel_id=1, source_target_pairs={{0,96},{1,33},{2,98},{3,35},{4,100},{5,37},{6,102},{7,39},{8,104},... | collective-permute-start | bytes 2752520 | tf_op jit(solution)/shard_map/ppermute | solution.py:588
  115.4 46.9 %all-to-all-start.4 = ((bf16[32,24,576]{2,1,0:T(8,128)(2,1)}), bf16[32,24,576]{2,1,0:T(8,128)(2,1)S(1)}, u32[]{:S(2)}, u32[]{:S(2)}) async-start(bf16[32,24,576]{2,1,0:T(8,128)(2,1)} %maximum_bitcast_fusion), calls=%async_computation.4 | async-start | bytes 1966080 | tf_op jit(solution)/shard_map/all_to_all | solution.py:589
  121.0 1.5 copy-start.1
  122.5 2.3 %copy-start.4 = (bf16[1,7168,256]{2,1,0:T(8,128)(2,1)S(1)}, bf16[1,7168,256]{2,1,0:T(8,128)(2,1)}, u32[]{:S(2)}) copy-start(bf16[1,7168,256]{2,1,0:T(8,128)(2,1)} %up_ref.1) | copy-start | bytes 11010052
  128.7 6.6 %collective-permute-start.10 = (bf16[256,512]{1,0:T(8,128)(2,1)S(1)}, bf16[256,512]{1,0:T(8,128)(2,1)S(1)}, u32[]{:S(2)}, u32[]{:S(2)}) collective-permute-start(bf16[256,512]{1,0:T(8,128)(2,1)S(1)} %gate_up.3), channel_id=1, source_target_pairs={{0,32},{1,97},{2,34},{3,99},{4,36},{5,101},{6,38},{7,103},{8,40},{... | collective-permute-start | bytes 786440 | tf_op jit(solution)/shard_map/ppermute | solution.py:597
  131.0 31.8 %collective-permute-start.14 = (bf16[256,1792]{1,0:T(8,128)(2,1)}, bf16[256,1792]{1,0:T(8,128)(2,1)}, u32[]{:S(2)}, u32[]{:S(2)}) collective-permute-start(bf16[256,1792]{1,0:T(8,128)(2,1)} %get-tuple-element.110), channel_id=1, source_target_pairs={{64,0},{96,32},{0,64},{32,96},{65,1},{97,33},{1,65},{33,97},{66,2}... | collective-permute-start | bytes 2752520 | tf_op jit(solution)/shard_map/ppermute | solution.py:45
  135.4 23.7 %collective-permute-start.11 = (bf16[256,256]{1,0:T(8,128)(2,1)S(1)}, bf16[256,256]{1,0:T(8,128)(2,1)S(1)}, u32[]{:S(2)}, u32[]{:S(2)}) collective-permute-start(bf16[256,256]{1,0:T(8,128)(2,1)S(1)} %fusion.50), channel_id=1, source_target_pairs={{32,0},{64,32},{96,64},{0,96},{33,1},{65,33},{97,65},{1,97},{34,2}... | collective-permute-start | bytes 393224 | tf_op jit(solution)/shard_map/ppermute | solution.py:45
  138.5 20.7 %collective-permute-start.12 = (bf16[256,256]{1,0:T(8,128)(2,1)S(1)}, bf16[256,256]{1,0:T(8,128)(2,1)S(1)}, u32[]{:S(2)}, u32[]{:S(2)}) collective-permute-start(bf16[256,256]{1,0:T(8,128)(2,1)S(1)} %fusion.50), channel_id=1, source_target_pairs={{64,0},{96,32},{0,64},{32,96},{65,1},{97,33},{1,65},{33,97},{66,2}... | collective-permute-start | bytes 393224 | tf_op jit(solution)/shard_map/ppermute | solution.py:45
  138.5 23.8 %collective-permute-start.13 = (bf16[256,256]{1,0:T(8,128)(2,1)S(1)}, bf16[256,256]{1,0:T(8,128)(2,1)S(1)}, u32[]{:S(2)}, u32[]{:S(2)}) collective-permute-start(bf16[256,256]{1,0:T(8,128)(2,1)S(1)} %fusion.50), channel_id=1, source_target_pairs={{96,0},{0,32},{32,64},{64,96},{97,1},{1,33},{33,65},{65,97},{98,2}... | collective-permute-start | bytes 393224 | tf_op jit(solution)/shard_map/ppermute | solution.py:45
  165.9 8.8 %copy-start.12 = (f32[512]{0:T(512)S(1)}, f32[512]{0:T(512)}, u32[]{:S(2)}) copy-start(f32[512]{0:T(512)} %param.21) | copy-start | bytes 6148
  167.2 24.9 %all-to-all-start.5 = ((bf16[128,2,1792]{2,1,0:T(2,128)(2,1)}), bf16[128,2,1792]{2,1,0:T(2,128)(2,1)S(1)}, u32[]{:S(2)}, u32[]{:S(2)}) async-start(bf16[128,2,1792]{2,1,0:T(2,128)(2,1)} %reshape.271), calls=%async_computation.5 | async-start | bytes 1835008 | tf_op jit(solution)/shard_map/all_to_all | solution.py:613

commit v10 on v9

--- a/solution.py
+++ b/solution.py
@@ -9,7 +9,10 @@
 LAT = 512
 UNIT = 32
 MOST = 3
-SLOTS = 8
+MAIN = 8
+SLOTS = 10
+PARTS = MAIN // (SLOTS - MAIN)
+EXTRA = LAT // PARTS
 VMEM = 58 * 1024 * 1024
 
 eps = 1e-06
@@ -115,9 +118,17 @@
     )
     lines = cells_ref.shape[0]
     line = lax.broadcasted_iota(I32, (lines, count), 0).astype(F32)
-    cell = jnp.where(rank < SLOTS, start_column * SLOTS + rank, -1.0)
-    found = jnp.sum(jnp.where(own & (row == line), cell, 0.0), axis=1, keepdims=True)
-    cells_ref[...] = jnp.broadcast_to(found, cells_ref.shape).astype(I32)
+    first_row = start_column * MAIN
+    main = jnp.where(rank < MAIN, first_row + rank, -1.0 * MAIN)
+    extra = jnp.where(
+        (rank >= MAIN) & (rank < SLOTS), first_row + (rank - MAIN) * PARTS, -1.0 * MAIN
+    )
+    found = [
+        jnp.sum(jnp.where(own & (row == line), cell, 0.0), axis=1, keepdims=True)
+        for cell in (main, extra)
+    ]
+    lane = lax.broadcasted_iota(I32, cells_ref.shape, 1)
+    cells_ref[...] = jnp.where(lane == 0, found[0], found[1]).astype(I32)
 
 
 def tables(where, lengths, owners, sizes):
@@ -212,7 +223,7 @@
     fresh[...] = new_ref[...].astype(F32)
 
     heads = out_ref.shape[0]
-    sent = out_ref.shape[1]
+    sent = SLOTS
     window = MOST * UNIT
     lanes = window + UNIT
     lane = lax.broadcasted_iota(I32, (heads, lanes), 1)
@@ -244,7 +255,11 @@
         fetch(slot).wait()
 
     for slot in range(sent):
-        held_out[slot] = jnp.where(slot < number, one(slot), 0.0)
+        value = jnp.where(slot < number, one(slot), 0.0)
+        if slot < MAIN:
+            held_out[slot, :, :LAT] = value
+        for i in range(PARTS if slot >= MAIN else 0):
+            held_out[(slot - MAIN) * PARTS + i, :, LAT:] = value[:, i * EXTRA : (i + 1) * EXTRA]
 
     out_ref[...] = jnp.swapaxes(held_out[...], 0, 1).astype(BF)
 
@@ -268,7 +283,7 @@
     return pl.pallas_call(
         body,
         out_shape=(
-            jax.ShapeDtypeStruct((heads, SLOTS, LAT), BF),
+            jax.ShapeDtypeStruct((heads, MAIN, LAT + EXTRA), BF),
             jax.ShapeDtypeStruct((most_slots - SLOTS, heads, LAT), BF),
         ),
         in_specs=[pl.BlockSpec(memory_space=pltpu.SMEM)]
@@ -279,7 +294,7 @@
             pltpu.VMEM((total_rows, queries.shape[2]), BF),
             pltpu.VMEM((most_slots,) + queries.shape[1:], BF),
             pltpu.VMEM(new_rows.shape, F32),
-            pltpu.VMEM((SLOTS, heads, LAT), F32),
+            pltpu.VMEM((MAIN, heads, LAT + EXTRA), F32),
             pltpu.VMEM((heads, LAT), BF),
             pltpu.SemaphoreType.DMA((most_slots,)),
             pltpu.SemaphoreType.DMA,
@@ -296,12 +311,19 @@
     requests = cells_ref.shape[0]
     sources, heads, slots, _ = came_ref.shape
     cells = sources * slots
-    pick = cells_ref[:, :1] == lax.broadcasted_iota(I32, (requests, cells), 1)
-    pick = jnp.where(pick, 1.0, 0.0).astype(BF)
+    cell = lax.broadcasted_iota(I32, (requests, cells), 1)
+
+    def pick(at):
+        return jnp.where(at == cell, 1.0, 0.0).astype(BF)
+
+    main = pick(cells_ref[:, :1])
+    extra = [pick(cells_ref[:, 1:2] + i) for i in range(PARTS)]
     projected = []
     for h in range(heads):
-        came = came_ref[:, h].astype(F32).reshape(cells, LAT).astype(BF)
-        rows = jnp.dot(pick, came, preferred_element_type=F32) + more_ref[h].astype(F32)
+        came = came_ref[:, h].astype(F32).reshape(cells, LAT + EXTRA).astype(BF)
+        rows = jnp.dot(main, came[:, :LAT], preferred_element_type=F32)
+        rest = [jnp.dot(part, came[:, LAT:], preferred_element_type=F32) for part in extra]
+        rows = rows + jnp.concatenate(rest, axis=1) + more_ref[h].astype(F32)
         projected.append(
             jnp.dot(rows.astype(BF), uv_ref[h], preferred_element_type=F32).astype(BF)
         )
@@ -490,7 +512,7 @@
 
     def to_heads(part):
         came = lax.all_to_all(part, "expert", split_axis=0, concat_axis=0, tiled=True)
-        return came.reshape(columns, head_share, part.shape[1], LAT)
+        return came.reshape((columns, head_share) + part.shape[1:])
 
     def spill():
         used = jnp.arange(SLOTS, most_slots, dtype=I32) < slot_table_rows[0, 4]
@@ -540,7 +562,9 @@
         tiled=True,
         axis_index_groups=[[2 * i + c for i in range(chips)] for c in range(2)],
     )
-    chip_sums, up_came = lax.optimization_barrier((chip_sums, up_came))
+    cut = down_far.shape[0] // 2
+    chip_sums, up_came, down_far = lax.optimization_barrier((chip_sums, up_came, down_far))
+    far_first = shift(down_far[:cut], 2, dp_count, "dp")
     attention_out = jnp.sum(chip_sums.astype(F32), axis=0)
     residual = resid[0].astype(F32) + attention_out
     normed = (
@@ -582,8 +606,8 @@
     to_rows = jnp.concatenate(
         [block[:local_rows].reshape(local_units, UNIT, width) for block in rows], axis=0
     ).transpose(1, 0, 2)
-    arrived, down_near, down_last, to_rows = lax.optimization_barrier(
-        (arrived, down_near, down_last, to_rows)
+    arrived, down_near, far_first, down_last, to_rows = lax.optimization_barrier(
+        (arrived, down_near, far_first, down_last, to_rows)
     )
     beside = lax.ppermute(arrived, ("dp", "expert"), token_perm)
     dealt = lax.all_to_all(to_rows, "expert", split_axis=0, concat_axis=0, tiled=True)
@@ -595,7 +619,7 @@
     beside, given, down_far, *first = lax.optimization_barrier((beside, given, down_far, *first))
     given = gate_up(beside, gate_came, up_came, 1, given)
     given = lax.ppermute(given, ("dp", "expert"), weight_perm).astype(F32)
-    down_far = shift(down_far, 2, dp_count, "dp")
+    far_second = shift(down_far[cut:], 2, dp_count, "dp")
     gate_sum, up_sum = (
         part + jnp.dot(beside, weight[1], preferred_element_type=F32)
         for part, weight in zip(first, own_halves)
@@ -608,7 +632,7 @@
         [hidden] + [shift(hidden, k, dp_count, "dp") for k in range(1, dp_count)], axis=1
     )
     hidden_all, dealt = lax.optimization_barrier((hidden_all, dealt))
-    downs = jnp.concatenate([lax.dynamic_slice_in_dim(w_down[0], group * piece, piece, 1), down_near, down_far, down_last], axis=0)
+    downs = jnp.concatenate([lax.dynamic_slice_in_dim(w_down[0], group * piece, piece, 1), down_near, far_first, far_second, down_last], axis=0)
     out = jnp.dot(hidden_all, downs, preferred_element_type=F32)
     returned = lax.all_to_all(
         out.astype(BF).reshape(devices, capacity, piece),

time: 196 us -> 204 us (1.041)
  waiting for transfers between devices: 88.1 us -> 76.7 us
  local copies, waits for them, and re-layouts: 16.5 us -> 25.7 us
  starting transfers between devices: 49.9 us -> 55.8 us
  Pallas kernels: 22.1 us -> 26.2 us
    all_to_all x1, waiting for transfers between devices: 15.3 us -> 8.55 us  [shards(): lax.all_to_all(outgoing, ('dp', 'expert'), split_axis=0, concat_axis=0, t...]
    unnamed x36 -> x44, local copies, waits for them, and re-layouts: 5.33 us -> 11.9 us
    ppermute x9 -> x10, waiting for transfers between devices: 27.6 us -> 22.1 us  [shift(): return lax.ppermute(x, axis, [((i + step) % size, i) for i in range(size)])]
    all_to_all x1, starting transfers between devices: 5.57 us -> 9.1 us  [shards(): lax.all_to_all(to_rows, 'expert', split_axis=0, concat_axis=0, tiled=True)]
    slice x0 -> x2, local copies, waits for them, and re-layouts: none -> 2.64 us  [the longest x1 1.82 us: shards(): far_first = shift(down_far[:cut], 2, dp_count, 'dp')]
    ppermute x9 -> x10, starting transfers between devices: 9.95 us -> 12.1 us  [shift(): return lax.ppermute(x, axis, [((i + step) % size, i) for i in range(size)])]
    dynamic_slice x1 -> x0, local copies, waits for them, and re-layouts: 2.17 us -> none  [shards(): lax.dynamic_slice_in_dim(w_down[0], group * piece, piece, 1)]
    concatenate x0 -> x1, local copies, waits for them, and re-layouts: none -> 2.16 us  [shards(): jnp.concatenate([lax.dynamic_slice_in_dim(w_down[0], group * piece, piece...]
  transfers between devices with their start and end apart: 20 -> 21, of which waited for: 10 -> 11; matrix products, arithmetic and copies ran while one was open for 9% -> 12% of each run, Pallas kernels for 11% -> 13%
where the time goes in v10:
time: 204 us; the launch traced here: 202 us
  waiting for transfers between devices  76.7 us (38%)
  starting transfers between devices  55.8 us (27%)
  Pallas kernels  26.2 us (13%)
  local copies, waits for them, and re-layouts  25.7 us (13%)
  matrix products  9.82 us (5%)
  other arithmetic  6.12 us (3%)
    ppermute x10, waiting for transfers between devices, shift(): return lax.ppermute(x, axis, [((i + step) % size, i) for i in range(size)])  22.1 us
    all_to_all x1, waiting for transfers between devices, shards(): lax.all_to_all(out.astype(BF).reshape(devices, capacity, piece), ('dp', '...  16.5 us
    all_to_all x1, waiting for transfers between devices, shards(): lax.all_to_all(pair_sums, 'expert', split_axis=0, concat_axis=0, tiled=Tr...  12.6 us
    ppermute x10, starting transfers between devices, shift(): return lax.ppermute(x, axis, [((i + step) % size, i) for i in range(size)])  12.1 us
    unnamed x44, local copies, waits for them, and re-layouts  11.9 us
    all_to_all x1, starting transfers between devices, to_heads(): lax.all_to_all(part, 'expert', split_axis=0, concat_axis=0, tiled=True)  10.2 us
    all_to_all x1, waiting for transfers between devices, to_heads(): lax.all_to_all(part, 'expert', split_axis=0, concat_axis=0, tiled=True)  10.1 us
    pallas_call x1, Pallas kernels, attend(): pl.pallas_call(body, out_shape=(jax.ShapeDtypeStruct((heads, MAIN, LAT +...  9.24 us
  transfers between devices with their start and end apart: 21, of which 11 were waited for; matrix products, arithmetic and copies ran while one was open for 12% of the time, Pallas kernels for 13%

profile of v10, /device:TPU:1, one launch (start us, length us, event | category | flops | bytes accessed | tf_op | source)
XLA Modules:
  0.0 202.4 jit_solution(17528717149515008219)
XLA Ops:
  0.6 0.9 slice.104
  1.5 1.4 collective-permute-start
  2.9 3.4 %collective-permute-done = bf16[64,576]{1,0:T(8,128)(2,1)S(1)} collective-permute-done((bf16[64,576]{1,0:T(8,128)(2,1)S(1)}, bf16[64,576]{1,0:T(8,128)(2,1)S(1)}, u32[]{:S(2)}, u32[]{:S(2)}) %collective-permute-start) | collective-permute-done | bytes 73760 | tf_op jit(solution)/shard_map/ppermute | solution.py:442
  6.3 1.0 pad_maximum_fusion.3.refs_1_
  7.3 2.5 %collective-permute-start.1 = (bf16[256,576]{1,0:T(8,128)(2,1)S(1)}, bf16[256,576]{1,0:T(8,128)(2,1)S(1)}, u32[]{:S(2)}, u32[]{:S(2)}) collective-permute-start(bf16[256,576]{1,0:T(8,128)(2,1)S(1)} %pad_maximum_fusion.3.refs_1_), channel_id=1, source_target_pairs={{32,0},{64,32},{96,64},{0,96},{33,1},{65,33},{97,65},{1,97},{34,2}... | collective-permute-start | bytes 884744 | tf_op jit(solution)/shard_map/ppermute | solution.py:48
  12.4 1.0 tables.1
  14.1 6.4 %weight_slices.1 = (bf16[2,1792,256]{2,1,0:T(8,128)(2,1)}, bf16[2,1792,256]{2,1,0:T(8,128)(2,1)}, bf16[256,1792]{1,0:T(8,128)(2,1)}, bf16[256,1792]{1,0:T(8,128)(2,1)}, bf16[256,1792]{1,0:T(8,128)(2,1)}) custom-call(s32[5]{0:T(128)} %stack.59.at_ref, bf16[1,7168,256]{2,1,0:T(8,128)(2,1)} %gate_ref.1, bf16[1,7168,256]{2,1,0:T(8,128)(2,1)} %up_ref.1, ...), custom_call_target="tpu_custom_call" | custom-call | flops 1000 | bytes 4096 | tf_op jit(solution)/shard_map/weight_slices/pallas_call | solution.py:183
  20.6 5.2 %collective-permute-done.3.refs_4_ = bf16[256,576]{1,0:T(8,128)(2,1)S(1)} collective-permute-done((bf16[256,576]{1,0:T(8,128)(2,1)S(1)}, bf16[256,576]{1,0:T(8,128)(2,1)S(1)}, u32[]{:S(2)}, u32[]{:S(2)}) %collective-permute-start.3) | collective-permute-done | bytes 294944 | tf_op jit(solution)/shard_map/ppermute | solution.py:48
  27.2 9.2 %attend.1 = (bf16[64,8,640]{2,1,0:T(8,128)(2,1)}, bf16[14,64,512]{2,1,0:T(8,128)(2,1)}) custom-call(s32[32,128]{1,0:T(8,128)S(1)} %get-tuple-element.81.refs_0_, bf16[256,576]{1,0:T(8,128)(2,1)} %copy-done.5, bf16[256,576]{1,0:T(8,128)(2,1)} %copy-done.7, bf16[256,576]{1,0:T(8,128)(2,1)} %copy-done.8, bf16[256,576]{1,0:T(8,128)(2,1)} %copy-done.9, ...), custom_call_target="tpu_custom_call" | custom-call | flops 100000000 | bytes 4000000 | tf_op jit(solution)/shard_map/attend/pallas_call | solution.py:283
  37.2 10.2 %all-to-all-start.1 = ((bf16[64,8,640]{2,1,0:T(8,128)(2,1)}), bf16[64,8,640]{2,1,0:T(8,128)(2,1)S(1)}, u32[]{:S(2)}, u32[]{:S(2)}) async-start(bf16[64,8,640]{2,1,0:T(8,128)(2,1)} %get-tuple-element.86), calls=%async_computation.1 | async-start | bytes 1310720 | tf_op jit(solution)/shard_map/all_to_all | solution.py:514
  47.4 2.5 %collective-permute-start.6 = (bf16[2,1792,256]{2,1,0:T(8,128)(2,1)}, bf16[2,1792,256]{2,1,0:T(8,128)(2,1)}, u32[]{:S(2)}, u32[]{:S(2)}) collective-permute-start(bf16[2,1792,256]{2,1,0:T(8,128)(2,1)} %get-tuple-element.96), channel_id=1, source_target_pairs={{0,32},{1,97},{2,34},{3,99},{4,36},{5,101},{6,38},{7,103},{8,40},{... | collective-permute-start | bytes 5505032 | tf_op jit(solution)/shard_map/ppermute | solution.py:498
  50.2 10.1 %all-to-all-done.1 = bf16[64,8,640]{2,1,0:T(8,128)(2,1)S(1)} async-done(((bf16[64,8,640]{2,1,0:T(8,128)(2,1)}), bf16[64,8,640]{2,1,0:T(8,128)(2,1)S(1)}, u32[]{:S(2)}, u32[]{:S(2)}) %all-to-all-start.1) | async-done | bytes 655392 | tf_op jit(solution)/shard_map/all_to_all | solution.py:514
  60.4 2.7 %copy-done.2 = bf16[256,7168]{1,0:T(8,128)(2,1)S(1)} copy-done((bf16[256,7168]{1,0:T(8,128)(2,1)S(1)}, bf16[256,7168]{1,0:T(8,128)(2,1)}, u32[]{:S(2)}) %copy-start.2) | copy-done | bytes 3670040
  63.1 3.1 %project.1 = (bf16[48,7168]{1,0:T(8,128)(2,1)S(1)}, bf16[48,7168]{1,0:T(8,128)(2,1)}) custom-call(s32[96,128]{1,0:T(8,128)S(1)} %get-tuple-element.75.cells_ref, bf16[32,2,8,640]{3,2,1,0:T(8,128)(2,1)S(1)} %bitcast.123, bf16[2,96,512]{2,1,0:T(8,128)(2,1)} %copy-done.11, bf16[2,512,128]{2,1,0:T(8,128)(2,1)S(1)} %copy-done.3, bf16[256,7168]{1,0:T(8,128)(2,1)S(1)} %copy-done.2), custom_call_target="tpu_custom_call" | custom-call | flops 400000000 | bytes 6000000 | tf_op jit(solution)/shard_map/project/pallas_call | solution.py:343
  67.5 1.4 collective-permute-done.5.other_ref
  68.9 2.5 %pair_sum.1 = bf16[16,3,7168]{2,1,0:T(4,128)(2,1)} custom-call(bf16[48,7168]{1,0:T(8,128)(2,1)S(1)} %get-tuple-element.94.mine_ref, bf16[48,7168]{1,0:T(8,128)(2,1)} %collective-permute-done.5.other_ref), custom_call_target="tpu_custom_call" | custom-call | flops 400000 | bytes 2000000 | tf_op jit(solution)/shard_map/pair_sum/pallas_call | solution.py:368
  71.4 3.6 %all-to-all-start.2 = ((bf16[16,3,7168]{2,1,0:T(4,128)(2,1)}), bf16[16,3,7168]{2,1,0:T(4,128)(2,1)S(1)}, u32[]{:S(2)}, u32[]{:S(2)}) async-start(bf16[16,3,7168]{2,1,0:T(4,128)(2,1)} %pair_sum.1), calls=%async_computation.2 | async-start | bytes 1835008 | tf_op jit(solution)/shard_map/all_to_all | solution.py:557
  75.1 2.5 %collective-permute-start.7 = (bf16[256,1792]{1,0:T(8,128)(2,1)}, bf16[256,1792]{1,0:T(8,128)(2,1)}, u32[]{:S(2)}, u32[]{:S(2)}) collective-permute-start(bf16[256,1792]{1,0:T(8,128)(2,1)} %get-tuple-element.99), channel_id=1, source_target_pairs={{32,0},{64,32},{96,64},{0,96},{33,1},{65,33},{97,65},{1,97},{34,2}... | collective-permute-start | bytes 2752520 | tf_op jit(solution)/shard_map/ppermute | solution.py:48
  77.6 12.6 %all-to-all-done.2 = bf16[16,3,7168]{2,1,0:T(4,128)(2,1)S(1)} async-done(((bf16[16,3,7168]{2,1,0:T(4,128)(2,1)}), bf16[16,3,7168]{2,1,0:T(4,128)(2,1)S(1)}, u32[]{:S(2)}, u32[]{:S(2)}) %all-to-all-start.2) | async-done | bytes 688160 | tf_op jit(solution)/shard_map/all_to_all | solution.py:557
  92.1 1.3 reshape.262
  93.4 6.4 %all-to-all-start.3 = ((bf16[128,2,1792]{2,1,0:T(2,128)(2,1)}), bf16[128,2,1792]{2,1,0:T(2,128)(2,1)S(1)}, u32[]{:S(2)}, u32[]{:S(2)}) async-start(bf16[128,2,1792]{2,1,0:T(2,128)(2,1)} %reshape.262), calls=%async_computation.3 | async-start | bytes 1835008 | tf_op jit(solution)/shard_map/all_to_all | solution.py:601
  100.1 1.8 slice.110
  101.9 2.9 %collective-permute-start.8 = (bf16[128,1792]{1,0:T(8,128)(2,1)}, bf16[128,1792]{1,0:T(8,128)(2,1)S(1)}, u32[]{:S(2)}, u32[]{:S(2)}) collective-permute-start(bf16[128,1792]{1,0:T(8,128)(2,1)} %slice.110), channel_id=1, source_target_pairs={{64,0},{96,32},{0,64},{32,96},{65,1},{97,33},{1,65},{33,97},{66,2}... | collective-permute-start | bytes 1376264 | tf_op jit(solution)/shard_map/ppermute | solution.py:48
  104.9 2.2 %bitcast_dynamic-update-slice_fusion = bf16[1024,1792]{1,0:T(8,128)(2,1)} fusion(bf16[1,256,7168]{2,1,0:T(8,128)(2,1)} %down_ref.1, s32[]{:T(128)S(6)} %select_n.230), kind=kLoop, calls=%fused_computation.50 | loop fusion | bytes 1835012
  107.5 1.6 maximum_bitcast_fusion
  109.0 8.5 %all-to-all-done.3 = bf16[128,2,1792]{2,1,0:T(2,128)(2,1)S(1)} async-done(((bf16[128,2,1792]{2,1,0:T(2,128)(2,1)}), bf16[128,2,1792]{2,1,0:T(2,128)(2,1)S(1)}, u32[]{:S(2)}, u32[]{:S(2)}) %all-to-all-start.3) | async-done | bytes 917536 | tf_op jit(solution)/shard_map/all_to_all | solution.py:601
  117.9 4.6 %collective-permute-done.8 = bf16[128,1792]{1,0:T(8,128)(2,1)S(1)} collective-permute-done((bf16[128,1792]{1,0:T(8,128)(2,1)}, bf16[128,1792]{1,0:T(8,128)(2,1)S(1)}, u32[]{:S(2)}, u32[]{:S(2)}) %collective-permute-start.8) | collective-permute-done | bytes 458784 | tf_op jit(solution)/shard_map/ppermute | solution.py:48
  123.6 9.1 %all-to-all-start.4 = ((bf16[32,24,576]{2,1,0:T(8,128)(2,1)}), bf16[32,24,576]{2,1,0:T(8,128)(2,1)S(1)}, u32[]{:S(2)}, u32[]{:S(2)}) async-start(bf16[32,24,576]{2,1,0:T(8,128)(2,1)} %maximum_bitcast_fusion), calls=%async_computation.4 | async-start | bytes 1966080 | tf_op jit(solution)/shard_map/all_to_all | solution.py:613
  132.7 1.5 copy-done.1
  134.2 2.0 gate_up.2.refs_0_
  136.1 2.2 %constant_dynamic-update-slice_fusion.3 = bf16[1024,1792]{1,0:T(8,128)(2,1)} fusion(bf16[1024,1792]{1,0:T(8,128)(2,1)} %bitcast_dynamic-update-slice_fusion, bf16[256,1792]{1,0:T(8,128)(2,1)} %collective-permute-done.7), kind=kLoop, calls=%fused_computation.114 | loop fusion | bytes 1835008
  138.4 1.6 fusion.26
  140.4 1.9 gate_up.3
  142.3 1.9 collective-permute-start.11
  144.6 0.8 slice.126
  145.5 1.6 fusion.22
  147.1 2.1 %collective-permute-done.11 = bf16[256,512]{1,0:T(8,128)(2,1)S(1)} collective-permute-done((bf16[256,512]{1,0:T(8,128)(2,1)S(1)}, bf16[256,512]{1,0:T(8,128)(2,1)S(1)}, u32[]{:S(2)}, u32[]{:S(2)}) %collective-permute-start.11) | collective-permute-done | bytes 262176 | tf_op jit(solution)/shard_map/ppermute | solution.py:621
  149.4 3.0 %collective-permute-start.13 = (bf16[256,256]{1,0:T(8,128)(2,1)S(1)}, bf16[256,256]{1,0:T(8,128)(2,1)S(1)}, u32[]{:S(2)}, u32[]{:S(2)}) collective-permute-start(bf16[256,256]{1,0:T(8,128)(2,1)S(1)} %fusion.39), channel_id=1, source_target_pairs={{64,0},{96,32},{0,64},{32,96},{65,1},{97,33},{1,65},{33,97},{66,2}... | collective-permute-start | bytes 393224 | tf_op jit(solution)/shard_map/ppermute | solution.py:48
  152.4 0.8 constant_dynamic-update-slice_fusion.2
  153.2 9.6 %collective-permute-done.14 = bf16[256,256]{1,0:T(8,128)(2,1)S(1)} collective-permute-done((bf16[256,256]{1,0:T(8,128)(2,1)S(1)}, bf16[256,256]{1,0:T(8,128)(2,1)S(1)}, u32[]{:S(2)}, u32[]{:S(2)}) %collective-permute-start.14) | collective-permute-done | bytes 131104 | tf_op jit(solution)/shard_map/ppermute | solution.py:48
  162.8 2.6 %collective-permute-done.13 = bf16[256,256]{1,0:T(8,128)(2,1)S(1)} collective-permute-done((bf16[256,256]{1,0:T(8,128)(2,1)S(1)}, bf16[256,256]{1,0:T(8,128)(2,1)S(1)}, u32[]{:S(2)}, u32[]{:S(2)}) %collective-permute-start.13) | collective-permute-done | bytes 131104 | tf_op jit(solution)/shard_map/ppermute | solution.py:48
  166.0 1.8 constant_dynamic-update-slice_fusion.1
  167.8 2.2 %constant_dynamic-update-slice_fusion = bf16[1024,1792]{1,0:T(8,128)(2,1)} fusion(bf16[1024,1792]{1,0:T(8,128)(2,1)} %constant_dynamic-update-slice_fusion.1, bf16[256,1792]{1,0:T(8,128)(2,1)} %collective-permute-done.9), kind=kLoop, calls=%fused_computation.111 | loop fusion | bytes 1835008 | tf_op jit(solution)/shard_map/concatenate | solution.py:635
  170.0 3.1 %convolution_convert_fusion.2 = bf16[256,1792]{1,0:T(8,128)(2,1)S(1)} fusion(bf16[256,1024]{1,0:T(8,128)(2,1)S(1)} %pad_maximum_fusion.2, bf16[1024,1792]{1,0:T(8,128)(2,1)} %constant_dynamic-update-slice_fusion), kind=kOutput, calls=%fused_computation.38 | convolution fusion | flops 939982848 | bytes 5111808 | tf_op jit(solution)/shard_map/dot_general | solution.py:636
  173.1 1.3 reshape.271
  174.4 7.7 %all-to-all-start.5 = ((bf16[128,2,1792]{2,1,0:T(2,128)(2,1)}), bf16[128,2,1792]{2,1,0:T(2,128)(2,1)S(1)}, u32[]{:S(2)}, u32[]{:S(2)}) async-start(bf16[128,2,1792]{2,1,0:T(2,128)(2,1)} %reshape.271), calls=%async_computation.5 | async-start | bytes 1835008 | tf_op jit(solution)/shard_map/all_to_all | solution.py:637
  183.3 16.5 %all-to-all-done.5 = bf16[128,2,1792]{2,1,0:T(2,128)(2,1)S(1)} async-done(((bf16[128,2,1792]{2,1,0:T(2,128)(2,1)}), bf16[128,2,1792]{2,1,0:T(2,128)(2,1)S(1)}, u32[]{:S(2)}, u32[]{:S(2)}) %all-to-all-start.5) | async-done | bytes 917536 | tf_op jit(solution)/shard_map/all_to_all | solution.py:637
  201.2 1.2 fusion.15
  (122 shorter events, 14.3 us)
Async XLA Ops:
  1.5 4.8 %collective-permute-start = (bf16[64,576]{1,0:T(8,128)(2,1)S(1)}, bf16[64,576]{1,0:T(8,128)(2,1)S(1)}, u32[]{:S(2)}, u32[]{:S(2)}) collective-permute-start(bf16[64,576]{1,0:T(8,128)(2,1)S(1)} %slice.104), channel_id=1, source_target_pairs={{1,0},{2,1},{3,2},{4,3},{5,4},{6,5},{7,6},{8,7},{9,8},{10,9},{11,1... | collective-permute-start | bytes 221192 | tf_op jit(solution)/shard_map/ppermute | solution.py:442
  7.3 13.3 %copy-start.5 = (bf16[256,576]{1,0:T(8,128)(2,1)}, bf16[256,576]{1,0:T(8,128)(2,1)S(1)}, u32[]{:S(2)}) copy-start(bf16[256,576]{1,0:T(8,128)(2,1)S(1)} %pad_maximum_fusion.3.refs_1_) | copy-start | bytes 884740
  7.3 13.3 %collective-permute-start.1 = (bf16[256,576]{1,0:T(8,128)(2,1)S(1)}, bf16[256,576]{1,0:T(8,128)(2,1)S(1)}, u32[]{:S(2)}, u32[]{:S(2)}) collective-permute-start(bf16[256,576]{1,0:T(8,128)(2,1)S(1)} %pad_maximum_fusion.3.refs_1_), channel_id=1, source_target_pairs={{32,0},{64,32},{96,64},{0,96},{33,1},{65,33},{97,65},{1,97},{34,2}... | collective-permute-start | bytes 884744 | tf_op jit(solution)/shard_map/ppermute | solution.py:48
  9.9 10.7 %collective-permute-start.2 = (bf16[256,576]{1,0:T(8,128)(2,1)S(1)}, bf16[256,576]{1,0:T(8,128)(2,1)S(1)}, u32[]{:S(2)}, u32[]{:S(2)}) collective-permute-start(bf16[256,576]{1,0:T(8,128)(2,1)S(1)} %pad_maximum_fusion.3.refs_1_), channel_id=1, source_target_pairs={{64,0},{96,32},{0,64},{32,96},{65,1},{97,33},{1,65},{33,97},{66,2}... | collective-permute-start | bytes 884744 | tf_op jit(solution)/shard_map/ppermute | solution.py:48
  10.4 15.5 %collective-permute-start.3 = (bf16[256,576]{1,0:T(8,128)(2,1)S(1)}, bf16[256,576]{1,0:T(8,128)(2,1)S(1)}, u32[]{:S(2)}, u32[]{:S(2)}) collective-permute-start(bf16[256,576]{1,0:T(8,128)(2,1)S(1)} %pad_maximum_fusion.3.refs_1_), channel_id=1, source_target_pairs={{96,0},{0,32},{32,64},{64,96},{97,1},{1,33},{33,65},{65,97},{98,2}... | collective-permute-start | bytes 884744 | tf_op jit(solution)/shard_map/ppermute | solution.py:48
  14.1 13.0 %copy-start.15 = (s32[384]{0:T(512)S(1)}, s32[384]{0:T(512)}, u32[]{:S(2)}) copy-start(s32[384]{0:T(512)} %param.23) | copy-start | bytes 4612
  20.6 6.6 %copy-start.7 = (bf16[256,576]{1,0:T(8,128)(2,1)}, bf16[256,576]{1,0:T(8,128)(2,1)S(1)}, u32[]{:S(2)}) copy-start(bf16[256,576]{1,0:T(8,128)(2,1)S(1)} %collective-permute-done.1.refs_2_) | copy-start | bytes 884740
  20.6 6.6 %copy-start.8 = (bf16[256,576]{1,0:T(8,128)(2,1)}, bf16[256,576]{1,0:T(8,128)(2,1)S(1)}, u32[]{:S(2)}) copy-start(bf16[256,576]{1,0:T(8,128)(2,1)S(1)} %collective-permute-done.2.refs_3_) | copy-start | bytes 884740
  25.9 1.3 copy-start.9
  25.9 34.5 %collective-permute-start.4 = (bf16[2,1792,256]{2,1,0:T(8,128)(2,1)}, bf16[2,1792,256]{2,1,0:T(8,128)(2,1)S(1)}, u32[]{:S(2)}, u32[]{:S(2)}) collective-permute-start(bf16[2,1792,256]{2,1,0:T(8,128)(2,1)} %get-tuple-element.87), channel_id=1, source_target_pairs={{0,32},{1,97},{2,34},{3,99},{4,36},{5,101},{6,38},{7,103},{8,40},{... | collective-permute-start | bytes 5505032 | tf_op jit(solution)/shard_map/ppermute | solution.py:497
  36.5 13.5 %copy-start.17 = (s32[1,3,8]{2,0,1:T(1,128)S(1)}, s32[1,3,8]{2,0,1:T(1,128)}, u32[]{:S(2)}) copy-start(s32[1,3,8]{2,0,1:T(1,128)} %param.29) | copy-start | bytes 292
  36.5 23.9 %copy-start.3 = (bf16[2,512,128]{2,1,0:T(8,128)(2,1)S(1)}, bf16[2,512,128]{2,1,0:T(8,128)(2,1)}, u32[]{:S(2)}) copy-start(bf16[2,512,128]{2,1,0:T(8,128)(2,1)} %uv_ref.1) | copy-start | bytes 786436
  36.5 0.7 copy-start.11
  36.6 30.6 %copy-start.18 = (f32[1,3,8]{2,0,1:T(1,128)S(1)}, f32[1,3,8]{2,0,1:T(1,128)}, u32[]{:S(2)}) copy-start(f32[1,3,8]{2,0,1:T(1,128)} %param.30) | copy-start | bytes 292
  36.6 30.6 %copy-start.16 = (s32[384]{0:T(512)S(1)}, s32[384]{0:T(512)}, u32[]{:S(2)}) copy-start(s32[384]{0:T(512)} %param.22) | copy-start | bytes 4612
  37.2 23.1 %all-to-all-start.1 = ((bf16[64,8,640]{2,1,0:T(8,128)(2,1)}), bf16[64,8,640]{2,1,0:T(8,128)(2,1)S(1)}, u32[]{:S(2)}, u32[]{:S(2)}) async-start(bf16[64,8,640]{2,1,0:T(8,128)(2,1)} %get-tuple-element.86), calls=%async_computation.1 | async-start | bytes 1310720 | tf_op jit(solution)/shard_map/all_to_all | solution.py:514
  47.4 30.1 %collective-permute-start.6 = (bf16[2,1792,256]{2,1,0:T(8,128)(2,1)}, bf16[2,1792,256]{2,1,0:T(8,128)(2,1)}, u32[]{:S(2)}, u32[]{:S(2)}) collective-permute-start(bf16[2,1792,256]{2,1,0:T(8,128)(2,1)} %get-tuple-element.96), channel_id=1, source_target_pairs={{0,32},{1,97},{2,34},{3,99},{4,36},{5,101},{6,38},{7,103},{8,40},{... | collective-permute-start | bytes 5505032 | tf_op jit(solution)/shard_map/ppermute | solution.py:498
  60.4 11.0 %copy-start = (bf16[2,1792,256]{2,1,0:T(8,128)(2,1)}, bf16[2,1792,256]{2,1,0:T(8,128)(2,1)S(1)}, u32[]{:S(2)}) copy-start(bf16[2,1792,256]{2,1,0:T(8,128)(2,1)S(1)} %collective-permute-done.4.gate_ref) | copy-start | bytes 5505028
  60.4 2.7 %copy-start.2 = (bf16[256,7168]{1,0:T(8,128)(2,1)S(1)}, bf16[256,7168]{1,0:T(8,128)(2,1)}, u32[]{:S(2)}) copy-start(bf16[256,7168]{1,0:T(8,128)(2,1)} %weight_ref.1) | copy-start | bytes 11010052
  66.2 24.4 %copy-start.12 = (bf16[1,3,7168]{2,1,0:T(4,128)(2,1)S(1)}, bf16[1,3,7168]{2,1,0:T(4,128)(2,1)}, u32[]{:S(2)}) copy-start(bf16[1,3,7168]{2,1,0:T(4,128)(2,1)} %param.27) | copy-start | bytes 129028
  66.2 24.6 %copy-start.13 = (f32[7168]{0:T(1024)S(1)}, f32[7168]{0:T(1024)}, u32[]{:S(2)}) copy-start(f32[7168]{0:T(1024)} %param.28) | copy-start | bytes 86020
  66.2 2.7 %collective-permute-start.5 = (bf16[48,7168]{1,0:T(8,128)(2,1)}, bf16[48,7168]{1,0:T(8,128)(2,1)}, u32[]{:S(2)}, u32[]{:S(2)}) collective-permute-start(bf16[48,7168]{1,0:T(8,128)(2,1)} %get-tuple-element.95), channel_id=1, source_target_pairs={{0,1},{1,0},{2,3},{3,2},{4,5},{5,4},{6,7},{7,6},{8,9},{9,8},{10,11... | collective-permute-start | bytes 2064392 | tf_op jit(solution)/shard_map/ppermute | solution.py:555
  71.4 18.8 %all-to-all-start.2 = ((bf16[16,3,7168]{2,1,0:T(4,128)(2,1)}), bf16[16,3,7168]{2,1,0:T(4,128)(2,1)S(1)}, u32[]{:S(2)}, u32[]{:S(2)}) async-start(bf16[16,3,7168]{2,1,0:T(4,128)(2,1)} %pair_sum.1), calls=%async_computation.2 | async-start | bytes 1835008 | tf_op jit(solution)/shard_map/all_to_all | solution.py:557
  75.1 42.8 %collective-permute-start.7 = (bf16[256,1792]{1,0:T(8,128)(2,1)}, bf16[256,1792]{1,0:T(8,128)(2,1)}, u32[]{:S(2)}, u32[]{:S(2)}) collective-permute-start(bf16[256,1792]{1,0:T(8,128)(2,1)} %get-tuple-element.99), channel_id=1, source_target_pairs={{32,0},{64,32},{96,64},{0,96},{33,1},{65,33},{97,65},{1,97},{34,2}... | collective-permute-start | bytes 2752520 | tf_op jit(solution)/shard_map/ppermute | solution.py:48
  77.5 40.4 %collective-permute-start.9 = (bf16[256,1792]{1,0:T(8,128)(2,1)}, bf16[256,1792]{1,0:T(8,128)(2,1)}, u32[]{:S(2)}, u32[]{:S(2)}) collective-permute-start(bf16[256,1792]{1,0:T(8,128)(2,1)} %get-tuple-element.101), channel_id=1, source_target_pairs={{96,0},{0,32},{32,64},{64,96},{97,1},{1,33},{33,65},{65,97},{98,2}... | collective-permute-start | bytes 2752520 | tf_op jit(solution)/shard_map/ppermute | solution.py:48
  92.1 14.9 %copy-start.6 = (bf16[256,576]{1,0:T(8,128)(2,1)S(1)}, bf16[256,576]{1,0:T(8,128)(2,1)}, u32[]{:S(2)}) copy-start(bf16[256,576]{1,0:T(8,128)(2,1)} %copy-done.5) | copy-start | bytes 884740
  93.4 13.6 %slice-start.2 = ((bf16[256,576]{1,0:T(8,128)(2,1)}), bf16[192,576]{1,0:T(8,128)(2,1)S(1)}, s32[]{:S(2)}) async-start(bf16[256,576]{1,0:T(8,128)(2,1)} %copy-done.9), calls=%async_computation.8 | async-start | bytes 491520 | tf_op jit(solution)/shard_map/slice | solution.py:607
  93.4 13.7 %slice-start.1 = ((bf16[256,576]{1,0:T(8,128)(2,1)}), bf16[192,576]{1,0:T(8,128)(2,1)S(1)}, s32[]{:S(2)}) async-start(bf16[256,576]{1,0:T(8,128)(2,1)} %copy-done.8), calls=%async_computation.7 | async-start | bytes 491520 | tf_op jit(solution)/shard_map/slice | solution.py:607
  93.4 13.8 %slice-start = ((bf16[256,576]{1,0:T(8,128)(2,1)}), bf16[192,576]{1,0:T(8,128)(2,1)S(1)}, s32[]{:S(2)}) async-start(bf16[256,576]{1,0:T(8,128)(2,1)} %copy-done.7), calls=%async_computation.6 | async-start | bytes 491520 | tf_op jit(solution)/shard_map/slice | solution.py:607
  93.4 24.1 %all-to-all-start.3 = ((bf16[128,2,1792]{2,1,0:T(2,128)(2,1)}), bf16[128,2,1792]{2,1,0:T(2,128)(2,1)S(1)}, u32[]{:S(2)}, u32[]{:S(2)}) async-start(bf16[128,2,1792]{2,1,0:T(2,128)(2,1)} %reshape.262), calls=%async_computation.3 | async-start | bytes 1835008 | tf_op jit(solution)/shard_map/all_to_all | solution.py:601
  101.9 20.6 %collective-permute-start.8 = (bf16[128,1792]{1,0:T(8,128)(2,1)}, bf16[128,1792]{1,0:T(8,128)(2,1)S(1)}, u32[]{:S(2)}, u32[]{:S(2)}) collective-permute-start(bf16[128,1792]{1,0:T(8,128)(2,1)} %slice.110), channel_id=1, source_target_pairs={{64,0},{96,32},{0,64},{32,96},{65,1},{97,33},{1,65},{33,97},{66,2}... | collective-permute-start | bytes 1376264 | tf_op jit(solution)/shard_map/ppermute | solution.py:48
  122.5 17.9 %collective-permute-start.10 = (bf16[256,1792]{1,0:T(8,128)(2,1)S(1)}, bf16[256,1792]{1,0:T(8,128)(2,1)S(1)}, u32[]{:S(2)}, u32[]{:S(2)}) collective-permute-start(bf16[256,1792]{1,0:T(8,128)(2,1)S(1)} %reshape.263.rows_ref), channel_id=1, source_target_pairs={{0,96},{1,33},{2,98},{3,35},{4,100},{5,37},{6,102},{7,39},{8,104},... | collective-permute-start | bytes 2752520 | tf_op jit(solution)/shard_map/ppermute | solution.py:612
  123.6 41.9 %all-to-all-start.4 = ((bf16[32,24,576]{2,1,0:T(8,128)(2,1)}), bf16[32,24,576]{2,1,0:T(8,128)(2,1)S(1)}, u32[]{:S(2)}, u32[]{:S(2)}) async-start(bf16[32,24,576]{2,1,0:T(8,128)(2,1)} %maximum_bitcast_fusion), calls=%async_computation.4 | async-start | bytes 1966080 | tf_op jit(solution)/shard_map/all_to_all | solution.py:613
  132.7 1.5 copy-start.1
  134.2 5.8 %copy-start.4 = (bf16[1,7168,256]{2,1,0:T(8,128)(2,1)S(1)}, bf16[1,7168,256]{2,1,0:T(8,128)(2,1)}, u32[]{:S(2)}) copy-start(bf16[1,7168,256]{2,1,0:T(8,128)(2,1)} %up_ref.1) | copy-start | bytes 11010052
  140.4 4.2 %copy-start.10 = (bf16[256,1792]{1,0:T(8,128)(2,1)S(1)}, bf16[256,1792]{1,0:T(8,128)(2,1)}, u32[]{:S(2)}) copy-start(bf16[256,1792]{1,0:T(8,128)(2,1)} %get-tuple-element.114) | copy-start | bytes 2752516
  142.3 6.8 %collective-permute-start.11 = (bf16[256,512]{1,0:T(8,128)(2,1)S(1)}, bf16[256,512]{1,0:T(8,128)(2,1)S(1)}, u32[]{:S(2)}, u32[]{:S(2)}) collective-permute-start(bf16[256,512]{1,0:T(8,128)(2,1)S(1)} %gate_up.3), channel_id=1, source_target_pairs={{0,32},{1,97},{2,34},{3,99},{4,36},{5,101},{6,38},{7,103},{8,40},{... | collective-permute-start | bytes 786440 | tf_op jit(solution)/shard_map/ppermute | solution.py:621
  145.5 20.5 %collective-permute-start.15 = (bf16[128,1792]{1,0:T(8,128)(2,1)}, bf16[128,1792]{1,0:T(8,128)(2,1)}, u32[]{:S(2)}, u32[]{:S(2)}) collective-permute-start(bf16[128,1792]{1,0:T(8,128)(2,1)} %slice.126), channel_id=1, source_target_pairs={{64,0},{96,32},{0,64},{32,96},{65,1},{97,33},{1,65},{33,97},{66,2}... | collective-permute-start | bytes 1376264 | tf_op jit(solution)/shard_map/ppermute | solution.py:48
  149.3 13.5 %collective-permute-start.14 = (bf16[256,256]{1,0:T(8,128)(2,1)S(1)}, bf16[256,256]{1,0:T(8,128)(2,1)S(1)}, u32[]{:S(2)}, u32[]{:S(2)}) collective-permute-start(bf16[256,256]{1,0:T(8,128)(2,1)S(1)} %fusion.39), channel_id=1, source_target_pairs={{96,0},{0,32},{32,64},{64,96},{97,1},{1,33},{33,65},{65,97},{98,2}... | collective-permute-start | bytes 393224 | tf_op jit(solution)/shard_map/ppermute | solution.py:48
  149.4 16.0 %collective-permute-start.13 = (bf16[256,256]{1,0:T(8,128)(2,1)S(1)}, bf16[256,256]{1,0:T(8,128)(2,1)S(1)}, u32[]{:S(2)}, u32[]{:S(2)}) collective-permute-start(bf16[256,256]{1,0:T(8,128)(2,1)S(1)} %fusion.39), channel_id=1, source_target_pairs={{64,0},{96,32},{0,64},{32,96},{65,1},{97,33},{1,65},{33,97},{66,2}... | collective-permute-start | bytes 393224 | tf_op jit(solution)/shard_map/ppermute | solution.py:48
  152.4 13.1 %collective-permute-start.12 = (bf16[256,256]{1,0:T(8,128)(2,1)S(1)}, bf16[256,256]{1,0:T(8,128)(2,1)S(1)}, u32[]{:S(2)}, u32[]{:S(2)}) collective-permute-start(bf16[256,256]{1,0:T(8,128)(2,1)S(1)} %fusion.39), channel_id=1, source_target_pairs={{32,0},{64,32},{96,64},{0,96},{33,1},{65,33},{97,65},{1,97},{34,2}... | collective-permute-start | bytes 393224 | tf_op jit(solution)/shard_map/ppermute | solution.py:48
  173.1 9.3 %copy-start.14 = (f32[512]{0:T(512)S(1)}, f32[512]{0:T(512)}, u32[]{:S(2)}) copy-start(f32[512]{0:T(512)} %param.21) | copy-start | bytes 6148
  174.4 25.4 %all-to-all-start.5 = ((bf16[128,2,1792]{2,1,0:T(2,128)(2,1)}), bf16[128,2,1792]{2,1,0:T(2,128)(2,1)S(1)}, u32[]{:S(2)}, u32[]{:S(2)}) async-start(bf16[128,2,1792]{2,1,0:T(2,128)(2,1)} %reshape.271), calls=%async_computation.5 | async-start | bytes 1835008 | tf_op jit(solution)/shard_map/all_to_all | solution.py:637

commit v11 on v10

--- a/solution.py
+++ b/solution.py
@@ -14,6 +14,7 @@
 PARTS = MAIN // (SLOTS - MAIN)
 EXTRA = LAT // PARTS
 VMEM = 58 * 1024 * 1024
+SMALL = 20 * 1024 * 1024
 
 eps = 1e-06
 theta = 10000.0
@@ -161,9 +162,12 @@
         for i in range(2):
             rows = pl.ds(pl.multiple_of(at_ref[i] * piece, 128), piece)
             copies.append((weight.at[0, rows, :], out.at[i]))
-    for i, out in enumerate(downs):
+    for i, outs in enumerate((downs[:1], downs[1:3], downs[3:])):
         columns = pl.ds(pl.multiple_of(at_ref[2 + i] * piece, 128), piece)
-        copies.append((down_ref.at[0, :, columns], out))
+        first = 0
+        for out in outs:
+            copies.append((down_ref.at[0, pl.ds(first, out.shape[0]), columns], out))
+            first += out.shape[0]
     copies = [
         pltpu.make_async_copy(source, target, sems.at[i])
         for i, (source, target) in enumerate(copies)
@@ -180,12 +184,13 @@
     whole = pl.BlockSpec(memory_space=pltpu.VMEM)
     halves = jax.ShapeDtypeStruct((2, piece, w_gate.shape[2]), BF)
     part = jax.ShapeDtypeStruct((w_down.shape[1], piece), BF)
+    cut = jax.ShapeDtypeStruct((w_down.shape[1] // 2, piece), BF)
     return pl.pallas_call(
         slice_kernel,
-        out_shape=(halves, halves) + (part,) * (dp_count - 1),
+        out_shape=(halves, halves, part, cut, cut, part),
         in_specs=[pl.BlockSpec(memory_space=pltpu.SMEM)] + [away] * 3,
-        out_specs=(whole,) * (dp_count + 1),
-        scratch_shapes=[pltpu.SemaphoreType.DMA((dp_count + 3,))],
+        out_specs=(whole,) * 6,
+        scratch_shapes=[pltpu.SemaphoreType.DMA((8,))],
         compiler_params=pltpu.CompilerParams(vmem_limit_bytes=VMEM),
         cost_estimate=pl.CostEstimate(flops=1000, bytes_accessed=4096, transcendentals=0),
         name="weight_slices",
@@ -345,7 +350,7 @@
         out_shape=(half, half),
         in_specs=[whole] * 5,
         out_specs=(whole, whole),
-        compiler_params=pltpu.CompilerParams(vmem_limit_bytes=32 * 1024 * 1024),
+        compiler_params=pltpu.CompilerParams(vmem_limit_bytes=SMALL),
         cost_estimate=pl.CostEstimate(
             flops=4 * 10**8, bytes_accessed=6 * 10**6, transcendentals=0
         ),
@@ -370,7 +375,7 @@
         out_shape=jax.ShapeDtypeStruct((chips, mine.shape[0] // chips, mine.shape[1]), BF),
         in_specs=[whole] * 2,
         out_specs=whole,
-        compiler_params=pltpu.CompilerParams(vmem_limit_bytes=32 * 1024 * 1024),
+        compiler_params=pltpu.CompilerParams(vmem_limit_bytes=SMALL),
         cost_estimate=pl.CostEstimate(
             flops=4 * 10**5, bytes_accessed=2 * 10**6, transcendentals=0
         ),
@@ -401,12 +406,44 @@
         in_specs=[pl.BlockSpec(rows.shape, lambda i: (0, 0)), weight, weight]
         + ([] if base is None else [whole]),
         out_specs=whole,
-        compiler_params=pltpu.CompilerParams(vmem_limit_bytes=32 * 1024 * 1024),
+        compiler_params=pltpu.CompilerParams(vmem_limit_bytes=SMALL),
         cost_estimate=pl.CostEstimate(
             flops=5 * 10**8, bytes_accessed=4 * 10**6, transcendentals=0
         ),
         name="gate_up",
     )(rows, gate, up, *(() if base is None else (base,)))
+
+
+def down_kernel(*refs):
+    blocks, weights, out_ref = refs[:4], refs[4:9], refs[9]
+    cut = weights[2].shape[0]
+    step = out_ref.shape[1] // 2
+    for first in range(0, out_ref.shape[1], step):
+        span = slice(first, first + step)
+        sums = jnp.dot(blocks[0][...], weights[0][:, span], preferred_element_type=F32)
+        for rows, weight in (
+            (blocks[1][...], weights[1]),
+            (blocks[2][:, :cut], weights[2]),
+            (blocks[2][:, cut:], weights[3]),
+            (blocks[3][...], weights[4]),
+        ):
+            sums = sums + jnp.dot(rows, weight[:, span], preferred_element_type=F32)
+        out_ref[:, span] = sums.astype(BF)
+
+
+def down_product(blocks, weights):
+    whole = pl.BlockSpec(memory_space=pltpu.VMEM)
+    return pl.pallas_call(
+        down_kernel,
+        out_shape=jax.ShapeDtypeStruct((blocks[0].shape[0], weights[0].shape[1]), BF),
+        in_specs=[whole] * 9,
+        out_specs=whole,
+        compiler_params=pltpu.CompilerParams(vmem_limit_bytes=SMALL),
+        cost_estimate=pl.CostEstimate(
+            flops=10**9, bytes_accessed=5 * 10**6, transcendentals=0
+        ),
+        name="down_product",
+    )(*blocks, *weights)
 
 
 def shards(
@@ -488,7 +525,7 @@
         [their_quarter, their_quarter ^ 1]
         + [(late_group - k + dp_count) % dp_count for k in range(1, dp_count)]
     ).astype(I32)
-    gate_sent, up_sent, down_near, down_far, down_last = weight_slices(
+    gate_sent, up_sent, down_near, far_first, far_second, down_last = weight_slices(
         at, w_gate, w_up, w_down, dp_count
     )
     gate_sent, up_sent, slot_table_rows, *rows = lax.optimization_barrier(
@@ -562,9 +599,8 @@
         tiled=True,
         axis_index_groups=[[2 * i + c for i in range(chips)] for c in range(2)],
     )
-    cut = down_far.shape[0] // 2
-    chip_sums, up_came, down_far = lax.optimization_barrier((chip_sums, up_came, down_far))
-    far_first = shift(down_far[:cut], 2, dp_count, "dp")
+    chip_sums, up_came, far_first = lax.optimization_barrier((chip_sums, up_came, far_first))
+    far_first = shift(far_first, 2, dp_count, "dp")
     attention_out = jnp.sum(chip_sums.astype(F32), axis=0)
     residual = resid[0].astype(F32) + attention_out
     normed = (
@@ -616,10 +652,12 @@
     own_halves = (gate_own, up_own)
     first = [jnp.dot(arrived, weight[0], preferred_element_type=F32) for weight in own_halves]
     given = gate_up(arrived, gate_came, up_came, 0)
-    beside, given, down_far, *first = lax.optimization_barrier((beside, given, down_far, *first))
+    beside, given, far_second, *first = lax.optimization_barrier(
+        (beside, given, far_second, *first)
+    )
     given = gate_up(beside, gate_came, up_came, 1, given)
     given = lax.ppermute(given, ("dp", "expert"), weight_perm).astype(F32)
-    far_second = shift(down_far[cut:], 2, dp_count, "dp")
+    far_second = shift(far_second, 2, dp_count, "dp")
     gate_sum, up_sum = (
         part + jnp.dot(beside, weight[1], preferred_element_type=F32)
         for part, weight in zip(first, own_halves)
@@ -628,14 +666,12 @@
     hidden = (
         jax.nn.silu(gate_sum + given[:, :half]) * (up_sum + given[:, half:])
     ).astype(BF)
-    hidden_all = jnp.concatenate(
-        [hidden] + [shift(hidden, k, dp_count, "dp") for k in range(1, dp_count)], axis=1
-    )
-    hidden_all, dealt = lax.optimization_barrier((hidden_all, dealt))
-    downs = jnp.concatenate([lax.dynamic_slice_in_dim(w_down[0], group * piece, piece, 1), down_near, far_first, far_second, down_last], axis=0)
-    out = jnp.dot(hidden_all, downs, preferred_element_type=F32)
+    blocks = [hidden] + [shift(hidden, k, dp_count, "dp") for k in range(1, dp_count)]
+    down_own = lax.dynamic_slice_in_dim(w_down[0], group * piece, piece, 1)
+    blocks[0], dealt = lax.optimization_barrier((blocks[0], dealt))
+    out = down_product(blocks, [down_own, down_near, far_first, far_second, down_last])
     returned = lax.all_to_all(
-        out.astype(BF).reshape(devices, capacity, piece),
+        out.reshape(devices, capacity, piece),
         ("dp", "expert"),
         split_axis=0,
         concat_axis=0,

time: 204 us -> 207 us (1.015)
  waiting for transfers between devices: 76.7 us -> 69.8 us
  starting transfers between devices: 55.8 us -> 60.3 us
  other arithmetic: 6.12 us -> 9.44 us
    ppermute x10, waiting for transfers between devices: 22.1 us -> 16.2 us  [shift(): return lax.ppermute(x, axis, [((i + step) % size, i) for i in range(size)])]
    dot_general x1 -> x0, matrix products: 3.15 us -> none  [shards(): out = jnp.dot(hidden_all, downs, preferred_element_type=F32)]
    slice x2 -> x0, local copies, waits for them, and re-layouts: 2.64 us -> none  [the longest x1 1.82 us: shards(): far_first = shift(down_far[:cut], 2, dp_count, 'dp')]
    ppermute x10, starting transfers between devices: 12.1 us -> 14.4 us  [shift(): return lax.ppermute(x, axis, [((i + step) % size, i) for i in range(size)])]
    concatenate x1 -> x0, local copies, waits for them, and re-layouts: 2.16 us -> none  [shards(): jnp.concatenate([lax.dynamic_slice_in_dim(w_down[0], group * piece, piece...]
    reshape x1, local copies, waits for them, and re-layouts: 0.34 us -> 2.46 us  [shards(): arrived = lax.all_to_all(outgoing, ('dp', 'expert'), split_axis=0, concat...]
    pallas_call x1 -> x2, Pallas kernels: 6.44 us -> 7.86 us  [the longest x1 6.4 us: weight_slices(): pl.pallas_call(slice_kernel, out_shape=(halves, halves, part, cut, cut, p...]
    unnamed x44 -> x60, local copies, waits for them, and re-layouts: 11.9 us -> 12.6 us
  transfers between devices with their start and end apart: 21 -> 21, of which waited for: 11 -> 11; matrix products, arithmetic and copies ran while one was open for 12% -> 13% of each run, Pallas kernels for 13% -> 13%
where the time goes in v11:
time: 207 us; the launch traced here: 205 us
  waiting for transfers between devices  69.8 us (34%)
  starting transfers between devices  60.3 us (29%)
  Pallas kernels  27.4 us (13%)
  local copies, waits for them, and re-layouts  25.9 us (13%)
  matrix products  10.4 us (5%)
  other arithmetic  9.44 us (5%)
    all_to_all x1, waiting for transfers between devices, shards(): lax.all_to_all(out.reshape(devices, capacity, piece), ('dp', 'expert'), s...  16.5 us
    ppermute x10, waiting for transfers between devices, shift(): return lax.ppermute(x, axis, [((i + step) % size, i) for i in range(size)])  16.2 us
    ppermute x10, starting transfers between devices, shift(): return lax.ppermute(x, axis, [((i + step) % size, i) for i in range(size)])  14.4 us
    unnamed x60, local copies, waits for them, and re-layouts  12.6 us
    all_to_all x1, waiting for transfers between devices, shards(): lax.all_to_all(pair_sums, 'expert', split_axis=0, concat_axis=0, tiled=Tr...  11.9 us
    all_to_all x1, waiting for transfers between devices, to_heads(): lax.all_to_all(part, 'expert', split_axis=0, concat_axis=0, tiled=True)  10.4 us
    all_to_all x1, starting transfers between devices, to_heads(): lax.all_to_all(part, 'expert', split_axis=0, concat_axis=0, tiled=True)  10.2 us
    all_to_all x1, waiting for transfers between devices, shards(): lax.all_to_all(outgoing, ('dp', 'expert'), split_axis=0, concat_axis=0, t...  10 us
  transfers between devices with their start and end apart: 21, of which 11 were waited for; matrix products, arithmetic and copies ran while one was open for 13% of the time, Pallas kernels for 13%

profile of v11, /device:TPU:1, one launch (start us, length us, event | category | flops | bytes accessed | tf_op | source)
XLA Modules:
  0.0 205.2 jit_solution(10824866177326924937)
XLA Ops:
  1.5 1.4 collective-permute-start
  2.9 3.4 %collective-permute-done = bf16[64,576]{1,0:T(8,128)(2,1)S(1)} collective-permute-done((bf16[64,576]{1,0:T(8,128)(2,1)S(1)}, bf16[64,576]{1,0:T(8,128)(2,1)S(1)}, u32[]{:S(2)}, u32[]{:S(2)}) %collective-permute-start) | collective-permute-done | bytes 73760 | tf_op jit(solution)/shard_map/ppermute | solution.py:479
  6.3 1.0 pad_maximum_fusion.2.refs_1_
  7.3 2.5 %collective-permute-start.1 = (bf16[256,576]{1,0:T(8,128)(2,1)S(1)}, bf16[256,576]{1,0:T(8,128)(2,1)S(1)}, u32[]{:S(2)}, u32[]{:S(2)}) collective-permute-start(bf16[256,576]{1,0:T(8,128)(2,1)S(1)} %pad_maximum_fusion.2.refs_1_), channel_id=1, source_target_pairs={{32,0},{64,32},{96,64},{0,96},{33,1},{65,33},{97,65},{1,97},{34,2}... | collective-permute-start | bytes 884744 | tf_op jit(solution)/shard_map/ppermute | solution.py:49
  12.4 1.0 tables.1
  14.1 6.4 %weight_slices.1 = (bf16[2,1792,256]{2,1,0:T(8,128)(2,1)}, bf16[2,1792,256]{2,1,0:T(8,128)(2,1)}, bf16[256,1792]{1,0:T(8,128)(2,1)}, bf16[128,1792]{1,0:T(8,128)...) custom-call(s32[5]{0:T(128)} %stack.59.at_ref, bf16[1,7168,256]{2,1,0:T(8,128)(2,1)} %gate_ref.1, ...), custom_call_target="tpu_custom_call" | custom-call | flops 1000 | bytes 4096 | tf_op jit(solution)/shard_map/weight_slices/pallas_call | solution.py:188
  20.6 5.3 %collective-permute-done.3.refs_4_ = bf16[256,576]{1,0:T(8,128)(2,1)S(1)} collective-permute-done((bf16[256,576]{1,0:T(8,128)(2,1)S(1)}, bf16[256,576]{1,0:T(8,128)(2,1)S(1)}, u32[]{:S(2)}, u32[]{:S(2)}) %collective-permute-start.3) | collective-permute-done | bytes 294944 | tf_op jit(solution)/shard_map/ppermute | solution.py:49
  27.2 9.2 %attend.1 = (bf16[64,8,640]{2,1,0:T(8,128)(2,1)}, bf16[14,64,512]{2,1,0:T(8,128)(2,1)}) custom-call(s32[32,128]{1,0:T(8,128)S(1)} %get-tuple-element.82.refs_0_, bf16[256,576]{1,0:T(8,128)(2,1)} %copy-done.14, bf16[256,576]{1,0:T(8,128)(2,1)} %copy-done.18, bf16[256,576]{1,0:T(8,128)(2,1)} %copy-done.19, bf16[256,576]{1,0:T(8,128)(2,1)} %copy-done.20, ...), custom_call_target="tpu_custom_call" | custom-call | flops 100000000 | bytes 4000000 | tf_op jit(solution)/shard_map/attend/pallas_call | solution.py:288
  37.2 10.2 %all-to-all-start.1 = ((bf16[64,8,640]{2,1,0:T(8,128)(2,1)}), bf16[64,8,640]{2,1,0:T(8,128)(2,1)S(1)}, u32[]{:S(2)}, u32[]{:S(2)}) async-start(bf16[64,8,640]{2,1,0:T(8,128)(2,1)} %get-tuple-element.87), calls=%async_computation.1 | async-start | bytes 1310720 | tf_op jit(solution)/shard_map/all_to_all | solution.py:551
  47.4 2.5 %collective-permute-start.6 = (bf16[2,1792,256]{2,1,0:T(8,128)(2,1)}, bf16[2,1792,256]{2,1,0:T(8,128)(2,1)}, u32[]{:S(2)}, u32[]{:S(2)}) collective-permute-start(bf16[2,1792,256]{2,1,0:T(8,128)(2,1)} %get-tuple-element.97), channel_id=1, source_target_pairs={{0,32},{1,97},{2,34},{3,99},{4,36},{5,101},{6,38},{7,103},{8,40},{... | collective-permute-start | bytes 5505032 | tf_op jit(solution)/shard_map/ppermute | solution.py:535
  50.0 10.4 %all-to-all-done.1 = bf16[64,8,640]{2,1,0:T(8,128)(2,1)S(1)} async-done(((bf16[64,8,640]{2,1,0:T(8,128)(2,1)}), bf16[64,8,640]{2,1,0:T(8,128)(2,1)S(1)}, u32[]{:S(2)}, u32[]{:S(2)}) %all-to-all-start.1) | async-done | bytes 655392 | tf_op jit(solution)/shard_map/all_to_all | solution.py:551
  60.4 2.7 %copy-done.2 = bf16[256,7168]{1,0:T(8,128)(2,1)S(1)} copy-done((bf16[256,7168]{1,0:T(8,128)(2,1)S(1)}, bf16[256,7168]{1,0:T(8,128)(2,1)}, u32[]{:S(2)}) %copy-start.2) | copy-done | bytes 3670040
  63.1 3.1 %project.1 = (bf16[48,7168]{1,0:T(8,128)(2,1)S(1)}, bf16[48,7168]{1,0:T(8,128)(2,1)}) custom-call(s32[96,128]{1,0:T(8,128)S(1)} %get-tuple-element.76.cells_ref, bf16[32,2,8,640]{3,2,1,0:T(8,128)(2,1)S(1)} %bitcast.121, bf16[2,96,512]{2,1,0:T(8,128)(2,1)} %copy-done.21, bf16[2,512,128]{2,1,0:T(8,128)(2,1)S(1)} %copy-done.9, bf16[256,7168]{1,0:T(8,128)(2,1)S(1)} %copy-done.2), custom_call_target="tpu_custom_call" | custom-call | flops 400000000 | bytes 6000000 | tf_op jit(solution)/shard_map/project/pallas_call | solution.py:348
  67.5 1.4 collective-permute-done.5.other_ref
  68.9 2.5 %pair_sum.1 = bf16[16,3,7168]{2,1,0:T(4,128)(2,1)} custom-call(bf16[48,7168]{1,0:T(8,128)(2,1)S(1)} %get-tuple-element.95.mine_ref, bf16[48,7168]{1,0:T(8,128)(2,1)} %collective-permute-done.5.other_ref), custom_call_target="tpu_custom_call" | custom-call | flops 400000 | bytes 2000000 | tf_op jit(solution)/shard_map/pair_sum/pallas_call | solution.py:373
  71.4 3.6 %all-to-all-start.2 = ((bf16[16,3,7168]{2,1,0:T(4,128)(2,1)}), bf16[16,3,7168]{2,1,0:T(4,128)(2,1)S(1)}, u32[]{:S(2)}, u32[]{:S(2)}) async-start(bf16[16,3,7168]{2,1,0:T(4,128)(2,1)} %pair_sum.1), calls=%async_computation.2 | async-start | bytes 1835008 | tf_op jit(solution)/shard_map/all_to_all | solution.py:594
  75.8 2.5 %collective-permute-start.7 = (bf16[256,1792]{1,0:T(8,128)(2,1)}, bf16[256,1792]{1,0:T(8,128)(2,1)S(1)}, u32[]{:S(2)}, u32[]{:S(2)}) collective-permute-start(bf16[256,1792]{1,0:T(8,128)(2,1)} %get-tuple-element.100), channel_id=1, source_target_pairs={{32,0},{64,32},{96,64},{0,96},{33,1},{65,33},{97,65},{1,97},{34,2}... | collective-permute-start | bytes 2752520 | tf_op jit(solution)/shard_map/ppermute | solution.py:49
  78.3 11.9 %all-to-all-done.2 = bf16[16,3,7168]{2,1,0:T(4,128)(2,1)S(1)} async-done(((bf16[16,3,7168]{2,1,0:T(4,128)(2,1)}), bf16[16,3,7168]{2,1,0:T(4,128)(2,1)S(1)}, u32[]{:S(2)}, u32[]{:S(2)}) %all-to-all-start.2) | async-done | bytes 688160 | tf_op jit(solution)/shard_map/all_to_all | solution.py:594
  90.6 1.0 multiply_reduce_fusion.1
  93.8 1.3 reshape.262
  95.1 6.8 %all-to-all-start.3 = ((bf16[128,2,1792]{2,1,0:T(2,128)(2,1)}), bf16[128,2,1792]{2,1,0:T(2,128)(2,1)}, u32[]{:S(2)}, u32[]{:S(2)}) async-start(bf16[128,2,1792]{2,1,0:T(2,128)(2,1)} %reshape.262), calls=%async_computation.3 | async-start | bytes 1835008 | tf_op jit(solution)/shard_map/all_to_all | solution.py:637
  102.2 3.0 %collective-permute-start.8 = (bf16[128,1792]{1,0:T(8,128)(2,1)}, bf16[128,1792]{1,0:T(8,128)(2,1)S(1)}, u32[]{:S(2)}, u32[]{:S(2)}) collective-permute-start(bf16[128,1792]{1,0:T(8,128)(2,1)} %get-tuple-element.101), channel_id=1, source_target_pairs={{64,0},{96,32},{0,64},{32,96},{65,1},{97,33},{1,65},{33,97},{66,2}... | collective-permute-start | bytes 1376264 | tf_op jit(solution)/shard_map/ppermute | solution.py:49
  106.5 1.0 slice.105
  107.9 1.5 maximum_bitcast_fusion
  109.4 10.0 %all-to-all-done.3 = bf16[128,2,1792]{2,1,0:T(2,128)(2,1)} async-done(((bf16[128,2,1792]{2,1,0:T(2,128)(2,1)}), bf16[128,2,1792]{2,1,0:T(2,128)(2,1)}, u32[]{:S(2)}, u32[]{:S(2)}) %all-to-all-start.3) | async-done | bytes 917536 | tf_op jit(solution)/shard_map/all_to_all | solution.py:637
  119.4 2.5 %reshape.263.rows_ref = bf16[256,1792]{1,0:T(8,128)(2,1)S(1)} reshape(bf16[128,2,1792]{2,1,0:T(2,128)(2,1)} %all-to-all-done.3) | data formatting | bytes 1835008 | tf_op jit(solution)/shard_map/reshape | solution.py:639
  125.3 1.2 dynamic-slice_bitcast_fusion.refs_4_
  126.5 9.2 %all-to-all-start.4 = ((bf16[32,24,576]{2,1,0:T(8,128)(2,1)}), bf16[32,24,576]{2,1,0:T(8,128)(2,1)}, u32[]{:S(2)}, u32[]{:S(2)}) async-start(bf16[32,24,576]{2,1,0:T(8,128)(2,1)} %maximum_bitcast_fusion), calls=%async_computation.4 | async-start | bytes 1966080 | tf_op jit(solution)/shard_map/all_to_all | solution.py:649
  135.7 1.7 fusion.24
  137.5 1.6 fusion.26
  139.1 1.8 gate_up.2.refs_0_
  140.9 1.8 gate_up.3
  142.7 1.9 collective-permute-start.11
  144.6 1.6 fusion.20
  146.2 2.8 %collective-permute-start.15 = (bf16[128,1792]{1,0:T(8,128)(2,1)}, bf16[128,1792]{1,0:T(8,128)(2,1)S(1)}, u32[]{:S(2)}, u32[]{:S(2)}) collective-permute-start(bf16[128,1792]{1,0:T(8,128)(2,1)} %get-tuple-element.116), channel_id=1, source_target_pairs={{64,0},{96,32},{0,64},{32,96},{65,1},{97,33},{1,65},{33,97},{66,2}... | collective-permute-start | bytes 1376264 | tf_op jit(solution)/shard_map/ppermute | solution.py:49
  149.0 1.6 fusion.22
  151.7 1.6 collective-permute-start.13
  153.3 1.6 fusion.32
  154.9 7.0 %collective-permute-done.12.refs_1_ = bf16[256,256]{1,0:T(8,128)(2,1)S(1)} collective-permute-done((bf16[256,256]{1,0:T(8,128)(2,1)S(1)}, bf16[256,256]{1,0:T(8,128)(2,1)S(1)}, u32[]{:S(2)}, u32[]{:S(2)}) %collective-permute-start.12) | collective-permute-done | bytes 131104 | tf_op jit(solution)/shard_map/ppermute | solution.py:49
  163.2 2.9 %collective-permute-done.14.refs_3_ = bf16[256,256]{1,0:T(8,128)(2,1)S(1)} collective-permute-done((bf16[256,256]{1,0:T(8,128)(2,1)S(1)}, bf16[256,256]{1,0:T(8,128)(2,1)S(1)}, u32[]{:S(2)}, u32[]{:S(2)}) %collective-permute-start.14) | collective-permute-done | bytes 131104 | tf_op jit(solution)/shard_map/ppermute | solution.py:49
  167.5 1.2 copy-done.4
  168.7 1.2 copy-done.6
  169.9 1.0 copy-done.8
  172.7 1.5 down_product.1
  174.2 1.3 reshape.271
  175.5 9.4 %all-to-all-start.5 = ((bf16[128,2,1792]{2,1,0:T(2,128)(2,1)}), bf16[128,2,1792]{2,1,0:T(2,128)(2,1)S(1)}, u32[]{:S(2)}, u32[]{:S(2)}) async-start(bf16[128,2,1792]{2,1,0:T(2,128)(2,1)} %reshape.271), calls=%async_computation.5 | async-start | bytes 1835008 | tf_op jit(solution)/shard_map/all_to_all | solution.py:673
  186.1 16.5 %all-to-all-done.5 = bf16[128,2,1792]{2,1,0:T(2,128)(2,1)S(1)} async-done(((bf16[128,2,1792]{2,1,0:T(2,128)(2,1)}), bf16[128,2,1792]{2,1,0:T(2,128)(2,1)S(1)}, u32[]{:S(2)}, u32[]{:S(2)}) %all-to-all-start.5) | async-done | bytes 917536 | tf_op jit(solution)/shard_map/all_to_all | solution.py:673
  204.0 1.2 fusion.15
  (134 shorter events, 23.5 us)
Async XLA Ops:
  1.5 4.8 %collective-permute-start = (bf16[64,576]{1,0:T(8,128)(2,1)S(1)}, bf16[64,576]{1,0:T(8,128)(2,1)S(1)}, u32[]{:S(2)}, u32[]{:S(2)}) collective-permute-start(bf16[64,576]{1,0:T(8,128)(2,1)S(1)} %slice.98), channel_id=1, source_target_pairs={{1,0},{2,1},{3,2},{4,3},{5,4},{6,5},{7,6},{8,7},{9,8},{10,9},{11,1... | collective-permute-start | bytes 221192 | tf_op jit(solution)/shard_map/ppermute | solution.py:479
  7.3 13.2 %copy-start.14 = (bf16[256,576]{1,0:T(8,128)(2,1)}, bf16[256,576]{1,0:T(8,128)(2,1)S(1)}, u32[]{:S(2)}) copy-start(bf16[256,576]{1,0:T(8,128)(2,1)S(1)} %pad_maximum_fusion.2.refs_1_) | copy-start | bytes 884740
  7.3 13.2 %collective-permute-start.1 = (bf16[256,576]{1,0:T(8,128)(2,1)S(1)}, bf16[256,576]{1,0:T(8,128)(2,1)S(1)}, u32[]{:S(2)}, u32[]{:S(2)}) collective-permute-start(bf16[256,576]{1,0:T(8,128)(2,1)S(1)} %pad_maximum_fusion.2.refs_1_), channel_id=1, source_target_pairs={{32,0},{64,32},{96,64},{0,96},{33,1},{65,33},{97,65},{1,97},{34,2}... | collective-permute-start | bytes 884744 | tf_op jit(solution)/shard_map/ppermute | solution.py:49
  9.9 10.7 %collective-permute-start.2 = (bf16[256,576]{1,0:T(8,128)(2,1)S(1)}, bf16[256,576]{1,0:T(8,128)(2,1)S(1)}, u32[]{:S(2)}, u32[]{:S(2)}) collective-permute-start(bf16[256,576]{1,0:T(8,128)(2,1)S(1)} %pad_maximum_fusion.2.refs_1_), channel_id=1, source_target_pairs={{64,0},{96,32},{0,64},{32,96},{65,1},{97,33},{1,65},{33,97},{66,2}... | collective-permute-start | bytes 884744 | tf_op jit(solution)/shard_map/ppermute | solution.py:49
  10.4 15.5 %collective-permute-start.3 = (bf16[256,576]{1,0:T(8,128)(2,1)S(1)}, bf16[256,576]{1,0:T(8,128)(2,1)S(1)}, u32[]{:S(2)}, u32[]{:S(2)}) collective-permute-start(bf16[256,576]{1,0:T(8,128)(2,1)S(1)} %pad_maximum_fusion.2.refs_1_), channel_id=1, source_target_pairs={{96,0},{0,32},{32,64},{64,96},{97,1},{1,33},{33,65},{65,97},{98,2}... | collective-permute-start | bytes 884744 | tf_op jit(solution)/shard_map/ppermute | solution.py:49
  14.1 13.0 %copy-start.24 = (s32[384]{0:T(512)S(1)}, s32[384]{0:T(512)}, u32[]{:S(2)}) copy-start(s32[384]{0:T(512)} %param.23) | copy-start | bytes 4612
  20.6 6.6 %copy-start.18 = (bf16[256,576]{1,0:T(8,128)(2,1)}, bf16[256,576]{1,0:T(8,128)(2,1)S(1)}, u32[]{:S(2)}) copy-start(bf16[256,576]{1,0:T(8,128)(2,1)S(1)} %collective-permute-done.1.refs_2_) | copy-start | bytes 884740
  20.6 6.6 %copy-start.19 = (bf16[256,576]{1,0:T(8,128)(2,1)}, bf16[256,576]{1,0:T(8,128)(2,1)S(1)}, u32[]{:S(2)}) copy-start(bf16[256,576]{1,0:T(8,128)(2,1)S(1)} %collective-permute-done.2.refs_3_) | copy-start | bytes 884740
  25.9 1.3 copy-start.20
  25.9 34.5 %collective-permute-start.4 = (bf16[2,1792,256]{2,1,0:T(8,128)(2,1)}, bf16[2,1792,256]{2,1,0:T(8,128)(2,1)S(1)}, u32[]{:S(2)}, u32[]{:S(2)}) collective-permute-start(bf16[2,1792,256]{2,1,0:T(8,128)(2,1)} %get-tuple-element.88), channel_id=1, source_target_pairs={{0,32},{1,97},{2,34},{3,99},{4,36},{5,101},{6,38},{7,103},{8,40},{... | collective-permute-start | bytes 5505032 | tf_op jit(solution)/shard_map/ppermute | solution.py:534
  36.5 23.9 %copy-start.9 = (bf16[2,512,128]{2,1,0:T(8,128)(2,1)S(1)}, bf16[2,512,128]{2,1,0:T(8,128)(2,1)}, u32[]{:S(2)}) copy-start(bf16[2,512,128]{2,1,0:T(8,128)(2,1)} %uv_ref.1) | copy-start | bytes 786436
  36.5 30.2 %copy-start.27 = (s32[1,3,8]{2,0,1:T(1,128)S(1)}, s32[1,3,8]{2,0,1:T(1,128)}, u32[]{:S(2)}) copy-start(s32[1,3,8]{2,0,1:T(1,128)} %param.29) | copy-start | bytes 292
  36.5 30.9 %copy-start.28 = (f32[1,3,8]{2,0,1:T(1,128)S(1)}, f32[1,3,8]{2,0,1:T(1,128)}, u32[]{:S(2)}) copy-start(f32[1,3,8]{2,0,1:T(1,128)} %param.30) | copy-start | bytes 292
  36.6 30.9 %copy-start.25 = (s32[384]{0:T(512)S(1)}, s32[384]{0:T(512)}, u32[]{:S(2)}) copy-start(s32[384]{0:T(512)} %param.22) | copy-start | bytes 4612
  37.2 23.2 %all-to-all-start.1 = ((bf16[64,8,640]{2,1,0:T(8,128)(2,1)}), bf16[64,8,640]{2,1,0:T(8,128)(2,1)S(1)}, u32[]{:S(2)}, u32[]{:S(2)}) async-start(bf16[64,8,640]{2,1,0:T(8,128)(2,1)} %get-tuple-element.87), calls=%async_computation.1 | async-start | bytes 1310720 | tf_op jit(solution)/shard_map/all_to_all | solution.py:551
  47.4 30.9 %collective-permute-start.6 = (bf16[2,1792,256]{2,1,0:T(8,128)(2,1)}, bf16[2,1792,256]{2,1,0:T(8,128)(2,1)}, u32[]{:S(2)}, u32[]{:S(2)}) collective-permute-start(bf16[2,1792,256]{2,1,0:T(8,128)(2,1)} %get-tuple-element.97), channel_id=1, source_target_pairs={{0,32},{1,97},{2,34},{3,99},{4,36},{5,101},{6,38},{7,103},{8,40},{... | collective-permute-start | bytes 5505032 | tf_op jit(solution)/shard_map/ppermute | solution.py:535
  60.4 11.0 %copy-start = (bf16[2,1792,256]{2,1,0:T(8,128)(2,1)}, bf16[2,1792,256]{2,1,0:T(8,128)(2,1)S(1)}, u32[]{:S(2)}) copy-start(bf16[2,1792,256]{2,1,0:T(8,128)(2,1)S(1)} %collective-permute-done.4.gate_ref) | copy-start | bytes 5505028
  60.4 2.7 %copy-start.2 = (bf16[256,7168]{1,0:T(8,128)(2,1)S(1)}, bf16[256,7168]{1,0:T(8,128)(2,1)}, u32[]{:S(2)}) copy-start(bf16[256,7168]{1,0:T(8,128)(2,1)} %weight_ref.1) | copy-start | bytes 11010052
  66.2 2.7 %collective-permute-start.5 = (bf16[48,7168]{1,0:T(8,128)(2,1)}, bf16[48,7168]{1,0:T(8,128)(2,1)}, u32[]{:S(2)}, u32[]{:S(2)}) collective-permute-start(bf16[48,7168]{1,0:T(8,128)(2,1)} %get-tuple-element.96), channel_id=1, source_target_pairs={{0,1},{1,0},{2,3},{3,2},{4,5},{5,4},{6,7},{7,6},{8,9},{9,8},{10,11... | collective-permute-start | bytes 2064392 | tf_op jit(solution)/shard_map/ppermute | solution.py:592
  71.4 18.8 %all-to-all-start.2 = ((bf16[16,3,7168]{2,1,0:T(4,128)(2,1)}), bf16[16,3,7168]{2,1,0:T(4,128)(2,1)S(1)}, u32[]{:S(2)}, u32[]{:S(2)}) async-start(bf16[16,3,7168]{2,1,0:T(4,128)(2,1)} %pair_sum.1), calls=%async_computation.2 | async-start | bytes 1835008 | tf_op jit(solution)/shard_map/all_to_all | solution.py:594
  75.8 46.0 %collective-permute-start.7 = (bf16[256,1792]{1,0:T(8,128)(2,1)}, bf16[256,1792]{1,0:T(8,128)(2,1)S(1)}, u32[]{:S(2)}, u32[]{:S(2)}) collective-permute-start(bf16[256,1792]{1,0:T(8,128)(2,1)} %get-tuple-element.100), channel_id=1, source_target_pairs={{32,0},{64,32},{96,64},{0,96},{33,1},{65,33},{97,65},{1,97},{34,2}... | collective-permute-start | bytes 2752520 | tf_op jit(solution)/shard_map/ppermute | solution.py:49
  78.3 44.5 %collective-permute-start.9 = (bf16[256,1792]{1,0:T(8,128)(2,1)}, bf16[256,1792]{1,0:T(8,128)(2,1)S(1)}, u32[]{:S(2)}, u32[]{:S(2)}) collective-permute-start(bf16[256,1792]{1,0:T(8,128)(2,1)} %get-tuple-element.102), channel_id=1, source_target_pairs={{96,0},{0,32},{32,64},{64,96},{97,1},{1,33},{33,65},{65,97},{98,2}... | collective-permute-start | bytes 2752520 | tf_op jit(solution)/shard_map/ppermute | solution.py:49
  90.6 2.9 %copy-start.16 = (f32[3,7168]{1,0:T(4,128)}, f32[3,7168]{1,0:T(4,128)S(1)}, u32[]{:S(2)}) copy-start(f32[3,7168]{1,0:T(4,128)S(1)} %convert_reduce_fusion) | copy-start | bytes 258052
  90.6 15.9 %copy-start.15 = (bf16[256,576]{1,0:T(8,128)(2,1)S(1)}, bf16[256,576]{1,0:T(8,128)(2,1)}, u32[]{:S(2)}) copy-start(bf16[256,576]{1,0:T(8,128)(2,1)} %copy-done.14) | copy-start | bytes 884740
  95.1 12.5 %slice-start = ((bf16[256,576]{1,0:T(8,128)(2,1)}), bf16[192,576]{1,0:T(8,128)(2,1)S(1)}, s32[]{:S(2)}) async-start(bf16[256,576]{1,0:T(8,128)(2,1)} %copy-done.19), calls=%async_computation.6 | async-start | bytes 491520 | tf_op jit(solution)/shard_map/slice | solution.py:643
  95.1 12.6 %slice-start.1 = ((bf16[256,576]{1,0:T(8,128)(2,1)}), bf16[192,576]{1,0:T(8,128)(2,1)S(1)}, s32[]{:S(2)}) async-start(bf16[256,576]{1,0:T(8,128)(2,1)} %copy-done.20), calls=%async_computation.7 | async-start | bytes 491520 | tf_op jit(solution)/shard_map/slice | solution.py:643
  95.1 24.3 %all-to-all-start.3 = ((bf16[128,2,1792]{2,1,0:T(2,128)(2,1)}), bf16[128,2,1792]{2,1,0:T(2,128)(2,1)}, u32[]{:S(2)}, u32[]{:S(2)}) async-start(bf16[128,2,1792]{2,1,0:T(2,128)(2,1)} %reshape.262), calls=%async_computation.3 | async-start | bytes 1835008 | tf_op jit(solution)/shard_map/all_to_all | solution.py:637
  102.2 22.1 %collective-permute-start.8 = (bf16[128,1792]{1,0:T(8,128)(2,1)}, bf16[128,1792]{1,0:T(8,128)(2,1)S(1)}, u32[]{:S(2)}, u32[]{:S(2)}) collective-permute-start(bf16[128,1792]{1,0:T(8,128)(2,1)} %get-tuple-element.101), channel_id=1, source_target_pairs={{64,0},{96,32},{0,64},{32,96},{65,1},{97,33},{1,65},{33,97},{66,2}... | collective-permute-start | bytes 1376264 | tf_op jit(solution)/shard_map/ppermute | solution.py:49
  121.9 1.0 copy-start.3
  122.8 0.9 copy-start.5
  124.2 16.6 %collective-permute-start.10 = (bf16[256,1792]{1,0:T(8,128)(2,1)S(1)}, bf16[256,1792]{1,0:T(8,128)(2,1)S(1)}, u32[]{:S(2)}, u32[]{:S(2)}) collective-permute-start(bf16[256,1792]{1,0:T(8,128)(2,1)S(1)} %reshape.263.rows_ref), channel_id=1, source_target_pairs={{0,96},{1,33},{2,98},{3,35},{4,100},{5,37},{6,102},{7,39},{8,104},... | collective-permute-start | bytes 2752520 | tf_op jit(solution)/shard_map/ppermute | solution.py:648
  126.5 26.7 %all-to-all-start.4 = ((bf16[32,24,576]{2,1,0:T(8,128)(2,1)}), bf16[32,24,576]{2,1,0:T(8,128)(2,1)}, u32[]{:S(2)}, u32[]{:S(2)}) async-start(bf16[32,24,576]{2,1,0:T(8,128)(2,1)} %maximum_bitcast_fusion), calls=%async_computation.4 | async-start | bytes 1966080 | tf_op jit(solution)/shard_map/all_to_all | solution.py:649
  135.7 3.4 %copy-start.1 = (bf16[2,1792,256]{2,1,0:T(8,128)(2,1)S(1)}, bf16[2,1792,256]{2,1,0:T(8,128)(2,1)}, u32[]{:S(2)}) copy-start(bf16[2,1792,256]{2,1,0:T(8,128)(2,1)} %copy-done) | copy-start | bytes 5505028
  142.7 7.9 %collective-permute-start.11 = (bf16[256,512]{1,0:T(8,128)(2,1)S(1)}, bf16[256,512]{1,0:T(8,128)(2,1)S(1)}, u32[]{:S(2)}, u32[]{:S(2)}) collective-permute-start(bf16[256,512]{1,0:T(8,128)(2,1)S(1)} %gate_up.3), channel_id=1, source_target_pairs={{0,32},{1,97},{2,34},{3,99},{4,36},{5,101},{6,38},{7,103},{8,40},{... | collective-permute-start | bytes 786440 | tf_op jit(solution)/shard_map/ppermute | solution.py:659
  146.2 20.5 %collective-permute-start.15 = (bf16[128,1792]{1,0:T(8,128)(2,1)}, bf16[128,1792]{1,0:T(8,128)(2,1)S(1)}, u32[]{:S(2)}, u32[]{:S(2)}) collective-permute-start(bf16[128,1792]{1,0:T(8,128)(2,1)} %get-tuple-element.116), channel_id=1, source_target_pairs={{64,0},{96,32},{0,64},{32,96},{65,1},{97,33},{1,65},{33,97},{66,2}... | collective-permute-start | bytes 1376264 | tf_op jit(solution)/shard_map/ppermute | solution.py:49
  150.8 11.1 %collective-permute-start.12 = (bf16[256,256]{1,0:T(8,128)(2,1)S(1)}, bf16[256,256]{1,0:T(8,128)(2,1)S(1)}, u32[]{:S(2)}, u32[]{:S(2)}) collective-permute-start(bf16[256,256]{1,0:T(8,128)(2,1)S(1)} %fusion.39.refs_0_), channel_id=1, source_target_pairs={{32,0},{64,32},{96,64},{0,96},{33,1},{65,33},{97,65},{1,97},{34,2}... | collective-permute-start | bytes 393224 | tf_op jit(solution)/shard_map/ppermute | solution.py:49
  151.7 10.8 %collective-permute-start.13 = (bf16[256,256]{1,0:T(8,128)(2,1)S(1)}, bf16[256,256]{1,0:T(8,128)(2,1)S(1)}, u32[]{:S(2)}, u32[]{:S(2)}) collective-permute-start(bf16[256,256]{1,0:T(8,128)(2,1)S(1)} %fusion.39.refs_0_), channel_id=1, source_target_pairs={{64,0},{96,32},{0,64},{32,96},{65,1},{97,33},{1,65},{33,97},{66,2}... | collective-permute-start | bytes 393224 | tf_op jit(solution)/shard_map/ppermute | solution.py:49
  153.3 12.8 %collective-permute-start.14 = (bf16[256,256]{1,0:T(8,128)(2,1)S(1)}, bf16[256,256]{1,0:T(8,128)(2,1)S(1)}, u32[]{:S(2)}, u32[]{:S(2)}) collective-permute-start(bf16[256,256]{1,0:T(8,128)(2,1)S(1)} %fusion.39.refs_0_), channel_id=1, source_target_pairs={{96,0},{0,32},{32,64},{64,96},{97,1},{1,33},{33,65},{65,97},{98,2}... | collective-permute-start | bytes 393224 | tf_op jit(solution)/shard_map/ppermute | solution.py:49
  153.3 31.7 %copy-start.26 = (pred[192]{0:T(512)(128)(4,1)S(1)}, pred[192]{0:T(512)(128)(4,1)}, u32[]{:S(2)}) copy-start(pred[192]{0:T(512)(128)(4,1)} %get-tuple-element.158) | copy-start | bytes 580
  153.3 31.9 %copy-start.23 = (f32[512]{0:T(512)S(1)}, f32[512]{0:T(512)}, u32[]{:S(2)}) copy-start(f32[512]{0:T(512)} %param.21) | copy-start | bytes 6148
  167.5 1.2 copy-start.4
  168.7 1.2 copy-start.6
  169.9 1.0 copy-start.8
  170.9 0.9 copy-start.11
  171.8 0.9 copy-start.13
  175.5 28.5 %copy-start.17 = (f32[3,7168]{1,0:T(4,128)S(1)}, f32[3,7168]{1,0:T(4,128)}, u32[]{:S(2)}) copy-start(f32[3,7168]{1,0:T(4,128)} %copy-done.16) | copy-start | bytes 258052
  175.5 28.5 %copy-start.22 = (bf16[1,3,7168]{2,1,0:T(4,128)(2,1)S(1)}, bf16[1,3,7168]{2,1,0:T(4,128)(2,1)}, u32[]{:S(2)}) copy-start(bf16[1,3,7168]{2,1,0:T(4,128)(2,1)} %param.27) | copy-start | bytes 129028
  175.5 27.1 %all-to-all-start.5 = ((bf16[128,2,1792]{2,1,0:T(2,128)(2,1)}), bf16[128,2,1792]{2,1,0:T(2,128)(2,1)S(1)}, u32[]{:S(2)}, u32[]{:S(2)}) async-start(bf16[128,2,1792]{2,1,0:T(2,128)(2,1)} %reshape.271), calls=%async_computation.5 | async-start | bytes 1835008 | tf_op jit(solution)/shard_map/all_to_all | solution.py:673
  (4 other events, 2.8 us)

commit v12 on v11

--- a/solution.py
+++ b/solution.py
@@ -14,7 +14,6 @@
 PARTS = MAIN // (SLOTS - MAIN)
 EXTRA = LAT // PARTS
 VMEM = 58 * 1024 * 1024
-SMALL = 20 * 1024 * 1024
 
 eps = 1e-06
 theta = 10000.0
@@ -312,7 +311,17 @@
     )(slots, *rows, cosine, sine, gain, new_rows, queries)
 
 
-def project_kernel(cells_ref, came_ref, more_ref, uv_ref, weight_ref, mine_ref, other_ref):
+def project_kernel(
+    cells_ref, came_ref, more_ref, uv_ref, weight_ref, mine_ref, other_ref, weight, sems
+):
+    step = weight.shape[1] // 4
+    spans = [slice(i * step, (i + 1) * step) for i in range(4)]
+    copies = [
+        pltpu.make_async_copy(weight_ref.at[:, span], weight.at[:, span], sems.at[i])
+        for i, span in enumerate(spans)
+    ]
+    for copy in copies:
+        copy.start()
     requests = cells_ref.shape[0]
     sources, heads, slots, _ = came_ref.shape
     cells = sources * slots
@@ -334,10 +343,9 @@
         )
     projected = jnp.concatenate(projected, axis=1)
     keep = mine_ref.shape[0]
-    step = weight_ref.shape[1] // 4
-    for first in range(0, weight_ref.shape[1], step):
-        span = slice(first, first + step)
-        sums = jnp.dot(projected, weight_ref[:, span], preferred_element_type=F32).astype(BF)
+    for span, copy in zip(spans, copies):
+        copy.wait()
+        sums = jnp.dot(projected, weight[:, span], preferred_element_type=F32).astype(BF)
         mine_ref[:, span] = sums[:keep]
         other_ref[:, span] = sums[keep:]
 
@@ -348,9 +356,10 @@
     return pl.pallas_call(
         project_kernel,
         out_shape=(half, half),
-        in_specs=[whole] * 5,
+        in_specs=[whole] * 4 + [pl.BlockSpec(memory_space=pltpu.HBM)],
         out_specs=(whole, whole),
-        compiler_params=pltpu.CompilerParams(vmem_limit_bytes=SMALL),
+        scratch_shapes=[pltpu.VMEM(w_out.shape, BF), pltpu.SemaphoreType.DMA((4,))],
+        compiler_params=pltpu.CompilerParams(vmem_limit_bytes=32 * 1024 * 1024),
         cost_estimate=pl.CostEstimate(
             flops=4 * 10**8, bytes_accessed=6 * 10**6, transcendentals=0
         ),
@@ -375,43 +384,12 @@
         out_shape=jax.ShapeDtypeStruct((chips, mine.shape[0] // chips, mine.shape[1]), BF),
         in_specs=[whole] * 2,
         out_specs=whole,
-        compiler_params=pltpu.CompilerParams(vmem_limit_bytes=SMALL),
+        compiler_params=pltpu.CompilerParams(vmem_limit_bytes=32 * 1024 * 1024),
         cost_estimate=pl.CostEstimate(
             flops=4 * 10**5, bytes_accessed=2 * 10**6, transcendentals=0
         ),
         name="pair_sum",
     )(mine, other)
-
-
-def gate_up_kernel(rows_ref, gate_ref, up_ref, *refs):
-    base_ref, out_ref = refs if len(refs) == 2 else (None, refs[0])
-    half = gate_ref.shape[2]
-    for i, weight_ref in enumerate((gate_ref, up_ref)):
-        span = slice(i * half, (i + 1) * half)
-        sums = jnp.dot(rows_ref[...], weight_ref[0], preferred_element_type=F32)
-        if base_ref is not None:
-            sums = sums + base_ref[:, span]
-        out_ref[:, span] = sums.astype(out_ref.dtype)
-
-
-def gate_up(rows, gate, up, quarter, base=None):
-    half = gate.shape[2]
-    shape = (rows.shape[0], 2 * half)
-    whole = pl.BlockSpec(shape, lambda i: (0, 0))
-    weight = pl.BlockSpec((1,) + gate.shape[1:], lambda i: (quarter, 0, 0))
-    return pl.pallas_call(
-        gate_up_kernel,
-        grid=(1,),
-        out_shape=jax.ShapeDtypeStruct(shape, F32 if base is None else BF),
-        in_specs=[pl.BlockSpec(rows.shape, lambda i: (0, 0)), weight, weight]
-        + ([] if base is None else [whole]),
-        out_specs=whole,
-        compiler_params=pltpu.CompilerParams(vmem_limit_bytes=SMALL),
-        cost_estimate=pl.CostEstimate(
-            flops=5 * 10**8, bytes_accessed=4 * 10**6, transcendentals=0
-        ),
-        name="gate_up",
-    )(rows, gate, up, *(() if base is None else (base,)))
 
 
 def down_kernel(*refs):
@@ -438,7 +416,7 @@
         out_shape=jax.ShapeDtypeStruct((blocks[0].shape[0], weights[0].shape[1]), BF),
         in_specs=[whole] * 9,
         out_specs=whole,
-        compiler_params=pltpu.CompilerParams(vmem_limit_bytes=SMALL),
+        compiler_params=pltpu.CompilerParams(vmem_limit_bytes=VMEM),
         cost_estimate=pl.CostEstimate(
             flops=10**9, bytes_accessed=5 * 10**6, transcendentals=0
         ),
@@ -649,19 +627,16 @@
     dealt = lax.all_to_all(to_rows, "expert", split_axis=0, concat_axis=0, tiled=True)
 
     gate_own, up_own = width_half(w_gate, my_quarter), width_half(w_up, my_quarter)
-    own_halves = (gate_own, up_own)
-    first = [jnp.dot(arrived, weight[0], preferred_element_type=F32) for weight in own_halves]
-    given = gate_up(arrived, gate_came, up_came, 0)
-    beside, given, far_second, *first = lax.optimization_barrier(
-        (beside, given, far_second, *first)
-    )
-    given = gate_up(beside, gate_came, up_came, 1, given)
+    weights = (gate_came, up_came, gate_own, up_own)
+    first = [jnp.dot(arrived, weight[0], preferred_element_type=F32) for weight in weights]
+    beside, far_second, *first = lax.optimization_barrier((beside, far_second, *first))
+    gate_given, up_given, gate_sum, up_sum = (
+        part + jnp.dot(beside, weight[1], preferred_element_type=F32)
+        for part, weight in zip(first, weights)
+    )
+    given = jnp.concatenate([gate_given, up_given], axis=1).astype(BF)
     given = lax.ppermute(given, ("dp", "expert"), weight_perm).astype(F32)
     far_second = shift(far_second, 2, dp_count, "dp")
-    gate_sum, up_sum = (
-        part + jnp.dot(beside, weight[1], preferred_element_type=F32)
-        for part, weight in zip(first, own_halves)
-    )
     half = gate_sum.shape[1]
     hidden = (
         jax.nn.silu(gate_sum + given[:, :half]) * (up_sum + given[:, half:])

time: 207 us -> 199 us (0.961)
  local copies, waits for them, and re-layouts: 25.9 us -> 16.5 us
  waiting for transfers between devices: 69.8 us -> 77.1 us
  matrix products: 10.4 us -> 15.4 us
  starting transfers between devices: 60.3 us -> 56 us
  other arithmetic: 9.44 us -> 6.16 us
  Pallas kernels: 27.4 us -> 24.8 us
    unnamed x60 -> x38, local copies, waits for them, and re-layouts: 12.6 us -> 2.73 us
    ppermute x10, waiting for transfers between devices: 16.2 us -> 23.5 us  [shift(): return lax.ppermute(x, axis, [((i + step) % size, i) for i in range(size)])]
    pallas_call x2 -> x0, Pallas kernels: 3.63 us -> none  [gate_up(): pl.pallas_call(gate_up_kernel, grid=(1,), out_shape=jax.ShapeDtypeStruct(...]
    dot_general x2 -> x4, matrix products: 3.17 us -> 6.36 us  [shards(): jnp.dot(beside, weight[1], preferred_element_type=F32)]
    pallas_call x1, Pallas kernels: 1.46 us -> 4.62 us  [down_product(): pl.pallas_call(down_kernel, out_shape=jax.ShapeDtypeStruct((blocks[0].sha...]
    dot_general x2 -> x4, matrix products: 3.32 us -> 6.36 us  [shards(): jnp.dot(arrived, weight[0], preferred_element_type=F32)]
    ppermute x10, starting transfers between devices: 14.4 us -> 11.9 us  [shift(): return lax.ppermute(x, axis, [((i + step) % size, i) for i in range(size)])]
    reshape x1, local copies, waits for them, and re-layouts: 2.46 us -> 0.34 us  [shards(): arrived = lax.all_to_all(outgoing, ('dp', 'expert'), split_axis=0, concat...]
  transfers between devices with their start and end apart: 21 -> 21, of which waited for: 11 -> 12; matrix products, arithmetic and copies ran while one was open for 13% -> 14% of each run, Pallas kernels for 13% -> 10%
where the time goes in v12:
time: 199 us; the launch traced here: 198 us
  waiting for transfers between devices  77.1 us (39%)
  starting transfers between devices  56 us (28%)
  Pallas kernels  24.8 us (12%)
  local copies, waits for them, and re-layouts  16.5 us (8%)
  matrix products  15.4 us (8%)
  other arithmetic  6.16 us (3%)
    ppermute x10, waiting for transfers between devices, shift(): return lax.ppermute(x, axis, [((i + step) % size, i) for i in range(size)])  23.5 us
    all_to_all x1, waiting for transfers between devices, shards(): lax.all_to_all(out.reshape(devices, capacity, piece), ('dp', 'expert'), s...  16.5 us
    all_to_all x1, waiting for transfers between devices, shards(): lax.all_to_all(pair_sums, 'expert', split_axis=0, concat_axis=0, tiled=Tr...  12.2 us
    ppermute x10, starting transfers between devices, shift(): return lax.ppermute(x, axis, [((i + step) % size, i) for i in range(size)])  11.9 us
    all_to_all x1, starting transfers between devices, to_heads(): lax.all_to_all(part, 'expert', split_axis=0, concat_axis=0, tiled=True)  10.4 us
    all_to_all x1, waiting for transfers between devices, to_heads(): lax.all_to_all(part, 'expert', split_axis=0, concat_axis=0, tiled=True)  10.3 us
    pallas_call x1, Pallas kernels, attend(): pl.pallas_call(body, out_shape=(jax.ShapeDtypeStruct((heads, MAIN, LAT +...  9.21 us
    all_to_all x1, starting transfers between devices, shards(): lax.all_to_all(to_rows, 'expert', split_axis=0, concat_axis=0, tiled=True)  9.11 us
  transfers between devices with their start and end apart: 21, of which 12 were waited for; matrix products, arithmetic and copies ran while one was open for 14% of the time, Pallas kernels for 10%

profile of v12, /device:TPU:1, one launch (start us, length us, event | category | flops | bytes accessed | tf_op | source)
XLA Modules:
  0.0 197.9 jit_solution(8195440560044049402)
XLA Ops:
  0.6 0.9 slice.110
  1.5 1.4 collective-permute-start
  2.9 3.4 %collective-permute-done = bf16[64,576]{1,0:T(8,128)(2,1)S(1)} collective-permute-done((bf16[64,576]{1,0:T(8,128)(2,1)S(1)}, bf16[64,576]{1,0:T(8,128)(2,1)S(1)}, u32[]{:S(2)}, u32[]{:S(2)}) %collective-permute-start) | collective-permute-done | bytes 73760 | tf_op jit(solution)/shard_map/ppermute | solution.py:457
  6.3 1.0 pad_maximum_fusion.2.refs_1_
  7.3 2.5 %collective-permute-start.1 = (bf16[256,576]{1,0:T(8,128)(2,1)S(1)}, bf16[256,576]{1,0:T(8,128)(2,1)S(1)}, u32[]{:S(2)}, u32[]{:S(2)}) collective-permute-start(bf16[256,576]{1,0:T(8,128)(2,1)S(1)} %pad_maximum_fusion.2.refs_1_), channel_id=1, source_target_pairs={{32,0},{64,32},{96,64},{0,96},{33,1},{65,33},{97,65},{1,97},{34,2}... | collective-permute-start | bytes 884744 | tf_op jit(solution)/shard_map/ppermute | solution.py:48
  12.4 1.0 tables.1
  14.1 6.4 %weight_slices.1 = (bf16[2,1792,256]{2,1,0:T(8,128)(2,1)}, bf16[2,1792,256]{2,1,0:T(8,128)(2,1)}, bf16[256,1792]{1,0:T(8,128)(2,1)}, bf16[128,1792]{1,0:T(8,128)...) custom-call(s32[5]{0:T(128)} %stack.59.at_ref, bf16[1,7168,256]{2,1,0:T(8,128)(2,1)} %gate_ref.1, ...), custom_call_target="tpu_custom_call" | custom-call | flops 1000 | bytes 4096 | tf_op jit(solution)/shard_map/weight_slices/pallas_call | solution.py:187
  20.6 5.3 %collective-permute-done.3.refs_4_ = bf16[256,576]{1,0:T(8,128)(2,1)S(1)} collective-permute-done((bf16[256,576]{1,0:T(8,128)(2,1)S(1)}, bf16[256,576]{1,0:T(8,128)(2,1)S(1)}, u32[]{:S(2)}, u32[]{:S(2)}) %collective-permute-start.3) | collective-permute-done | bytes 294944 | tf_op jit(solution)/shard_map/ppermute | solution.py:48
  27.3 9.2 %attend.1 = (bf16[64,8,640]{2,1,0:T(8,128)(2,1)}, bf16[14,64,512]{2,1,0:T(8,128)(2,1)S(1)}) custom-call(s32[32,128]{1,0:T(8,128)S(1)} %get-tuple-element.83.refs_0_, bf16[256,576]{1,0:T(8,128)(2,1)} %copy-done.2, bf16[256,576]{1,0:T(8,128)(2,1)} %copy-done.4, bf16[256,576]{1,0:T(8,128)(2,1)} %copy-done.5, bf16[256,576]{1,0:T(8,128)(2,1)} %copy-done.6, ...), custom_call_target="tpu_custom_call" | custom-call | flops 100000000 | bytes 4000000 | tf_op jit(solution)/shard_map/attend/pallas_call | solution.py:287
  36.6 10.4 %all-to-all-start.1 = ((bf16[64,8,640]{2,1,0:T(8,128)(2,1)}), bf16[64,8,640]{2,1,0:T(8,128)(2,1)S(1)}, u32[]{:S(2)}, u32[]{:S(2)}) async-start(bf16[64,8,640]{2,1,0:T(8,128)(2,1)} %get-tuple-element.88), calls=%async_computation.1 | async-start | bytes 1310720 | tf_op jit(solution)/shard_map/all_to_all | solution.py:529
  46.9 2.5 %collective-permute-start.6 = (bf16[2,1792,256]{2,1,0:T(8,128)(2,1)}, bf16[2,1792,256]{2,1,0:T(8,128)(2,1)}, u32[]{:S(2)}, u32[]{:S(2)}) collective-permute-start(bf16[2,1792,256]{2,1,0:T(8,128)(2,1)} %get-tuple-element.98), channel_id=1, source_target_pairs={{0,32},{1,97},{2,34},{3,99},{4,36},{5,101},{6,38},{7,103},{8,40},{... | collective-permute-start | bytes 5505032 | tf_op jit(solution)/shard_map/ppermute | solution.py:513
  49.5 10.3 %all-to-all-done.1 = bf16[64,8,640]{2,1,0:T(8,128)(2,1)S(1)} async-done(((bf16[64,8,640]{2,1,0:T(8,128)(2,1)}), bf16[64,8,640]{2,1,0:T(8,128)(2,1)S(1)}, u32[]{:S(2)}, u32[]{:S(2)}) %all-to-all-start.1) | async-done | bytes 655392 | tf_op jit(solution)/shard_map/all_to_all | solution.py:529
  59.9 2.0 %copy-done = bf16[256,7168]{1,0:T(8,128)(2,1)S(1)} copy-done((bf16[256,7168]{1,0:T(8,128)(2,1)S(1)}, bf16[256,7168]{1,0:T(8,128)(2,1)}, u32[]{:S(2)}) %copy-start) | copy-done | bytes 3670040
  61.9 2.2 %project.1 = (bf16[48,7168]{1,0:T(8,128)(2,1)S(1)}, bf16[48,7168]{1,0:T(8,128)(2,1)S(1)}) custom-call(s32[96,128]{1,0:T(8,128)S(1)} %get-tuple-element.77.cells_ref, bf16[32,2,8,640]{3,2,1,0:T(8,128)(2,1)S(1)} %bitcast.137, bf16[2,96,512]{2,1,0:T(8,128)(2,1)S(1)} %get-tuple-element.166.more_ref, bf16[2,512,128]{2,1,0:T(8,128)(2,1)S(1)} %copy-done.1, ...), custom_call_target="tpu_custom_call" | custom-call | flops 400000000 | bytes 6000000 | tf_op jit(solution)/shard_map/project/pallas_call | solution.py:356
  65.7 0.8 collective-permute-done.5.other_ref
  66.5 1.4 pair_sum.1
  67.9 3.8 %all-to-all-start.2 = ((bf16[16,3,7168]{2,1,0:T(4,128)(2,1)}), bf16[16,3,7168]{2,1,0:T(4,128)(2,1)S(1)}, u32[]{:S(2)}, u32[]{:S(2)}) async-start(bf16[16,3,7168]{2,1,0:T(4,128)(2,1)} %pair_sum.1), calls=%async_computation.2 | async-start | bytes 1835008 | tf_op jit(solution)/shard_map/all_to_all | solution.py:572
  72.0 2.6 %collective-permute-start.7 = (bf16[256,1792]{1,0:T(8,128)(2,1)}, bf16[256,1792]{1,0:T(8,128)(2,1)}, u32[]{:S(2)}, u32[]{:S(2)}) collective-permute-start(bf16[256,1792]{1,0:T(8,128)(2,1)} %get-tuple-element.101), channel_id=1, source_target_pairs={{32,0},{64,32},{96,64},{0,96},{33,1},{65,33},{97,65},{1,97},{34,2}... | collective-permute-start | bytes 2752520 | tf_op jit(solution)/shard_map/ppermute | solution.py:48
  74.6 12.2 %all-to-all-done.2 = bf16[16,3,7168]{2,1,0:T(4,128)(2,1)S(1)} async-done(((bf16[16,3,7168]{2,1,0:T(4,128)(2,1)}), bf16[16,3,7168]{2,1,0:T(4,128)(2,1)S(1)}, u32[]{:S(2)}, u32[]{:S(2)}) %all-to-all-start.2) | async-done | bytes 688160 | tf_op jit(solution)/shard_map/all_to_all | solution.py:572
  88.8 1.3 reshape.262
  90.1 6.4 %all-to-all-start.3 = ((bf16[128,2,1792]{2,1,0:T(2,128)(2,1)}), bf16[128,2,1792]{2,1,0:T(2,128)(2,1)S(1)}, u32[]{:S(2)}, u32[]{:S(2)}) async-start(bf16[128,2,1792]{2,1,0:T(2,128)(2,1)} %reshape.262), calls=%async_computation.3 | async-start | bytes 1835008 | tf_op jit(solution)/shard_map/all_to_all | solution.py:615
  96.6 3.0 %collective-permute-start.8 = (bf16[128,1792]{1,0:T(8,128)(2,1)}, bf16[128,1792]{1,0:T(8,128)(2,1)}, u32[]{:S(2)}, u32[]{:S(2)}) collective-permute-start(bf16[128,1792]{1,0:T(8,128)(2,1)} %get-tuple-element.102), channel_id=1, source_target_pairs={{64,0},{96,32},{0,64},{32,96},{65,1},{97,33},{1,65},{33,97},{66,2}... | collective-permute-start | bytes 1376264 | tf_op jit(solution)/shard_map/ppermute | solution.py:48
  99.5 0.8 fusion.82
  100.3 2.2 %dynamic-slice_bitcast_fusion.refs_4_ = bf16[256,1792]{1,0:T(8,128)(2,1)} fusion(bf16[1,256,7168]{2,1,0:T(8,128)(2,1)} %down_ref.1, s32[]{:T(128)S(6)} %select_n.230), kind=kLoop, calls=%fused_computation.66 | loop fusion | bytes 1835012 | tf_op jit(solution)/shard_map/dynamic_slice | solution.py:645
  103.7 1.5 maximum_bitcast_fusion
  105.2 9.0 %all-to-all-done.3 = bf16[128,2,1792]{2,1,0:T(2,128)(2,1)S(1)} async-done(((bf16[128,2,1792]{2,1,0:T(2,128)(2,1)}), bf16[128,2,1792]{2,1,0:T(2,128)(2,1)S(1)}, u32[]{:S(2)}, u32[]{:S(2)}) %all-to-all-start.3) | async-done | bytes 917536 | tf_op jit(solution)/shard_map/all_to_all | solution.py:615
  114.6 4.7 %collective-permute-done.8.refs_6_ = bf16[128,1792]{1,0:T(8,128)(2,1)} collective-permute-done((bf16[128,1792]{1,0:T(8,128)(2,1)}, bf16[128,1792]{1,0:T(8,128)(2,1)}, u32[]{:S(2)}, u32[]{:S(2)}) %collective-permute-start.8) | collective-permute-done | bytes 458784 | tf_op jit(solution)/shard_map/ppermute | solution.py:48
  119.6 1.6 fusion.28
  121.2 9.1 %all-to-all-start.4 = ((bf16[32,24,576]{2,1,0:T(8,128)(2,1)}), bf16[32,24,576]{2,1,0:T(8,128)(2,1)S(1)}, u32[]{:S(2)}, u32[]{:S(2)}) async-start(bf16[32,24,576]{2,1,0:T(8,128)(2,1)} %maximum_bitcast_fusion), calls=%async_computation.4 | async-start | bytes 1966080 | tf_op jit(solution)/shard_map/all_to_all | solution.py:627
  130.3 1.6 fusion.30
  131.9 1.6 fusion.32
  133.5 1.6 fusion.34
  135.1 1.6 fusion.24
  136.7 1.6 fusion.22
  138.4 1.9 collective-permute-start.11
  140.3 1.6 fusion.20
  141.9 1.6 fusion.26
  143.6 1.3 collective-permute-done.11
  145.1 1.9 collective-permute-start.12
  148.1 9.5 %collective-permute-done.12.refs_1_ = bf16[256,256]{1,0:T(8,128)(2,1)S(1)} collective-permute-done((bf16[256,256]{1,0:T(8,128)(2,1)S(1)}, bf16[256,256]{1,0:T(8,128)(2,1)S(1)}, u32[]{:S(2)}, u32[]{:S(2)}) %collective-permute-start.12) | collective-permute-done | bytes 131104 | tf_op jit(solution)/shard_map/ppermute | solution.py:48
  157.6 1.2 collective-permute-done.13.refs_2_
  158.8 2.7 %collective-permute-done.14.refs_3_ = bf16[256,256]{1,0:T(8,128)(2,1)S(1)} collective-permute-done((bf16[256,256]{1,0:T(8,128)(2,1)S(1)}, bf16[256,256]{1,0:T(8,128)(2,1)S(1)}, u32[]{:S(2)}, u32[]{:S(2)}) %collective-permute-start.14) | collective-permute-done | bytes 131104 | tf_op jit(solution)/shard_map/ppermute | solution.py:48
  162.2 4.6 %down_product.1 = bf16[256,1792]{1,0:T(8,128)(2,1)} custom-call(bf16[256,256]{1,0:T(8,128)(2,1)} %copy-done.7, bf16[256,256]{1,0:T(8,128)(2,1)} %copy-done.9, bf16[256,256]{1,0:T(8,128)(2,1)} %copy-done.10, bf16[256,256]{1,0:T(8,128)(2,1)} %copy-done.11, bf16[256,1792]{1,0:T(8,128)(2,1)} %dynamic-slice_bitcast_fusion.refs_4_, ...), custom_call_target="tpu_custom_call" | custom-call | flops 1000000000 | bytes 5000000 | tf_op jit(solution)/shard_map/down_product/pallas_call | solution.py:414
  166.8 3.1 %reshape.271 = bf16[128,2,1792]{2,1,0:T(2,128)(2,1)} reshape(bf16[256,1792]{1,0:T(8,128)(2,1)} %down_product.1) | data formatting | bytes 1835008 | tf_op jit(solution)/shard_map/reshape | solution.py:649
  169.9 7.7 %all-to-all-start.5 = ((bf16[128,2,1792]{2,1,0:T(2,128)(2,1)}), bf16[128,2,1792]{2,1,0:T(2,128)(2,1)S(1)}, u32[]{:S(2)}, u32[]{:S(2)}) async-start(bf16[128,2,1792]{2,1,0:T(2,128)(2,1)} %reshape.271), calls=%async_computation.5 | async-start | bytes 1835008 | tf_op jit(solution)/shard_map/all_to_all | solution.py:648
  178.0 0.8 pad_maximum_fusion.4
  178.8 16.5 %all-to-all-done.5 = bf16[128,2,1792]{2,1,0:T(2,128)(2,1)S(1)} async-done(((bf16[128,2,1792]{2,1,0:T(2,128)(2,1)}), bf16[128,2,1792]{2,1,0:T(2,128)(2,1)S(1)}, u32[]{:S(2)}, u32[]{:S(2)}) %all-to-all-start.5) | async-done | bytes 917536 | tf_op jit(solution)/shard_map/all_to_all | solution.py:648
  196.8 1.2 fusion.15
  (118 shorter events, 13.4 us)
Async XLA Ops:
  1.5 4.8 %collective-permute-start = (bf16[64,576]{1,0:T(8,128)(2,1)S(1)}, bf16[64,576]{1,0:T(8,128)(2,1)S(1)}, u32[]{:S(2)}, u32[]{:S(2)}) collective-permute-start(bf16[64,576]{1,0:T(8,128)(2,1)S(1)} %slice.110), channel_id=1, source_target_pairs={{1,0},{2,1},{3,2},{4,3},{5,4},{6,5},{7,6},{8,7},{9,8},{10,9},{11,1... | collective-permute-start | bytes 221192 | tf_op jit(solution)/shard_map/ppermute | solution.py:457
  7.3 13.2 %copy-start.2 = (bf16[256,576]{1,0:T(8,128)(2,1)}, bf16[256,576]{1,0:T(8,128)(2,1)S(1)}, u32[]{:S(2)}) copy-start(bf16[256,576]{1,0:T(8,128)(2,1)S(1)} %pad_maximum_fusion.2.refs_1_) | copy-start | bytes 884740
  7.3 13.2 %collective-permute-start.1 = (bf16[256,576]{1,0:T(8,128)(2,1)S(1)}, bf16[256,576]{1,0:T(8,128)(2,1)S(1)}, u32[]{:S(2)}, u32[]{:S(2)}) collective-permute-start(bf16[256,576]{1,0:T(8,128)(2,1)S(1)} %pad_maximum_fusion.2.refs_1_), channel_id=1, source_target_pairs={{32,0},{64,32},{96,64},{0,96},{33,1},{65,33},{97,65},{1,97},{34,2}... | collective-permute-start | bytes 884744 | tf_op jit(solution)/shard_map/ppermute | solution.py:48
  9.9 10.7 %collective-permute-start.2 = (bf16[256,576]{1,0:T(8,128)(2,1)S(1)}, bf16[256,576]{1,0:T(8,128)(2,1)S(1)}, u32[]{:S(2)}, u32[]{:S(2)}) collective-permute-start(bf16[256,576]{1,0:T(8,128)(2,1)S(1)} %pad_maximum_fusion.2.refs_1_), channel_id=1, source_target_pairs={{64,0},{96,32},{0,64},{32,96},{65,1},{97,33},{1,65},{33,97},{66,2}... | collective-permute-start | bytes 884744 | tf_op jit(solution)/shard_map/ppermute | solution.py:48
  10.4 15.5 %collective-permute-start.3 = (bf16[256,576]{1,0:T(8,128)(2,1)S(1)}, bf16[256,576]{1,0:T(8,128)(2,1)S(1)}, u32[]{:S(2)}, u32[]{:S(2)}) collective-permute-start(bf16[256,576]{1,0:T(8,128)(2,1)S(1)} %pad_maximum_fusion.2.refs_1_), channel_id=1, source_target_pairs={{96,0},{0,32},{32,64},{64,96},{97,1},{1,33},{33,65},{65,97},{98,2}... | collective-permute-start | bytes 884744 | tf_op jit(solution)/shard_map/ppermute | solution.py:48
  14.1 13.1 %copy-start.14 = (s32[384]{0:T(512)S(1)}, s32[384]{0:T(512)}, u32[]{:S(2)}) copy-start(s32[384]{0:T(512)} %param.23) | copy-start | bytes 4612
  20.5 6.7 %copy-start.4 = (bf16[256,576]{1,0:T(8,128)(2,1)}, bf16[256,576]{1,0:T(8,128)(2,1)S(1)}, u32[]{:S(2)}) copy-start(bf16[256,576]{1,0:T(8,128)(2,1)S(1)} %collective-permute-done.1.refs_2_) | copy-start | bytes 884740
  20.6 6.7 %copy-start.5 = (bf16[256,576]{1,0:T(8,128)(2,1)}, bf16[256,576]{1,0:T(8,128)(2,1)S(1)}, u32[]{:S(2)}) copy-start(bf16[256,576]{1,0:T(8,128)(2,1)S(1)} %collective-permute-done.2.refs_3_) | copy-start | bytes 884740
  25.9 1.4 copy-start.6
  25.9 34.0 %collective-permute-start.4 = (bf16[2,1792,256]{2,1,0:T(8,128)(2,1)}, bf16[2,1792,256]{2,1,0:T(8,128)(2,1)}, u32[]{:S(2)}, u32[]{:S(2)}) collective-permute-start(bf16[2,1792,256]{2,1,0:T(8,128)(2,1)} %get-tuple-element.89), channel_id=1, source_target_pairs={{0,32},{1,97},{2,34},{3,99},{4,36},{5,101},{6,38},{7,103},{8,40},{... | collective-permute-start | bytes 5505032 | tf_op jit(solution)/shard_map/ppermute | solution.py:512
  36.5 12.9 %copy-start.16 = (s32[1,3,8]{2,0,1:T(1,128)S(1)}, s32[1,3,8]{2,0,1:T(1,128)}, u32[]{:S(2)}) copy-start(s32[1,3,8]{2,0,1:T(1,128)} %param.29) | copy-start | bytes 292
  36.5 23.4 %copy-start.1 = (bf16[2,512,128]{2,1,0:T(8,128)(2,1)S(1)}, bf16[2,512,128]{2,1,0:T(8,128)(2,1)}, u32[]{:S(2)}) copy-start(bf16[2,512,128]{2,1,0:T(8,128)(2,1)} %uv_ref.1) | copy-start | bytes 786436
  36.6 23.3 %all-to-all-start.1 = ((bf16[64,8,640]{2,1,0:T(8,128)(2,1)}), bf16[64,8,640]{2,1,0:T(8,128)(2,1)S(1)}, u32[]{:S(2)}, u32[]{:S(2)}) async-start(bf16[64,8,640]{2,1,0:T(8,128)(2,1)} %get-tuple-element.88), calls=%async_computation.1 | async-start | bytes 1310720 | tf_op jit(solution)/shard_map/all_to_all | solution.py:529
  46.9 27.7 %collective-permute-start.6 = (bf16[2,1792,256]{2,1,0:T(8,128)(2,1)}, bf16[2,1792,256]{2,1,0:T(8,128)(2,1)}, u32[]{:S(2)}, u32[]{:S(2)}) collective-permute-start(bf16[2,1792,256]{2,1,0:T(8,128)(2,1)} %get-tuple-element.98), channel_id=1, source_target_pairs={{0,32},{1,97},{2,34},{3,99},{4,36},{5,101},{6,38},{7,103},{8,40},{... | collective-permute-start | bytes 5505032 | tf_op jit(solution)/shard_map/ppermute | solution.py:513
  59.9 2.0 %copy-start = (bf16[256,7168]{1,0:T(8,128)(2,1)S(1)}, bf16[256,7168]{1,0:T(8,128)(2,1)}, u32[]{:S(2)}) copy-start(bf16[256,7168]{1,0:T(8,128)(2,1)} %weight_ref.1) | copy-start | bytes 11010052
  61.9 3.4 %copy-start.17 = (f32[1,3,8]{2,0,1:T(1,128)S(1)}, f32[1,3,8]{2,0,1:T(1,128)}, u32[]{:S(2)}) copy-start(f32[1,3,8]{2,0,1:T(1,128)} %param.30) | copy-start | bytes 292
  61.9 3.8 %copy-start.15 = (s32[384]{0:T(512)S(1)}, s32[384]{0:T(512)}, u32[]{:S(2)}) copy-start(s32[384]{0:T(512)} %param.22) | copy-start | bytes 4612
  64.1 2.4 %collective-permute-start.5 = (bf16[48,7168]{1,0:T(8,128)(2,1)S(1)}, bf16[48,7168]{1,0:T(8,128)(2,1)S(1)}, u32[]{:S(2)}, u32[]{:S(2)}) collective-permute-start(bf16[48,7168]{1,0:T(8,128)(2,1)S(1)} %get-tuple-element.97), channel_id=1, source_target_pairs={{0,1},{1,0},{2,3},{3,2},{4,5},{5,4},{6,7},{7,6},{8,9},{9,8},{10,11... | collective-permute-start | bytes 2064392 | tf_op jit(solution)/shard_map/ppermute | solution.py:570
  67.9 19.3 %copy-start.8 = (bf16[1,3,7168]{2,1,0:T(4,128)(2,1)S(1)}, bf16[1,3,7168]{2,1,0:T(4,128)(2,1)}, u32[]{:S(2)}) copy-start(bf16[1,3,7168]{2,1,0:T(4,128)(2,1)} %param.27) | copy-start | bytes 129028
  67.9 19.5 %copy-start.12 = (f32[7168]{0:T(1024)S(1)}, f32[7168]{0:T(1024)}, u32[]{:S(2)}) copy-start(f32[7168]{0:T(1024)} %param.28) | copy-start | bytes 86020
  67.9 19.0 %all-to-all-start.2 = ((bf16[16,3,7168]{2,1,0:T(4,128)(2,1)}), bf16[16,3,7168]{2,1,0:T(4,128)(2,1)S(1)}, u32[]{:S(2)}, u32[]{:S(2)}) async-start(bf16[16,3,7168]{2,1,0:T(4,128)(2,1)} %pair_sum.1), calls=%async_computation.2 | async-start | bytes 1835008 | tf_op jit(solution)/shard_map/all_to_all | solution.py:572
  72.0 42.6 %collective-permute-start.7 = (bf16[256,1792]{1,0:T(8,128)(2,1)}, bf16[256,1792]{1,0:T(8,128)(2,1)}, u32[]{:S(2)}, u32[]{:S(2)}) collective-permute-start(bf16[256,1792]{1,0:T(8,128)(2,1)} %get-tuple-element.101), channel_id=1, source_target_pairs={{32,0},{64,32},{96,64},{0,96},{33,1},{65,33},{97,65},{1,97},{34,2}... | collective-permute-start | bytes 2752520 | tf_op jit(solution)/shard_map/ppermute | solution.py:48
  74.6 40.0 %collective-permute-start.9 = (bf16[256,1792]{1,0:T(8,128)(2,1)}, bf16[256,1792]{1,0:T(8,128)(2,1)}, u32[]{:S(2)}, u32[]{:S(2)}) collective-permute-start(bf16[256,1792]{1,0:T(8,128)(2,1)} %get-tuple-element.103), channel_id=1, source_target_pairs={{96,0},{0,32},{32,64},{64,96},{97,1},{1,33},{33,65},{65,97},{98,2}... | collective-permute-start | bytes 2752520 | tf_op jit(solution)/shard_map/ppermute | solution.py:48
  90.1 12.5 %copy-start.3 = (bf16[256,576]{1,0:T(8,128)(2,1)S(1)}, bf16[256,576]{1,0:T(8,128)(2,1)}, u32[]{:S(2)}) copy-start(bf16[256,576]{1,0:T(8,128)(2,1)} %copy-done.2) | copy-start | bytes 884740
  90.1 24.1 %all-to-all-start.3 = ((bf16[128,2,1792]{2,1,0:T(2,128)(2,1)}), bf16[128,2,1792]{2,1,0:T(2,128)(2,1)S(1)}, u32[]{:S(2)}, u32[]{:S(2)}) async-start(bf16[128,2,1792]{2,1,0:T(2,128)(2,1)} %reshape.262), calls=%async_computation.3 | async-start | bytes 1835008 | tf_op jit(solution)/shard_map/all_to_all | solution.py:615
  96.6 22.7 %collective-permute-start.8 = (bf16[128,1792]{1,0:T(8,128)(2,1)}, bf16[128,1792]{1,0:T(8,128)(2,1)}, u32[]{:S(2)}, u32[]{:S(2)}) collective-permute-start(bf16[128,1792]{1,0:T(8,128)(2,1)} %get-tuple-element.102), channel_id=1, source_target_pairs={{64,0},{96,32},{0,64},{32,96},{65,1},{97,33},{1,65},{33,97},{66,2}... | collective-permute-start | bytes 1376264 | tf_op jit(solution)/shard_map/ppermute | solution.py:48
  100.3 2.4 %slice-start = ((bf16[256,576]{1,0:T(8,128)(2,1)}), bf16[192,576]{1,0:T(8,128)(2,1)S(1)}, s32[]{:S(2)}) async-start(bf16[256,576]{1,0:T(8,128)(2,1)} %copy-done.4), calls=%async_computation.6 | async-start | bytes 491520 | tf_op jit(solution)/shard_map/slice | solution.py:621
  102.5 0.9 slice-start.1
  102.6 1.1 slice-start.2
  119.3 15.8 %collective-permute-start.10 = (bf16[256,1792]{1,0:T(8,128)(2,1)S(1)}, bf16[256,1792]{1,0:T(8,128)(2,1)S(1)}, u32[]{:S(2)}, u32[]{:S(2)}) collective-permute-start(bf16[256,1792]{1,0:T(8,128)(2,1)S(1)} %reshape.263), channel_id=1, source_target_pairs={{0,96},{1,33},{2,98},{3,35},{4,100},{5,37},{6,102},{7,39},{8,104},... | collective-permute-start | bytes 2752520 | tf_op jit(solution)/shard_map/ppermute | solution.py:626
  121.2 26.5 %all-to-all-start.4 = ((bf16[32,24,576]{2,1,0:T(8,128)(2,1)}), bf16[32,24,576]{2,1,0:T(8,128)(2,1)S(1)}, u32[]{:S(2)}, u32[]{:S(2)}) async-start(bf16[32,24,576]{2,1,0:T(8,128)(2,1)} %maximum_bitcast_fusion), calls=%async_computation.4 | async-start | bytes 1966080 | tf_op jit(solution)/shard_map/all_to_all | solution.py:627
  138.4 6.5 %collective-permute-start.11 = (bf16[256,512]{1,0:T(8,128)(2,1)S(1)}, bf16[256,512]{1,0:T(8,128)(2,1)S(1)}, u32[]{:S(2)}, u32[]{:S(2)}) collective-permute-start(bf16[256,512]{1,0:T(8,128)(2,1)S(1)} %pad_maximum_fusion.3), channel_id=1, source_target_pairs={{0,32},{1,97},{2,34},{3,99},{4,36},{5,101},{6,38},{7,103},{8,40},{... | collective-permute-start | bytes 786440 | tf_op jit(solution)/shard_map/ppermute | solution.py:638
  141.9 19.7 %collective-permute-start.15 = (bf16[128,1792]{1,0:T(8,128)(2,1)}, bf16[128,1792]{1,0:T(8,128)(2,1)}, u32[]{:S(2)}, u32[]{:S(2)}) collective-permute-start(bf16[128,1792]{1,0:T(8,128)(2,1)} %get-tuple-element.118), channel_id=1, source_target_pairs={{64,0},{96,32},{0,64},{32,96},{65,1},{97,33},{1,65},{33,97},{66,2}... | collective-permute-start | bytes 1376264 | tf_op jit(solution)/shard_map/ppermute | solution.py:48
  145.1 16.5 %copy-start.7 = (bf16[256,256]{1,0:T(8,128)(2,1)}, bf16[256,256]{1,0:T(8,128)(2,1)S(1)}, u32[]{:S(2)}) copy-start(bf16[256,256]{1,0:T(8,128)(2,1)S(1)} %fusion.51.refs_0_) | copy-start | bytes 393220
  145.1 12.5 %collective-permute-start.12 = (bf16[256,256]{1,0:T(8,128)(2,1)S(1)}, bf16[256,256]{1,0:T(8,128)(2,1)S(1)}, u32[]{:S(2)}, u32[]{:S(2)}) collective-permute-start(bf16[256,256]{1,0:T(8,128)(2,1)S(1)} %fusion.51.refs_0_), channel_id=1, source_target_pairs={{32,0},{64,32},{96,64},{0,96},{33,1},{65,33},{97,65},{1,97},{34,2}... | collective-permute-start | bytes 393224 | tf_op jit(solution)/shard_map/ppermute | solution.py:48
  147.0 11.8 %collective-permute-start.13 = (bf16[256,256]{1,0:T(8,128)(2,1)S(1)}, bf16[256,256]{1,0:T(8,128)(2,1)S(1)}, u32[]{:S(2)}, u32[]{:S(2)}) collective-permute-start(bf16[256,256]{1,0:T(8,128)(2,1)S(1)} %fusion.51.refs_0_), channel_id=1, source_target_pairs={{64,0},{96,32},{0,64},{32,96},{65,1},{97,33},{1,65},{33,97},{66,2}... | collective-permute-start | bytes 393224 | tf_op jit(solution)/shard_map/ppermute | solution.py:48
  147.1 14.5 %collective-permute-start.14 = (bf16[256,256]{1,0:T(8,128)(2,1)S(1)}, bf16[256,256]{1,0:T(8,128)(2,1)S(1)}, u32[]{:S(2)}, u32[]{:S(2)}) collective-permute-start(bf16[256,256]{1,0:T(8,128)(2,1)S(1)} %fusion.51.refs_0_), channel_id=1, source_target_pairs={{96,0},{0,32},{32,64},{64,96},{97,1},{1,33},{33,65},{65,97},{98,2}... | collective-permute-start | bytes 393224 | tf_op jit(solution)/shard_map/ppermute | solution.py:48
  157.6 4.0 %copy-start.9 = (bf16[256,256]{1,0:T(8,128)(2,1)}, bf16[256,256]{1,0:T(8,128)(2,1)S(1)}, u32[]{:S(2)}) copy-start(bf16[256,256]{1,0:T(8,128)(2,1)S(1)} %collective-permute-done.12.refs_1_) | copy-start | bytes 393220
  158.8 2.8 %copy-start.10 = (bf16[256,256]{1,0:T(8,128)(2,1)}, bf16[256,256]{1,0:T(8,128)(2,1)S(1)}, u32[]{:S(2)}) copy-start(bf16[256,256]{1,0:T(8,128)(2,1)S(1)} %collective-permute-done.13.refs_2_) | copy-start | bytes 393220
  161.6 0.6 copy-start.11
  166.8 11.1 %copy-start.13 = (f32[512]{0:T(512)S(1)}, f32[512]{0:T(512)}, u32[]{:S(2)}) copy-start(f32[512]{0:T(512)} %param.21) | copy-start | bytes 6148
  169.9 25.4 %all-to-all-start.5 = ((bf16[128,2,1792]{2,1,0:T(2,128)(2,1)}), bf16[128,2,1792]{2,1,0:T(2,128)(2,1)S(1)}, u32[]{:S(2)}, u32[]{:S(2)}) async-start(bf16[128,2,1792]{2,1,0:T(2,128)(2,1)} %reshape.271), calls=%async_computation.5 | async-start | bytes 1835008 | tf_op jit(solution)/shard_map/all_to_all | solution.py:648

commit v13 on v12

--- a/solution.py
+++ b/solution.py
@@ -390,38 +390,6 @@
         ),
         name="pair_sum",
     )(mine, other)
-
-
-def down_kernel(*refs):
-    blocks, weights, out_ref = refs[:4], refs[4:9], refs[9]
-    cut = weights[2].shape[0]
-    step = out_ref.shape[1] // 2
-    for first in range(0, out_ref.shape[1], step):
-        span = slice(first, first + step)
-        sums = jnp.dot(blocks[0][...], weights[0][:, span], preferred_element_type=F32)
-        for rows, weight in (
-            (blocks[1][...], weights[1]),
-            (blocks[2][:, :cut], weights[2]),
-            (blocks[2][:, cut:], weights[3]),
-            (blocks[3][...], weights[4]),
-        ):
-            sums = sums + jnp.dot(rows, weight[:, span], preferred_element_type=F32)
-        out_ref[:, span] = sums.astype(BF)
-
-
-def down_product(blocks, weights):
-    whole = pl.BlockSpec(memory_space=pltpu.VMEM)
-    return pl.pallas_call(
-        down_kernel,
-        out_shape=jax.ShapeDtypeStruct((blocks[0].shape[0], weights[0].shape[1]), BF),
-        in_specs=[whole] * 9,
-        out_specs=whole,
-        compiler_params=pltpu.CompilerParams(vmem_limit_bytes=VMEM),
-        cost_estimate=pl.CostEstimate(
-            flops=10**9, bytes_accessed=5 * 10**6, transcendentals=0
-        ),
-        name="down_product",
-    )(*blocks, *weights)
 
 
 def shards(
@@ -641,12 +609,16 @@
     hidden = (
         jax.nn.silu(gate_sum + given[:, :half]) * (up_sum + given[:, half:])
     ).astype(BF)
-    blocks = [hidden] + [shift(hidden, k, dp_count, "dp") for k in range(1, dp_count)]
+    near, far, last = (shift(hidden, k, dp_count, "dp") for k in range(1, dp_count))
+    cut = far_first.shape[0]
+    hidden_all = jnp.concatenate([hidden, near, last, far[:, :cut]], axis=1)
+    hidden_all, dealt = lax.optimization_barrier((hidden_all, dealt))
     down_own = lax.dynamic_slice_in_dim(w_down[0], group * piece, piece, 1)
-    blocks[0], dealt = lax.optimization_barrier((blocks[0], dealt))
-    out = down_product(blocks, [down_own, down_near, far_first, far_second, down_last])
+    downs = jnp.concatenate([down_own, down_near, down_last, far_first], axis=0)
+    out = jnp.dot(hidden_all, downs, preferred_element_type=F32)
+    out = out + jnp.dot(far[:, cut:], far_second, preferred_element_type=F32)
     returned = lax.all_to_all(
-        out.reshape(devices, capacity, piece),
+        out.astype(BF).reshape(devices, capacity, piece),
         ("dp", "expert"),
         split_axis=0,
         concat_axis=0,

time: 199 us -> 202 us (1.015)
  Pallas kernels: 24.8 us -> 20.2 us
  matrix products: 15.4 us -> 19.7 us
  starting transfers between devices: 56 us -> 59.4 us
    pallas_call x1 -> x0, Pallas kernels: 4.62 us -> none  [down_product(): pl.pallas_call(down_kernel, out_shape=jax.ShapeDtypeStruct((blocks[0].sha...]
    dot_general x0 -> x2, matrix products: none -> 4.33 us  [the longest x1 3.95 us: shards(): out = jnp.dot(hidden_all, downs, preferred_element_type=F32)]
  transfers between devices with their start and end apart: 21 -> 21, of which waited for: 12 -> 13; matrix products, arithmetic and copies ran while one was open for 14% -> 14% of each run, Pallas kernels for 10% -> 10%
where the time goes in v13:
time: 202 us; the launch traced here: 201 us
  waiting for transfers between devices  77.8 us (39%)
  starting transfers between devices  59.4 us (29%)
  Pallas kernels  20.2 us (10%)
  matrix products  19.7 us (10%)
  local copies, waits for them, and re-layouts  15.1 us (7%)
  other arithmetic  7.02 us (3%)
  between operations  2.08 us (1%)
    ppermute x10, waiting for transfers between devices, shift(): return lax.ppermute(x, axis, [((i + step) % size, i) for i in range(size)])  22.2 us
    all_to_all x1, waiting for transfers between devices, shards(): lax.all_to_all(out.astype(BF).reshape(devices, capacity, piece), ('dp', '...  16.5 us
    ppermute x10, starting transfers between devices, shift(): return lax.ppermute(x, axis, [((i + step) % size, i) for i in range(size)])  13.8 us
    all_to_all x1, waiting for transfers between devices, shards(): lax.all_to_all(pair_sums, 'expert', split_axis=0, concat_axis=0, tiled=Tr...  12.4 us
    all_to_all x1, waiting for transfers between devices, to_heads(): lax.all_to_all(part, 'expert', split_axis=0, concat_axis=0, tiled=True)  10.5 us
    all_to_all x1, starting transfers between devices, to_heads(): lax.all_to_all(part, 'expert', split_axis=0, concat_axis=0, tiled=True)  10.4 us
    all_to_all x1, waiting for transfers between devices, shards(): lax.all_to_all(outgoing, ('dp', 'expert'), split_axis=0, concat_axis=0, t...  10.3 us
    all_to_all x1, starting transfers between devices, shards(): lax.all_to_all(out.astype(BF).reshape(devices, capacity, piece), ('dp', '...  9.35 us
  transfers between devices with their start and end apart: 21, of which 13 were waited for; matrix products, arithmetic and copies ran while one was open for 14% of the time, Pallas kernels for 10%

profile of v13, /device:TPU:1, one launch (start us, length us, event | category | flops | bytes accessed | tf_op | source)
XLA Modules:
  0.0 201.3 jit_solution(18276314497606534730)
XLA Ops:
  0.6 0.9 slice.116
  1.5 1.4 collective-permute-start
  2.9 3.4 %collective-permute-done = bf16[64,576]{1,0:T(8,128)(2,1)S(1)} collective-permute-done((bf16[64,576]{1,0:T(8,128)(2,1)S(1)}, bf16[64,576]{1,0:T(8,128)(2,1)S(1)}, u32[]{:S(2)}, u32[]{:S(2)}) %collective-permute-start) | collective-permute-done | bytes 73760 | tf_op jit(solution)/shard_map/ppermute | solution.py:425
  6.3 1.0 pad_maximum_fusion.3.refs_1_
  7.3 2.5 %collective-permute-start.1 = (bf16[256,576]{1,0:T(8,128)(2,1)S(1)}, bf16[256,576]{1,0:T(8,128)(2,1)S(1)}, u32[]{:S(2)}, u32[]{:S(2)}) collective-permute-start(bf16[256,576]{1,0:T(8,128)(2,1)S(1)} %pad_maximum_fusion.3.refs_1_), channel_id=1, source_target_pairs={{32,0},{64,32},{96,64},{0,96},{33,1},{65,33},{97,65},{1,97},{34,2}... | collective-permute-start | bytes 884744 | tf_op jit(solution)/shard_map/ppermute | solution.py:48
  12.4 1.0 tables.1
  14.2 6.4 %weight_slices.1 = (bf16[2,1792,256]{2,1,0:T(8,128)(2,1)}, bf16[2,1792,256]{2,1,0:T(8,128)(2,1)}, bf16[256,1792]{1,0:T(8,128)(2,1)}, bf16[128,1792]{1,0:T(8,128)...) custom-call(s32[5]{0:T(128)} %stack.59.at_ref, bf16[1,7168,256]{2,1,0:T(8,128)(2,1)} %gate_ref.1, ...), custom_call_target="tpu_custom_call" | custom-call | flops 1000 | bytes 4096 | tf_op jit(solution)/shard_map/weight_slices/pallas_call | solution.py:187
  20.6 5.2 %collective-permute-done.3.refs_4_ = bf16[256,576]{1,0:T(8,128)(2,1)S(1)} collective-permute-done((bf16[256,576]{1,0:T(8,128)(2,1)S(1)}, bf16[256,576]{1,0:T(8,128)(2,1)S(1)}, u32[]{:S(2)}, u32[]{:S(2)}) %collective-permute-start.3) | collective-permute-done | bytes 294944 | tf_op jit(solution)/shard_map/ppermute | solution.py:48
  27.4 9.2 %attend.1 = (bf16[64,8,640]{2,1,0:T(8,128)(2,1)}, bf16[14,64,512]{2,1,0:T(8,128)(2,1)S(1)}) custom-call(s32[32,128]{1,0:T(8,128)S(1)} %get-tuple-element.83.refs_0_, bf16[256,576]{1,0:T(8,128)(2,1)} %copy-done.2, bf16[256,576]{1,0:T(8,128)(2,1)} %copy-done.4, bf16[256,576]{1,0:T(8,128)(2,1)} %copy-done.5, bf16[256,576]{1,0:T(8,128)(2,1)} %copy-done.6, ...), custom_call_target="tpu_custom_call" | custom-call | flops 100000000 | bytes 4000000 | tf_op jit(solution)/shard_map/attend/pallas_call | solution.py:287
  36.7 10.4 %all-to-all-start.1 = ((bf16[64,8,640]{2,1,0:T(8,128)(2,1)}), bf16[64,8,640]{2,1,0:T(8,128)(2,1)S(1)}, u32[]{:S(2)}, u32[]{:S(2)}) async-start(bf16[64,8,640]{2,1,0:T(8,128)(2,1)} %get-tuple-element.88), calls=%async_computation.1 | async-start | bytes 1310720 | tf_op jit(solution)/shard_map/all_to_all | solution.py:497
  47.1 2.5 %collective-permute-start.6 = (bf16[2,1792,256]{2,1,0:T(8,128)(2,1)}, bf16[2,1792,256]{2,1,0:T(8,128)(2,1)}, u32[]{:S(2)}, u32[]{:S(2)}) collective-permute-start(bf16[2,1792,256]{2,1,0:T(8,128)(2,1)} %get-tuple-element.98), channel_id=1, source_target_pairs={{0,32},{1,97},{2,34},{3,99},{4,36},{5,101},{6,38},{7,103},{8,40},{... | collective-permute-start | bytes 5505032 | tf_op jit(solution)/shard_map/ppermute | solution.py:481
  49.5 10.5 %all-to-all-done.1 = bf16[64,8,640]{2,1,0:T(8,128)(2,1)S(1)} async-done(((bf16[64,8,640]{2,1,0:T(8,128)(2,1)}), bf16[64,8,640]{2,1,0:T(8,128)(2,1)S(1)}, u32[]{:S(2)}, u32[]{:S(2)}) %all-to-all-start.1) | async-done | bytes 655392 | tf_op jit(solution)/shard_map/all_to_all | solution.py:497
  60.0 2.0 %copy-done = bf16[256,7168]{1,0:T(8,128)(2,1)S(1)} copy-done((bf16[256,7168]{1,0:T(8,128)(2,1)S(1)}, bf16[256,7168]{1,0:T(8,128)(2,1)}, u32[]{:S(2)}) %copy-start) | copy-done | bytes 3670040
  62.0 2.2 %project.1 = (bf16[48,7168]{1,0:T(8,128)(2,1)S(1)}, bf16[48,7168]{1,0:T(8,128)(2,1)S(1)}) custom-call(s32[96,128]{1,0:T(8,128)S(1)} %get-tuple-element.77.cells_ref, bf16[32,2,8,640]{3,2,1,0:T(8,128)(2,1)S(1)} %bitcast.139, bf16[2,96,512]{2,1,0:T(8,128)(2,1)S(1)} %get-tuple-element.166.more_ref, bf16[2,512,128]{2,1,0:T(8,128)(2,1)S(1)} %copy-done.1, ...), custom_call_target="tpu_custom_call" | custom-call | flops 400000000 | bytes 6000000 | tf_op jit(solution)/shard_map/project/pallas_call | solution.py:356
  65.7 1.0 collective-permute-done.5.other_ref
  66.7 1.4 pair_sum.1
  68.0 3.6 %all-to-all-start.2 = ((bf16[16,3,7168]{2,1,0:T(4,128)(2,1)}), bf16[16,3,7168]{2,1,0:T(4,128)(2,1)S(1)}, u32[]{:S(2)}, u32[]{:S(2)}) async-start(bf16[16,3,7168]{2,1,0:T(4,128)(2,1)} %pair_sum.1), calls=%async_computation.2 | async-start | bytes 1835008 | tf_op jit(solution)/shard_map/all_to_all | solution.py:540
  72.0 2.4 %collective-permute-start.7 = (bf16[256,1792]{1,0:T(8,128)(2,1)}, bf16[256,1792]{1,0:T(8,128)(2,1)}, u32[]{:S(2)}, u32[]{:S(2)}) collective-permute-start(bf16[256,1792]{1,0:T(8,128)(2,1)} %get-tuple-element.101), channel_id=1, source_target_pairs={{32,0},{64,32},{96,64},{0,96},{33,1},{65,33},{97,65},{1,97},{34,2}... | collective-permute-start | bytes 2752520 | tf_op jit(solution)/shard_map/ppermute | solution.py:48
  74.4 12.4 %all-to-all-done.2 = bf16[16,3,7168]{2,1,0:T(4,128)(2,1)S(1)} async-done(((bf16[16,3,7168]{2,1,0:T(4,128)(2,1)}), bf16[16,3,7168]{2,1,0:T(4,128)(2,1)S(1)}, u32[]{:S(2)}, u32[]{:S(2)}) %all-to-all-start.2) | async-done | bytes 688160 | tf_op jit(solution)/shard_map/all_to_all | solution.py:540
  88.8 1.3 reshape.262
  90.1 6.4 %all-to-all-start.3 = ((bf16[128,2,1792]{2,1,0:T(2,128)(2,1)}), bf16[128,2,1792]{2,1,0:T(2,128)(2,1)S(1)}, u32[]{:S(2)}, u32[]{:S(2)}) async-start(bf16[128,2,1792]{2,1,0:T(2,128)(2,1)} %reshape.262), calls=%async_computation.3 | async-start | bytes 1835008 | tf_op jit(solution)/shard_map/all_to_all | solution.py:583
  96.7 3.0 %collective-permute-start.8 = (bf16[128,1792]{1,0:T(8,128)(2,1)}, bf16[128,1792]{1,0:T(8,128)(2,1)}, u32[]{:S(2)}, u32[]{:S(2)}) collective-permute-start(bf16[128,1792]{1,0:T(8,128)(2,1)} %get-tuple-element.102), channel_id=1, source_target_pairs={{64,0},{96,32},{0,64},{32,96},{65,1},{97,33},{1,65},{33,97},{66,2}... | collective-permute-start | bytes 1376264 | tf_op jit(solution)/shard_map/ppermute | solution.py:48
  99.7 2.2 %dynamic-slice_bitcast_fusion = bf16[256,1792]{1,0:T(8,128)(2,1)} fusion(bf16[1,256,7168]{2,1,0:T(8,128)(2,1)} %down_ref.1, s32[]{:T(128)S(6)} %select_n.230), kind=kLoop, calls=%fused_computation.76 | loop fusion | bytes 1835012 | tf_op jit(solution)/shard_map/dynamic_slice | solution.py:616
  102.3 1.5 maximum_bitcast_fusion
  103.9 10.3 %all-to-all-done.3 = bf16[128,2,1792]{2,1,0:T(2,128)(2,1)S(1)} async-done(((bf16[128,2,1792]{2,1,0:T(2,128)(2,1)}), bf16[128,2,1792]{2,1,0:T(2,128)(2,1)S(1)}, u32[]{:S(2)}, u32[]{:S(2)}) %all-to-all-start.3) | async-done | bytes 917536 | tf_op jit(solution)/shard_map/all_to_all | solution.py:583
  114.6 4.7 %collective-permute-done.8 = bf16[128,1792]{1,0:T(8,128)(2,1)} collective-permute-done((bf16[128,1792]{1,0:T(8,128)(2,1)}, bf16[128,1792]{1,0:T(8,128)(2,1)}, u32[]{:S(2)}, u32[]{:S(2)}) %collective-permute-start.8) | collective-permute-done | bytes 458784 | tf_op jit(solution)/shard_map/ppermute | solution.py:48
  119.5 1.6 fusion.42
  121.1 9.1 %all-to-all-start.4 = ((bf16[32,24,576]{2,1,0:T(8,128)(2,1)}), bf16[32,24,576]{2,1,0:T(8,128)(2,1)S(1)}, u32[]{:S(2)}, u32[]{:S(2)}) async-start(bf16[32,24,576]{2,1,0:T(8,128)(2,1)} %maximum_bitcast_fusion), calls=%async_computation.4 | async-start | bytes 1966080 | tf_op jit(solution)/shard_map/all_to_all | solution.py:595
  130.2 1.6 fusion.44
  131.9 1.6 fusion.46
  133.4 1.6 fusion.48
  135.1 1.6 fusion.38
  136.6 1.6 fusion.36
  138.4 1.9 collective-permute-start.11
  140.2 1.6 fusion.34
  141.8 1.6 fusion.40
  143.4 1.4 collective-permute-done.11
  145.4 1.6 collective-permute-start.12
  147.6 2.3 %collective-permute-start.15 = (bf16[128,1792]{1,0:T(8,128)(2,1)}, bf16[128,1792]{1,0:T(8,128)(2,1)S(1)}, u32[]{:S(2)}, u32[]{:S(2)}) collective-permute-start(bf16[128,1792]{1,0:T(8,128)(2,1)} %get-tuple-element.119), channel_id=1, source_target_pairs={{64,0},{96,32},{0,64},{32,96},{65,1},{97,33},{1,65},{33,97},{66,2}... | collective-permute-start | bytes 1376264 | tf_op jit(solution)/shard_map/ppermute | solution.py:48
  150.7 0.9 collective-permute-done.14
  151.6 2.3 %collective-permute-done.12 = bf16[256,256]{1,0:T(8,128)(2,1)S(1)} collective-permute-done((bf16[256,256]{1,0:T(8,128)(2,1)S(1)}, bf16[256,256]{1,0:T(8,128)(2,1)S(1)}, u32[]{:S(2)}, u32[]{:S(2)}) %collective-permute-start.12) | collective-permute-done | bytes 131104 | tf_op jit(solution)/shard_map/ppermute | solution.py:48
  154.7 0.8 pad_maximum_fusion.2
  155.9 8.3 %collective-permute-done.15 = bf16[128,1792]{1,0:T(8,128)(2,1)S(1)} collective-permute-done((bf16[128,1792]{1,0:T(8,128)(2,1)}, bf16[128,1792]{1,0:T(8,128)(2,1)S(1)}, u32[]{:S(2)}, u32[]{:S(2)}) %collective-permute-start.15) | collective-permute-done | bytes 458784 | tf_op jit(solution)/shard_map/ppermute | solution.py:48
  164.6 3.9 %fusion.27 = bf16[256,1792]{1,0:T(8,128)(2,1)} fusion(f32[256,1792]{1,0:T(8,128)S(1)} %fusion.67, bf16[256,896]{1,0:T(8,128)(2,1)S(1)} %copy-done.8, bf16[128,1792]{1,0:T(8,128)(2,1)} %collective-permute-done.8, bf16[256,1792]{1,0:T(8,128)(2,1)} %collective-permute-done.9, bf16[256,1792]{1,0:T(8,128)(2,1)} %collective-permute-done.7, ...), kind=kOutput, calls=%fused_computation.47 | convolution fusion | flops 835846144 | bytes 6422528 | tf_op jit(solution)/shard_map/dot_general | solution.py:618
  168.6 3.1 %reshape.271 = bf16[128,2,1792]{2,1,0:T(2,128)(2,1)} reshape(bf16[256,1792]{1,0:T(8,128)(2,1)} %fusion.27) | data formatting | bytes 1835008 | tf_op jit(solution)/shard_map/reshape | solution.py:621
  171.6 9.3 %all-to-all-start.5 = ((bf16[128,2,1792]{2,1,0:T(2,128)(2,1)}), bf16[128,2,1792]{2,1,0:T(2,128)(2,1)S(1)}, u32[]{:S(2)}, u32[]{:S(2)}) async-start(bf16[128,2,1792]{2,1,0:T(2,128)(2,1)} %reshape.271), calls=%async_computation.5 | async-start | bytes 1835008 | tf_op jit(solution)/shard_map/all_to_all | solution.py:620
  182.2 16.5 %all-to-all-done.5 = bf16[128,2,1792]{2,1,0:T(2,128)(2,1)S(1)} async-done(((bf16[128,2,1792]{2,1,0:T(2,128)(2,1)}), bf16[128,2,1792]{2,1,0:T(2,128)(2,1)S(1)}, u32[]{:S(2)}, u32[]{:S(2)}) %all-to-all-start.5) | async-done | bytes 917536 | tf_op jit(solution)/shard_map/all_to_all | solution.py:620
  200.1 1.2 fusion.15
  (115 shorter events, 15.0 us)
Async XLA Ops:
  1.5 4.8 %collective-permute-start = (bf16[64,576]{1,0:T(8,128)(2,1)S(1)}, bf16[64,576]{1,0:T(8,128)(2,1)S(1)}, u32[]{:S(2)}, u32[]{:S(2)}) collective-permute-start(bf16[64,576]{1,0:T(8,128)(2,1)S(1)} %slice.116), channel_id=1, source_target_pairs={{1,0},{2,1},{3,2},{4,3},{5,4},{6,5},{7,6},{8,7},{9,8},{10,9},{11,1... | collective-permute-start | bytes 221192 | tf_op jit(solution)/shard_map/ppermute | solution.py:425
  7.3 13.3 %copy-start.2 = (bf16[256,576]{1,0:T(8,128)(2,1)}, bf16[256,576]{1,0:T(8,128)(2,1)S(1)}, u32[]{:S(2)}) copy-start(bf16[256,576]{1,0:T(8,128)(2,1)S(1)} %pad_maximum_fusion.3.refs_1_) | copy-start | bytes 884740
  7.3 13.3 %collective-permute-start.1 = (bf16[256,576]{1,0:T(8,128)(2,1)S(1)}, bf16[256,576]{1,0:T(8,128)(2,1)S(1)}, u32[]{:S(2)}, u32[]{:S(2)}) collective-permute-start(bf16[256,576]{1,0:T(8,128)(2,1)S(1)} %pad_maximum_fusion.3.refs_1_), channel_id=1, source_target_pairs={{32,0},{64,32},{96,64},{0,96},{33,1},{65,33},{97,65},{1,97},{34,2}... | collective-permute-start | bytes 884744 | tf_op jit(solution)/shard_map/ppermute | solution.py:48
  9.9 10.7 %collective-permute-start.2 = (bf16[256,576]{1,0:T(8,128)(2,1)S(1)}, bf16[256,576]{1,0:T(8,128)(2,1)S(1)}, u32[]{:S(2)}, u32[]{:S(2)}) collective-permute-start(bf16[256,576]{1,0:T(8,128)(2,1)S(1)} %pad_maximum_fusion.3.refs_1_), channel_id=1, source_target_pairs={{64,0},{96,32},{0,64},{32,96},{65,1},{97,33},{1,65},{33,97},{66,2}... | collective-permute-start | bytes 884744 | tf_op jit(solution)/shard_map/ppermute | solution.py:48
  10.4 15.5 %collective-permute-start.3 = (bf16[256,576]{1,0:T(8,128)(2,1)S(1)}, bf16[256,576]{1,0:T(8,128)(2,1)S(1)}, u32[]{:S(2)}, u32[]{:S(2)}) collective-permute-start(bf16[256,576]{1,0:T(8,128)(2,1)S(1)} %pad_maximum_fusion.3.refs_1_), channel_id=1, source_target_pairs={{96,0},{0,32},{32,64},{64,96},{97,1},{1,33},{33,65},{65,97},{98,2}... | collective-permute-start | bytes 884744 | tf_op jit(solution)/shard_map/ppermute | solution.py:48
  14.2 13.1 %copy-start.11 = (s32[384]{0:T(512)S(1)}, s32[384]{0:T(512)}, u32[]{:S(2)}) copy-start(s32[384]{0:T(512)} %param.23) | copy-start | bytes 4612
  20.6 6.7 %copy-start.4 = (bf16[256,576]{1,0:T(8,128)(2,1)}, bf16[256,576]{1,0:T(8,128)(2,1)S(1)}, u32[]{:S(2)}) copy-start(bf16[256,576]{1,0:T(8,128)(2,1)S(1)} %collective-permute-done.1.refs_2_) | copy-start | bytes 884740
  20.6 6.7 %copy-start.5 = (bf16[256,576]{1,0:T(8,128)(2,1)}, bf16[256,576]{1,0:T(8,128)(2,1)S(1)}, u32[]{:S(2)}) copy-start(bf16[256,576]{1,0:T(8,128)(2,1)S(1)} %collective-permute-done.2.refs_3_) | copy-start | bytes 884740
  25.9 1.5 copy-start.6
  25.9 34.1 %collective-permute-start.4 = (bf16[2,1792,256]{2,1,0:T(8,128)(2,1)}, bf16[2,1792,256]{2,1,0:T(8,128)(2,1)}, u32[]{:S(2)}, u32[]{:S(2)}) collective-permute-start(bf16[2,1792,256]{2,1,0:T(8,128)(2,1)} %get-tuple-element.89), channel_id=1, source_target_pairs={{0,32},{1,97},{2,34},{3,99},{4,36},{5,101},{6,38},{7,103},{8,40},{... | collective-permute-start | bytes 5505032 | tf_op jit(solution)/shard_map/ppermute | solution.py:480
  36.6 23.4 %copy-start.1 = (bf16[2,512,128]{2,1,0:T(8,128)(2,1)S(1)}, bf16[2,512,128]{2,1,0:T(8,128)(2,1)}, u32[]{:S(2)}) copy-start(bf16[2,512,128]{2,1,0:T(8,128)(2,1)} %uv_ref.1) | copy-start | bytes 786436
  36.6 28.3 %copy-start.13 = (s32[1,3,8]{2,0,1:T(1,128)S(1)}, s32[1,3,8]{2,0,1:T(1,128)}, u32[]{:S(2)}) copy-start(s32[1,3,8]{2,0,1:T(1,128)} %param.29) | copy-start | bytes 292
  36.7 29.0 %copy-start.14 = (f32[1,3,8]{2,0,1:T(1,128)S(1)}, f32[1,3,8]{2,0,1:T(1,128)}, u32[]{:S(2)}) copy-start(f32[1,3,8]{2,0,1:T(1,128)} %param.30) | copy-start | bytes 292
  36.7 29.0 %copy-start.12 = (s32[384]{0:T(512)S(1)}, s32[384]{0:T(512)}, u32[]{:S(2)}) copy-start(s32[384]{0:T(512)} %param.22) | copy-start | bytes 4612
  36.7 23.3 %all-to-all-start.1 = ((bf16[64,8,640]{2,1,0:T(8,128)(2,1)}), bf16[64,8,640]{2,1,0:T(8,128)(2,1)S(1)}, u32[]{:S(2)}, u32[]{:S(2)}) async-start(bf16[64,8,640]{2,1,0:T(8,128)(2,1)} %get-tuple-element.88), calls=%async_computation.1 | async-start | bytes 1310720 | tf_op jit(solution)/shard_map/all_to_all | solution.py:497
  47.1 27.3 %collective-permute-start.6 = (bf16[2,1792,256]{2,1,0:T(8,128)(2,1)}, bf16[2,1792,256]{2,1,0:T(8,128)(2,1)}, u32[]{:S(2)}, u32[]{:S(2)}) collective-permute-start(bf16[2,1792,256]{2,1,0:T(8,128)(2,1)} %get-tuple-element.98), channel_id=1, source_target_pairs={{0,32},{1,97},{2,34},{3,99},{4,36},{5,101},{6,38},{7,103},{8,40},{... | collective-permute-start | bytes 5505032 | tf_op jit(solution)/shard_map/ppermute | solution.py:481
  60.0 2.0 %copy-start = (bf16[256,7168]{1,0:T(8,128)(2,1)S(1)}, bf16[256,7168]{1,0:T(8,128)(2,1)}, u32[]{:S(2)}) copy-start(bf16[256,7168]{1,0:T(8,128)(2,1)} %weight_ref.1) | copy-start | bytes 11010052
  64.2 23.0 %copy-start.7 = (bf16[1,3,7168]{2,1,0:T(4,128)(2,1)S(1)}, bf16[1,3,7168]{2,1,0:T(4,128)(2,1)}, u32[]{:S(2)}) copy-start(bf16[1,3,7168]{2,1,0:T(4,128)(2,1)} %param.27) | copy-start | bytes 129028
  64.3 23.2 %copy-start.9 = (f32[7168]{0:T(1024)S(1)}, f32[7168]{0:T(1024)}, u32[]{:S(2)}) copy-start(f32[7168]{0:T(1024)} %param.28) | copy-start | bytes 86020
  64.3 2.4 %collective-permute-start.5 = (bf16[48,7168]{1,0:T(8,128)(2,1)S(1)}, bf16[48,7168]{1,0:T(8,128)(2,1)S(1)}, u32[]{:S(2)}, u32[]{:S(2)}) collective-permute-start(bf16[48,7168]{1,0:T(8,128)(2,1)S(1)} %get-tuple-element.97), channel_id=1, source_target_pairs={{0,1},{1,0},{2,3},{3,2},{4,5},{5,4},{6,7},{7,6},{8,9},{9,8},{10,11... | collective-permute-start | bytes 2064392 | tf_op jit(solution)/shard_map/ppermute | solution.py:538
  68.0 18.8 %all-to-all-start.2 = ((bf16[16,3,7168]{2,1,0:T(4,128)(2,1)}), bf16[16,3,7168]{2,1,0:T(4,128)(2,1)S(1)}, u32[]{:S(2)}, u32[]{:S(2)}) async-start(bf16[16,3,7168]{2,1,0:T(4,128)(2,1)} %pair_sum.1), calls=%async_computation.2 | async-start | bytes 1835008 | tf_op jit(solution)/shard_map/all_to_all | solution.py:540
  72.0 42.6 %collective-permute-start.7 = (bf16[256,1792]{1,0:T(8,128)(2,1)}, bf16[256,1792]{1,0:T(8,128)(2,1)}, u32[]{:S(2)}, u32[]{:S(2)}) collective-permute-start(bf16[256,1792]{1,0:T(8,128)(2,1)} %get-tuple-element.101), channel_id=1, source_target_pairs={{32,0},{64,32},{96,64},{0,96},{33,1},{65,33},{97,65},{1,97},{34,2}... | collective-permute-start | bytes 2752520 | tf_op jit(solution)/shard_map/ppermute | solution.py:48
  74.4 40.1 %collective-permute-start.9 = (bf16[256,1792]{1,0:T(8,128)(2,1)}, bf16[256,1792]{1,0:T(8,128)(2,1)}, u32[]{:S(2)}, u32[]{:S(2)}) collective-permute-start(bf16[256,1792]{1,0:T(8,128)(2,1)} %get-tuple-element.103), channel_id=1, source_target_pairs={{96,0},{0,32},{32,64},{64,96},{97,1},{1,33},{33,65},{65,97},{98,2}... | collective-permute-start | bytes 2752520 | tf_op jit(solution)/shard_map/ppermute | solution.py:48
  88.8 13.1 %copy-start.3 = (bf16[256,576]{1,0:T(8,128)(2,1)S(1)}, bf16[256,576]{1,0:T(8,128)(2,1)}, u32[]{:S(2)}) copy-start(bf16[256,576]{1,0:T(8,128)(2,1)} %copy-done.2) | copy-start | bytes 884740
  90.1 12.0 %slice-start = ((bf16[256,576]{1,0:T(8,128)(2,1)}), bf16[192,576]{1,0:T(8,128)(2,1)S(1)}, s32[]{:S(2)}) async-start(bf16[256,576]{1,0:T(8,128)(2,1)} %copy-done.4), calls=%async_computation.6 | async-start | bytes 491520 | tf_op jit(solution)/shard_map/slice | solution.py:589
  90.1 12.1 %slice-start.1 = ((bf16[256,576]{1,0:T(8,128)(2,1)}), bf16[192,576]{1,0:T(8,128)(2,1)S(1)}, s32[]{:S(2)}) async-start(bf16[256,576]{1,0:T(8,128)(2,1)} %copy-done.5), calls=%async_computation.7 | async-start | bytes 491520 | tf_op jit(solution)/shard_map/slice | solution.py:589
  90.1 24.1 %all-to-all-start.3 = ((bf16[128,2,1792]{2,1,0:T(2,128)(2,1)}), bf16[128,2,1792]{2,1,0:T(2,128)(2,1)S(1)}, u32[]{:S(2)}, u32[]{:S(2)}) async-start(bf16[128,2,1792]{2,1,0:T(2,128)(2,1)} %reshape.262), calls=%async_computation.3 | async-start | bytes 1835008 | tf_op jit(solution)/shard_map/all_to_all | solution.py:583
  96.5 5.8 %slice-start.2 = ((bf16[256,576]{1,0:T(8,128)(2,1)}), bf16[192,576]{1,0:T(8,128)(2,1)S(1)}, s32[]{:S(2)}) async-start(bf16[256,576]{1,0:T(8,128)(2,1)} %copy-done.6), calls=%async_computation.8 | async-start | bytes 491520 | tf_op jit(solution)/shard_map/slice | solution.py:589
  96.7 22.6 %collective-permute-start.8 = (bf16[128,1792]{1,0:T(8,128)(2,1)}, bf16[128,1792]{1,0:T(8,128)(2,1)}, u32[]{:S(2)}, u32[]{:S(2)}) collective-permute-start(bf16[128,1792]{1,0:T(8,128)(2,1)} %get-tuple-element.102), channel_id=1, source_target_pairs={{64,0},{96,32},{0,64},{32,96},{65,1},{97,33},{1,65},{33,97},{66,2}... | collective-permute-start | bytes 1376264 | tf_op jit(solution)/shard_map/ppermute | solution.py:48
  119.2 15.8 %collective-permute-start.10 = (bf16[256,1792]{1,0:T(8,128)(2,1)S(1)}, bf16[256,1792]{1,0:T(8,128)(2,1)S(1)}, u32[]{:S(2)}, u32[]{:S(2)}) collective-permute-start(bf16[256,1792]{1,0:T(8,128)(2,1)S(1)} %reshape.263), channel_id=1, source_target_pairs={{0,96},{1,33},{2,98},{3,35},{4,100},{5,37},{6,102},{7,39},{8,104},... | collective-permute-start | bytes 2752520 | tf_op jit(solution)/shard_map/ppermute | solution.py:594
  121.1 34.3 %all-to-all-start.4 = ((bf16[32,24,576]{2,1,0:T(8,128)(2,1)}), bf16[32,24,576]{2,1,0:T(8,128)(2,1)S(1)}, u32[]{:S(2)}, u32[]{:S(2)}) async-start(bf16[32,24,576]{2,1,0:T(8,128)(2,1)} %maximum_bitcast_fusion), calls=%async_computation.4 | async-start | bytes 1966080 | tf_op jit(solution)/shard_map/all_to_all | solution.py:595
  138.4 6.5 %collective-permute-start.11 = (bf16[256,512]{1,0:T(8,128)(2,1)S(1)}, bf16[256,512]{1,0:T(8,128)(2,1)S(1)}, u32[]{:S(2)}, u32[]{:S(2)}) collective-permute-start(bf16[256,512]{1,0:T(8,128)(2,1)S(1)} %pad_maximum_fusion.4), channel_id=1, source_target_pairs={{0,32},{1,97},{2,34},{3,99},{4,36},{5,101},{6,38},{7,103},{8,40},{... | collective-permute-start | bytes 786440 | tf_op jit(solution)/shard_map/ppermute | solution.py:606
  145.1 6.5 %collective-permute-start.14 = (bf16[256,256]{1,0:T(8,128)(2,1)S(1)}, bf16[256,256]{1,0:T(8,128)(2,1)S(1)}, u32[]{:S(2)}, u32[]{:S(2)}) collective-permute-start(bf16[256,256]{1,0:T(8,128)(2,1)S(1)} %fusion.65), channel_id=1, source_target_pairs={{64,0},{96,32},{0,64},{32,96},{65,1},{97,33},{1,65},{33,97},{66,2}... | collective-permute-start | bytes 393224 | tf_op jit(solution)/shard_map/ppermute | solution.py:48
  145.4 8.4 %collective-permute-start.12 = (bf16[256,256]{1,0:T(8,128)(2,1)S(1)}, bf16[256,256]{1,0:T(8,128)(2,1)S(1)}, u32[]{:S(2)}, u32[]{:S(2)}) collective-permute-start(bf16[256,256]{1,0:T(8,128)(2,1)S(1)} %fusion.65), channel_id=1, source_target_pairs={{32,0},{64,32},{96,64},{0,96},{33,1},{65,33},{97,65},{1,97},{34,2}... | collective-permute-start | bytes 393224 | tf_op jit(solution)/shard_map/ppermute | solution.py:48
  147.0 7.6 %collective-permute-start.13 = (bf16[256,256]{1,0:T(8,128)(2,1)S(1)}, bf16[256,256]{1,0:T(8,128)(2,1)S(1)}, u32[]{:S(2)}, u32[]{:S(2)}) collective-permute-start(bf16[256,256]{1,0:T(8,128)(2,1)S(1)} %fusion.65), channel_id=1, source_target_pairs={{96,0},{0,32},{32,64},{64,96},{97,1},{1,33},{33,65},{65,97},{98,2}... | collective-permute-start | bytes 393224 | tf_op jit(solution)/shard_map/ppermute | solution.py:48
  147.6 16.6 %collective-permute-start.15 = (bf16[128,1792]{1,0:T(8,128)(2,1)}, bf16[128,1792]{1,0:T(8,128)(2,1)S(1)}, u32[]{:S(2)}, u32[]{:S(2)}) collective-permute-start(bf16[128,1792]{1,0:T(8,128)(2,1)} %get-tuple-element.119), channel_id=1, source_target_pairs={{64,0},{96,32},{0,64},{32,96},{65,1},{97,33},{1,65},{33,97},{66,2}... | collective-permute-start | bytes 1376264 | tf_op jit(solution)/shard_map/ppermute | solution.py:48
  155.5 9.2 %copy-start.8 = (bf16[256,896]{1,0:T(8,128)(2,1)S(1)}, bf16[256,896]{1,0:T(8,128)(2,1)}, u32[]{:S(2)}) copy-start(bf16[256,896]{1,0:T(8,128)(2,1)} %pad_maximum_fusion.2) | copy-start | bytes 1376260
  168.6 12.7 %copy-start.10 = (f32[512]{0:T(512)S(1)}, f32[512]{0:T(512)}, u32[]{:S(2)}) copy-start(f32[512]{0:T(512)} %param.21) | copy-start | bytes 6148
  171.6 27.1 %all-to-all-start.5 = ((bf16[128,2,1792]{2,1,0:T(2,128)(2,1)}), bf16[128,2,1792]{2,1,0:T(2,128)(2,1)S(1)}, u32[]{:S(2)}, u32[]{:S(2)}) async-start(bf16[128,2,1792]{2,1,0:T(2,128)(2,1)} %reshape.271), calls=%async_computation.5 | async-start | bytes 1835008 | tf_op jit(solution)/shard_map/all_to_all | solution.py:620
